TPU v7x, 32 devices: a whole 2x2x4 slice. The times are simulated.
32 devices in a mesh: leaf: 8 (over z, core), row: 4 (over y, x).
Axes of the slice: x: 2, y: 2, z: 4, core: 2. Of those that a mesh axis runs over, the one named last changes fastest.
Arguments:
- inputs: bfloat16 [8, 1024, 2048], P('leaf', 'row'), may hold values from -6 to 6
- cotangent: bfloat16 [8, 1024, 2048], P('leaf', 'row'), may hold values from -6 to 6
- seg_lengths: int32 [8, 13], P('leaf'), may hold values from 1 to 256, 1024 in all within a row
- seg_parents: int32 [8, 13], P('leaf'), may hold values from 0 to 4, as said below
- w_query: float32 [2048, 2048], P(('leaf', 'row')), may hold values from -0.125 to 0.125
- w_key: float32 [2048, 2048], P(('leaf', 'row')), may hold values from -0.125 to 0.125
- w_value: float32 [2048, 2048], P(('leaf', 'row')), may hold values from -0.125 to 0.125
- w_output: float32 [2048, 2048], P(('leaf', 'row')), may hold values from -0.125 to 0.125
- gain_query: float32 [2048], P(('leaf', 'row')), may hold values from 0.1 to 1.9
- gain_key: float32 [2048], P(('leaf', 'row')), may hold values from 0.1 to 1.9
- gain_attn: float32 [2048], P(('leaf', 'row')), may hold values from 0.1 to 1.9
- w_gate: float32 [2048, 8192], P(('leaf', 'row')), may hold values from -0.125 to 0.125
- w_up: float32 [2048, 8192], P(('leaf', 'row')), may hold values from -0.125 to 0.125
- w_down: float32 [2048, 8192], P(('leaf', 'row')), may hold values from -0.0625 to 0.0625
- gain_mlp: float32 [2048], P(('leaf', 'row')), may hold values from 0.1 to 1.9
Outputs:
- outputs: bfloat16 [8, 1024, 2048], P('leaf', 'row')
- grad_inputs: bfloat16 [8, 1024, 2048], P('leaf', 'row')
- grad_query: float32 [2048, 2048], P(('leaf', 'row'))
- grad_key: float32 [2048, 2048], P(('leaf', 'row'))
- grad_value: float32 [2048, 2048], P(('leaf', 'row'))
- grad_output: float32 [2048, 2048], P(('leaf', 'row'))
- grad_gain_query: float32 [2048], P(('leaf', 'row'))
- grad_gain_key: float32 [2048], P(('leaf', 'row'))
- grad_gain_attn: float32 [2048], P(('leaf', 'row'))
- grad_gate: float32 [2048, 8192], P(('leaf', 'row'))
- grad_up: float32 [2048, 8192], P(('leaf', 'row'))
- grad_down: float32 [2048, 8192], P(('leaf', 'row'))
- grad_gain_mlp: float32 [2048], P(('leaf', 'row'))
Inputs may be any that keep to these rules, and one draw needn't show every extreme that they name: `seg_lengths`: each tree's lengths sum to 1024; in every tree the longest segment has exactly 256 tokens. `seg_parents`: segment 0 of a tree is its root and its own parent; segments 1 to 4 have parent 0; every later segment's parent is one of segments 1 to 4.
All inputs are finite; a program needn't handle non-finite values.
Results may differ from a plain program's by a relative error of at most 0.018.
Values may be sent and summed in bfloat16 or wider, within the bound.
A program may use at most 704 MiB of HBM per device.

v0:
```python
import math

import jax
import jax.numpy as jnp
from jax import lax
from jax.sharding import PartitionSpec as P

HEADS = 16
HEAD_DIM = 128


epsilon = 1e-06
rope_theta = 500000.0
masked_fill = -1e30
highest = lax.Precision.HIGHEST


def normalize(vector, gain_row):
    scaled = lax.rsqrt(jnp.mean(vector * vector, axis=-1, keepdims=True) + epsilon)
    unit_rows = vector * scaled
    return (unit_rows * gain_row, unit_rows, scaled)


def norm_back(grad_out, unit_rows, scaled, gain_row):
    weighted = grad_out * gain_row
    inner = jnp.mean(weighted * unit_rows, axis=-1, keepdims=True)
    return (scaled * (weighted - unit_rows * inner), jnp.sum(grad_out * unit_rows, axis=0))


def rotate(vector, cos_part, sin_part):
    half_dim = HEAD_DIM // 2
    by_head = vector.reshape(vector.shape[0], HEADS, HEAD_DIM)
    first_half = by_head[..., :half_dim]
    second_half = by_head[..., half_dim:]
    cos_wide = cos_part[:, None, :]
    sin_wide = sin_part[:, None, :]
    turned = jnp.concatenate(
        [
            first_half * cos_wide - second_half * sin_wide,
            second_half * cos_wide + first_half * sin_wide,
        ],
        axis=-1,
    )
    return turned.reshape(vector.shape)


def rotate_back(vector, cos_part, sin_part):
    half_dim = HEAD_DIM // 2
    by_head = vector.reshape(vector.shape[0], HEADS, HEAD_DIM)
    first_half = by_head[..., :half_dim]
    second_half = by_head[..., half_dim:]
    cos_wide = cos_part[:, None, :]
    sin_wide = sin_part[:, None, :]
    turned = jnp.concatenate(
        [
            first_half * cos_wide + second_half * sin_wide,
            second_half * cos_wide - first_half * sin_wide,
        ],
        axis=-1,
    )
    return turned.reshape(vector.shape)


def tree_tables(length_row, parent_row, total, first_row, row_count):
    seg_count = parent_row.shape[0]
    segment_ids = jnp.arange(seg_count, dtype=jnp.int32)
    ends = jnp.cumsum(length_row)
    offsets = ends - length_row
    all_rows = jnp.arange(total, dtype=jnp.int32)
    owned_from = (all_rows[:, None] >= offsets[None, :]).astype(jnp.float32)
    onehot_all = owned_from - jnp.concatenate(
        [owned_from[:, 1:], jnp.zeros((total, 1), jnp.float32)], axis=1
    )
    parent_link = (
        (parent_row[:, None] == segment_ids[None, :])
        | (segment_ids[:, None] == segment_ids[None, :])
    ).astype(jnp.float32)
    reached = parent_link
    for _ in range(4):
        reached = jnp.minimum(jnp.dot(reached, reached, precision=highest), 1.0)
    seg_float = length_row.astype(jnp.float32)
    path_start = jnp.dot(
        reached - jnp.eye(seg_count, dtype=jnp.float32), seg_float, precision=highest
    )
    local_hot = lax.dynamic_slice_in_dim(onehot_all, first_row, row_count, 0)
    my_rows = first_row + jnp.arange(row_count, dtype=jnp.int32)
    position = (
        my_rows.astype(jnp.float32)
        - jnp.dot(local_hot, offsets.astype(jnp.float32), precision=highest)
        + jnp.dot(local_hot, path_start, precision=highest)
    )
    seen = jnp.dot(jnp.dot(local_hot, reached, precision=highest), onehot_all.T, precision=highest)
    allowed = (seen > 0.5) & (all_rows[None, :] <= my_rows[:, None])
    frequency = jnp.exp(
        jnp.arange(HEAD_DIM // 2, dtype=jnp.float32) * (-2.0 * math.log(rope_theta) / HEAD_DIM)
    )
    angles = position[:, None] * frequency[None, :]
    return (allowed, jnp.cos(angles), jnp.sin(angles))


def heads_first(array):
    return jnp.moveaxis(array, 2, 0)


def gate_grads(grad_act, gate_pre, up_pre):
    sigmoid_gate = jax.nn.sigmoid(gate_pre)
    grad_gate_low = (
        grad_act * up_pre * sigmoid_gate * (1.0 + gate_pre * (1.0 - sigmoid_gate))
    ).astype(jnp.bfloat16)
    grad_up_low = (grad_act * gate_pre * sigmoid_gate).astype(jnp.bfloat16)
    return (grad_gate_low, grad_up_low)


def body(
    inputs,
    cotangent,
    seg_lengths,
    seg_parents,
    w_query,
    w_key,
    w_value,
    w_output,
    gain_query,
    gain_key,
    gain_attn,
    w_gate,
    w_up,
    w_down,
    gain_mlp,
):
    trees, rows_dev, width = inputs.shape
    tree_len = rows_dev * lax.axis_size("row")
    first_row = lax.axis_index("row") * rows_dev
    token_count = trees * rows_dev
    contract_last = (((1,), (1,)), ((), ()))
    contract_first = (((0,), (0,)), ((), ()))
    scale = 1.0 / math.sqrt(HEAD_DIM)
    allowed, cos_rows, sin_rows = jax.vmap(
        lambda length_row, parent_row: tree_tables(
            length_row, parent_row, tree_len, first_row, rows_dev
        )
    )(seg_lengths, seg_parents)
    cos_flat = cos_rows.reshape(token_count, cos_rows.shape[-1])
    sin_flat = sin_rows.reshape(token_count, sin_rows.shape[-1])
    tokens = inputs.reshape(token_count, width)
    attn_send = (
        w_query.astype(jnp.bfloat16),
        w_key.astype(jnp.bfloat16),
        w_value.astype(jnp.bfloat16),
        w_output.astype(jnp.bfloat16),
        gain_query.astype(jnp.bfloat16),
        gain_key.astype(jnp.bfloat16),
        gain_attn.astype(jnp.bfloat16),
        gain_mlp.astype(jnp.bfloat16),
    )
    attn_full = (
        lax.all_gather(attn_send[0], ("leaf", "row"), axis=0, tiled=True),
        lax.all_gather(attn_send[1], ("leaf", "row"), axis=0, tiled=True),
        lax.all_gather(attn_send[2], ("leaf", "row"), axis=0, tiled=True),
        lax.all_gather(attn_send[3], ("leaf", "row"), axis=0, tiled=True),
        lax.all_gather(attn_send[4], ("leaf", "row"), axis=0, tiled=True),
        lax.all_gather(attn_send[5], ("leaf", "row"), axis=0, tiled=True),
        lax.all_gather(attn_send[6], ("leaf", "row"), axis=0, tiled=True),
        lax.all_gather(attn_send[7], ("leaf", "row"), axis=0, tiled=True),
    )
    query_mat, key_mat, value_mat, output_mat, query_gain, key_gain, attn_gain, mlp_gain = attn_full
    query_pre = jnp.dot(tokens, query_mat, preferred_element_type=jnp.float32)
    key_pre = jnp.dot(tokens, key_mat, preferred_element_type=jnp.float32)
    value_low = jnp.dot(tokens, value_mat, preferred_element_type=jnp.float32).astype(jnp.bfloat16)
    query_normed, query_unit, query_scale = normalize(query_pre, query_gain.astype(jnp.float32))
    key_normed, key_unit, key_scale = normalize(key_pre, key_gain.astype(jnp.float32))
    query_low = rotate(query_normed, cos_flat, sin_flat).astype(jnp.bfloat16)
    key_low = rotate(key_normed, cos_flat, sin_flat).astype(jnp.bfloat16)
    keys_all, values_all = (
        lax.all_gather(key_low.reshape(trees, rows_dev, width), "row", axis=1, tiled=True),
        lax.all_gather(value_low.reshape(trees, rows_dev, width), "row", axis=1, tiled=True),
    )
    query_heads = heads_first(query_low.reshape(trees, rows_dev, HEADS, HEAD_DIM))
    key_heads = heads_first(keys_all.reshape(trees, tree_len, HEADS, HEAD_DIM))
    value_heads = heads_first(values_all.reshape(trees, tree_len, HEADS, HEAD_DIM))

    def masked_scores(query_head, key_head):
        scores = (
            jnp.einsum("tqd,tkd->tqk", query_head, key_head, preferred_element_type=jnp.float32)
            * scale
        )
        return jnp.where(allowed, scores, masked_fill)

    def attend(carry, items):
        query_head, key_head, value_head = items
        scores = masked_scores(query_head, key_head)
        log_total = jax.nn.logsumexp(scores, axis=-1, keepdims=True)
        probs_low = jnp.where(allowed, jnp.exp(scores - log_total), 0.0).astype(jnp.bfloat16)
        context_head = jnp.einsum(
            "tqk,tkd->tqd", probs_low, value_head, preferred_element_type=jnp.float32
        ).astype(jnp.bfloat16)
        return (carry, (context_head, log_total))

    _, (context_heads, log_totals) = lax.scan(
        attend, jnp.zeros((), jnp.float32), (query_heads, key_heads, value_heads)
    )
    context_low = jnp.moveaxis(context_heads, 0, 2).reshape(token_count, width)
    attn_pre = jnp.dot(context_low, output_mat, preferred_element_type=jnp.float32)
    attn_gain32 = attn_gain.astype(jnp.float32)
    attn_normed, attn_unit, attn_scale = normalize(attn_pre, attn_gain32)
    hidden = tokens.astype(jnp.float32) + attn_normed
    hidden_low = hidden.astype(jnp.bfloat16)
    mlp_send = (w_gate.astype(jnp.bfloat16), w_up.astype(jnp.bfloat16), w_down.astype(jnp.bfloat16))
    gate_mat, up_mat, down_mat = (
        lax.all_gather(mlp_send[0], ("leaf", "row"), axis=0, tiled=True),
        lax.all_gather(mlp_send[1], ("leaf", "row"), axis=0, tiled=True),
        lax.all_gather(mlp_send[2], ("leaf", "row"), axis=0, tiled=True),
    )
    gate_pre = jnp.dot(hidden_low, gate_mat, preferred_element_type=jnp.float32)
    up_pre = jnp.dot(hidden_low, up_mat, preferred_element_type=jnp.float32)
    activated = (jax.nn.silu(gate_pre) * up_pre).astype(jnp.bfloat16)
    mlp_pre = lax.dot_general(
        activated, down_mat, contract_last, preferred_element_type=jnp.float32
    )
    mlp_gain32 = mlp_gain.astype(jnp.float32)
    mlp_normed, mlp_unit, mlp_scale = normalize(mlp_pre, mlp_gain32)
    final = hidden + mlp_normed
    outputs = final.astype(jnp.bfloat16).reshape(trees, rows_dev, width)
    grad_final = cotangent.reshape(token_count, width).astype(jnp.float32)
    grad_mlp, grad_mlp_gain = norm_back(grad_final, mlp_unit, mlp_scale, mlp_gain32)
    grad_mlp_low = grad_mlp.astype(jnp.bfloat16)
    hidden_units = gate_pre.shape[1]
    grad_act = jnp.dot(grad_mlp_low, down_mat, preferred_element_type=jnp.float32)
    grad_gate_low, grad_up_low = gate_grads(grad_act, gate_pre, up_pre)
    grad_hidden = (
        grad_final
        + lax.dot_general(
            grad_gate_low, gate_mat, contract_last, preferred_element_type=jnp.float32
        )
        + lax.dot_general(grad_up_low, up_mat, contract_last, preferred_element_type=jnp.float32)
    )
    mlp_shards = lax.psum_scatter(
        jnp.concatenate(
            [
                lax.dot_general(
                    hidden_low, grad_gate_low, contract_first, preferred_element_type=jnp.float32
                ),
                lax.dot_general(
                    hidden_low, grad_up_low, contract_first, preferred_element_type=jnp.float32
                ),
                lax.dot_general(
                    grad_mlp_low, activated, contract_first, preferred_element_type=jnp.float32
                ),
            ],
            axis=1,
        ),
        ("leaf", "row"),
        scatter_dimension=0,
        tiled=True,
    )
    grad_gate = mlp_shards[:, :hidden_units]
    grad_up = mlp_shards[:, hidden_units : 2 * hidden_units]
    grad_down = mlp_shards[:, 2 * hidden_units :]
    attn_fresh = lax.optimization_barrier((attn_send, grad_hidden))[0]
    attn_back = (
        lax.all_gather(attn_fresh[0], ("leaf", "row"), axis=0, tiled=True),
        lax.all_gather(attn_fresh[1], ("leaf", "row"), axis=0, tiled=True),
        lax.all_gather(attn_fresh[2], ("leaf", "row"), axis=0, tiled=True),
        lax.all_gather(attn_fresh[3], ("leaf", "row"), axis=0, tiled=True),
        lax.all_gather(attn_fresh[4], ("leaf", "row"), axis=0, tiled=True),
        lax.all_gather(attn_fresh[5], ("leaf", "row"), axis=0, tiled=True),
        lax.all_gather(attn_fresh[6], ("leaf", "row"), axis=0, tiled=True),
        lax.all_gather(attn_fresh[7], ("leaf", "row"), axis=0, tiled=True),
    )
    (
        query_back,
        key_back,
        value_back,
        output_back,
        query_gain_back,
        key_gain_back,
        attn_gain_back,
        mlp_gain_back,
    ) = attn_back
    grad_attn, grad_attn_gain = norm_back(
        grad_hidden, attn_unit, attn_scale, attn_gain_back.astype(jnp.float32)
    )
    grad_attn_low = grad_attn.astype(jnp.bfloat16)
    grad_context_low = lax.dot_general(
        grad_attn_low, output_back, contract_last, preferred_element_type=jnp.float32
    ).astype(jnp.bfloat16)
    grad_context_heads = heads_first(grad_context_low.reshape(trees, rows_dev, HEADS, HEAD_DIM))

    def attend_back(carry, items):
        query_head, key_head, value_head, log_total, grad_head = items
        scores = masked_scores(query_head, key_head)
        probs_full = jnp.where(allowed, jnp.exp(scores - log_total), 0.0)
        probs_low = probs_full.astype(jnp.bfloat16)
        grad_probs = jnp.einsum(
            "tqd,tkd->tqk", grad_head, value_head, preferred_element_type=jnp.float32
        )
        inner = jnp.sum(probs_full * grad_probs, axis=-1, keepdims=True)
        grad_scores = (probs_full * (grad_probs - inner)).astype(jnp.bfloat16)
        grad_query_head = (
            jnp.einsum("tqk,tkd->tqd", grad_scores, key_head, preferred_element_type=jnp.float32)
            * scale
        )
        grad_key_head = (
            jnp.einsum("tqk,tqd->tkd", grad_scores, query_head, preferred_element_type=jnp.float32)
            * scale
        )
        grad_value_head = jnp.einsum(
            "tqk,tqd->tkd", probs_low, grad_head, preferred_element_type=jnp.float32
        )
        return (carry, (grad_query_head, grad_key_head, grad_value_head))

    _, (grad_query_heads, grad_key_heads, grad_value_heads) = lax.scan(
        attend_back,
        jnp.zeros((), jnp.float32),
        (query_heads, key_heads, value_heads, log_totals, grad_context_heads),
    )
    grad_query_flat = jnp.moveaxis(grad_query_heads, 0, 2).reshape(token_count, width)
    grad_key_tree = jnp.moveaxis(grad_key_heads, 0, 2).reshape(trees, tree_len, width)
    grad_value_tree = jnp.moveaxis(grad_value_heads, 0, 2).reshape(trees, tree_len, width)
    grad_key_mine, grad_value_mine = (
        lax.psum_scatter(
            grad_key_tree.astype(jnp.bfloat16), "row", scatter_dimension=1, tiled=True
        ).astype(jnp.float32),
        lax.psum_scatter(
            grad_value_tree.astype(jnp.bfloat16), "row", scatter_dimension=1, tiled=True
        ).astype(jnp.float32),
    )
    grad_query_pre, grad_query_gain = norm_back(
        rotate_back(grad_query_flat, cos_flat, sin_flat),
        query_unit,
        query_scale,
        query_gain_back.astype(jnp.float32),
    )
    grad_key_pre, grad_key_gain = norm_back(
        rotate_back(grad_key_mine.reshape(token_count, width), cos_flat, sin_flat),
        key_unit,
        key_scale,
        key_gain_back.astype(jnp.float32),
    )
    grad_query_low = grad_query_pre.astype(jnp.bfloat16)
    grad_key_low = grad_key_pre.astype(jnp.bfloat16)
    grad_value_low = grad_value_mine.reshape(token_count, width).astype(jnp.bfloat16)
    grad_tokens = grad_hidden + lax.dot_general(
        grad_query_low, query_back, contract_last, preferred_element_type=jnp.float32
    )
    grad_tokens = grad_tokens + lax.dot_general(
        grad_key_low, key_back, contract_last, preferred_element_type=jnp.float32
    )
    grad_tokens = grad_tokens + lax.dot_general(
        grad_value_low, value_back, contract_last, preferred_element_type=jnp.float32
    )
    grad_inputs = grad_tokens.astype(jnp.bfloat16).reshape(trees, rows_dev, width)
    query_term = lax.dot_general(
        tokens, grad_query_low, contract_first, preferred_element_type=jnp.float32
    )
    key_term = lax.dot_general(
        tokens, grad_key_low, contract_first, preferred_element_type=jnp.float32
    )
    value_term = lax.dot_general(
        tokens, grad_value_low, contract_first, preferred_element_type=jnp.float32
    )
    output_term = lax.dot_general(
        context_low, grad_attn_low, contract_first, preferred_element_type=jnp.float32
    )
    shards = (
        lax.psum_scatter(query_term, ("leaf", "row"), scatter_dimension=0, tiled=True),
        lax.psum_scatter(key_term, ("leaf", "row"), scatter_dimension=0, tiled=True),
        lax.psum_scatter(value_term, ("leaf", "row"), scatter_dimension=0, tiled=True),
        lax.psum_scatter(output_term, ("leaf", "row"), scatter_dimension=0, tiled=True),
        lax.psum_scatter(grad_query_gain, ("leaf", "row"), scatter_dimension=0, tiled=True),
        lax.psum_scatter(grad_key_gain, ("leaf", "row"), scatter_dimension=0, tiled=True),
        lax.psum_scatter(grad_attn_gain, ("leaf", "row"), scatter_dimension=0, tiled=True),
        lax.psum_scatter(grad_mlp_gain, ("leaf", "row"), scatter_dimension=0, tiled=True),
    )
    return (
        outputs,
        grad_inputs,
        shards[0],
        shards[1],
        shards[2],
        shards[3],
        shards[4],
        shards[5],
        shards[6],
        grad_gate,
        grad_up,
        grad_down,
        shards[7],
    )


def solution(mesh):
    return jax.shard_map(
        body,
        mesh=mesh,
        in_specs=(
            P("leaf", "row", None),
            P("leaf", "row", None),
            P("leaf", None),
            P("leaf", None),
            P(("leaf", "row"), None),
            P(("leaf", "row"), None),
            P(("leaf", "row"), None),
            P(("leaf", "row"), None),
            P(("leaf", "row")),
            P(("leaf", "row")),
            P(("leaf", "row")),
            P(("leaf", "row"), None),
            P(("leaf", "row"), None),
            P(("leaf", "row"), None),
            P(("leaf", "row")),
        ),
        out_specs=(
            P("leaf", "row", None),
            P("leaf", "row", None),
            P(("leaf", "row"), None),
            P(("leaf", "row"), None),
            P(("leaf", "row"), None),
            P(("leaf", "row"), None),
            P(("leaf", "row")),
            P(("leaf", "row")),
            P(("leaf", "row")),
            P(("leaf", "row"), None),
            P(("leaf", "row"), None),
            P(("leaf", "row"), None),
            P(("leaf", "row")),
        ),
        check_vma=False,
    )
```

profile of v0, /device:TPU:0, one launch (start us, length us, event | category | flops | bytes accessed | tf_op | source)
XLA Modules:
  0.0 4730.9 jit_solution(11095280209846855148)
XLA Ops:
  12.1 79.1 %all-gather.21.cloned.1.call-done = bf16[2048,2048]{1,0:T(8,128)(2,1)} async-done(((bf16[64,2048]{1,0:T(8,128)(2,1)}), bf16[2048,2048]{1,0:T(8,128)(2,1)}) %all-gather.21.cloned.1.call-update) | async-done | bytes 8388624 | tf_op jit(solution)/shard_map/all_gather | solution.py:159
  91.2 6.7 convolution_convert_fusion.2
  99.0 39.9 all-reduce.14
  141.6 28.8 all-gather.17.cloned.1.call-done
  170.4 5.8 multiply_reduce_fusion.9
  181.2 68.4 %all-gather.15.cloned.1.call-done = bf16[2048,2048]{1,0:T(8,128)(2,1)} async-done(((bf16[64,2048]{1,0:T(8,128)(2,1)}), bf16[2048,2048]{1,0:T(8,128)(2,1)}) %all-gather.15.cloned.1.call-update) | async-done | bytes 8388624 | tf_op jit(solution)/shard_map/all_gather | solution.py:157
  249.5 5.8 multiply_reduce_fusion.10
  278.7 24.4 all-gather.39.cloned.1.call-done
  303.1 3.6 copy.110
  309.8 48.2 %all-gather.19.cloned.1.call-done = bf16[1,1024,2048]{1,2,0:T(8,128)(2,1)} async-done(((bf16[1,256,2048]{1,2,0:T(8,128)(2,1)}), bf16[1,1024,2048]{1,2,0:T(8,128)(2,1)}) %all-gather.19.cloned.1.call-update) | async-done | bytes 4194320 | tf_op jit(solution)/shard_map/all_gather | solution.py:175
  358.0 6.4 copy.66
  364.4 61.1 %while.27 = (s32[]{:T(128)}, bf16[16,1,256,128]{2,3,0,1:T(8,128)(2,1)S(1)}, f32[16,1,256,1]{2,3,1,0:T(1,128)}, pred[1,256,1024]{2,1,0:T(32,128)(4,1)S(1)}, bf16[...) while((s32[]{:T(128)}, ...), condition=%wide.region_6.7_spmd, body=%wide.region_3.6_spmd.sunk | while | flops 136349440 | bytes 4601961 | solution.py:199
  425.5 13.4 all-gather.23.cloned.1.call-done
  438.9 6.1 multiply_reduce_fusion.8
  446.4 189.3 %all-gather.25.cloned.1.call-done = bf16[2048,8192]{1,0:T(8,128)(2,1)} async-done(((bf16[64,8192]{1,0:T(8,128)(2,1)}), bf16[2048,8192]{1,0:T(8,128)(2,1)}) %all-gather.25.cloned.1.call-update) | async-done | bytes 33554448 | tf_op jit(solution)/shard_map/all_gather | solution.py:210
  635.8 18.0 fusion.95
  653.8 178.4 %all-gather.27.cloned.1.call-done = bf16[2048,8192]{1,0:T(8,128)(2,1)} async-done(((bf16[64,8192]{1,0:T(8,128)(2,1)}), bf16[2048,8192]{1,0:T(8,128)(2,1)}) %all-gather.27.cloned.1.call-update) | async-done | bytes 33554448 | tf_op jit(solution)/shard_map/all_gather | solution.py:211
  832.2 24.2 multiply_convert_fusion.3
  856.5 171.6 %all-gather.29.cloned.1.call-done = bf16[2048,8192]{1,0:T(8,128)(2,1)} async-done(((bf16[64,8192]{1,0:T(8,128)(2,1)}), bf16[2048,8192]{1,0:T(8,128)(2,1)}) %all-gather.29.cloned.1.call-update) | async-done | bytes 33554448 | tf_op jit(solution)/shard_map/all_gather | solution.py:212
  1028.1 17.2 multiply_reduce_fusion.7
  1050.4 27.1 multiply_convert_fusion.1
  1077.5 17.5 convert_add_fusion
  1095.1 17.8 convolution_add_fusion
  1113.8 39.2 all-reduce.13
  1156.4 32.5 all-gather.31.cloned.1.call-done
  1188.9 5.7 fusion.51
  1195.6 140.7 %while.28 = (s32[]{:T(128)}, f32[16,1,256,128]{2,3,0,1:T(8,128)}, bf16[16,1,1024,128]{2,3,0,1:T(8,128)(2,1)}, bf16[16,1,1024,128]{2,3,0,1:T(8,128)(2,1)}, pred[1...) while((s32[]{:T(128)}, f32[16,1,256,128]{2,3,0,1:T(8,128)}, ...), condition=%wide.region_13.14_spmd, body=%wide.region_11.13_spmd.sunk | while | flops 338460416 | bytes 11673737 | solution.py:312
  1338.5 26.6 fusion.98
  1365.2 26.4 fusion.97
  1391.6 27.2 fusion.99
  1418.8 133.9 %pad_maximum_fusion = f32[2048,24576]{1,0:T(8,128)} fusion(f32[2048,8192]{1,0:T(8,128)} %fusion.99, f32[2048,8192]{1,0:T(8,128)} %fusion.98, f32[2048,8192]{1,0:T(8,128)} %fusion.97), kind=kLoop, calls=%fused_computation.61 | loop fusion | flops 100663296 | bytes 402653184 | tf_op jit(solution)/shard_map/concatenate | solution.py:238
  1554.3 8.2 fusion.96
  1563.7 9.7 convolution_bitcast_fusion.1
  1573.4 18.1 copy.85
  1603.6 8.1 convolution_bitcast_fusion.2
  1611.7 17.7 copy.83
  1637.0 8.2 convolution_bitcast_fusion.3
  1645.2 17.5 copy.81
  1663.5 39.2 all-reduce.12
  1705.1 9.3 convolution_add_fusion.3
  1714.4 9.9 convolution_add_fusion.2
  1724.3 9.5 fusion.46
  1733.8 1544.8 %reduce-scatter.20.cloned.1.call-done = f32[64,24576]{1,0:T(8,128)} async-done(((f32[2048,24576]{1,0:T(8,128)}), f32[64,24576]{1,0:T(8,128)}) %reduce-scatter.20.cloned.1.call-update) | async-done | bytes 6291472 | tf_op jit(solution)/shard_map/reduce_scatter | solution.py:237
  3278.6 5.7 fusion.94
  3284.3 353.7 %reduce-scatter.18.cloned.1.call-done = f32[64,2048]{1,0:T(8,128)} async-done(((f32[2048,2048]{1,0:T(8,128)}), f32[64,2048]{1,0:T(8,128)}) %reduce-scatter.18.cloned.1.call-update) | async-done | bytes 524304 | tf_op jit(solution)/shard_map/reduce_scatter | solution.py:369
  3637.9 361.8 %reduce-scatter.26.cloned.1.call-done = f32[64,2048]{1,0:T(8,128)} async-done(((f32[2048,2048]{1,0:T(8,128)}), f32[64,2048]{1,0:T(8,128)}) %reduce-scatter.26.cloned.1.call-update) | async-done | bytes 524304
  3999.8 362.0 %reduce-scatter.24.cloned.1.call-done = f32[64,2048]{1,0:T(8,128)} async-done(((f32[2048,2048]{1,0:T(8,128)}), f32[64,2048]{1,0:T(8,128)}) %reduce-scatter.24.cloned.1.call-update) | async-done | bytes 524304
  4361.7 361.8 %reduce-scatter.22.cloned.1.call-done = f32[64,2048]{1,0:T(8,128)} async-done(((f32[2048,2048]{1,0:T(8,128)}), f32[64,2048]{1,0:T(8,128)}) %reduce-scatter.22.cloned.1.call-update) | async-done | bytes 524304
  (552 shorter events, 279.3 us)
Async XLA Ops:
  7.2 3.9 copy-start.34
  7.2 4.7 copy-start.43
  7.2 84.0 %copy-start.2 = (bf16[1,256,2048]{2,1,0:T(8,128)(2,1)S(1)}, bf16[1,256,2048]{2,1,0:T(8,128)(2,1)}, u32[]{:S(2)}) copy-start(bf16[1,256,2048]{2,1,0:T(8,128)(2,1)} %param.19) | copy-start | bytes 3145732
  7.2 84.0 %all-gather.21.cloned.1.call-start = ((), (), s32[]{:S(2)}) async-start(), calls=%async_computation.10 | async-start | bytes 8650752 | tf_op jit(solution)/shard_map/all_gather | solution.py:159
  9.2 161.3 %all-gather.17.cloned.1.call-start = ((), (), s32[]{:S(2)}) async-start(), calls=%async_computation.8 | async-start | bytes 8650752 | tf_op jit(solution)/shard_map/all_gather | solution.py:158
  11.0 238.5 %all-gather.15.cloned.1.call-start = ((), (), s32[]{:S(2)}) async-start(), calls=%async_computation.7 | async-start | bytes 8650752 | tf_op jit(solution)/shard_map/all_gather | solution.py:157
  11.8 291.3 %all-gather.39.cloned.1.call-start = ((), (), s32[]{:S(2)}) async-start(), calls=%async_computation.23 | async-start | bytes 5242880 | tf_op jit(solution)/shard_map/all_gather | solution.py:176
  12.1 85.9 %copy-start.44 = (f32[64]{0:T(128)S(1)}, f32[64]{0:T(128)}, u32[]{:S(2)}) copy-start(f32[64]{0:T(128)} %param.27) | copy-start | bytes 772
  12.1 85.9 %copy-start.45 = (f32[64]{0:T(128)S(1)}, f32[64]{0:T(128)}, u32[]{:S(2)}) copy-start(f32[64]{0:T(128)} %param.28) | copy-start | bytes 772
  12.1 86.0 %copy-start.46 = (f32[64]{0:T(128)S(1)}, f32[64]{0:T(128)}, u32[]{:S(2)}) copy-start(f32[64]{0:T(128)} %param.29) | copy-start | bytes 772
  12.1 86.0 %copy-start.47 = (f32[64]{0:T(128)S(1)}, f32[64]{0:T(128)}, u32[]{:S(2)}) copy-start(f32[64]{0:T(128)} %param.33) | copy-start | bytes 772
  97.9 41.5 copy-start.48
  97.9 260.0 %all-gather.19.cloned.1.call-start = ((), (), s32[]{:S(2)}) async-start(), calls=%async_computation.9 | async-start | bytes 5242880 | tf_op jit(solution)/shard_map/all_gather | solution.py:175
  98.0 41.0 copy-start.51
  98.1 40.9 copy-start.53
  98.1 41.2 copy-start.49
  141.6 119.6 %copy-start.30 = (f32[256,64]{0,1:T(8,128)}, f32[256,64]{0,1:T(8,128)S(1)}, u32[]{:S(2)}) copy-start(f32[256,64]{0,1:T(8,128)S(1)} %get-tuple-element.303) | copy-start | bytes 196612
  141.6 119.6 %copy-start.32 = (f32[256,64]{0,1:T(8,128)}, f32[256,64]{0,1:T(8,128)S(1)}, u32[]{:S(2)}) copy-start(f32[256,64]{0,1:T(8,128)S(1)} %get-tuple-element.304) | copy-start | bytes 196612
  265.3 173.6 %all-gather.23.cloned.1.call-start = ((), (), s32[]{:S(2)}) async-start(), calls=%async_computation.11 | async-start | bytes 8650752 | tf_op jit(solution)/shard_map/all_gather | solution.py:160
  267.2 368.6 %all-gather.25.cloned.1.call-start = ((), (), s32[]{:S(2)}) async-start(), calls=%async_computation.12 | async-start | bytes 34603008 | tf_op jit(solution)/shard_map/all_gather | solution.py:210
  268.4 563.9 %all-gather.27.cloned.1.call-start = ((), (), s32[]{:S(2)}) async-start(), calls=%async_computation.13 | async-start | bytes 34603008 | tf_op jit(solution)/shard_map/all_gather | solution.py:211
  271.2 756.9 %all-gather.29.cloned.1.call-start = ((), (), s32[]{:S(2)}) async-start(), calls=%async_computation.14 | async-start | bytes 34603008 | tf_op jit(solution)/shard_map/all_gather | solution.py:212
  272.4 916.5 %all-gather.31.cloned.1.call-start = ((), (), s32[]{:S(2)}) async-start(), calls=%async_computation.15 | async-start | bytes 8650752 | tf_op jit(solution)/shard_map/all_gather | solution.py:264
  425.5 13.4 copy-start.14
  425.5 19.6 copy-start
  1028.1 17.2 copy-start.23
  1050.4 27.1 copy-start.16
  1050.4 27.1 copy-start.24
  1095.1 17.9 copy-start.54
  1095.1 18.2 copy-start.52
  1095.1 18.5 copy-start.50
  1112.9 449.9 %reduce-scatter.16.cloned.1.call-start = ((), (), s32[]{:S(2)}) async-start(), calls=%async_computation.19 | async-start | bytes 5242880 | tf_op jit(solution)/shard_map/reduce_scatter | solution.py:324
  1156.4 32.5 copy-start.18
  1336.3 255.9 %reduce-scatter.14.cloned.1.call-start = ((), (), s32[]{:S(2)}) async-start(), calls=%async_computation.17 | async-start | bytes 5242880 | tf_op jit(solution)/shard_map/reduce_scatter | solution.py:321
  1336.9 368.2 %all-gather.33.cloned.1.call-start = ((), (), s32[]{:S(2)}) async-start(), calls=%async_computation.16 | async-start | bytes 8650752 | tf_op jit(solution)/shard_map/all_gather | solution.py:261
  1337.6 376.7 %all-gather.35.cloned.1.call-start = ((), (), s32[]{:S(2)}) async-start(), calls=%async_computation.18 | async-start | bytes 8650752 | tf_op jit(solution)/shard_map/all_gather | solution.py:262
  1338.2 386.1 %all-gather.37.cloned.1.call-start = ((), (), s32[]{:S(2)}) async-start(), calls=%async_computation.20 | async-start | bytes 8650752 | tf_op jit(solution)/shard_map/all_gather | solution.py:263
  1365.1 26.5 copy-start.17
  1365.1 1913.4 %reduce-scatter.20.cloned.1.call-start = ((), (), s32[]{:S(2)}) async-start(), calls=%async_computation.22 | async-start | bytes 207618048 | tf_op jit(solution)/shard_map/reduce_scatter | solution.py:237
  1552.8 2085.2 %reduce-scatter.18.cloned.1.call-start = ((), (), s32[]{:S(2)}) async-start(), calls=%async_computation.21 | async-start | bytes 17301504 | tf_op jit(solution)/shard_map/reduce_scatter | solution.py:369
  1562.5 2437.3 %reduce-scatter.26.cloned.1.call-start = ((), (), s32[]{:S(2)}) async-start(), calls=%async_computation.26 | async-start | bytes 17301504
  1591.6 2770.1 %reduce-scatter.24.cloned.1.call-start = ((), (), s32[]{:S(2)}) async-start(), calls=%async_computation.25 | async-start | bytes 17301504
  1629.4 3094.1 %reduce-scatter.22.cloned.1.call-start = ((), (), s32[]{:S(2)}) async-start(), calls=%async_computation.24 | async-start | bytes 17301504
  1630.1 3.1 copy-start.5
  1630.1 3.1 copy-start.38
  1662.8 42.3 copy-start.13
  1705.1 9.3 copy-start.21
  1714.4 9.9 copy-start.29
  (27 other events, 47.4 us)
Sparse Core Ops, SparseCore 0:
  10.9 80.2 all-gather.20
  94.1 76.2 all-gather.16
  173.3 76.1 all-gather.14
  251.8 51.2 all-gather.38
  305.4 52.5 all-gather.18
  361.3 77.5 all-gather.22
  442.4 193.3 all-gather.24
  639.2 192.9 all-gather.26
  835.1 192.9 all-gather.28
  1113.0 75.8 all-gather.30
  1336.4 51.2 reduce-scatter.15
  1390.8 52.6 reduce-scatter.13
  1446.4 77.5 all-gather.32
  1526.7 76.1 all-gather.34
  1605.6 76.2 all-gather.36
  1688.2 1590.3 reduce-scatter.19
  3281.3 356.6 reduce-scatter.17
  3640.7 359.0 reduce-scatter.25
  4002.6 359.0 reduce-scatter.23
  4364.4 359.0 reduce-scatter.21
where the time goes:
time: 4740 us; the launch traced here: 4730 us
  waiting for transfers between devices  3820 us (81%)
  matrix products  444 us (9%)
  other arithmetic  192 us (4%)
  local copies, waits for them, and re-layouts  138 us (3%)
  blocking collectives  118 us (2%)
    reduce_scatter x1, waiting for transfers between devices, body(): lax.psum_scatter(jnp.concatenate([lax.dot_general(hidden_low, grad_gate_l...  1540 us
    unnamed x23, waiting for transfers between devices  1090 us
    reduce_scatter x1, waiting for transfers between devices, body(): lax.psum_scatter(output_term, ('leaf', 'row'), scatter_dimension=0, tiled...  354 us
    all_gather x1, waiting for transfers between devices, body(): lax.all_gather(mlp_send[0], ('leaf', 'row'), axis=0, tiled=True)  189 us
    all_gather x1, waiting for transfers between devices, body(): lax.all_gather(mlp_send[1], ('leaf', 'row'), axis=0, tiled=True)  178 us
    all_gather x1, waiting for transfers between devices, body(): lax.all_gather(mlp_send[2], ('leaf', 'row'), axis=0, tiled=True)  172 us
    concatenate x1, other arithmetic, body(): jnp.concatenate([lax.dot_general(hidden_low, grad_gate_low, contract_firs...  134 us
    unnamed x3, blocking collectives  118 us
  transfers between devices with their start and end apart: 20, of which 15 were waited for; matrix products, arithmetic and copies ran while one was open for 11% of the time, Pallas kernels for 0%

commit v1 on v0

v1 whole, which is shorter than its diff:
```python
import functools
import math

import jax
import jax.numpy as jnp
from jax import lax
from jax.experimental import pallas as pl
from jax.experimental.pallas import tpu as pltpu
from jax.sharding import PartitionSpec as P

HEAD_DIM = 128

epsilon = 1e-06
rope_theta = 500000.0
masked_fill = -1e30
bf16 = jnp.bfloat16
f32 = jnp.float32
NN = (((1,), (0,)), ((), ()))
NT = (((1,), (1,)), ((), ()))
TN = (((0,), (0,)), ((), ()))


def dot(left, right, dims, kind=f32):
    return lax.dot_general(left, right, dims, preferred_element_type=f32).astype(kind)


def swap(piece, hop):
    count = lax.axis_size("row")
    return lax.ppermute(piece, "row", [(i, i ^ hop) for i in range(count)])


def gather_rows(rows):
    count, me = lax.axis_size("row"), lax.axis_index("row")
    size = rows.shape[0]
    whole = jnp.zeros((count * size,) + rows.shape[1:], rows.dtype)
    for hop in range(count):
        piece = swap(rows, hop) if hop else rows
        whole = lax.dynamic_update_slice_in_dim(whole, piece, (me ^ hop) * size, 0)
    return whole


def scatter_rows(partial):
    count, me = lax.axis_size("row"), lax.axis_index("row")
    size = partial.shape[0] // count
    total = lax.dynamic_slice_in_dim(partial, me * size, size, 0).astype(f32)
    for hop in range(1, count):
        piece = lax.dynamic_slice_in_dim(partial, (me ^ hop) * size, size, 0)
        total = total + swap(piece, hop).astype(f32)
    return total


def tie(value, *others):
    return lax.optimization_barrier((value,) + others)[0]


def columns_in(*weights):
    count, me = lax.axis_size("row"), lax.axis_index("row")
    size, wide = weights[0].shape[0], weights[0].shape[1] // count
    whole = jnp.zeros((count * size, wide * len(weights)), bf16)
    for hop in range(count):
        piece = jnp.concatenate(
            [lax.dynamic_slice_in_dim(w, (me ^ hop) * wide, wide, 1).astype(bf16) for w in weights], axis=1
        )
        if hop:
            piece = swap(piece, hop)
        whole = lax.dynamic_update_slice_in_dim(whole, piece, (me ^ hop) * size, 0)
    return whole


def columns_out(block):
    count, me = lax.axis_size("row"), lax.axis_index("row")
    size, wide = block.shape[0] // count, block.shape[1]
    whole = jnp.zeros((size, wide * count), f32)
    for hop in range(count):
        piece = lax.dynamic_slice_in_dim(block, (me ^ hop) * size, size, 0)
        if hop:
            piece = swap(piece, hop)
        whole = lax.dynamic_update_slice_in_dim(whole, piece.astype(f32), (me ^ hop) * wide, 1)
    return whole


def sum_rows(small):
    count = lax.axis_size("row")
    total = small
    for hop in range(1, count):
        total = total + swap(small, hop)
    return total


def norm_back(grad_out, unit_rows, scaled, gain_row):
    weighted = grad_out * gain_row
    inner = jnp.mean(weighted * unit_rows, axis=-1, keepdims=True)
    return (scaled * (weighted - unit_rows * inner), jnp.sum(grad_out * unit_rows, axis=0))


def rotate(vector, cos_part, sin_part):
    half_dim = HEAD_DIM // 2
    by_head = vector.reshape(vector.shape[0], vector.shape[1] // HEAD_DIM, HEAD_DIM)
    swapped = jnp.concatenate([by_head[..., half_dim:], by_head[..., :half_dim]], axis=-1)
    turned = by_head * cos_part[:, None, :] + swapped * sin_part[:, None, :]
    return turned.reshape(vector.shape)


def tree_tables(length_row, parent_row, total):
    seg_count = parent_row.shape[0]
    segment_ids = jnp.arange(seg_count, dtype=jnp.int32)
    ends = jnp.cumsum(length_row)
    offsets = ends - length_row
    all_rows = jnp.arange(total, dtype=jnp.int32)
    owned_from = (all_rows[:, None] >= offsets[None, :]).astype(f32)
    onehot_all = owned_from - jnp.concatenate(
        [owned_from[:, 1:], jnp.zeros((total, 1), f32)], axis=1
    )
    reached = (
        (parent_row[:, None] == segment_ids[None, :])
        | (segment_ids[:, None] == segment_ids[None, :])
    ).astype(f32)
    for _ in range(2):
        reached = jnp.minimum(jnp.sum(reached[:, :, None] * reached[None, :, :], axis=1), 1.0)
    strict = reached - jnp.eye(seg_count, dtype=f32)
    path_start = jnp.sum(strict * length_row.astype(f32)[None, :], axis=1)
    position = all_rows.astype(f32) + jnp.sum(
        onehot_all * (path_start - offsets.astype(f32))[None, :], axis=1
    )
    onehot_low = onehot_all.astype(bf16)
    row_reach = dot(onehot_low, reached.astype(bf16), NN, bf16)
    seen = dot(onehot_low, row_reach, NT)
    allowed = (seen > 0.5) & (all_rows[:, None] <= all_rows[None, :])
    bias = jnp.where(allowed, 0.0, masked_fill).astype(bf16)
    frequency = jnp.exp(
        jnp.arange(HEAD_DIM // 2, dtype=f32) * (-2.0 * math.log(rope_theta) / HEAD_DIM)
    )
    angles = position[:, None] * frequency[None, :]
    cos_half, sin_half = jnp.cos(angles), jnp.sin(angles)
    cos_wide = jnp.concatenate([cos_half, cos_half], axis=1)
    sin_wide = jnp.concatenate([-sin_half, sin_half], axis=1)
    return (bias, cos_wide, sin_wide)


def attend_kernel(block, scale, query_ref, key_ref, value_ref, bias_ref, context_ref, lse_ref):
    total = key_ref.shape[0]
    for first in range(0, total, block):
        last = first + block
        scores = dot(key_ref[:last], query_ref[first:last], NT) * scale
        scores = scores + bias_ref[:last, first:last].astype(f32)
        top = jnp.max(scores, axis=0, keepdims=True)
        probs = jnp.exp(scores - top)
        mass = jnp.sum(probs, axis=0, keepdims=True)
        probs_low = (probs * (1.0 / mass)).astype(bf16)
        turned = dot(value_ref[:last], probs_low, TN)
        context_ref[first:last, :] = turned.T.astype(bf16)
        lse_ref[:, first:last] = jnp.broadcast_to(top + jnp.log(mass), (8, block))


def attend(query, key, value, bias):
    total, width = query.shape
    heads = width // HEAD_DIM
    part = pl.BlockSpec((total, HEAD_DIM), lambda h: (0, h))
    return pl.pallas_call(
        functools.partial(attend_kernel, 256, 1.0 / math.sqrt(HEAD_DIM)),
        grid=(heads,),
        in_specs=[part, part, part, pl.BlockSpec((total, total), lambda h: (0, 0))],
        out_specs=[part, pl.BlockSpec((8, total), lambda h: (h, 0))],
        out_shape=[
            jax.ShapeDtypeStruct((total, width), bf16),
            jax.ShapeDtypeStruct((8 * heads, total), f32),
        ],
        compiler_params=pltpu.CompilerParams(vmem_limit_bytes=48 * 2**20),
        cost_estimate=pl.CostEstimate(
            flops=4 * total * total * width, bytes_accessed=10 * total * width, transcendentals=total * total * heads
        ),
    )(query, key, value, bias)


def attend_back_kernel(
    block,
    scale,
    query_ref,
    key_ref,
    value_ref,
    bias_ref,
    lse_ref,
    grad_ref,
    grad_query_ref,
    grad_key_ref,
    grad_value_ref,
):
    total = key_ref.shape[0]
    grad_key_ref[...] = jnp.zeros_like(grad_key_ref)
    grad_value_ref[...] = jnp.zeros_like(grad_value_ref)
    for first in range(0, total, block):
        last = first + block
        scores = dot(key_ref[:last], query_ref[first:last], NT) * scale
        scores = scores + bias_ref[:last, first:last].astype(f32)
        probs = jnp.exp(scores - lse_ref[0:1, first:last])
        grad_probs = dot(value_ref[:last], grad_ref[first:last], NT)
        inner = jnp.sum(probs * grad_probs, axis=0, keepdims=True)
        grad_scores = (probs * (grad_probs - inner)).astype(bf16)
        turned = dot(key_ref[:last], grad_scores, TN)
        grad_query_ref[first:last, :] = turned.T * scale
        grad_key_ref[:last, :] += dot(grad_scores, query_ref[first:last], NN) * scale
        grad_value_ref[:last, :] += dot(probs.astype(bf16), grad_ref[first:last], NN)


def attend_back(query, key, value, bias, lse, grad_context):
    total, width = query.shape
    heads = width // HEAD_DIM
    part = pl.BlockSpec((total, HEAD_DIM), lambda h: (0, h))
    return pl.pallas_call(
        functools.partial(attend_back_kernel, 256, 1.0 / math.sqrt(HEAD_DIM)),
        grid=(heads,),
        in_specs=[
            part,
            part,
            part,
            pl.BlockSpec((total, total), lambda h: (0, 0)),
            pl.BlockSpec((8, total), lambda h: (h, 0)),
            part,
        ],
        out_specs=[part, part, part],
        out_shape=[jax.ShapeDtypeStruct((total, width), f32)] * 3,
        compiler_params=pltpu.CompilerParams(vmem_limit_bytes=56 * 2**20),
        cost_estimate=pl.CostEstimate(
            flops=10 * total * total * width, bytes_accessed=24 * total * width, transcendentals=total * total * heads
        ),
    )(query, key, value, bias, lse, grad_context)


def body(
    inputs,
    cotangent,
    seg_lengths,
    seg_parents,
    w_query,
    w_key,
    w_value,
    w_output,
    gain_query,
    gain_key,
    gain_attn,
    w_gate,
    w_up,
    w_down,
    gain_mlp,
):
    trees, rows_dev, width = inputs.shape
    count, leaves, me = lax.axis_size("row"), lax.axis_size("leaf"), lax.axis_index("row")
    tree_len = rows_dev * count
    part = width // count
    own = w_query.shape[0]
    units = w_gate.shape[1] // count
    tokens = inputs.reshape(rows_dev, width)

    def leaf_gather(block):
        return lax.all_gather(block, "leaf", axis=0, tiled=True)

    def leaf_scatter(block):
        return lax.psum_scatter(block, "leaf", scatter_dimension=0, tiled=True)

    qkv_block = columns_in(w_query, w_key, w_value)
    gains_own = jnp.stack([gain_query, gain_key, gain_attn, gain_mlp]).astype(bf16).reshape(1, 4 * own)
    gains_leaf = gather_rows(gains_own).reshape(own, 4 * count)
    qkv_mat = leaf_gather(qkv_block)
    all_tokens = gather_rows(tie(tokens, qkv_block))
    output_block = jnp.concatenate(
        [w_output.astype(bf16), gains_leaf, jnp.zeros((own, HEAD_DIM - 4 * count), bf16)], axis=1
    )
    output_block = tie(output_block, qkv_block)
    output_rows = leaf_gather(output_block)
    gains_all = output_rows[:, width : width + 4 * count].reshape(leaves, count, 4, own)
    gains_all = jnp.moveaxis(gains_all, 2, 0).reshape(4, width).astype(f32)
    output_rows = output_rows[:, :width].reshape(count, leaves // count, own, width)
    output_mat = jnp.zeros((leaves // count, count, own, width), bf16)
    for hop in range(count):
        piece = lax.dynamic_index_in_dim(output_rows, me ^ hop, 0, keepdims=False)
        if hop:
            piece = swap(piece, hop)
        output_mat = lax.dynamic_update_index_in_dim(output_mat, piece, me ^ hop, 1)
    output_mat = output_mat.reshape(part, width)
    gate_block = columns_in(tie(w_gate, output_block))
    up_block = columns_in(tie(w_up, gate_block))
    down_block = columns_in(tie(w_down, up_block))
    gate_mat = leaf_gather(gate_block)
    up_mat = leaf_gather(up_block)
    down_mat = leaf_gather(down_block)

    bias, cos_wide, sin_wide = tree_tables(seg_lengths[0], seg_parents[0], tree_len)

    query_pre = dot(all_tokens, qkv_mat[:, :part], NN)
    key_pre = dot(all_tokens, qkv_mat[:, part : 2 * part], NN)
    value = dot(all_tokens, qkv_mat[:, 2 * part :], NN, bf16)
    squares = sum_rows(jnp.stack([jnp.sum(query_pre * query_pre, axis=1), jnp.sum(key_pre * key_pre, axis=1)]))
    scales = lax.rsqrt(squares / width + epsilon)
    query_scale, key_scale = scales[0][:, None], scales[1][:, None]
    query_gain = lax.dynamic_slice_in_dim(gains_all[0], me * part, part)
    key_gain = lax.dynamic_slice_in_dim(gains_all[1], me * part, part)
    attn_gain, mlp_gain = gains_all[2], gains_all[3]
    query_unit = query_pre * query_scale
    key_unit = key_pre * key_scale
    query = rotate(query_unit * query_gain, cos_wide, sin_wide).astype(bf16)
    key = rotate(key_unit * key_gain, cos_wide, sin_wide).astype(bf16)
    context, lse = attend(query, key, value, bias)
    attn_pre = scatter_rows(dot(context, output_mat, NN, bf16))
    attn_scale = lax.rsqrt(jnp.mean(attn_pre * attn_pre, axis=-1, keepdims=True) + epsilon)
    attn_unit = attn_pre * attn_scale
    hidden = tokens.astype(f32) + attn_unit * attn_gain
    hidden_all = gather_rows(hidden.astype(bf16))

    gate_pre = dot(hidden_all, gate_mat, NN)
    up_pre = dot(hidden_all, up_mat, NN)
    sigmoid_gate = jax.nn.sigmoid(gate_pre)
    activated = (gate_pre * sigmoid_gate * up_pre).astype(bf16)
    mlp_pre = scatter_rows(dot(activated, down_mat, NT, bf16))
    mlp_scale = lax.rsqrt(jnp.mean(mlp_pre * mlp_pre, axis=-1, keepdims=True) + epsilon)
    mlp_unit = mlp_pre * mlp_scale
    outputs = (hidden + mlp_unit * mlp_gain).astype(bf16).reshape(inputs.shape)

    grad_final = cotangent.reshape(rows_dev, width).astype(f32)
    grad_mlp, grad_mlp_gain = norm_back(grad_final, mlp_unit, mlp_scale, mlp_gain)
    grad_mlp_all = gather_rows(grad_mlp.astype(bf16))
    grad_act = dot(grad_mlp_all, down_mat, NN)
    down_sum = dot(grad_mlp_all, activated, TN, bf16)
    down_shard = leaf_scatter(down_sum)
    grad_act = tie(grad_act, down_sum)
    grad_gate = (grad_act * up_pre * sigmoid_gate * (1.0 + gate_pre * (1.0 - sigmoid_gate))).astype(bf16)
    grad_up = (grad_act * gate_pre * sigmoid_gate).astype(bf16)
    grad_hidden_part = dot(grad_gate, gate_mat, NT) + dot(grad_up, up_mat, NT)
    grad_hidden = grad_final + scatter_rows(grad_hidden_part.astype(bf16))
    gate_sum = dot(hidden_all, tie(grad_gate, grad_hidden_part), TN, bf16)
    up_sum = dot(hidden_all, tie(grad_up, gate_sum), TN, bf16)
    gate_sum = tie(gate_sum, down_shard, up_sum, grad_hidden)
    gate_shard = leaf_scatter(gate_sum)
    grad_hidden = tie(grad_hidden, gate_sum)

    grad_attn, grad_attn_gain = norm_back(grad_hidden, attn_unit, attn_scale, attn_gain)
    grad_attn_all = gather_rows(grad_attn.astype(bf16))
    grad_context = dot(grad_attn_all, output_mat, NT, bf16)
    grad_query, grad_key, grad_value = attend_back(query, key, value, bias, lse, grad_context)
    grad_query, grad_key, grad_value, up_sum = lax.optimization_barrier(
        (grad_query, grad_key, grad_value, tie(up_sum, gate_shard))
    )
    up_shard = leaf_scatter(up_sum)
    grad_value_low = grad_value.astype(bf16)
    grad_query = rotate(grad_query, cos_wide, -sin_wide)
    grad_key = rotate(grad_key, cos_wide, -sin_wide)
    inner = sum_rows(
        jnp.stack(
            [
                jnp.sum(grad_query * query_gain * query_unit, axis=1),
                jnp.sum(grad_key * key_gain * key_unit, axis=1),
            ]
        )
    ) / width
    grad_query_gain = jnp.sum(grad_query * query_unit, axis=0)
    grad_key_gain = jnp.sum(grad_key * key_unit, axis=0)
    grad_query_low = (query_scale * (grad_query * query_gain - query_unit * inner[0][:, None])).astype(bf16)
    grad_key_low = (key_scale * (grad_key * key_gain - key_unit * inner[1][:, None])).astype(bf16)
    grad_qkv = jnp.concatenate([grad_query_low, grad_key_low, grad_value_low], axis=1)
    grad_tokens = grad_hidden + scatter_rows(dot(grad_qkv, qkv_mat, NT, bf16))
    grad_inputs = grad_tokens.astype(bf16).reshape(inputs.shape)

    output_part = dot(context, grad_attn_all, TN, bf16).reshape(leaves // count, count, own, width)
    output_turned = jnp.zeros((count, leaves // count, own, width), bf16)
    for hop in range(count):
        piece = lax.dynamic_index_in_dim(output_part, me ^ hop, 1, keepdims=False)
        if hop:
            piece = swap(piece, hop)
        output_turned = lax.dynamic_update_index_in_dim(output_turned, piece, me ^ hop, 0)
    qkv_sum = dot(all_tokens, grad_qkv, TN, bf16)
    output_shard = leaf_scatter(tie(output_turned.reshape(leaves * own, width), up_shard, qkv_sum))
    qkv_shard = leaf_scatter(tie(qkv_sum, output_shard))
    grad_output = output_shard.astype(f32)

    wide_part = jnp.stack([grad_attn_gain, grad_mlp_gain]).reshape(2, leaves, count, own)
    narrow_part = jnp.stack([grad_query_gain, grad_key_gain]).reshape(2, leaves // count, count, own)
    wide_sum = jnp.zeros((2, leaves, own), f32)
    narrow_all = jnp.zeros((2, leaves, own), f32)
    for hop in range(count):
        piece = lax.dynamic_index_in_dim(jnp.concatenate([wide_part, narrow_part], axis=1), me ^ hop, 2, keepdims=False)
        if hop:
            piece = swap(piece, hop)
        wide_sum = wide_sum + piece[:, :leaves]
        narrow_all = lax.dynamic_update_slice_in_dim(
            narrow_all, piece[:, leaves:], (me ^ hop) * (leaves // count), 1
        )
    grad_gains = jnp.concatenate([narrow_all, wide_sum], axis=0)
    stride = 1
    while stride < leaves:
        grad_gains = grad_gains + lax.ppermute(
            grad_gains, "leaf", [(i, i ^ stride) for i in range(leaves)]
        )
        stride *= 2
    grad_gains = lax.dynamic_index_in_dim(grad_gains, lax.axis_index("leaf"), 1, keepdims=False)
    return (
        outputs,
        grad_inputs,
        columns_out(qkv_shard[:, :part]),
        columns_out(qkv_shard[:, part : 2 * part]),
        columns_out(qkv_shard[:, 2 * part :]),
        grad_output,
        grad_gains[0],
        grad_gains[1],
        grad_gains[2],
        columns_out(gate_shard),
        columns_out(up_shard),
        columns_out(down_shard),
        grad_gains[3],
    )


def solution(mesh):
    both = ("leaf", "row")
    token_spec, tree_spec, matrix_spec, gain_spec = P("leaf", "row", None), P("leaf", None), P(both, None), P(both)
    return jax.shard_map(
        body,
        mesh=mesh,
        in_specs=(token_spec,) * 2 + (tree_spec,) * 2 + (matrix_spec,) * 4 + (gain_spec,) * 3 + (matrix_spec,) * 3 + (gain_spec,),
        out_specs=(token_spec,) * 2 + (matrix_spec,) * 4 + (gain_spec,) * 3 + (matrix_spec,) * 3 + (gain_spec,),
        check_vma=False,
    )
```

time: 4740 us -> 957 us (0.20)
  waiting for transfers between devices: 3820 us -> 492 us
  matrix products: 444 us -> 173 us
  other arithmetic: 192 us -> 58.8 us
  blocking collectives: 118 us -> 0 us
  starting transfers between devices: 1.38 us -> 89.3 us
    reduce_scatter x4 -> x5, waiting for transfers between devices: 1900 us -> 73.2 us  [leaf_scatter(): return lax.psum_scatter(block, 'leaf', scatter_dimension=0, tiled=True)]
    unnamed x23 -> x10, waiting for transfers between devices: 1090 us -> 0.16 us
    all_gather x13 -> x5, waiting for transfers between devices: 834 us -> 36.3 us  [leaf_gather(): return lax.all_gather(block, 'leaf', axis=0, tiled=True)]
    ppermute x0 -> x75, waiting for transfers between devices: none -> 382 us  [the longest x72 381 us: swap(): return lax.ppermute(piece, 'row', [(i, i ^ hop) for i in range(count)])]
    dot_general x142 -> x18, matrix products: 444 us -> 173 us  [dot(): lax.dot_general(left, right, dims, preferred_element_type=f32).astype(kind)]
    concatenate x4 -> x5, other arithmetic: 137 us -> 0.07 us  [the longest x3 0.04 us: columns_in(): jnp.concatenate([lax.dynamic_slice_in_dim(w, (me ^ hop) * wide, wide, 1)....]
    unnamed x3 -> x0, blocking collectives: 118 us -> none
    ppermute x0 -> x75, starting transfers between devices: none -> 88.4 us  [the longest x72 84.5 us: swap(): return lax.ppermute(piece, 'row', [(i, i ^ hop) for i in range(count)])]
  transfers between devices with their start and end apart: 20 -> 85, of which waited for: 15 -> 41; matrix products, arithmetic and copies ran while one was open for 11% -> 29% of each run, Pallas kernels for 0% -> 3%
where the time goes in v1:
time: 957 us; the launch traced here: 951 us
  waiting for transfers between devices  492 us (51%)
  matrix products  173 us (18%)
  local copies, waits for them, and re-layouts  94.5 us (10%)
  starting transfers between devices  89.3 us (9%)
  other arithmetic  58.8 us (6%)
  Pallas kernels  26.7 us (3%)
  between operations  16.4 us (2%)
    ppermute x72, waiting for transfers between devices, swap(): return lax.ppermute(piece, 'row', [(i, i ^ hop) for i in range(count)])  381 us
    dot_general x18, matrix products, dot(): lax.dot_general(left, right, dims, preferred_element_type=f32).astype(kind)  173 us
    ppermute x72, starting transfers between devices, swap(): return lax.ppermute(piece, 'row', [(i, i ^ hop) for i in range(count)])  84.5 us
    reduce_scatter x5, waiting for transfers between devices, leaf_scatter(): return lax.psum_scatter(block, 'leaf', scatter_dimension=0, tiled=True)  73.2 us
    all_gather x5, waiting for transfers between devices, leaf_gather(): return lax.all_gather(block, 'leaf', axis=0, tiled=True)  36.3 us
    unnamed x142, local copies, waits for them, and re-layouts  21.8 us
  transfers between devices with their start and end apart: 85, of which 41 were waited for; matrix products, arithmetic and copies ran while one was open for 29% of the time, Pallas kernels for 3%

profile of v1, /device:TPU:0, one launch (start us, length us, event | category | flops | bytes accessed | tf_op | source)
XLA Modules:
  0.0 951.0 jit_solution(18355719668915331604)
XLA Ops:
  23.1 4.6 collective-permute-done.1
  34.1 5.7 collective-permute-done.21
  51.1 4.8 collective-permute-done.25
  75.5 19.5 %collective-permute-done.27 = bf16[64,2048]{1,0:T(8,128)(2,1)S(1)} collective-permute-done((bf16[64,2048]{1,0:T(8,128)(2,1)}, bf16[64,2048]{1,0:T(8,128)(2,1)S(1)}, u32[]{:S(2)}, u32[]{:S(2)}) %collective-permute-start.27) | collective-permute-done | bytes 262176 | tf_op jit(solution)/shard_map/ppermute | solution.py:29
  96.5 26.6 %collective-permute-done.28 = bf16[64,2048]{1,0:T(8,128)(2,1)S(1)} collective-permute-done((bf16[64,2048]{1,0:T(8,128)(2,1)}, bf16[64,2048]{1,0:T(8,128)(2,1)S(1)}, u32[]{:S(2)}, u32[]{:S(2)}) %collective-permute-start.28) | collective-permute-done | bytes 262176 | tf_op jit(solution)/shard_map/ppermute | solution.py:29
  145.6 4.3 collective-permute-done.13
  151.6 5.4 multiply_reduce_fusion.8
  171.4 3.9 multiply_multiply_fusion
  193.3 11.9 %shard_map.246 = (bf16[1024,512]{1,0:T(8,128)(2,1)S(1)}, f32[32,1024]{1,0:T(8,128)S(1)}) custom-call(bf16[1024,512]{1,0:T(8,128)(2,1)S(1)} %get-tuple-element.124.query_ref, bf16[1024,512]{1,0:T(8,128)(2,1)S(1)} %get-tuple-element.123.key_ref, bf16[1024,512]{1,0:T(8,128)(2,1)S(1)} %fusion.15.value_ref, bf16[1024,1024]{1,0:T(8,128)(2,1)} %select_convert_fusion.bias_ref), custom_call_target="tpu_custom_call" | custom-call | flops 2147483648 | bytes 5242880 | tf_op jit(solution)/shard_map/pallas_call | solution.py:159
  205.2 4.4 convolution_convert_fusion.6
  215.8 22.3 %collective-permute-done.17 = bf16[256,2048]{1,0:T(8,128)(2,1)S(1)} collective-permute-done((bf16[256,2048]{1,0:T(8,128)(2,1)}, bf16[256,2048]{1,0:T(8,128)(2,1)S(1)}, u32[]{:S(2)}, u32[]{:S(2)}) %collective-permute-start.17) | collective-permute-done | bytes 1048608 | tf_op jit(solution)/shard_map/ppermute | solution.py:29
  238.1 11.0 %collective-permute-done.16 = bf16[256,2048]{1,0:T(8,128)(2,1)S(1)} collective-permute-done((bf16[256,2048]{1,0:T(8,128)(2,1)}, bf16[256,2048]{1,0:T(8,128)(2,1)S(1)}, u32[]{:S(2)}, u32[]{:S(2)}) %collective-permute-start.16) | collective-permute-done | bytes 1048608 | tf_op jit(solution)/shard_map/ppermute | solution.py:29
  258.9 22.6 %collective-permute-done.18 = bf16[256,2048]{1,0:T(8,128)(2,1)S(1)} collective-permute-done((bf16[256,2048]{1,0:T(8,128)(2,1)S(1)}, bf16[256,2048]{1,0:T(8,128)(2,1)S(1)}, u32[]{:S(2)}, u32[]{:S(2)}) %collective-permute-start.18) | collective-permute-done | bytes 1048608 | tf_op jit(solution)/shard_map/ppermute | solution.py:29
  282.6 18.7 %collective-permute-done.19 = bf16[256,2048]{1,0:T(8,128)(2,1)S(1)} collective-permute-done((bf16[256,2048]{1,0:T(8,128)(2,1)S(1)}, bf16[256,2048]{1,0:T(8,128)(2,1)S(1)}, u32[]{:S(2)}, u32[]{:S(2)}) %collective-permute-start.19) | collective-permute-done | bytes 1048608 | tf_op jit(solution)/shard_map/ppermute | solution.py:29
  303.4 14.6 %fusion.53 = f32[1024,2048]{1,0:T(8,128)} fusion(bf16[1024,2048]{1,0:T(8,128)(2,1)} %constant_dynamic-update-slice_fusion.21, bf16[2048,2048]{1,0:T(8,128)(2,1)} %all-gather.10.cloned.1.call-done), kind=kOutput, calls=%fused_computation.282 | convolution fusion | flops 8589934592 | bytes 20971520 | tf_op jit(solution)/shard_map/dot_general | solution.py:24
  318.0 17.1 %multiply_convert_fusion.2 = (bf16[1024,2048]{1,0:T(8,128)(2,1)}, f32[1024,2048]{1,0:T(8,128)}) fusion(f32[1024,2048]{1,0:T(8,128)} %fusion.53, bf16[1024,2048]{1,0:T(8,128)(2,1)} %constant_dynamic-update-slice_fusion.21, bf16[2048,2048]{1,0:T(8,128)(2,1)} %all-gather.12.cloned.1.call-done), kind=kOutput, calls=%fused_computation.2 | convolution fusion | flops 8602517504 | bytes 33554432 | tf_op jit(solution)/shard_map/dot_general | solution.py:24
  335.0 36.3 %all-gather.14.cloned.1.call-done = bf16[2048,2048]{1,0:T(8,128)(2,1)} async-done(((bf16[256,2048]{1,0:T(8,128)(2,1)}), bf16[2048,2048]{1,0:T(8,128)(2,1)}) %all-gather.14.cloned.1.call-update) | async-done | bytes 8388624 | tf_op jit(solution)/shard_map/all_gather | solution.py:255
  371.3 12.7 %convolution_convert_fusion.5 = bf16[1024,2048]{1,0:T(8,128)(2,1)S(1)} fusion(bf16[1024,2048]{1,0:T(8,128)(2,1)} %get-tuple-element.187, bf16[2048,2048]{1,0:T(8,128)(2,1)} %all-gather.14.cloned.1.call-done), kind=kOutput, calls=%fused_computation.13 | convolution fusion | flops 8592031744 | bytes 16777216 | tf_op jit(solution)/shard_map/dot_general | solution.py:24
  390.5 23.6 %collective-permute-done.32 = bf16[256,2048]{1,0:T(8,128)(2,1)S(1)} collective-permute-done((bf16[256,2048]{1,0:T(8,128)(2,1)}, bf16[256,2048]{1,0:T(8,128)(2,1)S(1)}, u32[]{:S(2)}, u32[]{:S(2)}) %collective-permute-start.32) | collective-permute-done | bytes 1048608 | tf_op jit(solution)/shard_map/ppermute | solution.py:29
  414.1 21.8 %collective-permute-done.31 = bf16[256,2048]{1,0:T(8,128)(2,1)S(1)} collective-permute-done((bf16[256,2048]{1,0:T(8,128)(2,1)}, bf16[256,2048]{1,0:T(8,128)(2,1)S(1)}, u32[]{:S(2)}, u32[]{:S(2)}) %collective-permute-start.31) | collective-permute-done | bytes 1048608 | tf_op jit(solution)/shard_map/ppermute | solution.py:29
  444.2 22.5 %collective-permute-done.33 = bf16[256,2048]{1,0:T(8,128)(2,1)S(1)} collective-permute-done((bf16[256,2048]{1,0:T(8,128)(2,1)S(1)}, bf16[256,2048]{1,0:T(8,128)(2,1)S(1)}, u32[]{:S(2)}, u32[]{:S(2)}) %collective-permute-start.33) | collective-permute-done | bytes 1048608 | tf_op jit(solution)/shard_map/ppermute | solution.py:29
  466.9 22.5 %collective-permute-done.34 = bf16[256,2048]{1,0:T(8,128)(2,1)S(1)} collective-permute-done((bf16[256,2048]{1,0:T(8,128)(2,1)S(1)}, bf16[256,2048]{1,0:T(8,128)(2,1)S(1)}, u32[]{:S(2)}, u32[]{:S(2)}) %collective-permute-start.34) | collective-permute-done | bytes 1048608 | tf_op jit(solution)/shard_map/ppermute | solution.py:29
  491.6 11.5 %convolution_convert_fusion.3 = bf16[2048,2048]{1,0:T(8,128)(2,1)} fusion(bf16[1024,2048]{1,0:T(8,128)(2,1)S(1)} %constant_dynamic-update-slice_fusion.8, bf16[1024,2048]{1,0:T(8,128)(2,1)S(1)} %copy-done.70), kind=kOutput, calls=%fused_computation.7 | convolution fusion | flops 8594128896 | bytes 16777216 | tf_op jit(solution)/shard_map/dot_general | solution.py:24
  503.1 12.9 %fusion.54 = f32[1024,2048]{1,0:T(8,128)S(1)} fusion(bf16[1024,2048]{1,0:T(8,128)(2,1)} %copy-done.26, bf16[2048,2048]{1,0:T(8,128)(2,1)} %all-gather.14.cloned.1.call-done), kind=kOutput, calls=%fused_computation.283 | convolution fusion | flops 8589934592 | bytes 20971520 | tf_op jit(solution)/shard_map/dot_general | solution.py:24
  516.0 9.7 %multiply_convert_fusion.1 = (bf16[1024,2048]{1,0:T(8,128)(2,1)}, bf16[1024,2048]{1,0:T(8,128)(2,1)S(1)}) fusion(f32[1024,2048]{1,0:T(8,128)} %fusion.53, f32[1024,2048]{1,0:T(8,128)S(1)} %fusion.54, f32[1024,2048]{1,0:T(8,128)} %get-tuple-element.188), kind=kLoop, calls=%fused_computation.1 | loop fusion | flops 27262976 | bytes 33554432 | tf_op jit(solution)/shard_map/convert_element_type | solution.py:325
  525.7 14.9 %fusion.55 = f32[1024,2048]{1,0:T(8,128)} fusion(bf16[1024,2048]{1,0:T(8,128)(2,1)S(1)} %get-tuple-element.43, bf16[2048,2048]{1,0:T(8,128)(2,1)} %all-gather.12.cloned.1.call-done), kind=kOutput, calls=%fused_computation.284 | convolution fusion | flops 8589934592 | bytes 20971520 | tf_op jit(solution)/shard_map/dot_general | solution.py:24
  540.6 14.3 %convolution_add_fusion = bf16[1024,2048]{1,0:T(8,128)(2,1)S(1)} fusion(f32[1024,2048]{1,0:T(8,128)} %fusion.55, bf16[1024,2048]{1,0:T(8,128)(2,1)} %get-tuple-element.42, bf16[2048,2048]{1,0:T(8,128)(2,1)} %all-gather.10.cloned.1.call-done), kind=kOutput, calls=%fused_computation.11 | convolution fusion | flops 8594128896 | bytes 25165824 | tf_op jit(solution)/shard_map/dot_general | solution.py:24
  561.0 13.5 %convolution_convert_fusion.2 = bf16[2048,2048]{1,0:T(8,128)(2,1)} fusion(bf16[1024,2048]{1,0:T(8,128)(2,1)} %constant_dynamic-update-slice_fusion.21, bf16[1024,2048]{1,0:T(8,128)(2,1)S(1)} %copy-done.37), kind=kOutput, calls=%fused_computation.6 | convolution fusion | flops 8594128896 | bytes 16777216 | tf_op jit(solution)/shard_map/dot_general | solution.py:24
  574.5 14.3 %convolution_convert_fusion.1 = bf16[2048,2048]{1,0:T(8,128)(2,1)} fusion(bf16[1024,2048]{1,0:T(8,128)(2,1)} %constant_dynamic-update-slice_fusion.21, bf16[1024,2048]{1,0:T(8,128)(2,1)} %copy-done.36), kind=kOutput, calls=%fused_computation.5 | convolution fusion | flops 8594128896 | bytes 16777216 | tf_op jit(solution)/shard_map/dot_general | solution.py:24
  588.8 15.9 %collective-permute-done.37 = bf16[256,2048]{1,0:T(8,128)(2,1)} collective-permute-done((bf16[256,2048]{1,0:T(8,128)(2,1)S(1)}, bf16[256,2048]{1,0:T(8,128)(2,1)}, u32[]{:S(2)}, u32[]{:S(2)}) %collective-permute-start.37) | collective-permute-done | bytes 1048608 | tf_op jit(solution)/shard_map/ppermute | solution.py:29
  604.8 4.3 convert_add_fusion
  610.9 5.1 multiply_reduce_fusion.2
  621.7 22.6 %collective-permute-done.39 = bf16[256,2048]{1,0:T(8,128)(2,1)S(1)} collective-permute-done((bf16[256,2048]{1,0:T(8,128)(2,1)S(1)}, bf16[256,2048]{1,0:T(8,128)(2,1)S(1)}, u32[]{:S(2)}, u32[]{:S(2)}) %collective-permute-start.39) | collective-permute-done | bytes 1048608 | tf_op jit(solution)/shard_map/ppermute | solution.py:29
  644.4 21.2 %collective-permute-done.40 = bf16[256,2048]{1,0:T(8,128)(2,1)S(1)} collective-permute-done((bf16[256,2048]{1,0:T(8,128)(2,1)S(1)}, bf16[256,2048]{1,0:T(8,128)(2,1)S(1)}, u32[]{:S(2)}, u32[]{:S(2)}) %collective-permute-start.40) | collective-permute-done | bytes 1048608 | tf_op jit(solution)/shard_map/ppermute | solution.py:29
  665.8 6.4 convolution_convert_fusion.8.grad_ref
  672.3 14.8 %shard_map.247 = (f32[1024,512]{1,0:T(8,128)}, f32[1024,512]{1,0:T(8,128)}, f32[1024,512]{1,0:T(8,128)}) custom-call(bf16[1024,512]{1,0:T(8,128)(2,1)} %copy-done.1, bf16[1024,512]{1,0:T(8,128)(2,1)} %copy-done, bf16[1024,512]{1,0:T(8,128)(2,1)} %copy-done.4, bf16[1024,1024]{1,0:T(8,128)(2,1)} %select_convert_fusion.bias_ref, f32[32,1024]{1,0:T(8,128)} %copy-done.5, ...), custom_call_target="tpu_custom_call" | custom-call | flops 5368709120 | bytes 12582912 | tf_op jit(solution)/shard_map/pallas_call | solution.py:209
  687.1 9.4 reduce-scatter.8.cloned.1.call-done
  697.8 4.6 convolution_convert_fusion.7
  708.5 8.9 collective-permute-done.48
  718.2 8.3 collective-permute-done.49
  749.8 9.5 convolution_convert_fusion
  759.2 27.6 %reduce-scatter.10.cloned.1.call-done = bf16[256,2048]{1,0:T(8,128)(2,1)} async-done(((bf16[2048,2048]{1,0:T(8,128)(2,1)}), bf16[256,2048]{1,0:T(8,128)(2,1)}) %reduce-scatter.10.cloned.1.call-update) | async-done | bytes 1048592 | tf_op jit(solution)/shard_map/reduce_scatter | solution.py:258
  787.1 36.1 %reduce-scatter.12.cloned.1.call-done = bf16[64,2048]{1,0:T(8,128)(2,1)} async-done(((bf16[512,2048]{1,0:T(8,128)(2,1)}), bf16[64,2048]{1,0:T(8,128)(2,1)}) %reduce-scatter.12.cloned.1.call-update) | async-done | bytes 262160 | tf_op jit(solution)/shard_map/reduce_scatter | solution.py:258
  849.4 8.8 convolution_convert_fusion.4
  858.3 3.8 collective-permute-start.65
  868.7 20.8 %collective-permute-done.47 = bf16[256,2048]{1,0:T(8,128)(2,1)S(1)} collective-permute-done((bf16[256,2048]{1,0:T(8,128)(2,1)S(1)}, bf16[256,2048]{1,0:T(8,128)(2,1)S(1)}, u32[]{:S(2)}, u32[]{:S(2)}) %collective-permute-start.47) | collective-permute-done | bytes 1048608 | tf_op jit(solution)/shard_map/ppermute | solution.py:29
  889.5 21.3 %collective-permute-done.46 = bf16[256,2048]{1,0:T(8,128)(2,1)S(1)} collective-permute-done((bf16[256,2048]{1,0:T(8,128)(2,1)S(1)}, bf16[256,2048]{1,0:T(8,128)(2,1)S(1)}, u32[]{:S(2)}, u32[]{:S(2)}) %collective-permute-start.46) | collective-permute-done | bytes 1048608 | tf_op jit(solution)/shard_map/ppermute | solution.py:29
  916.2 10.3 %collective-permute-done.70 = bf16[64,2048]{1,0:T(8,128)(2,1)S(1)} collective-permute-done((bf16[64,2048]{1,0:T(8,128)(2,1)S(1)}, bf16[64,2048]{1,0:T(8,128)(2,1)S(1)}, u32[]{:S(2)}, u32[]{:S(2)}) %collective-permute-start.70) | collective-permute-done | bytes 262176 | tf_op jit(solution)/shard_map/ppermute | solution.py:29
  (489 shorter events, 247.0 us)
Async XLA Ops:
  7.2 123.0 %all-gather.8.cloned.1.call-start = ((), (), s32[]{:S(2)}) async-start(), calls=%async_computation.6 | async-start | bytes 2506752 | tf_op jit(solution)/shard_map/all_gather | solution.py:255
  27.8 123.7 %all-gather.6.cloned.1.call-start = ((), (), s32[]{:S(2)}) async-start(), calls=%async_computation.5 | async-start | bytes 7077888 | tf_op jit(solution)/shard_map/all_gather | solution.py:255
  28.7 274.7 %all-gather.10.cloned.1.call-start = ((), (), s32[]{:S(2)}) async-start(), calls=%async_computation.7 | async-start | bytes 9437184 | tf_op jit(solution)/shard_map/all_gather | solution.py:255
  44.3 273.7 %all-gather.12.cloned.1.call-start = ((), (), s32[]{:S(2)}) async-start(), calls=%async_computation.8 | async-start | bytes 9437184 | tf_op jit(solution)/shard_map/all_gather | solution.py:255
  57.1 314.3 %all-gather.14.cloned.1.call-start = ((), (), s32[]{:S(2)}) async-start(), calls=%async_computation.9 | async-start | bytes 9437184 | tf_op jit(solution)/shard_map/all_gather | solution.py:255
  63.3 61.2 %collective-permute-start.3 = (bf16[256,2048]{1,0:T(8,128)(2,1)S(1)}, bf16[256,2048]{1,0:T(8,128)(2,1)}, u32[]{:S(2)}, u32[]{:S(2)}) collective-permute-start(bf16[256,2048]{1,0:T(8,128)(2,1)S(1)} %bitcast.162), channel_id=1, source_target_pairs={{0,1},{1,0},{2,3},{3,2},{4,5},{5,4},{6,7},{7,6},{8,9},{9,8},{10,11... | collective-permute-start | bytes 3145736 | tf_op jit(solution)/shard_map/ppermute | solution.py:29
  66.6 28.4 %collective-permute-start.27 = (bf16[64,2048]{1,0:T(8,128)(2,1)}, bf16[64,2048]{1,0:T(8,128)(2,1)S(1)}, u32[]{:S(2)}, u32[]{:S(2)}) collective-permute-start(bf16[64,2048]{1,0:T(8,128)(2,1)} %get-tuple-element.110), channel_id=1, source_target_pairs={{0,1},{1,0},{2,3},{3,2},{4,5},{5,4},{6,7},{7,6},{8,9},{9,8},{10,11... | collective-permute-start | bytes 786440 | tf_op jit(solution)/shard_map/ppermute | solution.py:29
  69.4 57.4 %collective-permute-start.4 = (bf16[256,2048]{1,0:T(8,128)(2,1)S(1)}, bf16[256,2048]{1,0:T(8,128)(2,1)}, u32[]{:S(2)}, u32[]{:S(2)}) collective-permute-start(bf16[256,2048]{1,0:T(8,128)(2,1)S(1)} %bitcast.163), channel_id=1, source_target_pairs={{0,2},{1,3},{2,0},{3,1},{4,6},{5,7},{6,4},{7,5},{8,10},{9,11},{10,... | collective-permute-start | bytes 3145736 | tf_op jit(solution)/shard_map/ppermute | solution.py:29
  70.2 58.9 %collective-permute-start.5 = (bf16[256,2048]{1,0:T(8,128)(2,1)S(1)}, bf16[256,2048]{1,0:T(8,128)(2,1)S(1)}, u32[]{:S(2)}, u32[]{:S(2)}) collective-permute-start(bf16[256,2048]{1,0:T(8,128)(2,1)S(1)} %bitcast.164), channel_id=1, source_target_pairs={{0,3},{1,2},{2,1},{3,0},{4,7},{5,6},{6,5},{7,4},{8,11},{9,10},{10,... | collective-permute-start | bytes 3145736 | tf_op jit(solution)/shard_map/ppermute | solution.py:29
  71.6 51.6 %collective-permute-start.28 = (bf16[64,2048]{1,0:T(8,128)(2,1)}, bf16[64,2048]{1,0:T(8,128)(2,1)S(1)}, u32[]{:S(2)}, u32[]{:S(2)}) collective-permute-start(bf16[64,2048]{1,0:T(8,128)(2,1)} %get-tuple-element.109), channel_id=1, source_target_pairs={{0,2},{1,3},{2,0},{3,1},{4,6},{5,7},{6,4},{7,5},{8,10},{9,11},{10,... | collective-permute-start | bytes 786440 | tf_op jit(solution)/shard_map/ppermute | solution.py:29
  95.0 28.1 %collective-permute-start.29 = (bf16[64,2048]{1,0:T(8,128)(2,1)S(1)}, bf16[64,2048]{1,0:T(8,128)(2,1)S(1)}, u32[]{:S(2)}, u32[]{:S(2)}) collective-permute-start(bf16[64,2048]{1,0:T(8,128)(2,1)S(1)} %copy-done.53), channel_id=1, source_target_pairs={{0,3},{1,2},{2,1},{3,0},{4,7},{5,6},{6,5},{7,4},{8,11},{9,10},{10,... | collective-permute-start | bytes 786440 | tf_op jit(solution)/shard_map/ppermute | solution.py:29
  124.2 484.9 %reduce-scatter.6.cloned.1.call-start = ((), (), s32[]{:S(2)}) async-start(), calls=%async_computation.10 | async-start | bytes 9437184 | tf_op jit(solution)/shard_map/reduce_scatter | solution.py:258
  134.9 15.0 %collective-permute-start.13 = (bf16[2,64,2048]{2,1,0:T(8,128)(2,1)S(1)}, bf16[2,64,2048]{2,1,0:T(8,128)(2,1)S(1)}, u32[]{:S(2)}, u32[]{:S(2)}) collective-permute-start(bf16[2,64,2048]{2,1,0:T(8,128)(2,1)S(1)} %get-tuple-element.121), channel_id=1, source_target_pairs={{0,2},{1,3},{2,0},{3,1},{4,6},{5,7},{6,4},{7,5},{8,10},{9,11},{10,... | collective-permute-start | bytes 1572872 | tf_op jit(solution)/shard_map/ppermute | solution.py:29
  139.0 11.7 %collective-permute-start.14 = (bf16[2,64,2048]{2,1,0:T(8,128)(2,1)S(1)}, bf16[2,64,2048]{2,1,0:T(8,128)(2,1)S(1)}, u32[]{:S(2)}, u32[]{:S(2)}) collective-permute-start(bf16[2,64,2048]{2,1,0:T(8,128)(2,1)S(1)} %get-tuple-element.120), channel_id=1, source_target_pairs={{0,3},{1,2},{2,1},{3,0},{4,7},{5,6},{6,5},{7,4},{8,11},{9,10},{10,... | collective-permute-start | bytes 1572872 | tf_op jit(solution)/shard_map/ppermute | solution.py:29
  212.2 25.9 %collective-permute-start.17 = (bf16[256,2048]{1,0:T(8,128)(2,1)}, bf16[256,2048]{1,0:T(8,128)(2,1)S(1)}, u32[]{:S(2)}, u32[]{:S(2)}) collective-permute-start(bf16[256,2048]{1,0:T(8,128)(2,1)} %get-tuple-element.95), channel_id=1, source_target_pairs={{0,3},{1,2},{2,1},{3,0},{4,7},{5,6},{6,5},{7,4},{8,11},{9,10},{10,... | collective-permute-start | bytes 3145736 | tf_op jit(solution)/shard_map/ppermute | solution.py:29
  213.6 35.5 %collective-permute-start.16 = (bf16[256,2048]{1,0:T(8,128)(2,1)}, bf16[256,2048]{1,0:T(8,128)(2,1)S(1)}, u32[]{:S(2)}, u32[]{:S(2)}) collective-permute-start(bf16[256,2048]{1,0:T(8,128)(2,1)} %get-tuple-element.96), channel_id=1, source_target_pairs={{0,2},{1,3},{2,0},{3,1},{4,6},{5,7},{6,4},{7,5},{8,10},{9,11},{10,... | collective-permute-start | bytes 3145736 | tf_op jit(solution)/shard_map/ppermute | solution.py:29
  215.2 33.9 %collective-permute-start.15 = (bf16[256,2048]{1,0:T(8,128)(2,1)S(1)}, bf16[256,2048]{1,0:T(8,128)(2,1)}, u32[]{:S(2)}, u32[]{:S(2)}) collective-permute-start(bf16[256,2048]{1,0:T(8,128)(2,1)S(1)} %get-tuple-element.94), channel_id=1, source_target_pairs={{0,1},{1,0},{2,3},{3,2},{4,5},{5,4},{6,7},{7,6},{8,9},{9,8},{10,11... | collective-permute-start | bytes 3145736 | tf_op jit(solution)/shard_map/ppermute | solution.py:29
  255.4 26.1 %collective-permute-start.18 = (bf16[256,2048]{1,0:T(8,128)(2,1)S(1)}, bf16[256,2048]{1,0:T(8,128)(2,1)S(1)}, u32[]{:S(2)}, u32[]{:S(2)}) collective-permute-start(bf16[256,2048]{1,0:T(8,128)(2,1)S(1)} %get-tuple-element.80), channel_id=1, source_target_pairs={{0,1},{1,0},{2,3},{3,2},{4,5},{5,4},{6,7},{7,6},{8,9},{9,8},{10,11... | collective-permute-start | bytes 3145736 | tf_op jit(solution)/shard_map/ppermute | solution.py:29
  255.9 45.4 %collective-permute-start.19 = (bf16[256,2048]{1,0:T(8,128)(2,1)S(1)}, bf16[256,2048]{1,0:T(8,128)(2,1)S(1)}, u32[]{:S(2)}, u32[]{:S(2)}) collective-permute-start(bf16[256,2048]{1,0:T(8,128)(2,1)S(1)} %get-tuple-element.80), channel_id=1, source_target_pairs={{0,2},{1,3},{2,0},{3,1},{4,6},{5,7},{6,4},{7,5},{8,10},{9,11},{10,... | collective-permute-start | bytes 3145736 | tf_op jit(solution)/shard_map/ppermute | solution.py:29
  257.1 45.2 %collective-permute-start.20 = (bf16[256,2048]{1,0:T(8,128)(2,1)S(1)}, bf16[256,2048]{1,0:T(8,128)(2,1)S(1)}, u32[]{:S(2)}, u32[]{:S(2)}) collective-permute-start(bf16[256,2048]{1,0:T(8,128)(2,1)S(1)} %get-tuple-element.80), channel_id=1, source_target_pairs={{0,3},{1,2},{2,1},{3,0},{4,7},{5,6},{6,5},{7,4},{8,11},{9,10},{10,... | collective-permute-start | bytes 3145736 | tf_op jit(solution)/shard_map/ppermute | solution.py:29
  387.0 27.1 %collective-permute-start.32 = (bf16[256,2048]{1,0:T(8,128)(2,1)}, bf16[256,2048]{1,0:T(8,128)(2,1)S(1)}, u32[]{:S(2)}, u32[]{:S(2)}) collective-permute-start(bf16[256,2048]{1,0:T(8,128)(2,1)} %get-tuple-element.92), channel_id=1, source_target_pairs={{0,3},{1,2},{2,1},{3,0},{4,7},{5,6},{6,5},{7,4},{8,11},{9,10},{10,... | collective-permute-start | bytes 3145736 | tf_op jit(solution)/shard_map/ppermute | solution.py:29
  389.4 46.5 %collective-permute-start.31 = (bf16[256,2048]{1,0:T(8,128)(2,1)}, bf16[256,2048]{1,0:T(8,128)(2,1)S(1)}, u32[]{:S(2)}, u32[]{:S(2)}) collective-permute-start(bf16[256,2048]{1,0:T(8,128)(2,1)} %get-tuple-element.93), channel_id=1, source_target_pairs={{0,2},{1,3},{2,0},{3,1},{4,6},{5,7},{6,4},{7,5},{8,10},{9,11},{10,... | collective-permute-start | bytes 3145736 | tf_op jit(solution)/shard_map/ppermute | solution.py:29
  389.9 46.1 %collective-permute-start.30 = (bf16[256,2048]{1,0:T(8,128)(2,1)}, bf16[256,2048]{1,0:T(8,128)(2,1)}, u32[]{:S(2)}, u32[]{:S(2)}) collective-permute-start(bf16[256,2048]{1,0:T(8,128)(2,1)} %get-tuple-element.91), channel_id=1, source_target_pairs={{0,1},{1,0},{2,3},{3,2},{4,5},{5,4},{6,7},{7,6},{8,9},{9,8},{10,11... | collective-permute-start | bytes 3145736 | tf_op jit(solution)/shard_map/ppermute | solution.py:29
  440.7 26.1 %collective-permute-start.33 = (bf16[256,2048]{1,0:T(8,128)(2,1)S(1)}, bf16[256,2048]{1,0:T(8,128)(2,1)S(1)}, u32[]{:S(2)}, u32[]{:S(2)}) collective-permute-start(bf16[256,2048]{1,0:T(8,128)(2,1)S(1)} %get-tuple-element.76), channel_id=1, source_target_pairs={{0,1},{1,0},{2,3},{3,2},{4,5},{5,4},{6,7},{7,6},{8,9},{9,8},{10,11... | collective-permute-start | bytes 3145736 | tf_op jit(solution)/shard_map/ppermute | solution.py:29
  442.2 47.2 %collective-permute-start.34 = (bf16[256,2048]{1,0:T(8,128)(2,1)S(1)}, bf16[256,2048]{1,0:T(8,128)(2,1)S(1)}, u32[]{:S(2)}, u32[]{:S(2)}) collective-permute-start(bf16[256,2048]{1,0:T(8,128)(2,1)S(1)} %get-tuple-element.76), channel_id=1, source_target_pairs={{0,2},{1,3},{2,0},{3,1},{4,6},{5,7},{6,4},{7,5},{8,10},{9,11},{10,... | collective-permute-start | bytes 3145736 | tf_op jit(solution)/shard_map/ppermute | solution.py:29
  442.8 46.7 %collective-permute-start.35 = (bf16[256,2048]{1,0:T(8,128)(2,1)S(1)}, bf16[256,2048]{1,0:T(8,128)(2,1)S(1)}, u32[]{:S(2)}, u32[]{:S(2)}) collective-permute-start(bf16[256,2048]{1,0:T(8,128)(2,1)S(1)} %get-tuple-element.76), channel_id=1, source_target_pairs={{0,3},{1,2},{2,1},{3,0},{4,7},{5,6},{6,5},{7,4},{8,11},{9,10},{10,... | collective-permute-start | bytes 3145736 | tf_op jit(solution)/shard_map/ppermute | solution.py:29
  503.0 193.5 %reduce-scatter.8.cloned.1.call-start = ((), (), s32[]{:S(2)}) async-start(), calls=%async_computation.11 | async-start | bytes 9437184 | tf_op jit(solution)/shard_map/reduce_scatter | solution.py:258
  557.5 31.3 %collective-permute-start.38 = (bf16[256,2048]{1,0:T(8,128)(2,1)}, bf16[256,2048]{1,0:T(8,128)(2,1)}, u32[]{:S(2)}, u32[]{:S(2)}) collective-permute-start(bf16[256,2048]{1,0:T(8,128)(2,1)} %get-tuple-element.90), channel_id=1, source_target_pairs={{0,3},{1,2},{2,1},{3,0},{4,7},{5,6},{6,5},{7,4},{8,11},{9,10},{10,... | collective-permute-start | bytes 3145736 | tf_op jit(solution)/shard_map/ppermute | solution.py:29
  558.6 46.2 %collective-permute-start.37 = (bf16[256,2048]{1,0:T(8,128)(2,1)S(1)}, bf16[256,2048]{1,0:T(8,128)(2,1)}, u32[]{:S(2)}, u32[]{:S(2)}) collective-permute-start(bf16[256,2048]{1,0:T(8,128)(2,1)S(1)} %get-tuple-element.89), channel_id=1, source_target_pairs={{0,2},{1,3},{2,0},{3,1},{4,6},{5,7},{6,4},{7,5},{8,10},{9,11},{10,... | collective-permute-start | bytes 3145736 | tf_op jit(solution)/shard_map/ppermute | solution.py:29
  559.2 45.5 %collective-permute-start.36 = (bf16[256,2048]{1,0:T(8,128)(2,1)S(1)}, bf16[256,2048]{1,0:T(8,128)(2,1)}, u32[]{:S(2)}, u32[]{:S(2)}) collective-permute-start(bf16[256,2048]{1,0:T(8,128)(2,1)S(1)} %get-tuple-element.88), channel_id=1, source_target_pairs={{0,1},{1,0},{2,3},{3,2},{4,5},{5,4},{6,7},{7,6},{8,9},{9,8},{10,11... | collective-permute-start | bytes 3145736 | tf_op jit(solution)/shard_map/ppermute | solution.py:29
  609.1 177.7 %reduce-scatter.10.cloned.1.call-start = ((), (), s32[]{:S(2)}) async-start(), calls=%async_computation.12 | async-start | bytes 9437184 | tf_op jit(solution)/shard_map/reduce_scatter | solution.py:258
  618.1 26.1 %collective-permute-start.39 = (bf16[256,2048]{1,0:T(8,128)(2,1)S(1)}, bf16[256,2048]{1,0:T(8,128)(2,1)S(1)}, u32[]{:S(2)}, u32[]{:S(2)}) collective-permute-start(bf16[256,2048]{1,0:T(8,128)(2,1)S(1)} %get-tuple-element.74), channel_id=1, source_target_pairs={{0,1},{1,0},{2,3},{3,2},{4,5},{5,4},{6,7},{7,6},{8,9},{9,8},{10,11... | collective-permute-start | bytes 3145736 | tf_op jit(solution)/shard_map/ppermute | solution.py:29
  618.5 47.1 %collective-permute-start.40 = (bf16[256,2048]{1,0:T(8,128)(2,1)S(1)}, bf16[256,2048]{1,0:T(8,128)(2,1)S(1)}, u32[]{:S(2)}, u32[]{:S(2)}) collective-permute-start(bf16[256,2048]{1,0:T(8,128)(2,1)S(1)} %get-tuple-element.74), channel_id=1, source_target_pairs={{0,2},{1,3},{2,0},{3,1},{4,6},{5,7},{6,4},{7,5},{8,10},{9,11},{10,... | collective-permute-start | bytes 3145736 | tf_op jit(solution)/shard_map/ppermute | solution.py:29
  619.9 45.8 %collective-permute-start.41 = (bf16[256,2048]{1,0:T(8,128)(2,1)S(1)}, bf16[256,2048]{1,0:T(8,128)(2,1)S(1)}, u32[]{:S(2)}, u32[]{:S(2)}) collective-permute-start(bf16[256,2048]{1,0:T(8,128)(2,1)S(1)} %get-tuple-element.74), channel_id=1, source_target_pairs={{0,3},{1,2},{2,1},{3,0},{4,7},{5,6},{6,5},{7,4},{8,11},{9,10},{10,... | collective-permute-start | bytes 3145736 | tf_op jit(solution)/shard_map/ppermute | solution.py:29
  696.6 126.7 %reduce-scatter.12.cloned.1.call-start = ((), (), s32[]{:S(2)}) async-start(), calls=%async_computation.13 | async-start | bytes 2359296 | tf_op jit(solution)/shard_map/reduce_scatter | solution.py:258
  702.4 14.9 %collective-permute-start.48 = (bf16[2,64,2048]{2,1,0:T(8,128)(2,1)S(1)}, bf16[2,64,2048]{2,1,0:T(8,128)(2,1)S(1)}, u32[]{:S(2)}, u32[]{:S(2)}) collective-permute-start(bf16[2,64,2048]{2,1,0:T(8,128)(2,1)S(1)} %get-tuple-element.100), channel_id=1, source_target_pairs={{0,1},{1,0},{2,3},{3,2},{4,5},{5,4},{6,7},{7,6},{8,9},{9,8},{10,11... | collective-permute-start | bytes 1572872 | tf_op jit(solution)/shard_map/ppermute | solution.py:29
  704.0 22.5 %collective-permute-start.49 = (bf16[2,64,2048]{2,1,0:T(8,128)(2,1)S(1)}, bf16[2,64,2048]{2,1,0:T(8,128)(2,1)S(1)}, u32[]{:S(2)}, u32[]{:S(2)}) collective-permute-start(bf16[2,64,2048]{2,1,0:T(8,128)(2,1)S(1)} %get-tuple-element.99), channel_id=1, source_target_pairs={{0,2},{1,3},{2,0},{3,1},{4,6},{5,7},{6,4},{7,5},{8,10},{9,11},{10,... | collective-permute-start | bytes 1572872 | tf_op jit(solution)/shard_map/ppermute | solution.py:29
  707.9 37.5 %collective-permute-start.50 = (bf16[2,64,2048]{2,1,0:T(8,128)(2,1)S(1)}, bf16[2,64,2048]{2,1,0:T(8,128)(2,1)S(1)}, u32[]{:S(2)}, u32[]{:S(2)}) collective-permute-start(bf16[2,64,2048]{2,1,0:T(8,128)(2,1)S(1)} %get-tuple-element.98), channel_id=1, source_target_pairs={{0,3},{1,2},{2,1},{3,0},{4,7},{5,6},{6,5},{7,4},{8,11},{9,10},{10,... | collective-permute-start | bytes 1572872 | tf_op jit(solution)/shard_map/ppermute | solution.py:29
  786.9 140.7 %reduce-scatter.14.cloned.1.call-start = ((), (), s32[]{:S(2)}) async-start(), calls=%async_computation.14 | async-start | bytes 7077888 | tf_op jit(solution)/shard_map/reduce_scatter | solution.py:258
  844.4 22.0 %collective-permute-start.66 = (bf16[64,2048]{1,0:T(8,128)(2,1)S(1)}, bf16[64,2048]{1,0:T(8,128)(2,1)S(1)}, u32[]{:S(2)}, u32[]{:S(2)}) collective-permute-start(bf16[64,2048]{1,0:T(8,128)(2,1)S(1)} %get-tuple-element.137), channel_id=1, source_target_pairs={{0,1},{1,0},{2,3},{3,2},{4,5},{5,4},{6,7},{7,6},{8,9},{9,8},{10,11... | collective-permute-start | bytes 786440 | tf_op jit(solution)/shard_map/ppermute | solution.py:29
  844.7 21.9 %collective-permute-start.67 = (bf16[64,2048]{1,0:T(8,128)(2,1)S(1)}, bf16[64,2048]{1,0:T(8,128)(2,1)S(1)}, u32[]{:S(2)}, u32[]{:S(2)}) collective-permute-start(bf16[64,2048]{1,0:T(8,128)(2,1)S(1)} %get-tuple-element.136), channel_id=1, source_target_pairs={{0,2},{1,3},{2,0},{3,1},{4,6},{5,7},{6,4},{7,5},{8,10},{9,11},{10,... | collective-permute-start | bytes 786440 | tf_op jit(solution)/shard_map/ppermute | solution.py:29
  846.6 20.0 %collective-permute-start.68 = (bf16[64,2048]{1,0:T(8,128)(2,1)S(1)}, bf16[64,2048]{1,0:T(8,128)(2,1)S(1)}, u32[]{:S(2)}, u32[]{:S(2)}) collective-permute-start(bf16[64,2048]{1,0:T(8,128)(2,1)S(1)} %get-tuple-element.135), channel_id=1, source_target_pairs={{0,3},{1,2},{2,1},{3,0},{4,7},{5,6},{6,5},{7,4},{8,11},{9,10},{10,... | collective-permute-start | bytes 786440 | tf_op jit(solution)/shard_map/ppermute | solution.py:29
  862.5 27.0 %collective-permute-start.47 = (bf16[256,2048]{1,0:T(8,128)(2,1)S(1)}, bf16[256,2048]{1,0:T(8,128)(2,1)S(1)}, u32[]{:S(2)}, u32[]{:S(2)}) collective-permute-start(bf16[256,2048]{1,0:T(8,128)(2,1)S(1)} %get-tuple-element.86), channel_id=1, source_target_pairs={{0,3},{1,2},{2,1},{3,0},{4,7},{5,6},{6,5},{7,4},{8,11},{9,10},{10,... | collective-permute-start | bytes 3145736 | tf_op jit(solution)/shard_map/ppermute | solution.py:29
  864.8 46.0 %collective-permute-start.46 = (bf16[256,2048]{1,0:T(8,128)(2,1)S(1)}, bf16[256,2048]{1,0:T(8,128)(2,1)S(1)}, u32[]{:S(2)}, u32[]{:S(2)}) collective-permute-start(bf16[256,2048]{1,0:T(8,128)(2,1)S(1)} %get-tuple-element.87), channel_id=1, source_target_pairs={{0,2},{1,3},{2,0},{3,1},{4,6},{5,7},{6,4},{7,5},{8,10},{9,11},{10,... | collective-permute-start | bytes 3145736 | tf_op jit(solution)/shard_map/ppermute | solution.py:29
  866.4 45.3 %collective-permute-start.45 = (bf16[256,2048]{1,0:T(8,128)(2,1)S(1)}, bf16[256,2048]{1,0:T(8,128)(2,1)S(1)}, u32[]{:S(2)}, u32[]{:S(2)}) collective-permute-start(bf16[256,2048]{1,0:T(8,128)(2,1)S(1)} %get-tuple-element.85), channel_id=1, source_target_pairs={{0,1},{1,0},{2,3},{3,2},{4,5},{5,4},{6,7},{7,6},{8,9},{9,8},{10,11... | collective-permute-start | bytes 3145736 | tf_op jit(solution)/shard_map/ppermute | solution.py:29
  866.8 49.4 %collective-permute-start.69 = (bf16[64,2048]{1,0:T(8,128)(2,1)S(1)}, bf16[64,2048]{1,0:T(8,128)(2,1)S(1)}, u32[]{:S(2)}, u32[]{:S(2)}) collective-permute-start(bf16[64,2048]{1,0:T(8,128)(2,1)S(1)} %get-tuple-element.134), channel_id=1, source_target_pairs={{0,1},{1,0},{2,3},{3,2},{4,5},{5,4},{6,7},{7,6},{8,9},{9,8},{10,11... | collective-permute-start | bytes 786440 | tf_op jit(solution)/shard_map/ppermute | solution.py:29
  913.4 13.1 %collective-permute-start.70 = (bf16[64,2048]{1,0:T(8,128)(2,1)S(1)}, bf16[64,2048]{1,0:T(8,128)(2,1)S(1)}, u32[]{:S(2)}, u32[]{:S(2)}) collective-permute-start(bf16[64,2048]{1,0:T(8,128)(2,1)S(1)} %get-tuple-element.133), channel_id=1, source_target_pairs={{0,2},{1,3},{2,0},{3,1},{4,6},{5,7},{6,4},{7,5},{8,10},{9,11},{10,... | collective-permute-start | bytes 786440 | tf_op jit(solution)/shard_map/ppermute | solution.py:29
  914.3 12.2 %collective-permute-start.71 = (bf16[64,2048]{1,0:T(8,128)(2,1)S(1)}, bf16[64,2048]{1,0:T(8,128)(2,1)S(1)}, u32[]{:S(2)}, u32[]{:S(2)}) collective-permute-start(bf16[64,2048]{1,0:T(8,128)(2,1)S(1)} %get-tuple-element.132), channel_id=1, source_target_pairs={{0,3},{1,2},{2,1},{3,0},{4,7},{5,6},{6,5},{7,4},{8,11},{9,10},{10,... | collective-permute-start | bytes 786440 | tf_op jit(solution)/shard_map/ppermute | solution.py:29
  (108 other events, 1000.1 us)
Sparse Core Ops, SparseCore 0:
  27.9 30.3 all-gather.7
  60.6 64.2 all-gather.5
  126.4 80.6 all-gather.9
  208.6 80.5 all-gather.11
  290.7 80.5 all-gather.13
  503.2 87.0 reduce-scatter.5
  609.3 87.2 reduce-scatter.7
  698.8 87.9 reduce-scatter.9
  789.1 34.1 reduce-scatter.11
  825.4 69.2 reduce-scatter.13

commit v2 on v1

v2 whole, which is shorter than its diff:
```python
import functools
import math

import jax
import jax.numpy as jnp
from jax import lax
from jax.experimental import pallas as pl
from jax.experimental.pallas import tpu as pltpu
from jax.sharding import PartitionSpec as P

HEAD_DIM = 128
MESH = pl.DeviceIdType.MESH

epsilon = 1e-06
rope_theta = 500000.0
masked_fill = -1e30
bf16 = jnp.bfloat16
f32 = jnp.float32
NN = (((1,), (0,)), ((), ()))
NT = (((1,), (1,)), ((), ()))
TN = (((0,), (0,)), ((), ()))


def dot(left, right, dims, kind=f32):
    return lax.dot_general(left, right, dims, preferred_element_type=f32).astype(kind)


def swap(piece, hop):
    count = lax.axis_size("row")
    return lax.ppermute(piece, "row", [(i, i ^ hop) for i in range(count)])


def gather_rows(rows, *meanwhile):
    count, me = lax.axis_size("row"), lax.axis_index("row")
    size = rows.shape[0]
    whole = jnp.zeros((count * size,) + rows.shape[1:], rows.dtype)
    for hop in range(1, count):
        whole = lax.dynamic_update_slice_in_dim(whole, swap(rows, hop), (me ^ hop) * size, 0)
    return lax.dynamic_update_slice_in_dim(whole, tie(rows, *meanwhile), me * size, 0)


def dot_scatter(lefts, rights, dims, *meanwhile):
    count, me = lax.axis_size("row"), lax.axis_index("row")
    size = lefts[0].shape[0] // count

    def rows_of(hop, lefts):
        parts = [lax.dynamic_slice_in_dim(left, (me ^ hop) * size, size, 0) for left in lefts]
        return sum(dot(part, right, dims) for part, right in zip(parts, rights))

    coming = [swap(rows_of(hop, lefts).astype(bf16), hop) for hop in reversed(range(1, count))]
    total = rows_of(0, [tie(left, *meanwhile) for left in lefts])
    for piece in coming:
        total = total + piece.astype(f32)
    return total


def tie(value, *others):
    return lax.optimization_barrier((value,) + others)[0]


def columns_in(*weights):
    count, me = lax.axis_size("row"), lax.axis_index("row")
    size, wide = weights[0].shape[0], weights[0].shape[1] // count
    whole = jnp.zeros((count * size, wide * len(weights)), bf16)
    for hop in range(count):
        piece = jnp.concatenate(
            [lax.dynamic_slice_in_dim(w, (me ^ hop) * wide, wide, 1).astype(bf16) for w in weights], axis=1
        )
        if hop:
            piece = swap(piece, hop)
        whole = lax.dynamic_update_slice_in_dim(whole, piece, (me ^ hop) * size, 0)
    return whole


def columns_out(block, many=1):
    count, me = lax.axis_size("row"), lax.axis_index("row")
    size, wide = block.shape[0] // count, block.shape[1] // many
    whole = [jnp.zeros((size, wide * count), f32)] * many
    for hop in range(count):
        piece = lax.dynamic_slice_in_dim(block, (me ^ hop) * size, size, 0)
        if hop:
            piece = swap(piece, hop)
        for i in range(many):
            own = piece[:, i * wide : (i + 1) * wide].astype(f32)
            whole[i] = lax.dynamic_update_slice_in_dim(whole[i], own, (me ^ hop) * wide, 1)
    return whole


def sum_rows(small):
    count = lax.axis_size("row")
    total = small
    for hop in range(1, count):
        total = total + swap(small, hop)
    return total


def norm_back(grad_out, unit_rows, scaled, gain_row):
    weighted = grad_out * gain_row
    inner = jnp.mean(weighted * unit_rows, axis=-1, keepdims=True)
    return (scaled * (weighted - unit_rows * inner), jnp.sum(grad_out * unit_rows, axis=0))


def tree_tables(length_row, parent_row, total):
    seg_count = parent_row.shape[0]
    segment_ids = jnp.arange(seg_count, dtype=jnp.int32)
    ends = jnp.cumsum(length_row)
    offsets = ends - length_row
    all_rows = jnp.arange(total, dtype=jnp.int32)
    owned_from = (all_rows[:, None] >= offsets[None, :]).astype(f32)
    onehot_all = owned_from - jnp.concatenate(
        [owned_from[:, 1:], jnp.zeros((total, 1), f32)], axis=1
    )
    reached = (
        (parent_row[:, None] == segment_ids[None, :])
        | (segment_ids[:, None] == segment_ids[None, :])
    ).astype(f32)
    for _ in range(2):
        reached = jnp.minimum(jnp.sum(reached[:, :, None] * reached[None, :, :], axis=1), 1.0)
    strict = reached - jnp.eye(seg_count, dtype=f32)
    path_start = jnp.sum(strict * length_row.astype(f32)[None, :], axis=1)
    position = all_rows.astype(f32) + jnp.sum(
        onehot_all * (path_start - offsets.astype(f32))[None, :], axis=1
    )
    onehot_low = onehot_all.astype(bf16)
    row_reach = dot(onehot_low, reached.astype(bf16), NN, bf16)
    seen = dot(onehot_low, row_reach, NT)
    allowed = (seen > 0.5) & (all_rows[:, None] <= all_rows[None, :])
    bias = jnp.where(allowed, 0.0, masked_fill).astype(bf16)
    frequency = jnp.exp(
        jnp.arange(HEAD_DIM // 2, dtype=f32) * (-2.0 * math.log(rope_theta) / HEAD_DIM)
    )
    angles = position[:, None] * frequency[None, :]
    cos_half, sin_half = jnp.cos(angles), jnp.sin(angles)
    cos_wide = jnp.concatenate([cos_half, cos_half], axis=1)
    sin_wide = jnp.concatenate([-sin_half, sin_half], axis=1)
    return (bias, cos_wide, sin_wide)


def turn(vector, cos_part, sin_part):
    return vector * cos_part + pltpu.roll(vector, HEAD_DIM // 2, 1) * sin_part


def project_kernel(tokens_ref, weights_ref, query_ref, key_ref, value_ref, squares_ref):
    part = query_ref.shape[1]
    tokens = tokens_ref[...]
    for i, out_ref in enumerate((query_ref, key_ref)):
        product = dot(tokens, weights_ref[:, i * part : (i + 1) * part], NN)
        out_ref[...] = product
        square = jnp.sum(product * product, axis=1, keepdims=True)
        squares_ref[i : i + 1, :] = jnp.broadcast_to(square, (square.shape[0], HEAD_DIM)).T[0:1]
    value_ref[...] = dot(tokens, weights_ref[:, 2 * part :], NN, bf16)


def project(tokens, weights, part):
    total, width = tokens.shape
    size = 256
    rows = pl.BlockSpec((size, part), lambda i: (i, 0))
    wide = jax.ShapeDtypeStruct((total, part), f32)
    return pl.pallas_call(
        project_kernel,
        grid=(total // size,),
        in_specs=[
            pl.BlockSpec((size, width), lambda i: (i, 0)),
            pl.BlockSpec((width, 3 * part), lambda i: (0, 0)),
        ],
        out_specs=[rows, rows, rows, pl.BlockSpec((2, size), lambda i: (0, i))],
        out_shape=[
            wide,
            wide,
            jax.ShapeDtypeStruct((total, part), bf16),
            jax.ShapeDtypeStruct((2, total), f32),
        ],
        compiler_params=pltpu.CompilerParams(vmem_limit_bytes=48 * 2**20),
        cost_estimate=pl.CostEstimate(
            flops=6 * total * width * part, bytes_accessed=2 * width * (total + 3 * part) + 10 * total * part, transcendentals=0
        ),
    )(tokens, weights)


def attend_kernel(
    block,
    scale,
    query_pre_ref,
    key_pre_ref,
    value_ref,
    scales_ref,
    gains_ref,
    cos_ref,
    sin_ref,
    bias_ref,
    query_ref,
    key_ref,
    context_ref,
    lse_ref,
):
    total = key_ref.shape[0]
    cos_part, sin_part = cos_ref[...], sin_ref[...]
    query_ref[...] = turn(query_pre_ref[...] * scales_ref[:, 0:1] * gains_ref[0:1], cos_part, sin_part).astype(bf16)
    key_ref[...] = turn(key_pre_ref[...] * scales_ref[:, 1:2] * gains_ref[1:2], cos_part, sin_part).astype(bf16)
    for first in range(0, total, block):
        last = first + block
        scores = dot(key_ref[:last], query_ref[first:last], NT) * scale
        scores = scores + bias_ref[:last, first:last].astype(f32)
        top = jnp.max(scores, axis=0, keepdims=True)
        probs = jnp.exp(scores - top)
        mass = jnp.sum(probs, axis=0, keepdims=True)
        probs_low = (probs * (1.0 / mass)).astype(bf16)
        turned = dot(value_ref[:last], probs_low, TN)
        context_ref[first:last, :] = turned.T.astype(bf16)
        lse_ref[:, first:last] = jnp.broadcast_to(top + jnp.log(mass), (8, block))


def head_specs(total):
    part = pl.BlockSpec((total, HEAD_DIM), lambda h: (0, h))
    whole = pl.BlockSpec((total, HEAD_DIM), lambda h: (0, 0))
    gains = pl.BlockSpec((2, HEAD_DIM), lambda h: (0, h))
    scales = pl.BlockSpec((total, 2), lambda h: (0, 0))
    bias = pl.BlockSpec((total, total), lambda h: (0, 0))
    lse = pl.BlockSpec((8, total), lambda h: (h, 0))
    return part, whole, gains, scales, bias, lse


def attend(query_pre, key_pre, value, scales, gains, cos_wide, sin_wide, bias):
    total, width = query_pre.shape
    heads = width // HEAD_DIM
    part, whole, gain, scale, square, lse = head_specs(total)
    low = jax.ShapeDtypeStruct((total, width), bf16)
    return pl.pallas_call(
        functools.partial(attend_kernel, 256, 1.0 / math.sqrt(HEAD_DIM)),
        grid=(heads,),
        in_specs=[part, part, part, scale, gain, whole, whole, square],
        out_specs=[part, part, part, lse],
        out_shape=[low, low, low, jax.ShapeDtypeStruct((8 * heads, total), f32)],
        compiler_params=pltpu.CompilerParams(vmem_limit_bytes=56 * 2**20),
        cost_estimate=pl.CostEstimate(
            flops=4 * total * total * width, bytes_accessed=16 * total * width, transcendentals=total * total * heads
        ),
    )(query_pre, key_pre, value, scales, gains, cos_wide, sin_wide, bias)


def attend_back_kernel(
    block,
    scale,
    query_ref,
    key_ref,
    value_ref,
    bias_ref,
    lse_ref,
    grad_ref,
    query_pre_ref,
    key_pre_ref,
    scales_ref,
    gains_ref,
    cos_ref,
    sin_ref,
    grad_query_ref,
    grad_key_ref,
    grad_value_ref,
    inner_query_ref,
    inner_key_ref,
    grad_gains_ref,
    key_sum,
    value_sum,
):
    total = key_ref.shape[0]

    @pl.when(pl.program_id(0) == 0)
    def _():
        inner_query_ref[...] = jnp.zeros_like(inner_query_ref)
        inner_key_ref[...] = jnp.zeros_like(inner_key_ref)

    key_sum[...] = jnp.zeros_like(key_sum)
    value_sum[...] = jnp.zeros_like(value_sum)
    for first in range(0, total, block):
        last = first + block
        scores = dot(key_ref[:last], query_ref[first:last], NT) * scale
        scores = scores + bias_ref[:last, first:last].astype(f32)
        probs = jnp.exp(scores - lse_ref[0:1, first:last])
        grad_probs = dot(value_ref[:last], grad_ref[first:last], NT)
        inner = jnp.sum(probs * grad_probs, axis=0, keepdims=True)
        grad_scores = (probs * (grad_probs - inner)).astype(bf16)
        turned = dot(key_ref[:last], grad_scores, TN)
        grad_query_ref[first:last, :] = turned.T
        key_sum[:last, :] += dot(grad_scores, query_ref[first:last], NN)
        value_sum[:last, :] += dot(probs.astype(bf16), grad_ref[first:last], NN)
    grad_value_ref[...] = value_sum[...].astype(bf16)
    cos_part, sin_part = cos_ref[...], -sin_ref[...]
    for row, (grad, out_ref, pre_ref, inner_ref) in enumerate(
        (
            (grad_query_ref[...], grad_query_ref, query_pre_ref, inner_query_ref),
            (key_sum[...], grad_key_ref, key_pre_ref, inner_key_ref),
        )
    ):
        grad = turn(grad * scale, cos_part, sin_part)
        by_unit = grad * (pre_ref[...] * scales_ref[:, row : row + 1])
        inner_ref[...] += by_unit * gains_ref[row : row + 1]
        grad_gains_ref[row : row + 1, :] = jnp.sum(by_unit, axis=0, keepdims=True)
        out_ref[...] = grad


def attend_back(query, key, value, bias, lse, grad_context, query_pre, key_pre, scales, gains, cos_wide, sin_wide):
    total, width = query.shape
    heads = width // HEAD_DIM
    part, whole, gain, scale, square, lse_spec = head_specs(total)
    wide = jax.ShapeDtypeStruct((total, width), f32)
    narrow = jax.ShapeDtypeStruct((total, HEAD_DIM), f32)
    return pl.pallas_call(
        functools.partial(attend_back_kernel, 256, 1.0 / math.sqrt(HEAD_DIM)),
        grid=(heads,),
        in_specs=[part, part, part, square, lse_spec, part, part, part, scale, gain, whole, whole],
        out_specs=[part, part, part, whole, whole, gain],
        out_shape=[
            wide,
            wide,
            jax.ShapeDtypeStruct((total, width), bf16),
            narrow,
            narrow,
            jax.ShapeDtypeStruct((2, width), f32),
        ],
        scratch_shapes=[pltpu.VMEM((total, HEAD_DIM), f32)] * 2,
        compiler_params=pltpu.CompilerParams(vmem_limit_bytes=58 * 2**20),
        cost_estimate=pl.CostEstimate(
            flops=10 * total * total * width, bytes_accessed=30 * total * width, transcendentals=total * total * heads
        ),
    )(query, key, value, bias, lse, grad_context, query_pre, key_pre, scales, gains, cos_wide, sin_wide)


def sums_kernel(tokens_ref, grads_ref, side_ref, out_ref):
    wide = grads_ref.shape[1]
    out_ref[:, :wide] = dot(tokens_ref[...], grads_ref[...], TN, bf16)
    out_ref[:, wide:] = side_ref[...]


def sums_beside(tokens, grads, side):
    total, rows = tokens.shape
    wide, extra = grads.shape[1], side.shape[1]
    size = 256
    return pl.pallas_call(
        sums_kernel,
        grid=(rows // size,),
        in_specs=[
            pl.BlockSpec((total, size), lambda i: (0, i)),
            pl.BlockSpec((total, wide), lambda i: (0, 0)),
            pl.BlockSpec((size, extra), lambda i: (i, 0)),
        ],
        out_specs=pl.BlockSpec((size, wide + extra), lambda i: (i, 0)),
        out_shape=jax.ShapeDtypeStruct((rows, wide + extra), bf16),
        compiler_params=pltpu.CompilerParams(vmem_limit_bytes=40 * 2**20),
        cost_estimate=pl.CostEstimate(
            flops=2 * total * rows * wide, bytes_accessed=2 * rows * (total + wide + 2 * extra), transcendentals=0
        ),
    )(tokens, grads, side)


def landed(ref, sem):
    pltpu.make_async_copy(ref, ref, sem).wait()


def line_order(z):
    far, inner = z // 2, ((z + 1) // 2) % 2
    blocks = []
    for end, middle in ((3, 0), (2, 2), (1, 3), (0, 1)):
        first = end + inner * (middle - end)
        blocks.append(first + far * (3 - 2 * first))
    near = 1 + far
    chips = [near + inner * (blocks[0] - near), blocks[1], blocks[2]]
    slots = [3 + inner * (-2 - far), 2 + inner * (far - 2), far + inner * (2 - far)]
    return far, inner, blocks, chips, slots


def other(index, hop):
    return (index, index + 1 - 2 * (index % 2), (index + 2) % 4, 3 - index)[hop]


def final_kernel(
    tokens_hbm,
    grads_hbm,
    weights_hbm,
    output_hbm,
    hidden_hbm,
    up_hbm,
    query_out,
    key_out,
    value_out,
    output_out,
    inputs_out,
    up_out,
    tokens,
    grads,
    weights,
    hidden,
    core_out,
    core_in,
    mine,
    line_in,
    side,
    side_in,
    side_mine,
    side_line_in,
    tokens_send,
    tokens_in,
    rows_send,
    rows_in,
    up_in,
    load_sem,
    row_send_sem,
    row_recv_sem,
    core_send_sem,
    core_recv_sem,
    line_send_sem,
    line_recv_sem,
):
    leaf, row = lax.axis_index("leaf"), lax.axis_index("row")
    z, core = leaf // 2, leaf % 2
    far, inner, blocks, chips, slots = line_order(z)
    wide, own = grads.shape[1], query_out.shape[0]
    part, size = wide // 3, mine.shape[1]
    rows = tokens_in.shape[1]
    hops = (3, 1, 2)

    loads = [
        pltpu.make_async_copy(tokens_hbm, tokens, load_sem.at[0]),
        pltpu.make_async_copy(grads_hbm, grads, load_sem.at[1]),
        pltpu.make_async_copy(weights_hbm.at[:, pl.ds(0, wide)], weights, load_sem.at[2]),
        pltpu.make_async_copy(hidden_hbm, hidden, load_sem.at[3]),
        pltpu.make_async_copy(output_hbm.at[:, row], side.at[pl.ds(2 * row, 2)], load_sem.at[4]),
    ]
    for load in loads:
        load.start()
    barrier = pltpu.get_barrier_semaphore()
    for hop in hops:
        pl.semaphore_signal(barrier, inc=1, device_id={"row": other(row, hop)}, device_id_type=MESH)
        pl.semaphore_signal(barrier, inc=1, device_id={"leaf": 2 * other(z, hop) + core}, device_id_type=MESH)
    pl.semaphore_signal(barrier, inc=1, device_id={"leaf": 2 * z + 1 - core}, device_id_type=MESH)
    pl.semaphore_wait(barrier, 7)

    sent = []

    def row_copy(source, target, kind, hop):
        copy = pltpu.make_async_remote_copy(
            source,
            target,
            row_send_sem.at[kind, hop - 1],
            row_recv_sem.at[kind, hop - 1],
            device_id={"row": other(row, hop)},
            device_id_type=MESH,
        )
        copy.start()
        sent.append(copy)

    def core_copy(source, target, kind, i):
        copy = pltpu.make_async_remote_copy(
            source,
            target,
            core_send_sem.at[kind, i],
            core_recv_sem.at[kind, i],
            device_id={"leaf": 2 * z + 1 - core},
            device_id_type=MESH,
        )
        copy.start()
        sent.append(copy)

    def line_copy(source, target, kind, i):
        return pltpu.make_async_remote_copy(
            source,
            target.at[slots[i]],
            line_send_sem.at[kind, i],
            line_recv_sem.at[kind, slots[i]],
            device_id={"leaf": 2 * chips[i] + core},
            device_id_type=MESH,
        )

    for hop in hops:
        row_copy(output_hbm.at[:, other(row, hop)], side.at[pl.ds(2 * row, 2)], 0, hop)

    loads[0].wait()
    loads[1].wait()

    def product(block):
        return dot(tokens[:, pl.ds(pl.multiple_of(block * size, size), size)], grads[...], TN)

    for i in range(4):
        core_out[i] = product(2 * blocks[i] + 1 - core).astype(bf16)
        core_copy(core_out.at[i], core_in.at[i], 0, i)

    def pair(i):
        mine[i] = (product(2 * blocks[i] + core) + core_in[i].astype(f32)).astype(bf16)

    for i in range(4):
        landed(core_in.at[i], core_recv_sem.at[0, i])
        pair(i)
        if i < 2:
            copy = line_copy(mine.at[i], line_in, 0, i)
            copy.start()
            sent.append(copy)
        if i == 2:
            last = line_copy(mine.at[2], line_in, 0, 2)
            sent.append(last)

            @pl.when(inner == 0)
            def _():
                last.start()

    loads[2].wait()

    def tokens_part(hop, store):
        lines = grads[pl.ds(pl.multiple_of((other(row, hop)) * rows, rows), rows), :]

        def step(j, carry):
            columns = pl.ds(pl.multiple_of(j * part, part), part)
            store(columns, dot(lines, weights[columns, :], NT))
            return carry

        lax.fori_loop(0, weights.shape[0] // part, step, 0)

    for hop in hops:

        def store(columns, values):
            tokens_send[hop - 1, :, columns] = values.astype(bf16)

        tokens_part(hop, store)
        row_copy(tokens_send.at[hop - 1], tokens_in.at[hop - 1], 1, hop)

    loads[4].wait()
    for hop in hops:
        landed(side.at[pl.ds(2 * (other(row, hop)), 2)], row_recv_sem.at[0, hop - 1])
    for i in range(4):
        core_copy(side.at[2 * blocks[i] + 1 - core], side_in.at[i], 1, i)

    for hop in hops:
        row_copy(up_hbm.at[pl.ds((other(row, hop)) * own, own)], up_in.at[row], 2, hop)
    keep = pltpu.make_async_copy(up_hbm.at[pl.ds(row * own, own)], up_in.at[row], load_sem.at[5])
    keep.start()

    @pl.when(inner == 1)
    def _():
        landed(line_in.at[3], line_recv_sem.at[0, 3])
        mine[2] = (mine[2].astype(f32) + line_in[3].astype(f32)).astype(bf16)
        last.start()

    for i in range(4):
        landed(side_in.at[i], core_recv_sem.at[1, i])
        side_mine[i] = (side[2 * blocks[i] + core].astype(f32) + side_in[i].astype(f32)).astype(bf16)
        if i < 2:
            copy = line_copy(side_mine.at[i], side_line_in, 1, i)
            copy.start()
            sent.append(copy)
        if i == 2:
            side_last = line_copy(side_mine.at[2], side_line_in, 1, 2)
            sent.append(side_last)

            @pl.when(inner == 0)
            def _():
                side_last.start()

    loads[3].wait()

    def own_store(columns, values):
        hidden[:, columns] += values

    tokens_part(0, own_store)

    def total(kind, came, kept):
        landed(came.at[2], line_recv_sem.at[kind, 2])
        kept[3] = (kept[3].astype(f32) + came[2].astype(f32)).astype(bf16)
        for slot in range(2):

            @pl.when(inner + (1 - far) * slot + far * (1 - slot) > 0)
            def _():
                landed(came.at[slot], line_recv_sem.at[kind, slot])
                kept[3] = (kept[3].astype(f32) + came[slot].astype(f32)).astype(bf16)

    @pl.when(inner == 1)
    def _():
        landed(side_line_in.at[3], line_recv_sem.at[1, 3])
        side_mine[2] = (side_mine[2].astype(f32) + side_line_in[3].astype(f32)).astype(bf16)
        side_last.start()

    for hop in hops:
        landed(tokens_in.at[hop - 1], row_recv_sem.at[1, hop - 1])
        hidden[...] += tokens_in[hop - 1].astype(f32)
    inputs_out[...] = hidden[...].astype(bf16)

    keep.wait()
    for hop in hops:
        landed(up_in.at[other(row, hop)], row_recv_sem.at[2, hop - 1])
    for source in range(4):
        up_out[:, source * up_in.shape[2] : (source + 1) * up_in.shape[2]] = up_in[source].astype(f32)

    total(0, line_in, mine)
    rows_send[...] = mine[3]
    for hop in hops:
        row_copy(rows_send.at[pl.ds((other(row, hop)) * own, own)], rows_in.at[hop - 1], 3, hop)

    def give(source, values):
        columns = pl.ds(pl.multiple_of(source * part, part), part)
        for i, out in enumerate((query_out, key_out, value_out)):
            out[:, columns] = values[:, i * part : (i + 1) * part].astype(f32)

    give(row, rows_send[pl.ds(pl.multiple_of(row * own, own), own), :])
    total(1, side_line_in, side_mine)
    output_out[...] = side_mine[3].astype(f32)
    for hop in hops:
        landed(rows_in.at[hop - 1], row_recv_sem.at[3, hop - 1])
        give(other(row, hop), rows_in[hop - 1])
    for copy in sent:
        copy.wait_send()


def finish(tokens, grads, weights, output_part, hidden, up_shard):
    total, width = tokens.shape
    wide = grads.shape[1]
    own = output_part.shape[2]
    size, rows, units = 4 * own, hidden.shape[0], up_shard.shape[1]
    matrix = jax.ShapeDtypeStruct((own, width), f32)
    dma = pltpu.SemaphoreType.DMA
    return pl.pallas_call(
        final_kernel,
        in_specs=[pl.BlockSpec(memory_space=pl.ANY)] * 6,
        out_specs=[pl.BlockSpec(memory_space=pltpu.VMEM)] * 6,
        out_shape=[
            matrix,
            matrix,
            matrix,
            matrix,
            jax.ShapeDtypeStruct((rows, width), bf16),
            jax.ShapeDtypeStruct((own, 4 * units), f32),
        ],
        scratch_shapes=[
            pltpu.VMEM((total, width), bf16),
            pltpu.VMEM((total, wide), bf16),
            pltpu.VMEM((width, wide), bf16),
            pltpu.VMEM((rows, width), f32),
            pltpu.VMEM((4, size, wide), bf16),
            pltpu.VMEM((4, size, wide), bf16),
            pltpu.VMEM((4, size, wide), bf16),
            pltpu.VMEM((4, size, wide), bf16),
            pltpu.VMEM((8, own, width), bf16),
            pltpu.VMEM((4, own, width), bf16),
            pltpu.VMEM((4, own, width), bf16),
            pltpu.VMEM((4, own, width), bf16),
            pltpu.VMEM((3, rows, width), bf16),
            pltpu.VMEM((3, rows, width), bf16),
            pltpu.VMEM((size, wide), bf16),
            pltpu.VMEM((3, own, wide), bf16),
            pltpu.VMEM((4, own, units), bf16),
            dma((6,)),
            dma((4, 3)),
            dma((4, 3)),
            dma((2, 4)),
            dma((2, 4)),
            dma((2, 3)),
            dma((2, 4)),
        ],
        compiler_params=pltpu.CompilerParams(
            collective_id=1, has_side_effects=True, vmem_limit_bytes=60 * 2**20
        ),
        cost_estimate=pl.CostEstimate(
            flops=4 * total * width * wide, bytes_accessed=100 * 2**20, transcendentals=0
        ),
    )(tokens, grads, weights, output_part, hidden, up_shard)


def body(
    inputs,
    cotangent,
    seg_lengths,
    seg_parents,
    w_query,
    w_key,
    w_value,
    w_output,
    gain_query,
    gain_key,
    gain_attn,
    w_gate,
    w_up,
    w_down,
    gain_mlp,
):
    trees, rows_dev, width = inputs.shape
    count, leaves, me = lax.axis_size("row"), lax.axis_size("leaf"), lax.axis_index("row")
    tree_len = rows_dev * count
    part = width // count
    own = w_query.shape[0]
    group = count * own // 2
    units = w_gate.shape[1] // count
    tokens = inputs.reshape(rows_dev, width)

    def leaf_gather(block):
        return lax.all_gather(block, "leaf", axis=0, tiled=True)

    def leaf_scatter(block):
        return lax.psum_scatter(block, "leaf", scatter_dimension=0, tiled=True)

    qkv_block = columns_in(w_query, w_key, w_value)
    gains_own = jnp.stack([gain_query, gain_key, gain_attn, gain_mlp]).astype(bf16).reshape(1, 4 * own)
    gains_leaf = gather_rows(gains_own).reshape(count * own, 4)
    attn_block = jnp.concatenate(
        [
            qkv_block,
            w_output.astype(bf16).reshape(count * own, part),
            jnp.pad(gains_leaf, ((0, 0), (0, HEAD_DIM - 4))),
        ],
        axis=1,
    )
    attn_mat = leaf_gather(attn_block)
    qkv_mat = attn_mat[:, : 3 * part]
    output_rows = attn_mat[:, 3 * part : 4 * part].reshape(count, leaves // count, own, width)
    gains_all = attn_mat[:, 4 * part : 4 * part + 4].reshape(leaves, count, 4, own)
    gains_all = jnp.moveaxis(gains_all, 2, 0).reshape(4, width).astype(f32)
    gate_block = columns_in(tie(w_gate, qkv_block))
    up_block = columns_in(tie(w_up, qkv_block))
    down_block = columns_in(tie(w_down, qkv_block))
    all_tokens = gather_rows(tie(tokens, gate_block, up_block, down_block))
    bias, cos_wide, sin_wide = tree_tables(seg_lengths[0], seg_parents[0], tree_len)

    query_pre, key_pre, value, squares = project(all_tokens, attn_mat, part)
    gate_mat = leaf_gather(gate_block)
    up_mat = leaf_gather(up_block)
    down_halves = [leaf_gather(down_block[h * group : (h + 1) * group]) for h in range(2)]

    squares = sum_rows(squares)
    scales = lax.rsqrt(squares / width + epsilon)
    query_scale, key_scale = scales[0][:, None], scales[1][:, None]
    attn_gain, mlp_gain = gains_all[2], gains_all[3]
    head_gains = lax.dynamic_slice_in_dim(gains_all[:2], me * part, part, 1)
    output_rows = tie(output_rows, scales)
    output_mat = jnp.zeros((leaves // count, count, own, width), bf16)
    for hop in range(count):
        piece = lax.dynamic_index_in_dim(output_rows, me ^ hop, 0, keepdims=False)
        if hop:
            piece = swap(piece, hop)
        output_mat = lax.dynamic_update_index_in_dim(output_mat, piece, me ^ hop, 1)
    output_mat = output_mat.reshape(part, width)
    query, key, context, lse = attend(
        query_pre, key_pre, value, scales.T, head_gains, cos_wide, sin_wide, bias
    )
    attn_pre = dot_scatter([context], [output_mat], NN)
    attn_scale = lax.rsqrt(jnp.mean(attn_pre * attn_pre, axis=-1, keepdims=True) + epsilon)
    attn_unit = attn_pre * attn_scale
    hidden = tokens.astype(f32) + attn_unit * attn_gain
    hidden_all = gather_rows(hidden.astype(bf16))

    gate_pre = dot(hidden_all, gate_mat, NN)
    up_pre = dot(hidden_all, up_mat, NN)
    sigmoid_gate = jax.nn.sigmoid(gate_pre)
    activated = (gate_pre * sigmoid_gate * up_pre).astype(bf16)
    mlp_halves = [dot_scatter([activated], [down_halves[h]], NT) for h in range(2)]
    grad_final = cotangent.reshape(rows_dev, width).astype(f32)
    halves = range(2)

    def split(rows):
        rows = rows.reshape(rows.shape[:-1] + (leaves, 2, group))
        return [rows[..., h, :].reshape(rows.shape[:-3] + (width // 2,)) for h in halves]

    weighted = tie(split(grad_final * mlp_gain), hidden_all)
    square = sum(jnp.sum(m * m, axis=-1, keepdims=True) for m in mlp_halves) / width
    cross = sum(jnp.sum(m * w, axis=-1, keepdims=True) for m, w in zip(mlp_halves, weighted)) / width
    mlp_scale = lax.rsqrt(square + epsilon)
    grad_mlp = [
        (mlp_scale * (w - m * (mlp_scale * mlp_scale * cross))).astype(bf16) for m, w in zip(mlp_halves, weighted)
    ]
    grad_mlp_halves = [gather_rows(grad_mlp[h]) for h in halves]
    down_sums = [dot(grad_mlp_halves[h], activated, TN, bf16) for h in range(2)]
    down_shards = [leaf_scatter(down_sums[h]) for h in range(2)]
    grad_act = dot(tie(grad_mlp_halves[0], down_sums[0]), down_halves[0], NN)
    grad_act = grad_act + dot(tie(grad_mlp_halves[1], down_sums[1]), down_halves[1], NN)
    grad_gate = (grad_act * up_pre * sigmoid_gate * (1.0 + gate_pre * (1.0 - sigmoid_gate))).astype(bf16)
    grad_up = (grad_act * gate_pre * sigmoid_gate).astype(bf16)
    gate_sum = tie(dot(hidden_all, grad_gate, TN, bf16), *down_sums)
    grad_hidden = grad_final + dot_scatter([grad_gate, grad_up], [gate_mat, up_mat], NT, gate_sum)
    gate_shard = leaf_scatter(gate_sum)

    grad_attn, grad_attn_gain = norm_back(grad_hidden, attn_unit, attn_scale, attn_gain)
    grad_attn_low = grad_attn.astype(bf16)
    up_sum = dot(hidden_all, tie(grad_up, grad_attn_low), TN, bf16)
    grad_attn_all = gather_rows(tie(grad_attn_low, *down_shards), up_sum)
    grad_context = dot(grad_attn_all, output_mat, NT, bf16)
    up_shard = leaf_scatter(tie(up_sum, gate_sum))
    grad_context = tie(grad_context, gate_shard)
    grad_query, grad_key, grad_value, inner_query, inner_key, grad_head_gains = attend_back(
        query, key, value, bias, lse, grad_context, query_pre, key_pre, scales.T, head_gains, cos_wide, sin_wide
    )
    inner = sum_rows(jnp.stack([jnp.sum(inner_query, axis=1), jnp.sum(inner_key, axis=1)])) / width
    output_part = dot(context, tie(grad_attn_all, inner), TN, bf16).reshape(leaves // count, count, own, width)
    grad_query_low = (
        query_scale * (grad_query * head_gains[0] - query_pre * (query_scale * inner[0][:, None]))
    ).astype(bf16)
    grad_key_low = (
        key_scale * (grad_key * head_gains[1] - key_pre * (key_scale * inner[1][:, None]))
    ).astype(bf16)
    grad_qkv = jnp.concatenate([grad_query_low, grad_key_low, grad_value], axis=1)
    gate_out = columns_out(tie(gate_shard, inner))
    down_out = columns_out(tie(jnp.concatenate(down_shards), inner))
    mlp_unit = jnp.stack([m.reshape(rows_dev, leaves, group) for m in mlp_halves], axis=2).reshape(rows_dev, width)
    mlp_unit = mlp_unit * mlp_scale
    outputs = (hidden + mlp_unit * mlp_gain).astype(bf16).reshape(inputs.shape)
    grad_mlp_gain = jnp.sum(grad_final * mlp_unit, axis=0)

    wide_part = jnp.stack([grad_attn_gain, grad_mlp_gain]).reshape(2, leaves, count, own)
    narrow_part = grad_head_gains.reshape(2, leaves // count, count, own)
    wide_sum = jnp.zeros((2, leaves, own), f32)
    narrow_all = jnp.zeros((2, leaves, own), f32)
    for hop in range(count):
        piece = lax.dynamic_index_in_dim(jnp.concatenate([wide_part, narrow_part], axis=1), me ^ hop, 2, keepdims=False)
        if hop:
            piece = swap(piece, hop)
        wide_sum = wide_sum + piece[:, :leaves]
        narrow_all = lax.dynamic_update_slice_in_dim(
            narrow_all, piece[:, leaves:], (me ^ hop) * (leaves // count), 1
        )
    grad_gains = jnp.concatenate([narrow_all, wide_sum], axis=0)
    stride = 1
    while stride < leaves:
        grad_gains = grad_gains + lax.ppermute(
            grad_gains, "leaf", [(i, i ^ stride) for i in range(leaves)]
        )
        stride *= 2
    grad_gains = lax.dynamic_index_in_dim(grad_gains, lax.axis_index("leaf"), 1, keepdims=False)
    grad_qkv = tie(grad_qkv, gate_out, down_out, outputs, grad_gains)
    if leaves == 8 and count == 4:
        *grad_mats, grad_output, grad_tokens, up_out = finish(
            all_tokens, grad_qkv, attn_mat, output_part, grad_hidden, up_shard
        )
        grad_inputs, up_out = grad_tokens.reshape(inputs.shape), [up_out]
    else:
        output_turned = jnp.zeros((count, leaves // count, own, width), bf16)
        for hop in range(count):
            piece = lax.dynamic_index_in_dim(output_part, me ^ hop, 1, keepdims=False)
            if hop:
                piece = swap(piece, hop)
            output_turned = lax.dynamic_update_index_in_dim(output_turned, piece, me ^ hop, 0)
        attn_sum = sums_beside(all_tokens, grad_qkv, output_turned.reshape(leaves * count * own, part))
        grad_tokens = grad_hidden + dot_scatter([grad_qkv], [qkv_mat], NT)
        grad_inputs = grad_tokens.astype(bf16).reshape(inputs.shape)
        attn_shard = leaf_scatter(tie(attn_sum, up_shard))
        up_out = columns_out(up_shard)
        grad_mats = columns_out(attn_shard[:, : 3 * part], 3)
        grad_output = attn_shard[:, 3 * part :].reshape(own, width).astype(f32)
    return (
        outputs,
        grad_inputs,
        *grad_mats,
        grad_output,
        grad_gains[0],
        grad_gains[1],
        grad_gains[2],
        *gate_out,
        *up_out,
        *down_out,
        grad_gains[3],
    )


def solution(mesh):
    both = ("leaf", "row")
    token_spec, tree_spec, matrix_spec, gain_spec = P("leaf", "row", None), P("leaf", None), P(both, None), P(both)
    return jax.shard_map(
        body,
        mesh=mesh,
        in_specs=(token_spec,) * 2 + (tree_spec,) * 2 + (matrix_spec,) * 4 + (gain_spec,) * 3 + (matrix_spec,) * 3 + (gain_spec,),
        out_specs=(token_spec,) * 2 + (matrix_spec,) * 4 + (gain_spec,) * 3 + (matrix_spec,) * 3 + (gain_spec,),
        check_vma=False,
    )
```

time: 957 us -> 865 us (0.904)
  waiting for transfers between devices: 492 us -> 327 us
  Pallas kernels: 26.7 us -> 135 us
  other arithmetic: 58.8 us -> 27.7 us
  matrix products: 173 us -> 186 us
  starting transfers between devices: 89.3 us -> 78.4 us
    pallas_call x0 -> x2, Pallas kernels: none -> 105 us  [the longest x1 95 us: finish(): pl.pallas_call(final_kernel, in_specs=[pl.BlockSpec(memory_space=pl.ANY)]...]
    ppermute x72 -> x60, waiting for transfers between devices: 381 us -> 281 us  [swap(): return lax.ppermute(piece, 'row', [(i, i ^ hop) for i in range(count)])]
    reduce_scatter x5 -> x4, waiting for transfers between devices: 73.2 us -> 0.06 us  [leaf_scatter(): return lax.psum_scatter(block, 'leaf', scatter_dimension=0, tiled=True)]
    dot_general x18 -> x31, matrix products: 173 us -> 186 us  [dot(): lax.dot_general(left, right, dims, preferred_element_type=f32).astype(kind)]
    reduce_sum x5 -> x2, other arithmetic: 12.9 us -> 2.59 us  [the longest x1 1.34 us: body(): jnp.sum(inner_query, axis=1)]
    ppermute x72 -> x60, starting transfers between devices: 84.5 us -> 75.6 us  [swap(): return lax.ppermute(piece, 'row', [(i, i ^ hop) for i in range(count)])]
    unnamed x142 -> x130, local copies, waits for them, and re-layouts: 21.8 us -> 28.9 us
  transfers between devices with their start and end apart: 85 -> 72, of which waited for: 41 -> 37; matrix products, arithmetic and copies ran while one was open for 29% -> 31% of each run, Pallas kernels for 3% -> 5%
where the time goes in v2:
time: 865 us; the launch traced here: 858 us
  waiting for transfers between devices  327 us (38%)
  matrix products  186 us (22%)
  Pallas kernels  135 us (16%)
  local copies, waits for them, and re-layouts  88.6 us (10%)
  starting transfers between devices  78.4 us (9%)
  other arithmetic  27.7 us (3%)
  between operations  15.7 us (2%)
    ppermute x60, waiting for transfers between devices, swap(): return lax.ppermute(piece, 'row', [(i, i ^ hop) for i in range(count)])  281 us
    dot_general x31, matrix products, dot(): lax.dot_general(left, right, dims, preferred_element_type=f32).astype(kind)  186 us
    pallas_call x1, Pallas kernels, finish(): pl.pallas_call(final_kernel, in_specs=[pl.BlockSpec(memory_space=pl.ANY)]...  95 us
    ppermute x60, starting transfers between devices, swap(): return lax.ppermute(piece, 'row', [(i, i ^ hop) for i in range(count)])  75.6 us
    all_gather x5, waiting for transfers between devices, leaf_gather(): return lax.all_gather(block, 'leaf', axis=0, tiled=True)  41.5 us
    unnamed x130, local copies, waits for them, and re-layouts  28.9 us
  transfers between devices with their start and end apart: 72, of which 37 were waited for; matrix products, arithmetic and copies ran while one was open for 31% of the time, Pallas kernels for 5%

profile of v2, /device:TPU:0, one launch (start us, length us, event | category | flops | bytes accessed | tf_op | source)
XLA Modules:
  0.0 858.1 jit_solution(1662999813850859708)
XLA Ops:
  24.1 5.2 collective-permute-done.1
  35.3 3.6 collective-permute-done.3
  38.9 4.2 collective-permute-done.4
  69.1 5.6 collective-permute-done.11
  83.3 17.7 %collective-permute-done.12 = bf16[256,2048]{1,0:T(8,128)(2,1)S(1)} collective-permute-done((bf16[256,2048]{1,0:T(8,128)(2,1)S(1)}, bf16[256,2048]{1,0:T(8,128)(2,1)S(1)}, u32[]{:S(2)}, u32[]{:S(2)}) %collective-permute-start.12) | collective-permute-done | bytes 1048608 | tf_op jit(solution)/shard_map/ppermute | solution.py:30
  104.5 10.5 %collective-permute-done.13 = bf16[256,2048]{1,0:T(8,128)(2,1)} collective-permute-done((bf16[256,2048]{1,0:T(8,128)(2,1)S(1)}, bf16[256,2048]{1,0:T(8,128)(2,1)}, u32[]{:S(2)}, u32[]{:S(2)}) %collective-permute-start.13) | collective-permute-done | bytes 1048608 | tf_op jit(solution)/shard_map/ppermute | solution.py:30
  120.8 10.3 %shard_map.246 = (f32[1024,512]{1,0:T(8,128)S(1)}, f32[1024,512]{1,0:T(8,128)S(1)}, bf16[1024,512]{1,0:T(8,128)(2,1)S(1)}, f32[2,1024]{1,0:T(2,128)S(1)}) custom-call(bf16[1024,2048]{1,0:T(8,128)(2,1)} %constant_dynamic-update-slice_fusion.20.tokens_ref.tokens_hbm, bf16[2048,2176]{1,0:T(8,128)(2,1)} %all-gather.6.cloned.1.call-done.weights_ref.weights_hbm), custom_call_target="tpu_custom_call" | custom-call | flops 6442450944 | bytes 15728640 | tf_op jit(solution)/shard_map/pallas_call | solution.py:159
  150.9 9.1 %collective-permute-done.19 = f32[2,1024]{0,1:T(8,128)} collective-permute-done((f32[2,1024]{0,1:T(8,128)}, f32[2,1024]{0,1:T(8,128)}, u32[]{:S(2)}, u32[]{:S(2)}) %collective-permute-start.19) | collective-permute-done | bytes 8224 | tf_op jit(solution)/shard_map/ppermute | solution.py:30
  168.1 13.9 %shard_map.247 = (bf16[1024,512]{1,0:T(8,128)(2,1)}, bf16[1024,512]{1,0:T(8,128)(2,1)}, bf16[1024,512]{1,0:T(8,128)(2,1)}, f32[32,1024]{1,0:T(8,128)}) custom-call(f32[1024,512]{1,0:T(8,128)} %copy-done.2, f32[1024,512]{1,0:T(8,128)} %copy-done, bf16[1024,512]{1,0:T(8,128)(2,1)} %copy-done.4, f32[1024,2]{1,0:T(8,128)} %bitcast.145, ...), custom_call_target="tpu_custom_call" | custom-call | flops 2147483648 | bytes 8388608 | tf_op jit(solution)/shard_map/pallas_call | solution.py:228
  194.3 23.1 %collective-permute-done.24 = bf16[256,2048]{1,0:T(8,128)(2,1)} collective-permute-done((bf16[256,2048]{1,0:T(8,128)(2,1)}, bf16[256,2048]{1,0:T(8,128)(2,1)}, u32[]{:S(2)}, u32[]{:S(2)}) %collective-permute-start.24) | collective-permute-done | bytes 1048608 | tf_op jit(solution)/shard_map/ppermute | solution.py:30
  217.3 15.5 %collective-permute-done.25 = bf16[256,2048]{1,0:T(8,128)(2,1)} collective-permute-done((bf16[256,2048]{1,0:T(8,128)(2,1)}, bf16[256,2048]{1,0:T(8,128)(2,1)}, u32[]{:S(2)}, u32[]{:S(2)}) %collective-permute-start.25) | collective-permute-done | bytes 1048608 | tf_op jit(solution)/shard_map/ppermute | solution.py:30
  246.4 17.4 %collective-permute-done.27 = bf16[256,2048]{1,0:T(8,128)(2,1)} collective-permute-done((bf16[256,2048]{1,0:T(8,128)(2,1)S(1)}, bf16[256,2048]{1,0:T(8,128)(2,1)}, u32[]{:S(2)}, u32[]{:S(2)}) %collective-permute-start.27) | collective-permute-done | bytes 1048608 | tf_op jit(solution)/shard_map/ppermute | solution.py:30
  271.1 14.8 %collective-permute-done.29 = bf16[256,2048]{1,0:T(8,128)(2,1)} collective-permute-done((bf16[256,2048]{1,0:T(8,128)(2,1)S(1)}, bf16[256,2048]{1,0:T(8,128)(2,1)}, u32[]{:S(2)}, u32[]{:S(2)}) %collective-permute-start.29) | collective-permute-done | bytes 1048608 | tf_op jit(solution)/shard_map/ppermute | solution.py:30
  289.3 14.8 %fusion.84 = f32[1024,2048]{1,0:T(8,128)} fusion(bf16[1024,2048]{1,0:T(8,128)(2,1)} %constant_dynamic-update-slice_fusion.16, bf16[2048,2048]{1,0:T(8,128)(2,1)} %all-gather.8.cloned.1.call-done), kind=kOutput, calls=%fused_computation.276 | convolution fusion | flops 8589934592 | bytes 20971520 | tf_op jit(solution)/shard_map/dot_general | solution.py:25
  304.2 17.2 %multiply_convert_fusion.2 = (bf16[1024,2048]{1,0:T(8,128)(2,1)}, f32[1024,2048]{1,0:T(8,128)}) fusion(f32[1024,2048]{1,0:T(8,128)} %fusion.84, bf16[1024,2048]{1,0:T(8,128)(2,1)} %constant_dynamic-update-slice_fusion.16, bf16[2048,2048]{1,0:T(8,128)(2,1)} %all-gather.10.cloned.1.call-done), kind=kOutput, calls=%fused_computation.2 | convolution fusion | flops 8602517504 | bytes 33554432 | tf_op jit(solution)/shard_map/dot_general | solution.py:25
  321.3 8.5 all-gather.14.cloned.1.call-done
  329.8 4.8 convolution_convert_fusion.11
  344.7 33.0 %all-gather.12.cloned.1.call-done = bf16[1024,2048]{1,0:T(8,128)(2,1)} async-done(((bf16[128,2048]{1,0:T(8,128)(2,1)}), bf16[1024,2048]{1,0:T(8,128)(2,1)}) %all-gather.12.cloned.1.call-update) | async-done | bytes 4194320 | tf_op jit(solution)/shard_map/all_gather | solution.py:691
  377.7 3.9 convolution_convert_fusion.14
  389.5 6.0 slice_reduce_fusion
  400.4 7.5 collective-permute-done.31
  413.6 11.3 %collective-permute-done.36 = bf16[256,1024]{1,0:T(8,128)(2,1)S(1)} collective-permute-done((bf16[256,1024]{1,0:T(8,128)(2,1)S(1)}, bf16[256,1024]{1,0:T(8,128)(2,1)S(1)}, u32[]{:S(2)}, u32[]{:S(2)}) %collective-permute-start.36) | collective-permute-done | bytes 524320 | tf_op jit(solution)/shard_map/ppermute | solution.py:30
  425.3 11.1 %collective-permute-done.37 = bf16[256,1024]{1,0:T(8,128)(2,1)S(1)} collective-permute-done((bf16[256,1024]{1,0:T(8,128)(2,1)S(1)}, bf16[256,1024]{1,0:T(8,128)(2,1)S(1)}, u32[]{:S(2)}, u32[]{:S(2)}) %collective-permute-start.37) | collective-permute-done | bytes 524320 | tf_op jit(solution)/shard_map/ppermute | solution.py:30
  437.8 6.3 convolution_convert_fusion.3
  447.8 11.4 %collective-permute-done.39 = bf16[256,1024]{1,0:T(8,128)(2,1)S(1)} collective-permute-done((bf16[256,1024]{1,0:T(8,128)(2,1)S(1)}, bf16[256,1024]{1,0:T(8,128)(2,1)S(1)}, u32[]{:S(2)}, u32[]{:S(2)}) %collective-permute-start.39) | collective-permute-done | bytes 524320 | tf_op jit(solution)/shard_map/ppermute | solution.py:30
  459.4 9.9 %collective-permute-done.40 = bf16[256,1024]{1,0:T(8,128)(2,1)S(1)} collective-permute-done((bf16[256,1024]{1,0:T(8,128)(2,1)S(1)}, bf16[256,1024]{1,0:T(8,128)(2,1)S(1)}, u32[]{:S(2)}, u32[]{:S(2)}) %collective-permute-start.40) | collective-permute-done | bytes 524320 | tf_op jit(solution)/shard_map/ppermute | solution.py:30
  470.8 6.3 convolution_convert_fusion.2
  477.4 10.9 %fusion.85 = f32[1024,2048]{1,0:T(8,128)} fusion(bf16[1024,1024]{1,0:T(8,128)(2,1)} %copy-done.25, bf16[1024,2048]{1,0:T(8,128)(2,1)} %all-gather.14.cloned.1.call-done), kind=kOutput, calls=%fused_computation.277 | convolution fusion | flops 4294967296 | bytes 14680064 | tf_op jit(solution)/shard_map/dot_general | solution.py:25
  488.2 15.6 %multiply_convert_fusion.1 = (bf16[1024,2048]{1,0:T(8,128)(2,1)S(1)}, bf16[1024,2048]{1,0:T(8,128)(2,1)}) fusion(f32[1024,2048]{1,0:T(8,128)} %fusion.84, f32[1024,2048]{1,0:T(8,128)} %get-tuple-element.172, f32[1024,2048]{1,0:T(8,128)} %fusion.85, bf16[1024,1024]{1,0:T(8,128)(2,1)S(1)} %copy-done.24, bf16[1024,2048]{1,0:T(8,128)(2,1)} %all-gather.12.cloned.1.call-done), kind=kOutput, calls=%fused_computation.1 | convolution fusion | flops 4324327424 | bytes 39845888 | tf_op jit(solution)/shard_map/dot_general | solution.py:25
  506.0 13.5 %convolution_convert_fusion.1 = bf16[2048,2048]{1,0:T(8,128)(2,1)} fusion(bf16[1024,2048]{1,0:T(8,128)(2,1)} %constant_dynamic-update-slice_fusion.16, bf16[1024,2048]{1,0:T(8,128)(2,1)S(1)} %get-tuple-element.72), kind=kOutput, calls=%fused_computation.5 | convolution fusion | flops 8594128896 | bytes 16777216 | tf_op jit(solution)/shard_map/dot_general | solution.py:25
  520.0 6.3 fusion.25
  526.4 7.0 fusion.7
  534.6 5.8 fusion.22
  540.4 3.4 fusion.8
  544.7 5.7 fusion.19
  550.5 3.6 fusion.9
  560.6 6.3 fusion.28
  567.0 12.0 %collective-permute-done.43 = bf16[256,2048]{1,0:T(8,128)(2,1)} collective-permute-done((bf16[256,2048]{1,0:T(8,128)(2,1)}, bf16[256,2048]{1,0:T(8,128)(2,1)}, u32[]{:S(2)}, u32[]{:S(2)}) %collective-permute-start.43) | collective-permute-done | bytes 1048608 | tf_op jit(solution)/shard_map/ppermute | solution.py:30
  579.1 8.1 multiply_reduce_fusion
  591.0 13.7 %convolution_convert_fusion = bf16[2048,2048]{1,0:T(8,128)(2,1)} fusion(bf16[1024,2048]{1,0:T(8,128)(2,1)} %constant_dynamic-update-slice_fusion.16, bf16[1024,2048]{1,0:T(8,128)(2,1)S(1)} %copy-done.57), kind=kOutput, calls=%fused_computation.4 | convolution fusion | flops 8594128896 | bytes 16777216 | tf_op jit(solution)/shard_map/dot_general | solution.py:25
  612.2 19.9 %collective-permute-done.45 = bf16[256,2048]{1,0:T(8,128)(2,1)} collective-permute-done((bf16[256,2048]{1,0:T(8,128)(2,1)S(1)}, bf16[256,2048]{1,0:T(8,128)(2,1)}, u32[]{:S(2)}, u32[]{:S(2)}) %collective-permute-start.45) | collective-permute-done | bytes 1048608 | tf_op jit(solution)/shard_map/ppermute | solution.py:30
  634.0 20.8 %collective-permute-done.46 = bf16[256,2048]{1,0:T(8,128)(2,1)} collective-permute-done((bf16[256,2048]{1,0:T(8,128)(2,1)S(1)}, bf16[256,2048]{1,0:T(8,128)(2,1)}, u32[]{:S(2)}, u32[]{:S(2)}) %collective-permute-start.46) | collective-permute-done | bytes 1048608 | tf_op jit(solution)/shard_map/ppermute | solution.py:30
  661.7 16.3 %shard_map.248 = (f32[1024,512]{1,0:T(8,128)}, f32[1024,512]{1,0:T(8,128)}, bf16[1024,512]{1,0:T(8,128)(2,1)}, f32[1024,128]{1,0:T(8,128)}, f32[1024,128]{1,0:T(8,128)}, /*index=5*/f32[2,512]{1,0:T(2,128)}) custom-call(bf16[1024,512]{1,0:T(8,128)(2,1)} %get-tuple-element.64.query_ref, bf16[1024,512]{1,0:T(8,128)(2,1)} %get-tuple-element.65.key_ref, ...), custom_call_target="tpu_custom_call" | custom-call | flops 5368709120 | bytes 15728640 | tf_op jit(solution)/shard_map/pallas_call | solution.py:307
  687.4 16.5 %collective-permute-done.57 = f32[2,10,64]{2,0,1:T(2,128)S(1)} collective-permute-done((f32[2,10,64]{2,0,1:T(2,128)S(1)}, f32[2,10,64]{2,0,1:T(2,128)S(1)}, u32[]{:S(2)}, u32[]{:S(2)}) %collective-permute-start.57) | collective-permute-done | bytes 5152 | tf_op jit(solution)/shard_map/ppermute | solution.py:30
  716.1 3.8 convolution_convert_fusion.4
  734.0 9.5 %collective-permute-done.55 = bf16[64,2048]{1,0:T(8,128)(2,1)S(1)} collective-permute-done((bf16[64,2048]{1,0:T(8,128)(2,1)S(1)}, bf16[64,2048]{1,0:T(8,128)(2,1)S(1)}, u32[]{:S(2)}, u32[]{:S(2)}) %collective-permute-start.55) | collective-permute-done | bytes 262176 | tf_op jit(solution)/shard_map/ppermute | solution.py:30
  743.7 4.5 collective-permute-done.52
  748.4 95.0 %shard_map.249 = (f32[64,2048]{1,0:T(8,128)}, f32[64,2048]{1,0:T(8,128)}, f32[64,2048]{1,0:T(8,128)}, f32[64,2048]{1,0:T(8,128)}, bf16[256,2048]{1,0:T(8,128)(2,1)}, /*index=5*/f32[64,8192]{1,0:T(8,128)}) custom-call(bf16[1024,2048]{1,0:T(8,128)(2,1)} %constant_dynamic-update-slice_fusion.20.tokens_ref.tokens_hbm, ...), custom_call_target="tpu_custom_call" | custom-call | flops 12884901888 | bytes 104857600 | tf_op jit(solution)/shard_map/pallas_call | solution.py:617
  (427 shorter events, 241.3 us)
Async XLA Ops:
  7.2 113.6 %all-gather.6.cloned.1.call-start = ((), (), s32[]{:S(2)}) async-start(), calls=%async_computation.4 | async-start | bytes 10027008 | tf_op jit(solution)/shard_map/all_gather | solution.py:691
  31.3 258.0 %all-gather.8.cloned.1.call-start = ((), (), s32[]{:S(2)}) async-start(), calls=%async_computation.5 | async-start | bytes 9437184 | tf_op jit(solution)/shard_map/all_gather | solution.py:691
  44.3 259.9 %all-gather.10.cloned.1.call-start = ((), (), s32[]{:S(2)}) async-start(), calls=%async_computation.6 | async-start | bytes 9437184 | tf_op jit(solution)/shard_map/all_gather | solution.py:691
  55.9 273.9 %all-gather.14.cloned.1.call-start = ((), (), s32[]{:S(2)}) async-start(), calls=%async_computation.8 | async-start | bytes 4718592 | tf_op jit(solution)/shard_map/all_gather | solution.py:691
  74.8 26.2 %collective-permute-start.12 = (bf16[256,2048]{1,0:T(8,128)(2,1)S(1)}, bf16[256,2048]{1,0:T(8,128)(2,1)S(1)}, u32[]{:S(2)}, u32[]{:S(2)}) collective-permute-start(bf16[256,2048]{1,0:T(8,128)(2,1)S(1)} %bitcast.141), channel_id=1, source_target_pairs={{0,1},{1,0},{2,3},{3,2},{4,5},{5,4},{6,7},{7,6},{8,9},{9,8},{10,11... | collective-permute-start | bytes 3145736 | tf_op jit(solution)/shard_map/ppermute | solution.py:30
  75.3 39.7 %collective-permute-start.13 = (bf16[256,2048]{1,0:T(8,128)(2,1)S(1)}, bf16[256,2048]{1,0:T(8,128)(2,1)}, u32[]{:S(2)}, u32[]{:S(2)}) collective-permute-start(bf16[256,2048]{1,0:T(8,128)(2,1)S(1)} %bitcast.142), channel_id=1, source_target_pairs={{0,2},{1,3},{2,0},{3,1},{4,6},{5,7},{6,4},{7,5},{8,10},{9,11},{10,... | collective-permute-start | bytes 3145736 | tf_op jit(solution)/shard_map/ppermute | solution.py:30
  78.1 39.3 %collective-permute-start.14 = (bf16[256,2048]{1,0:T(8,128)(2,1)S(1)}, bf16[256,2048]{1,0:T(8,128)(2,1)}, u32[]{:S(2)}, u32[]{:S(2)}) collective-permute-start(bf16[256,2048]{1,0:T(8,128)(2,1)S(1)} %bitcast.143), channel_id=1, source_target_pairs={{0,3},{1,2},{2,1},{3,0},{4,7},{5,6},{6,5},{7,4},{8,11},{9,10},{10,... | collective-permute-start | bytes 3145736 | tf_op jit(solution)/shard_map/ppermute | solution.py:30
  82.8 295.0 %all-gather.12.cloned.1.call-start = ((), (), s32[]{:S(2)}) async-start(), calls=%async_computation.7 | async-start | bytes 4718592 | tf_op jit(solution)/shard_map/all_gather | solution.py:691
  137.4 22.6 %collective-permute-start.19 = (f32[2,1024]{0,1:T(8,128)}, f32[2,1024]{0,1:T(8,128)}, u32[]{:S(2)}, u32[]{:S(2)}) collective-permute-start(f32[2,1024]{0,1:T(8,128)} %copy.74), channel_id=1, source_target_pairs={{0,2},{1,3},{2,0},{3,1},{4,6},{5,7},{6,4},{7,5},{8,10},{9,11},{10,... | collective-permute-start | bytes 24584 | tf_op jit(solution)/shard_map/ppermute | solution.py:30
  139.9 20.1 %collective-permute-start.20 = (f32[2,1024]{0,1:T(8,128)}, f32[2,1024]{0,1:T(8,128)}, u32[]{:S(2)}, u32[]{:S(2)}) collective-permute-start(f32[2,1024]{0,1:T(8,128)} %copy.74), channel_id=1, source_target_pairs={{0,3},{1,2},{2,1},{3,0},{4,7},{5,6},{6,5},{7,4},{8,11},{9,10},{10,... | collective-permute-start | bytes 24584 | tf_op jit(solution)/shard_map/ppermute | solution.py:30
  162.6 19.4 %collective-permute-start.21 = (bf16[2,64,2048]{2,1,0:T(8,128)(2,1)S(1)}, bf16[2,64,2048]{2,1,0:T(8,128)(2,1)S(1)}, u32[]{:S(2)}, u32[]{:S(2)}) collective-permute-start(bf16[2,64,2048]{2,1,0:T(8,128)(2,1)S(1)} %get-tuple-element.118), channel_id=1, source_target_pairs={{0,1},{1,0},{2,3},{3,2},{4,5},{5,4},{6,7},{7,6},{8,9},{9,8},{10,11... | collective-permute-start | bytes 1572872 | tf_op jit(solution)/shard_map/ppermute | solution.py:30
  164.5 20.3 %collective-permute-start.22 = (bf16[2,64,2048]{2,1,0:T(8,128)(2,1)S(1)}, bf16[2,64,2048]{2,1,0:T(8,128)(2,1)S(1)}, u32[]{:S(2)}, u32[]{:S(2)}) collective-permute-start(bf16[2,64,2048]{2,1,0:T(8,128)(2,1)S(1)} %get-tuple-element.117), channel_id=1, source_target_pairs={{0,2},{1,3},{2,0},{3,1},{4,6},{5,7},{6,4},{7,5},{8,10},{9,11},{10,... | collective-permute-start | bytes 1572872 | tf_op jit(solution)/shard_map/ppermute | solution.py:30
  165.3 19.6 %collective-permute-start.23 = (bf16[2,64,2048]{2,1,0:T(8,128)(2,1)S(1)}, bf16[2,64,2048]{2,1,0:T(8,128)(2,1)S(1)}, u32[]{:S(2)}, u32[]{:S(2)}) collective-permute-start(bf16[2,64,2048]{2,1,0:T(8,128)(2,1)S(1)} %get-tuple-element.116), channel_id=1, source_target_pairs={{0,3},{1,2},{2,1},{3,0},{4,7},{5,6},{6,5},{7,4},{8,11},{9,10},{10,... | collective-permute-start | bytes 1572872 | tf_op jit(solution)/shard_map/ppermute | solution.py:30
  190.0 27.3 %collective-permute-start.24 = (bf16[256,2048]{1,0:T(8,128)(2,1)}, bf16[256,2048]{1,0:T(8,128)(2,1)}, u32[]{:S(2)}, u32[]{:S(2)}) collective-permute-start(bf16[256,2048]{1,0:T(8,128)(2,1)} %convolution_convert_fusion.7), channel_id=1, source_target_pairs={{0,3},{1,2},{2,1},{3,0},{4,7},{5,6},{6,5},{7,4},{8,11},{9,10},{10,... | collective-permute-start | bytes 3145736 | tf_op jit(solution)/shard_map/ppermute | solution.py:30
  191.8 41.1 %collective-permute-start.25 = (bf16[256,2048]{1,0:T(8,128)(2,1)}, bf16[256,2048]{1,0:T(8,128)(2,1)}, u32[]{:S(2)}, u32[]{:S(2)}) collective-permute-start(bf16[256,2048]{1,0:T(8,128)(2,1)} %convolution_convert_fusion.6), channel_id=1, source_target_pairs={{0,2},{1,3},{2,0},{3,1},{4,6},{5,7},{6,4},{7,5},{8,10},{9,11},{10,... | collective-permute-start | bytes 3145736 | tf_op jit(solution)/shard_map/ppermute | solution.py:30
  192.4 40.4 %collective-permute-start.26 = (bf16[256,2048]{1,0:T(8,128)(2,1)}, bf16[256,2048]{1,0:T(8,128)(2,1)}, u32[]{:S(2)}, u32[]{:S(2)}) collective-permute-start(bf16[256,2048]{1,0:T(8,128)(2,1)} %convolution_convert_fusion.5), channel_id=1, source_target_pairs={{0,1},{1,0},{2,3},{3,2},{4,5},{5,4},{6,7},{7,6},{8,9},{9,8},{10,11... | collective-permute-start | bytes 3145736 | tf_op jit(solution)/shard_map/ppermute | solution.py:30
  237.6 26.2 %collective-permute-start.27 = (bf16[256,2048]{1,0:T(8,128)(2,1)S(1)}, bf16[256,2048]{1,0:T(8,128)(2,1)}, u32[]{:S(2)}, u32[]{:S(2)}) collective-permute-start(bf16[256,2048]{1,0:T(8,128)(2,1)S(1)} %fusion.16), channel_id=1, source_target_pairs={{0,1},{1,0},{2,3},{3,2},{4,5},{5,4},{6,7},{7,6},{8,9},{9,8},{10,11... | collective-permute-start | bytes 3145736 | tf_op jit(solution)/shard_map/ppermute | solution.py:30
  239.1 29.7 %collective-permute-start.28 = (bf16[256,2048]{1,0:T(8,128)(2,1)S(1)}, bf16[256,2048]{1,0:T(8,128)(2,1)}, u32[]{:S(2)}, u32[]{:S(2)}) collective-permute-start(bf16[256,2048]{1,0:T(8,128)(2,1)S(1)} %fusion.16), channel_id=1, source_target_pairs={{0,2},{1,3},{2,0},{3,1},{4,6},{5,7},{6,4},{7,5},{8,10},{9,11},{10,... | collective-permute-start | bytes 3145736 | tf_op jit(solution)/shard_map/ppermute | solution.py:30
  240.6 364.2 %reduce-scatter.5.cloned.1.call-start = ((), (), s32[]{:S(2)}) async-start(), calls=%async_computation.9 | async-start | bytes 4718592 | tf_op jit(solution)/shard_map/reduce_scatter | solution.py:694
  240.8 45.1 %collective-permute-start.29 = (bf16[256,2048]{1,0:T(8,128)(2,1)S(1)}, bf16[256,2048]{1,0:T(8,128)(2,1)}, u32[]{:S(2)}, u32[]{:S(2)}) collective-permute-start(bf16[256,2048]{1,0:T(8,128)(2,1)S(1)} %fusion.16), channel_id=1, source_target_pairs={{0,3},{1,2},{2,1},{3,0},{4,7},{5,6},{6,5},{7,4},{8,11},{9,10},{10,... | collective-permute-start | bytes 3145736 | tf_op jit(solution)/shard_map/ppermute | solution.py:30
  334.6 54.0 %collective-permute-start.33 = (bf16[256,1024]{1,0:T(8,128)(2,1)}, bf16[256,1024]{1,0:T(8,128)(2,1)S(1)}, u32[]{:S(2)}, u32[]{:S(2)}) collective-permute-start(bf16[256,1024]{1,0:T(8,128)(2,1)} %convolution_convert_fusion.11), channel_id=1, source_target_pairs={{0,3},{1,2},{2,1},{3,0},{4,7},{5,6},{6,5},{7,4},{8,11},{9,10},{10,... | collective-permute-start | bytes 1572872 | tf_op jit(solution)/shard_map/ppermute | solution.py:30
  340.3 55.6 %collective-permute-start.34 = (bf16[256,1024]{1,0:T(8,128)(2,1)}, bf16[256,1024]{1,0:T(8,128)(2,1)S(1)}, u32[]{:S(2)}, u32[]{:S(2)}) collective-permute-start(bf16[256,1024]{1,0:T(8,128)(2,1)} %convolution_convert_fusion.10), channel_id=1, source_target_pairs={{0,2},{1,3},{2,0},{3,1},{4,6},{5,7},{6,4},{7,5},{8,10},{9,11},{10,... | collective-permute-start | bytes 1572872 | tf_op jit(solution)/shard_map/ppermute | solution.py:30
  344.1 51.9 %collective-permute-start.35 = (bf16[256,1024]{1,0:T(8,128)(2,1)}, bf16[256,1024]{1,0:T(8,128)(2,1)}, u32[]{:S(2)}, u32[]{:S(2)}) collective-permute-start(bf16[256,1024]{1,0:T(8,128)(2,1)} %convolution_convert_fusion.9), channel_id=1, source_target_pairs={{0,1},{1,0},{2,3},{3,2},{4,5},{5,4},{6,7},{7,6},{8,9},{9,8},{10,11... | collective-permute-start | bytes 1572872 | tf_op jit(solution)/shard_map/ppermute | solution.py:30
  381.7 18.8 %collective-permute-start.30 = (bf16[256,1024]{1,0:T(8,128)(2,1)S(1)}, bf16[256,1024]{1,0:T(8,128)(2,1)S(1)}, u32[]{:S(2)}, u32[]{:S(2)}) collective-permute-start(bf16[256,1024]{1,0:T(8,128)(2,1)S(1)} %convolution_convert_fusion.14), channel_id=1, source_target_pairs={{0,3},{1,2},{2,1},{3,0},{4,7},{5,6},{6,5},{7,4},{8,11},{9,10},{10,... | collective-permute-start | bytes 1572872 | tf_op jit(solution)/shard_map/ppermute | solution.py:30
  386.6 21.3 %collective-permute-start.31 = (bf16[256,1024]{1,0:T(8,128)(2,1)S(1)}, bf16[256,1024]{1,0:T(8,128)(2,1)S(1)}, u32[]{:S(2)}, u32[]{:S(2)}) collective-permute-start(bf16[256,1024]{1,0:T(8,128)(2,1)S(1)} %convolution_convert_fusion.13), channel_id=1, source_target_pairs={{0,2},{1,3},{2,0},{3,1},{4,6},{5,7},{6,4},{7,5},{8,10},{9,11},{10,... | collective-permute-start | bytes 1572872 | tf_op jit(solution)/shard_map/ppermute | solution.py:30
  388.5 19.4 %collective-permute-start.32 = (bf16[256,1024]{1,0:T(8,128)(2,1)S(1)}, bf16[256,1024]{1,0:T(8,128)(2,1)S(1)}, u32[]{:S(2)}, u32[]{:S(2)}) collective-permute-start(bf16[256,1024]{1,0:T(8,128)(2,1)S(1)} %convolution_convert_fusion.12), channel_id=1, source_target_pairs={{0,1},{1,0},{2,3},{3,2},{4,5},{5,4},{6,7},{7,6},{8,9},{9,8},{10,11... | collective-permute-start | bytes 1572872 | tf_op jit(solution)/shard_map/ppermute | solution.py:30
  411.6 24.8 %collective-permute-start.37 = (bf16[256,1024]{1,0:T(8,128)(2,1)S(1)}, bf16[256,1024]{1,0:T(8,128)(2,1)S(1)}, u32[]{:S(2)}, u32[]{:S(2)}) collective-permute-start(bf16[256,1024]{1,0:T(8,128)(2,1)S(1)} %get-tuple-element.165), channel_id=1, source_target_pairs={{0,2},{1,3},{2,0},{3,1},{4,6},{5,7},{6,4},{7,5},{8,10},{9,11},{10,... | collective-permute-start | bytes 1572872 | tf_op jit(solution)/shard_map/ppermute | solution.py:30
  413.0 23.4 %collective-permute-start.38 = (bf16[256,1024]{1,0:T(8,128)(2,1)S(1)}, bf16[256,1024]{1,0:T(8,128)(2,1)S(1)}, u32[]{:S(2)}, u32[]{:S(2)}) collective-permute-start(bf16[256,1024]{1,0:T(8,128)(2,1)S(1)} %get-tuple-element.165), channel_id=1, source_target_pairs={{0,3},{1,2},{2,1},{3,0},{4,7},{5,6},{6,5},{7,4},{8,11},{9,10},{10,... | collective-permute-start | bytes 1572872 | tf_op jit(solution)/shard_map/ppermute | solution.py:30
  444.1 160.7 %reduce-scatter.7.cloned.1.call-start = ((), (), s32[]{:S(2)}) async-start(), calls=%async_computation.10 | async-start | bytes 4718592 | tf_op jit(solution)/shard_map/reduce_scatter | solution.py:694
  445.4 23.9 %collective-permute-start.40 = (bf16[256,1024]{1,0:T(8,128)(2,1)S(1)}, bf16[256,1024]{1,0:T(8,128)(2,1)S(1)}, u32[]{:S(2)}, u32[]{:S(2)}) collective-permute-start(bf16[256,1024]{1,0:T(8,128)(2,1)S(1)} %get-tuple-element.166), channel_id=1, source_target_pairs={{0,2},{1,3},{2,0},{3,1},{4,6},{5,7},{6,4},{7,5},{8,10},{9,11},{10,... | collective-permute-start | bytes 1572872 | tf_op jit(solution)/shard_map/ppermute | solution.py:30
  446.3 23.1 %collective-permute-start.41 = (bf16[256,1024]{1,0:T(8,128)(2,1)S(1)}, bf16[256,1024]{1,0:T(8,128)(2,1)S(1)}, u32[]{:S(2)}, u32[]{:S(2)}) collective-permute-start(bf16[256,1024]{1,0:T(8,128)(2,1)S(1)} %get-tuple-element.166), channel_id=1, source_target_pairs={{0,3},{1,2},{2,1},{3,0},{4,7},{5,6},{6,5},{7,4},{8,11},{9,10},{10,... | collective-permute-start | bytes 1572872 | tf_op jit(solution)/shard_map/ppermute | solution.py:30
  477.1 184.6 %reduce-scatter.9.cloned.1.call-start = ((), (), s32[]{:S(2)}) async-start(), calls=%async_computation.11 | async-start | bytes 9437184 | tf_op jit(solution)/shard_map/reduce_scatter | solution.py:694
  519.5 228.8 %reduce-scatter.11.cloned.1.call-start = ((), (), s32[]{:S(2)}) async-start(), calls=%async_computation.12 | async-start | bytes 9437184 | tf_op jit(solution)/shard_map/reduce_scatter | solution.py:694
  533.4 33.6 %collective-permute-start.42 = (bf16[256,2048]{1,0:T(8,128)(2,1)}, bf16[256,2048]{1,0:T(8,128)(2,1)S(1)}, u32[]{:S(2)}, u32[]{:S(2)}) collective-permute-start(bf16[256,2048]{1,0:T(8,128)(2,1)} %fusion.7), channel_id=1, source_target_pairs={{0,3},{1,2},{2,1},{3,0},{4,7},{5,6},{6,5},{7,4},{8,11},{9,10},{10,... | collective-permute-start | bytes 3145736 | tf_op jit(solution)/shard_map/ppermute | solution.py:30
  543.8 35.2 %collective-permute-start.43 = (bf16[256,2048]{1,0:T(8,128)(2,1)}, bf16[256,2048]{1,0:T(8,128)(2,1)}, u32[]{:S(2)}, u32[]{:S(2)}) collective-permute-start(bf16[256,2048]{1,0:T(8,128)(2,1)} %fusion.8), channel_id=1, source_target_pairs={{0,2},{1,3},{2,0},{3,1},{4,6},{5,7},{6,4},{7,5},{8,10},{9,11},{10,... | collective-permute-start | bytes 3145736 | tf_op jit(solution)/shard_map/ppermute | solution.py:30
  554.0 25.1 %collective-permute-start.44 = (bf16[256,2048]{1,0:T(8,128)(2,1)}, bf16[256,2048]{1,0:T(8,128)(2,1)}, u32[]{:S(2)}, u32[]{:S(2)}) collective-permute-start(bf16[256,2048]{1,0:T(8,128)(2,1)} %fusion.9), channel_id=1, source_target_pairs={{0,1},{1,0},{2,3},{3,2},{4,5},{5,4},{6,7},{7,6},{8,9},{9,8},{10,11... | collective-permute-start | bytes 3145736 | tf_op jit(solution)/shard_map/ppermute | solution.py:30
  606.0 26.1 %collective-permute-start.45 = (bf16[256,2048]{1,0:T(8,128)(2,1)S(1)}, bf16[256,2048]{1,0:T(8,128)(2,1)}, u32[]{:S(2)}, u32[]{:S(2)}) collective-permute-start(bf16[256,2048]{1,0:T(8,128)(2,1)S(1)} %copy-done.21), channel_id=1, source_target_pairs={{0,1},{1,0},{2,3},{3,2},{4,5},{5,4},{6,7},{7,6},{8,9},{9,8},{10,11... | collective-permute-start | bytes 3145736 | tf_op jit(solution)/shard_map/ppermute | solution.py:30
  607.6 47.2 %collective-permute-start.46 = (bf16[256,2048]{1,0:T(8,128)(2,1)S(1)}, bf16[256,2048]{1,0:T(8,128)(2,1)}, u32[]{:S(2)}, u32[]{:S(2)}) collective-permute-start(bf16[256,2048]{1,0:T(8,128)(2,1)S(1)} %copy-done.21), channel_id=1, source_target_pairs={{0,2},{1,3},{2,0},{3,1},{4,6},{5,7},{6,4},{7,5},{8,10},{9,11},{10,... | collective-permute-start | bytes 3145736 | tf_op jit(solution)/shard_map/ppermute | solution.py:30
  609.0 47.1 %collective-permute-start.47 = (bf16[256,2048]{1,0:T(8,128)(2,1)S(1)}, bf16[256,2048]{1,0:T(8,128)(2,1)S(1)}, u32[]{:S(2)}, u32[]{:S(2)}) collective-permute-start(bf16[256,2048]{1,0:T(8,128)(2,1)S(1)} %copy-done.21), channel_id=1, source_target_pairs={{0,3},{1,2},{2,1},{3,0},{4,7},{5,6},{6,5},{7,4},{8,11},{9,10},{10,... | collective-permute-start | bytes 3145736 | tf_op jit(solution)/shard_map/ppermute | solution.py:30
  680.9 27.8 %collective-permute-start.48 = (f32[2,1024]{0,1:T(8,128)S(1)}, f32[2,1024]{0,1:T(8,128)S(1)}, u32[]{:S(2)}, u32[]{:S(2)}) collective-permute-start(f32[2,1024]{0,1:T(8,128)S(1)} %copy.81), channel_id=1, source_target_pairs={{0,1},{1,0},{2,3},{3,2},{4,5},{5,4},{6,7},{7,6},{8,9},{9,8},{10,11... | collective-permute-start | bytes 24584 | tf_op jit(solution)/shard_map/ppermute | solution.py:30
  680.9 27.7 %collective-permute-start.49 = (f32[2,1024]{0,1:T(8,128)S(1)}, f32[2,1024]{0,1:T(8,128)}, u32[]{:S(2)}, u32[]{:S(2)}) collective-permute-start(f32[2,1024]{0,1:T(8,128)S(1)} %copy.81), channel_id=1, source_target_pairs={{0,2},{1,3},{2,0},{3,1},{4,6},{5,7},{6,4},{7,5},{8,10},{9,11},{10,... | collective-permute-start | bytes 24584 | tf_op jit(solution)/shard_map/ppermute | solution.py:30
  683.0 25.7 %collective-permute-start.50 = (f32[2,1024]{0,1:T(8,128)S(1)}, f32[2,1024]{0,1:T(8,128)}, u32[]{:S(2)}, u32[]{:S(2)}) collective-permute-start(f32[2,1024]{0,1:T(8,128)S(1)} %copy.81), channel_id=1, source_target_pairs={{0,3},{1,2},{2,1},{3,0},{4,7},{5,6},{6,5},{7,4},{8,11},{9,10},{10,... | collective-permute-start | bytes 24584 | tf_op jit(solution)/shard_map/ppermute | solution.py:30
  685.3 18.6 %collective-permute-start.57 = (f32[2,10,64]{2,0,1:T(2,128)S(1)}, f32[2,10,64]{2,0,1:T(2,128)S(1)}, u32[]{:S(2)}, u32[]{:S(2)}) collective-permute-start(f32[2,10,64]{2,0,1:T(2,128)S(1)} %bitcast.172), channel_id=1, source_target_pairs={{0,1},{1,0},{2,3},{3,2},{4,5},{5,4},{6,7},{7,6},{8,9},{9,8},{10,11... | collective-permute-start | bytes 15368 | tf_op jit(solution)/shard_map/ppermute | solution.py:30
  685.6 21.1 %collective-permute-start.58 = (f32[2,10,64]{2,0,1:T(2,128)S(1)}, f32[2,10,64]{2,0,1:T(2,128)S(1)}, u32[]{:S(2)}, u32[]{:S(2)}) collective-permute-start(f32[2,10,64]{2,0,1:T(2,128)S(1)} %bitcast.170), channel_id=1, source_target_pairs={{0,2},{1,3},{2,0},{3,1},{4,6},{5,7},{6,4},{7,5},{8,10},{9,11},{10,... | collective-permute-start | bytes 15368 | tf_op jit(solution)/shard_map/ppermute | solution.py:30
  710.2 23.7 %collective-permute-start.54 = (bf16[64,2048]{1,0:T(8,128)(2,1)S(1)}, bf16[64,2048]{1,0:T(8,128)(2,1)S(1)}, u32[]{:S(2)}, u32[]{:S(2)}) collective-permute-start(bf16[64,2048]{1,0:T(8,128)(2,1)S(1)} %get-tuple-element.133), channel_id=1, source_target_pairs={{0,1},{1,0},{2,3},{3,2},{4,5},{5,4},{6,7},{7,6},{8,9},{9,8},{10,11... | collective-permute-start | bytes 786440 | tf_op jit(solution)/shard_map/ppermute | solution.py:30
  712.1 31.6 %collective-permute-start.51 = (bf16[64,2048]{1,0:T(8,128)(2,1)S(1)}, bf16[64,2048]{1,0:T(8,128)(2,1)S(1)}, u32[]{:S(2)}, u32[]{:S(2)}) collective-permute-start(bf16[64,2048]{1,0:T(8,128)(2,1)S(1)} %get-tuple-element.136), channel_id=1, source_target_pairs={{0,1},{1,0},{2,3},{3,2},{4,5},{5,4},{6,7},{7,6},{8,9},{9,8},{10,11... | collective-permute-start | bytes 786440 | tf_op jit(solution)/shard_map/ppermute | solution.py:30
  722.1 21.4 %collective-permute-start.55 = (bf16[64,2048]{1,0:T(8,128)(2,1)S(1)}, bf16[64,2048]{1,0:T(8,128)(2,1)S(1)}, u32[]{:S(2)}, u32[]{:S(2)}) collective-permute-start(bf16[64,2048]{1,0:T(8,128)(2,1)S(1)} %get-tuple-element.132), channel_id=1, source_target_pairs={{0,2},{1,3},{2,0},{3,1},{4,6},{5,7},{6,4},{7,5},{8,10},{9,11},{10,... | collective-permute-start | bytes 786440 | tf_op jit(solution)/shard_map/ppermute | solution.py:30
  725.1 18.4 %collective-permute-start.56 = (bf16[64,2048]{1,0:T(8,128)(2,1)S(1)}, bf16[64,2048]{1,0:T(8,128)(2,1)S(1)}, u32[]{:S(2)}, u32[]{:S(2)}) collective-permute-start(bf16[64,2048]{1,0:T(8,128)(2,1)S(1)} %get-tuple-element.131), channel_id=1, source_target_pairs={{0,3},{1,2},{2,1},{3,0},{4,7},{5,6},{6,5},{7,4},{8,11},{9,10},{10,... | collective-permute-start | bytes 786440 | tf_op jit(solution)/shard_map/ppermute | solution.py:30
  (84 other events, 926.3 us)
Sparse Core Ops, SparseCore 0:
  31.4 86.7 all-gather.5
  119.8 80.5 all-gather.7
  202.0 80.6 all-gather.9
  284.1 45.6 all-gather.13
  331.8 45.8 all-gather.11
  444.3 47.7 reduce-scatter.4
  494.4 48.1 reduce-scatter.6
  544.9 87.7 reduce-scatter.8
  634.9 87.9 reduce-scatter.10

commit v3 on v2

--- a/solution.py
+++ b/solution.py
@@ -52,6 +52,20 @@
     for piece in coming:
         total = total + piece.astype(f32)
     return total
+
+
+def send_rows(partial):
+    count, me = lax.axis_size("row"), lax.axis_index("row")
+    size = partial.shape[0] // count
+    return [
+        swap(lax.dynamic_slice_in_dim(partial, (me ^ hop) * size, size, 0), hop) for hop in reversed(range(1, count))
+    ]
+
+
+def add_rows(partial, coming, *meanwhile):
+    size = partial.shape[0] // lax.axis_size("row")
+    mine = lax.dynamic_slice_in_dim(tie(partial, *meanwhile), lax.axis_index("row") * size, size, 0)
+    return sum([piece.astype(f32) for piece in coming], mine.astype(f32))
 
 
 def tie(value, *others):
@@ -110,21 +124,14 @@
     onehot_all = owned_from - jnp.concatenate(
         [owned_from[:, 1:], jnp.zeros((total, 1), f32)], axis=1
     )
-    reached = (
-        (parent_row[:, None] == segment_ids[None, :])
-        | (segment_ids[:, None] == segment_ids[None, :])
-    ).astype(f32)
-    for _ in range(2):
-        reached = jnp.minimum(jnp.sum(reached[:, :, None] * reached[None, :, :], axis=1), 1.0)
-    strict = reached - jnp.eye(seg_count, dtype=f32)
-    path_start = jnp.sum(strict * length_row.astype(f32)[None, :], axis=1)
-    position = all_rows.astype(f32) + jnp.sum(
-        onehot_all * (path_start - offsets.astype(f32))[None, :], axis=1
-    )
-    onehot_low = onehot_all.astype(bf16)
-    row_reach = dot(onehot_low, reached.astype(bf16), NN, bf16)
-    seen = dot(onehot_low, row_reach, NT)
-    allowed = (seen > 0.5) & (all_rows[:, None] <= all_rows[None, :])
+    parents = jnp.sum(onehot_all * parent_row.astype(f32)[None, :], axis=1)
+    segments = jnp.sum(onehot_all * segment_ids.astype(f32)[None, :], axis=1)
+    lengths = length_row.astype(f32)
+    parent_lengths = jnp.sum((parent_row[:, None] == segment_ids[None, :]) * lengths[None, :], axis=1)
+    above = jnp.where(segment_ids > 0, lengths[0], 0.0) + jnp.where(parent_row > 0, parent_lengths, 0.0)
+    position = all_rows.astype(f32) + jnp.sum(onehot_all * (above - offsets.astype(f32))[None, :], axis=1)
+    on_path = (segments[:, None] == segments[None, :]) | (segments[:, None] == parents[None, :]) | (segments[:, None] == 0.0)
+    allowed = on_path & (all_rows[:, None] <= all_rows[None, :])
     bias = jnp.where(allowed, 0.0, masked_fill).astype(bf16)
     frequency = jnp.exp(
         jnp.arange(HEAD_DIM // 2, dtype=f32) * (-2.0 * math.log(rope_theta) / HEAD_DIM)
@@ -379,12 +386,14 @@
     output_hbm,
     hidden_hbm,
     up_hbm,
+    gains_hbm,
     query_out,
     key_out,
     value_out,
     output_out,
     inputs_out,
     up_out,
+    gains_out,
     tokens,
     grads,
     weights,
@@ -402,6 +411,9 @@
     rows_send,
     rows_in,
     up_in,
+    gains,
+    gains_in,
+    gains_line,
     load_sem,
     row_send_sem,
     row_recv_sem,
@@ -409,6 +421,8 @@
     core_recv_sem,
     line_send_sem,
     line_recv_sem,
+    leaf_send_sem,
+    leaf_recv_sem,
 ):
     leaf, row = lax.axis_index("leaf"), lax.axis_index("row")
     z, core = leaf // 2, leaf % 2
@@ -424,15 +438,16 @@
         pltpu.make_async_copy(weights_hbm.at[:, pl.ds(0, wide)], weights, load_sem.at[2]),
         pltpu.make_async_copy(hidden_hbm, hidden, load_sem.at[3]),
         pltpu.make_async_copy(output_hbm.at[:, row], side.at[pl.ds(2 * row, 2)], load_sem.at[4]),
+        pltpu.make_async_copy(gains_hbm.at[row], gains, load_sem.at[6]),
     ]
     for load in loads:
         load.start()
     barrier = pltpu.get_barrier_semaphore()
     for hop in hops:
         pl.semaphore_signal(barrier, inc=1, device_id={"row": other(row, hop)}, device_id_type=MESH)
-        pl.semaphore_signal(barrier, inc=1, device_id={"leaf": 2 * other(z, hop) + core}, device_id_type=MESH)
-    pl.semaphore_signal(barrier, inc=1, device_id={"leaf": 2 * z + 1 - core}, device_id_type=MESH)
-    pl.semaphore_wait(barrier, 7)
+    for step in range(1, 8):
+        pl.semaphore_signal(barrier, inc=1, device_id={"leaf": (leaf + step) % 8}, device_id_type=MESH)
+    pl.semaphore_wait(barrier, 10)
 
     sent = []
 
@@ -470,6 +485,8 @@
             device_id_type=MESH,
         )
 
+    for hop in hops:
+        row_copy(gains_hbm.at[other(row, hop)], gains_in.at[hop - 1], 4, hop)
     for hop in hops:
         row_copy(output_hbm.at[:, other(row, hop)], side.at[pl.ds(2 * row, 2)], 0, hop)
 
@@ -501,6 +518,22 @@
             def _():
                 last.start()
 
+    loads[5].wait()
+    for hop in hops:
+        landed(gains_in.at[hop - 1], row_recv_sem.at[4, hop - 1])
+        gains[...] += gains_in[hop - 1]
+    for step in range(1, 8):
+        copy = pltpu.make_async_remote_copy(
+            gains.at[(leaf + step) % 8],
+            gains_line.at[step - 1],
+            leaf_send_sem.at[step - 1],
+            leaf_recv_sem.at[step - 1],
+            device_id={"leaf": (leaf + step) % 8},
+            device_id_type=MESH,
+        )
+        copy.start()
+        sent.append(copy)
+
     loads[2].wait()
 
     def tokens_part(hop, store):
@@ -587,6 +620,11 @@
     for source in range(4):
         up_out[:, source * up_in.shape[2] : (source + 1) * up_in.shape[2]] = up_in[source].astype(f32)
 
+    gains_out[...] = gains[leaf]
+    for step in range(1, 8):
+        landed(gains_line.at[step - 1], leaf_recv_sem.at[step - 1])
+        gains_out[...] += gains_line[step - 1]
+
     total(0, line_in, mine)
     rows_send[...] = mine[3]
     for hop in hops:
@@ -607,7 +645,7 @@
         copy.wait_send()
 
 
-def finish(tokens, grads, weights, output_part, hidden, up_shard):
+def finish(tokens, grads, weights, output_part, hidden, up_shard, gain_part):
     total, width = tokens.shape
     wide = grads.shape[1]
     own = output_part.shape[2]
@@ -616,8 +654,8 @@
     dma = pltpu.SemaphoreType.DMA
     return pl.pallas_call(
         final_kernel,
-        in_specs=[pl.BlockSpec(memory_space=pl.ANY)] * 6,
-        out_specs=[pl.BlockSpec(memory_space=pltpu.VMEM)] * 6,
+        in_specs=[pl.BlockSpec(memory_space=pl.ANY)] * 7,
+        out_specs=[pl.BlockSpec(memory_space=pltpu.VMEM)] * 7,
         out_shape=[
             matrix,
             matrix,
@@ -625,6 +663,7 @@
             matrix,
             jax.ShapeDtypeStruct((rows, width), bf16),
             jax.ShapeDtypeStruct((own, 4 * units), f32),
+            jax.ShapeDtypeStruct((8, HEAD_DIM), f32),
         ],
         scratch_shapes=[
             pltpu.VMEM((total, width), bf16),
@@ -644,13 +683,18 @@
             pltpu.VMEM((size, wide), bf16),
             pltpu.VMEM((3, own, wide), bf16),
             pltpu.VMEM((4, own, units), bf16),
-            dma((6,)),
-            dma((4, 3)),
-            dma((4, 3)),
+            pltpu.VMEM((8, 8, HEAD_DIM), f32),
+            pltpu.VMEM((3, 8, 8, HEAD_DIM), f32),
+            pltpu.VMEM((7, 8, HEAD_DIM), f32),
+            dma((7,)),
+            dma((5, 3)),
+            dma((5, 3)),
             dma((2, 4)),
             dma((2, 4)),
             dma((2, 3)),
             dma((2, 4)),
+            dma((7,)),
+            dma((7,)),
         ],
         compiler_params=pltpu.CompilerParams(
             collective_id=1, has_side_effects=True, vmem_limit_bytes=60 * 2**20
@@ -658,7 +702,491 @@
         cost_estimate=pl.CostEstimate(
             flops=4 * total * width * wide, bytes_accessed=100 * 2**20, transcendentals=0
         ),
-    )(tokens, grads, weights, output_part, hidden, up_shard)
+    )(tokens, grads, weights, output_part, hidden, up_shard, gain_part)
+
+
+def front_kernel(
+    tokens_hbm,
+    pack_hbm,
+    output_hbm,
+    gate_hbm,
+    up_hbm,
+    down_hbm,
+    gains_hbm,
+    cos_hbm,
+    sin_hbm,
+    bias_hbm,
+    attn_out,
+    gate_out,
+    up_out,
+    down_out,
+    tokens_out,
+    query_pre_out,
+    key_pre_out,
+    value_out,
+    scales_out,
+    query_out,
+    key_out,
+    context_out,
+    lse_out,
+    output_out,
+    unit_out,
+    unit_scale_out,
+    hidden_out,
+    hidden_all_out,
+    gains_out,
+    block,
+    attn_mat,
+    gate_block,
+    up_block,
+    down_block,
+    tokens,
+    query_pre,
+    key_pre,
+    value,
+    query,
+    key,
+    context,
+    lse,
+    bias,
+    cos_part,
+    sin_part,
+    scale_columns,
+    output_in,
+    output_mat,
+    rows_send,
+    rows_in,
+    half_in,
+    attn,
+    unit_scale,
+    hidden,
+    hidden_all,
+    squares,
+    squares_in,
+    scale_rows,
+    gains_leaf,
+    gains_all,
+    gains,
+    load_sem,
+    save_sem,
+    row_send_sem,
+    row_recv_sem,
+    leaf_send_sem,
+    leaf_recv_sem,
+    core_send_sem,
+    core_recv_sem,
+    line_send_sem,
+    line_recv_sem,
+):
+    leaf, row = lax.axis_index("leaf"), lax.axis_index("row")
+    z, core = leaf // 2, leaf % 2
+    far, inner = z // 2, ((z + 1) // 2) % 2
+    own = pack_hbm.shape[1]
+    wide = pack_hbm.shape[2]
+    part, size = wide // 3, 4 * own
+    rows, width = tokens_hbm.shape
+    units = gate_block.shape[1]
+    heads = part // HEAD_DIM
+    scale = 1.0 / math.sqrt(HEAD_DIM)
+    hops = (3, 1, 2)
+    sent, saved = [], []
+
+    def lines(index, count):
+        return pl.ds(pl.multiple_of(index * count, count), count)
+
+    def load(source, target, i):
+        copy = pltpu.make_async_copy(source, target, load_sem.at[i])
+        copy.start()
+        return copy
+
+    def save(source, target):
+        copy = pltpu.make_async_copy(source, target, save_sem.at[len(saved)])
+        copy.start()
+        saved.append(copy)
+
+    mine = lines(row, own)
+    load_pack = load(pack_hbm.at[row], block.at[mine, pl.ds(0, wide)], 0)
+    load_output = load(output_hbm, block.at[:, pl.ds(wide, part)], 1)
+    load_gains = load(gains_hbm, gains_leaf.at[row], 2)
+    load_gate = load(gate_hbm.at[:, lines(row, units)], gate_block.at[mine], 3)
+    load_tokens = load(tokens_hbm, tokens.at[lines(row, rows)], 4)
+    load_up = load(up_hbm.at[:, lines(row, units)], up_block.at[mine], 5)
+    load_down = load(down_hbm.at[:, lines(row, units)], down_block.at[mine], 6)
+    load_tables = [load(cos_hbm, cos_part, 7), load(sin_hbm, sin_part, 8), load(bias_hbm, bias, 9)]
+
+    barrier = pltpu.get_barrier_semaphore()
+    for hop in hops:
+        pl.semaphore_signal(barrier, inc=1, device_id={"row": other(row, hop)}, device_id_type=MESH)
+    for step in range(1, 8):
+        pl.semaphore_signal(barrier, inc=1, device_id={"leaf": (leaf + step) % 8}, device_id_type=MESH)
+    pl.semaphore_wait(barrier, 10)
+
+    def row_copy(source, target, kind, hop):
+        copy = pltpu.make_async_remote_copy(
+            source,
+            target,
+            row_send_sem.at[kind, hop - 1],
+            row_recv_sem.at[kind, hop - 1],
+            device_id={"row": other(row, hop)},
+            device_id_type=MESH,
+        )
+        copy.start()
+        sent.append(copy)
+
+    def row_landed(target, kind):
+        for hop in hops:
+            landed(target(other(row, hop), hop), row_recv_sem.at[kind, hop - 1])
+
+    def leaf_copy(source, target, send_sem, recv_sem, to):
+        return pltpu.make_async_remote_copy(
+            source, target, send_sem, recv_sem, device_id={"leaf": to}, device_id_type=MESH
+        )
+
+    for hop in hops:
+        row_copy(pack_hbm.at[other(row, hop)], block.at[mine, pl.ds(0, wide)], 0, hop)
+    for hop in hops:
+        row_copy(gains_hbm, gains_leaf.at[row], 1, hop)
+    for hop in hops:
+        row_copy(gate_hbm.at[:, lines(other(row, hop), units)], gate_block.at[mine], 2, hop)
+    for hop in hops:
+        row_copy(tokens_hbm, tokens.at[lines(row, rows)], 3, hop)
+    for hop in hops:
+        row_copy(up_hbm.at[:, lines(other(row, hop), units)], up_block.at[mine], 4, hop)
+    for hop in hops:
+        row_copy(down_hbm.at[:, lines(other(row, hop), units)], down_block.at[mine], 5, hop)
+
+    def spread(kind, source, whole):
+        place = whole.at[lines(leaf, size)]
+        across = leaf_copy(
+            source, place, line_send_sem.at[kind, 2], line_recv_sem.at[kind, 2], 2 * other(z, 2) + core
+        )
+        across.start()
+        sent.append(across)
+        forth = leaf_copy(source, place, line_send_sem.at[kind, 0], line_recv_sem.at[kind, 0], 2 * z + 2 + core)
+        back = leaf_copy(source, place, line_send_sem.at[kind, 1], line_recv_sem.at[kind, 1], 2 * z - 2 + core)
+
+        @pl.when(z < 3)
+        def _():
+            forth.start()
+
+        @pl.when(z > 0)
+        def _():
+            back.start()
+
+        beside = leaf_copy(source, place, core_send_sem.at[kind, 3], core_recv_sem.at[kind, 3], 2 * z + 1 - core)
+        beside.start()
+        sent.append(beside)
+        save(source, place)
+
+        def done():
+            @pl.when(z < 3)
+            def _():
+                forth.wait_send()
+
+            @pl.when(z > 0)
+            def _():
+                back.wait_send()
+
+        return done
+
+    def arrival(step):
+        inner_slot, inner_chip = ((2, other(z, 2)), (0, z - 1), (1, z + 1))[step]
+        end_slot, end_chip = ((1 - far, 1 + far), (2, other(z, 2)), (3, 3 - z))[step]
+        return end_slot + inner * (inner_slot - end_slot), end_chip + inner * (inner_chip - end_chip)
+
+    def pass_on(kind, whole, step):
+        slot, chip = arrival(step)
+        place = whole.at[lines(2 * chip + core, size)]
+        landed(place, line_recv_sem.at[kind, slot])
+        beside = leaf_copy(place, place, core_send_sem.at[kind, step], core_recv_sem.at[kind, step], 2 * z + 1 - core)
+        beside.start()
+        sent.append(beside)
+        if step == 0:
+            onward = leaf_copy(place, place, line_send_sem.at[kind, 3], line_recv_sem.at[kind, 3], 6 * far + core)
+
+            @pl.when(inner == 1)
+            def _():
+                onward.start()
+
+            def done():
+                @pl.when(inner == 1)
+                def _():
+                    onward.wait_send()
+
+            return done
+
+    def gathered(kind, whole):
+        landed(whole.at[lines(2 * z + 1 - core, size)], core_recv_sem.at[kind, 3])
+        for step in range(3):
+            chip = arrival(step)[1]
+            landed(whole.at[lines(2 * chip + 1 - core, size)], core_recv_sem.at[kind, step])
+
+    load_pack.wait()
+    load_output.wait()
+    row_landed(lambda source, hop: block.at[lines(source, own), pl.ds(0, wide)], 0)
+    done = [spread(0, block, attn_mat)]
+
+    load_gains.wait()
+    row_landed(lambda source, hop: gains_leaf.at[source], 1)
+    for step in range(1, 8):
+        copy = leaf_copy(
+            gains_leaf, gains_all.at[leaf], leaf_send_sem.at[step - 1], leaf_recv_sem.at[step - 1], (leaf + step) % 8
+        )
+        copy.start()
+        sent.append(copy)
+    gains_all[leaf] = gains_leaf[...]
+
+    load_gate.wait()
+    row_landed(lambda source, hop: gate_block.at[lines(source, own)], 2)
+    done.append(pass_on(0, attn_mat, 0))
+    pass_on(0, attn_mat, 1)
+    done.append(spread(1, gate_block, gate_out))
+    pass_on(0, attn_mat, 2)
+    gathered(0, attn_mat)
+    saved[0].wait()
+
+    load_tokens.wait()
+    row_landed(lambda source, hop: tokens.at[lines(source, rows)], 3)
+
+    def project_step(j, carry):
+        at = lines(j, rows)
+        some = tokens[at, :]
+        for i, out in enumerate((query_pre, key_pre)):
+            product = dot(some, attn_mat[:, i * part : (i + 1) * part], NN)
+            out[at, :] = product
+            square = jnp.sum(product * product, axis=1, keepdims=True)
+            squares[i : i + 1, at] = jnp.broadcast_to(square, (rows, HEAD_DIM)).T[0:1]
+        value[at, :] = dot(some, attn_mat[:, 2 * part : wide], NN, bf16)
+        return carry
+
+    squares[...] = jnp.zeros_like(squares)
+    lax.fori_loop(0, 4, project_step, 0)
+    for hop in hops:
+        row_copy(squares, squares_in.at[hop - 1], 7, hop)
+    for hop in hops:
+        row_copy(
+            attn_mat.at[lines(other(row, hop), 2 * size), pl.ds(wide, part)], output_in.at[row], 6, hop
+        )
+    keep = load(attn_mat.at[lines(row, 2 * size), pl.ds(wide, part)], output_in.at[row], 10)
+    load_up.wait()
+    row_landed(lambda source, hop: up_block.at[lines(source, own)], 4)
+    done.append(spread(2, up_block, up_out))
+    save(attn_mat, attn_out)
+    save(tokens, tokens_out)
+    save(query_pre, query_pre_out)
+    save(key_pre, key_pre_out)
+    save(value, value_out)
+    for step in range(1, 8):
+        landed(gains_all.at[(leaf - step + 8) % 8], leaf_recv_sem.at[step - 1])
+    for source in range(8):
+        for pair in range(2):
+            first = (2 * source + pair) * HEAD_DIM
+            gains[:, first : first + HEAD_DIM] = gains_all[source, 2 * pair] + gains_all[source, 2 * pair + 1]
+    save(gains, gains_out)
+    for table in load_tables:
+        table.wait()
+    row_landed(lambda source, hop: squares_in.at[hop - 1], 7)
+    scales = lax.rsqrt((squares[...] + squares_in[0] + squares_in[1] + squares_in[2]) / width + epsilon)
+    scale_rows[...] = scales
+    save(scale_rows, scales_out)
+    for i in range(2):
+        scale_columns[i] = jnp.broadcast_to(scales[i : i + 1], (HEAD_DIM, 4 * rows)).T
+
+    def head_step(h, carry):
+        at = lines(h, HEAD_DIM)
+        at_gain = lines(row * heads + h, HEAD_DIM)
+        for i, (pre, out) in enumerate(((query_pre, query), (key_pre, key))):
+            scaled = pre[:, at] * scale_columns[i] * gains[i : i + 1, at_gain]
+            out[:, at] = turn(scaled, cos_part[...], sin_part[...]).astype(bf16)
+        for first in range(0, 4 * rows, rows):
+            last = first + rows
+            scores = dot(key[:last, at], query[first:last, at], NT) * scale
+            scores = scores + bias[:last, first:last].astype(f32)
+            top = jnp.max(scores, axis=0, keepdims=True)
+            probs = jnp.exp(scores - top)
+            mass = jnp.sum(probs, axis=0, keepdims=True)
+            probs_low = (probs * (1.0 / mass)).astype(bf16)
+            turned = dot(value[:last, at], probs_low, TN)
+            context[first:last, at] = turned.T.astype(bf16)
+            lse[lines(h, 8), first:last] = jnp.broadcast_to(top + jnp.log(mass), (8, rows))
+        return carry
+
+    lax.fori_loop(0, heads, head_step, 0)
+    done.append(pass_on(1, gate_out, 0))
+    save(query, query_out)
+    save(key, key_out)
+    save(context, context_out)
+    save(lse, lse_out)
+
+    keep.wait()
+    row_landed(lambda source, hop: output_in.at[source], 6)
+    for i in range(2):
+        for source in range(4):
+            for j in range(4):
+                output_mat[i * size + source * own : i * size + (source + 1) * own, j * part : (j + 1) * part] = (
+                    output_in[source, i * size + j * own : i * size + (j + 1) * own, :]
+                )
+    save(output_mat, output_out)
+
+    def output_part(hop, store):
+        some = context[lines(other(row, hop), rows), :]
+        for j in range(4):
+            columns = slice(j * part, (j + 1) * part)
+            store(columns, dot(some, output_mat[:, columns], NN))
+
+    half = rows // 2
+    top, bottom = pl.ds(0, half), pl.ds(half, half)
+    for hop in hops:
+
+        def store(columns, values):
+            rows_send[hop - 1, :, columns] = values.astype(bf16)
+
+        output_part(hop, store)
+        if hop == 3:
+            row_copy(rows_send.at[2, top], half_in.at[0], 8, 1)
+            row_copy(rows_send.at[2, bottom], half_in.at[1], 8, 2)
+        else:
+            early = (top, bottom)[hop - 1]
+            row_copy(rows_send.at[hop - 1, early], rows_in.at[hop - 1, early], 10, hop)
+    for hop in (1, 2):
+        late = (bottom, top)[hop - 1]
+        landed(half_in.at[2 - hop], row_recv_sem.at[8, 2 - hop])
+        rows_send[hop - 1, late] = (rows_send[hop - 1, late].astype(f32) + half_in[2 - hop].astype(f32)).astype(bf16)
+        row_copy(rows_send.at[hop - 1, late], rows_in.at[hop - 1, late], 11, hop)
+
+    def own_store(columns, values):
+        attn[:, columns] = values
+
+    output_part(0, own_store)
+
+    pass_on(1, gate_out, 1)
+    done.append(pass_on(2, up_out, 0))
+    for hop in (1, 2):
+        early, late = ((top, bottom), (bottom, top))[hop - 1]
+        landed(rows_in.at[hop - 1, early], row_recv_sem.at[10, hop - 1])
+        landed(rows_in.at[hop - 1, late], row_recv_sem.at[11, hop - 1])
+        attn[...] += rows_in[hop - 1].astype(f32)
+    mean = jnp.sum(attn[...] * attn[...], axis=1, keepdims=True) / width
+    factor = lax.rsqrt(mean + epsilon)
+    unit_scale[...] = jnp.broadcast_to(factor, unit_scale.shape)
+    attn[...] = attn[...] * factor
+    hidden[...] = tokens[lines(row, rows), :].astype(f32) + attn[...] * gains[2:3, :]
+    hidden_all[lines(row, rows), :] = hidden[...].astype(bf16)
+    for hop in (1, 2):
+        place = hidden_all.at[lines(row, rows)]
+        row_copy(place, place, 9, hop)
+    save(attn, unit_out)
+    save(unit_scale, unit_scale_out)
+    save(hidden, hidden_out)
+    load_down.wait()
+    row_landed(lambda source, hop: down_block.at[lines(source, own)], 5)
+    save(down_block, down_out)
+
+    for hop in (1, 2):
+        landed(hidden_all.at[lines(other(row, hop), rows)], row_recv_sem.at[9, hop - 1])
+        place = hidden_all.at[lines(2 * other(row, hop) + hop - 1, half)]
+        row_copy(place, place, 12, 3 - hop)
+    for hop in (1, 2):
+        landed(hidden_all.at[lines(2 * other(row, 3) + 2 - hop, half)], row_recv_sem.at[12, hop - 1])
+    save(hidden_all, hidden_all_out)
+    pass_on(1, gate_out, 2)
+    pass_on(2, up_out, 1)
+    pass_on(2, up_out, 2)
+    gathered(1, gate_out)
+    gathered(2, up_out)
+
+    for finish_sends in done:
+        finish_sends()
+    for copy in sent:
+        copy.wait_send()
+    for copy in saved[1:]:
+        copy.wait()
+
+
+def front(tokens, pack, output_block, gate, up, down, gain_tile, cos_wide, sin_wide, bias):
+    rows, width = tokens.shape
+    total, part, own = 4 * rows, width // 4, pack.shape[1]
+    wide, units, size = 3 * part, gate.shape[1] // 4, 4 * own
+    heads = part // HEAD_DIM
+    shape = jax.ShapeDtypeStruct
+    outs = [
+        shape((width, width), bf16),
+        shape((width, units), bf16),
+        shape((width, units), bf16),
+        shape((size, units), bf16),
+        shape((total, width), bf16),
+        shape((total, part), f32),
+        shape((total, part), f32),
+        shape((total, part), bf16),
+        shape((8, total), f32),
+        shape((total, part), bf16),
+        shape((total, part), bf16),
+        shape((total, part), bf16),
+        shape((8 * heads, total), f32),
+        shape((part, width), bf16),
+        shape((rows, width), f32),
+        shape((rows, HEAD_DIM), f32),
+        shape((rows, width), f32),
+        shape((total, width), bf16),
+        shape((8, width), f32),
+    ]
+    vmem, dma = pltpu.VMEM, pltpu.SemaphoreType.DMA
+    return pl.pallas_call(
+        front_kernel,
+        in_specs=[pl.BlockSpec(memory_space=pl.ANY)] * 10,
+        out_specs=[pl.BlockSpec(memory_space=pl.ANY)] * len(outs),
+        out_shape=outs,
+        scratch_shapes=[
+            vmem((size, width), bf16),
+            vmem((width, width), bf16),
+            vmem((size, units), bf16),
+            vmem((size, units), bf16),
+            vmem((size, units), bf16),
+            vmem((total, width), bf16),
+            vmem((total, part), f32),
+            vmem((total, part), f32),
+            vmem((total, part), bf16),
+            vmem((total, part), bf16),
+            vmem((total, part), bf16),
+            vmem((total, part), bf16),
+            vmem((8 * heads, total), f32),
+            vmem((total, total), bf16),
+            vmem((total, HEAD_DIM), f32),
+            vmem((total, HEAD_DIM), f32),
+            vmem((2, total, HEAD_DIM), f32),
+            vmem((4, part, part), bf16),
+            vmem((part, width), bf16),
+            vmem((3, rows, width), bf16),
+            vmem((2, rows, width), bf16),
+            vmem((2, rows // 2, width), bf16),
+            vmem((rows, width), f32),
+            vmem((rows, HEAD_DIM), f32),
+            vmem((rows, width), f32),
+            vmem((total, width), bf16),
+            vmem((8, total), f32),
+            vmem((3, 8, total), f32),
+            vmem((8, total), f32),
+            vmem((4, 8, HEAD_DIM), f32),
+            vmem((8, 4, 8, HEAD_DIM), f32),
+            vmem((8, width), f32),
+            dma((11,)),
+            dma((24,)),
+            dma((13, 3)),
+            dma((13, 3)),
+            dma((7,)),
+            dma((7,)),
+            dma((3, 4)),
+            dma((3, 4)),
+            dma((3, 4)),
+            dma((3, 4)),
+        ],
+        compiler_params=pltpu.CompilerParams(
+            collective_id=2, has_side_effects=True, vmem_limit_bytes=62 * 2**20
+        ),
+        cost_estimate=pl.CostEstimate(
+            flops=10 * total * width * part, bytes_accessed=100 * 2**20, transcendentals=0
+        ),
+    )(tokens, pack, output_block, gate, up, down, gain_tile, cos_wide, sin_wide, bias)
 
 
 def body(
@@ -693,54 +1221,99 @@
     def leaf_scatter(block):
         return lax.psum_scatter(block, "leaf", scatter_dimension=0, tiled=True)
 
-    qkv_block = columns_in(w_query, w_key, w_value)
-    gains_own = jnp.stack([gain_query, gain_key, gain_attn, gain_mlp]).astype(bf16).reshape(1, 4 * own)
-    gains_leaf = gather_rows(gains_own).reshape(count * own, 4)
-    attn_block = jnp.concatenate(
-        [
-            qkv_block,
-            w_output.astype(bf16).reshape(count * own, part),
-            jnp.pad(gains_leaf, ((0, 0), (0, HEAD_DIM - 4))),
-        ],
-        axis=1,
-    )
-    attn_mat = leaf_gather(attn_block)
-    qkv_mat = attn_mat[:, : 3 * part]
-    output_rows = attn_mat[:, 3 * part : 4 * part].reshape(count, leaves // count, own, width)
-    gains_all = attn_mat[:, 4 * part : 4 * part + 4].reshape(leaves, count, 4, own)
-    gains_all = jnp.moveaxis(gains_all, 2, 0).reshape(4, width).astype(f32)
-    gate_block = columns_in(tie(w_gate, qkv_block))
-    up_block = columns_in(tie(w_up, qkv_block))
-    down_block = columns_in(tie(w_down, qkv_block))
-    all_tokens = gather_rows(tie(tokens, gate_block, up_block, down_block))
     bias, cos_wide, sin_wide = tree_tables(seg_lengths[0], seg_parents[0], tree_len)
-
-    query_pre, key_pre, value, squares = project(all_tokens, attn_mat, part)
-    gate_mat = leaf_gather(gate_block)
-    up_mat = leaf_gather(up_block)
-    down_halves = [leaf_gather(down_block[h * group : (h + 1) * group]) for h in range(2)]
-
-    squares = sum_rows(squares)
-    scales = lax.rsqrt(squares / width + epsilon)
-    query_scale, key_scale = scales[0][:, None], scales[1][:, None]
-    attn_gain, mlp_gain = gains_all[2], gains_all[3]
-    head_gains = lax.dynamic_slice_in_dim(gains_all[:2], me * part, part, 1)
-    output_rows = tie(output_rows, scales)
-    output_mat = jnp.zeros((leaves // count, count, own, width), bf16)
-    for hop in range(count):
-        piece = lax.dynamic_index_in_dim(output_rows, me ^ hop, 0, keepdims=False)
-        if hop:
-            piece = swap(piece, hop)
-        output_mat = lax.dynamic_update_index_in_dim(output_mat, piece, me ^ hop, 1)
-    output_mat = output_mat.reshape(part, width)
-    query, key, context, lse = attend(
-        query_pre, key_pre, value, scales.T, head_gains, cos_wide, sin_wide, bias
-    )
-    attn_pre = dot_scatter([context], [output_mat], NN)
-    attn_scale = lax.rsqrt(jnp.mean(attn_pre * attn_pre, axis=-1, keepdims=True) + epsilon)
-    attn_unit = attn_pre * attn_scale
-    hidden = tokens.astype(f32) + attn_unit * attn_gain
-    hidden_all = gather_rows(hidden.astype(bf16))
+    fast = leaves == 8 and count == 4
+    if fast:
+        def split_columns(weight):
+            return jnp.swapaxes(weight.astype(bf16).reshape(own, count, -1), 0, 1)
+
+        gain_own = jnp.stack([gain_query, gain_key, gain_attn, gain_mlp]).astype(bf16).astype(f32)
+        gain_tile = lax.dynamic_update_slice(jnp.zeros((8, HEAD_DIM), f32), gain_own, (0, (me % 2) * own))
+        (
+            attn_mat,
+            gate_mat,
+            up_mat,
+            down_block,
+            all_tokens,
+            query_pre,
+            key_pre,
+            value,
+            scales,
+            query,
+            key,
+            context,
+            lse,
+            output_mat,
+            attn_unit,
+            attn_scale,
+            hidden,
+            hidden_all,
+            gains_all,
+        ) = front(
+            tokens,
+            jnp.concatenate([split_columns(w) for w in (w_query, w_key, w_value)], axis=2),
+            split_columns(w_output).reshape(count * own, part),
+            w_gate.astype(bf16),
+            w_up.astype(bf16),
+            w_down.astype(bf16),
+            gain_tile,
+            cos_wide,
+            sin_wide,
+            bias,
+        )
+        scales, attn_scale = scales[:2], attn_scale[:, :1]
+        down_halves = [leaf_gather(down_block[h * group : (h + 1) * group]) for h in range(2)]
+        query_scale, key_scale = scales[0][:, None], scales[1][:, None]
+        attn_gain, mlp_gain = gains_all[2], gains_all[3]
+        head_gains = lax.dynamic_slice_in_dim(gains_all[:2], me * part, part, 1)
+    else:
+        qkv_block = columns_in(w_query, w_key, w_value)
+        gains_own = jnp.stack([gain_query, gain_key, gain_attn, gain_mlp]).astype(bf16).reshape(1, 4 * own)
+        gains_leaf = gather_rows(gains_own).reshape(count * own, 4)
+        attn_block = jnp.concatenate(
+            [
+                qkv_block,
+                w_output.astype(bf16).reshape(count * own, part),
+                jnp.pad(gains_leaf, ((0, 0), (0, HEAD_DIM - 4))),
+            ],
+            axis=1,
+        )
+        attn_mat = leaf_gather(attn_block)
+        qkv_mat = attn_mat[:, : 3 * part]
+        output_rows = attn_mat[:, 3 * part : 4 * part].reshape(count, leaves // count, own, width)
+        gains_all = attn_mat[:, 4 * part : 4 * part + 4].reshape(leaves, count, 4, own)
+        gains_all = jnp.moveaxis(gains_all, 2, 0).reshape(4, width).astype(f32)
+        gate_block = columns_in(tie(w_gate, qkv_block))
+        up_block = columns_in(tie(w_up, qkv_block))
+        down_block = columns_in(tie(w_down, qkv_block))
+        all_tokens = gather_rows(tie(tokens, gate_block, up_block, down_block))
+
+        query_pre, key_pre, value, squares = project(all_tokens, attn_mat, part)
+        gate_mat = leaf_gather(gate_block)
+        up_mat = leaf_gather(up_block)
+        down_halves = [leaf_gather(down_block[h * group : (h + 1) * group]) for h in range(2)]
+
+        squares = sum_rows(squares)
+        scales = lax.rsqrt(squares / width + epsilon)
+        query_scale, key_scale = scales[0][:, None], scales[1][:, None]
+        attn_gain, mlp_gain = gains_all[2], gains_all[3]
+        head_gains = lax.dynamic_slice_in_dim(gains_all[:2], me * part, part, 1)
+        output_rows = tie(output_rows, scales)
+        output_mat = jnp.zeros((leaves // count, count, own, width), bf16)
+        for hop in range(count):
+            piece = lax.dynamic_index_in_dim(output_rows, me ^ hop, 0, keepdims=False)
+            if hop:
+                piece = swap(piece, hop)
+            output_mat = lax.dynamic_update_index_in_dim(output_mat, piece, me ^ hop, 1)
+        output_mat = output_mat.reshape(part, width)
+        query, key, context, lse = attend(
+            query_pre, key_pre, value, scales.T, head_gains, cos_wide, sin_wide, bias
+        )
+        attn_pre = dot_scatter([context], [output_mat], NN)
+        attn_scale = lax.rsqrt(jnp.mean(attn_pre * attn_pre, axis=-1, keepdims=True) + epsilon)
+        attn_unit = attn_pre * attn_scale
+        hidden = tokens.astype(f32) + attn_unit * attn_gain
+        hidden_all = gather_rows(hidden.astype(bf16))
 
     gate_pre = dot(hidden_all, gate_mat, NN)
     up_pre = dot(hidden_all, up_mat, NN)
@@ -768,8 +1341,20 @@
     grad_act = grad_act + dot(tie(grad_mlp_halves[1], down_sums[1]), down_halves[1], NN)
     grad_gate = (grad_act * up_pre * sigmoid_gate * (1.0 + gate_pre * (1.0 - sigmoid_gate))).astype(bf16)
     grad_up = (grad_act * gate_pre * sigmoid_gate).astype(bf16)
-    gate_sum = tie(dot(hidden_all, grad_gate, TN, bf16), *down_sums)
-    grad_hidden = grad_final + dot_scatter([grad_gate, grad_up], [gate_mat, up_mat], NT, gate_sum)
+    wide = width // 2
+    parts, coming = [], []
+    for h in range(2):
+        one = tie(grad_gate, *parts), tie(grad_up, *parts)
+        part_h = sum(
+            dot(left, right[h * wide : (h + 1) * wide], NT) for left, right in zip(one, (gate_mat, up_mat))
+        ).astype(bf16)
+        parts.append(part_h)
+        coming.append(send_rows(part_h))
+    gate_sum = dot(hidden_all, tie(grad_gate, *parts), TN, bf16)
+    grad_hidden = grad_final + jnp.concatenate(
+        [add_rows(part_h, pieces, gate_sum) for part_h, pieces in zip(parts, coming)], axis=1
+    )
+    gate_sum = tie(gate_sum, *down_sums)
     gate_shard = leaf_scatter(gate_sum)
 
     grad_attn, grad_attn_gain = norm_back(grad_hidden, attn_unit, attn_scale, attn_gain)
@@ -791,40 +1376,46 @@
         key_scale * (grad_key * head_gains[1] - key_pre * (key_scale * inner[1][:, None]))
     ).astype(bf16)
     grad_qkv = jnp.concatenate([grad_query_low, grad_key_low, grad_value], axis=1)
-    gate_out = columns_out(tie(gate_shard, inner))
-    down_out = columns_out(tie(jnp.concatenate(down_shards), inner))
+    gate_out = columns_out(tie(gate_shard, inner_query))
+    down_out = columns_out(tie(jnp.concatenate(down_shards), inner_query))
+    mlp_halves = tie(mlp_halves, inner_query)
     mlp_unit = jnp.stack([m.reshape(rows_dev, leaves, group) for m in mlp_halves], axis=2).reshape(rows_dev, width)
     mlp_unit = mlp_unit * mlp_scale
     outputs = (hidden + mlp_unit * mlp_gain).astype(bf16).reshape(inputs.shape)
     grad_mlp_gain = jnp.sum(grad_final * mlp_unit, axis=0)
 
-    wide_part = jnp.stack([grad_attn_gain, grad_mlp_gain]).reshape(2, leaves, count, own)
+    wide_part = jnp.stack([tie(grad_attn_gain, inner), grad_mlp_gain]).reshape(2, leaves, count, own)
     narrow_part = grad_head_gains.reshape(2, leaves // count, count, own)
-    wide_sum = jnp.zeros((2, leaves, own), f32)
-    narrow_all = jnp.zeros((2, leaves, own), f32)
-    for hop in range(count):
-        piece = lax.dynamic_index_in_dim(jnp.concatenate([wide_part, narrow_part], axis=1), me ^ hop, 2, keepdims=False)
-        if hop:
-            piece = swap(piece, hop)
-        wide_sum = wide_sum + piece[:, :leaves]
-        narrow_all = lax.dynamic_update_slice_in_dim(
-            narrow_all, piece[:, leaves:], (me ^ hop) * (leaves // count), 1
-        )
-    grad_gains = jnp.concatenate([narrow_all, wide_sum], axis=0)
-    stride = 1
-    while stride < leaves:
-        grad_gains = grad_gains + lax.ppermute(
-            grad_gains, "leaf", [(i, i ^ stride) for i in range(leaves)]
-        )
-        stride *= 2
-    grad_gains = lax.dynamic_index_in_dim(grad_gains, lax.axis_index("leaf"), 1, keepdims=False)
-    grad_qkv = tie(grad_qkv, gate_out, down_out, outputs, grad_gains)
-    if leaves == 8 and count == 4:
-        *grad_mats, grad_output, grad_tokens, up_out = finish(
-            all_tokens, grad_qkv, attn_mat, output_part, grad_hidden, up_shard
-        )
-        grad_inputs, up_out = grad_tokens.reshape(inputs.shape), [up_out]
+    grad_qkv = tie(grad_qkv, gate_out, down_out, outputs)
+    if fast:
+        gain_part = jnp.zeros((count, leaves, 8, HEAD_DIM), f32)
+        gain_part = lax.dynamic_update_slice(
+            gain_part, jnp.transpose(narrow_part, (2, 1, 0, 3)), (0, me * (leaves // count), 0, 0)
+        )
+        gain_part = lax.dynamic_update_slice(gain_part, jnp.transpose(wide_part, (2, 1, 0, 3)), (0, 0, 2, 0))
+        *grad_mats, grad_output, grad_tokens, up_out, grad_gains = finish(
+            all_tokens, grad_qkv, attn_mat, output_part, grad_hidden, up_shard, gain_part
+        )
+        grad_inputs, up_out, grad_gains = grad_tokens.reshape(inputs.shape), [up_out], grad_gains[:4, :own]
     else:
+        wide_sum = jnp.zeros((2, leaves, own), f32)
+        narrow_all = jnp.zeros((2, leaves, own), f32)
+        for hop in range(count):
+            piece = lax.dynamic_index_in_dim(jnp.concatenate([wide_part, narrow_part], axis=1), me ^ hop, 2, keepdims=False)
+            if hop:
+                piece = swap(piece, hop)
+            wide_sum = wide_sum + piece[:, :leaves]
+            narrow_all = lax.dynamic_update_slice_in_dim(
+                narrow_all, piece[:, leaves:], (me ^ hop) * (leaves // count), 1
+            )
+        grad_gains = jnp.concatenate([narrow_all, wide_sum], axis=0)
+        stride = 1
+        while stride < leaves:
+            grad_gains = grad_gains + lax.ppermute(
+                grad_gains, "leaf", [(i, i ^ stride) for i in range(leaves)]
+            )
+            stride *= 2
+        grad_gains = lax.dynamic_index_in_dim(grad_gains, lax.axis_index("leaf"), 1, keepdims=False)
         output_turned = jnp.zeros((count, leaves // count, own, width), bf16)
         for hop in range(count):
             piece = lax.dynamic_index_in_dim(output_part, me ^ hop, 1, keepdims=False)

time: 865 us -> 844 us (0.976)
  Pallas kernels: 135 us -> 354 us
  waiting for transfers between devices: 327 us -> 178 us
  starting transfers between devices: 78.4 us -> 34.9 us
  matrix products: 186 us -> 152 us
  local copies, waits for them, and re-layouts: 88.6 us -> 56.8 us
  other arithmetic: 27.7 us -> 49.2 us
    pallas_call x2 -> x1, Pallas kernels: 24.2 us -> 239 us  [front(): pl.pallas_call(front_kernel, in_specs=[pl.BlockSpec(memory_space=pl.ANY)]...]
    ppermute x60 -> x30, waiting for transfers between devices: 281 us -> 124 us  [swap(): return lax.ppermute(piece, 'row', [(i, i ^ hop) for i in range(count)])]
    ppermute x60 -> x30, starting transfers between devices: 75.6 us -> 34.6 us  [swap(): return lax.ppermute(piece, 'row', [(i, i ^ hop) for i in range(count)])]
    dot_general x31 -> x22, matrix products: 186 us -> 152 us  [dot(): lax.dot_general(left, right, dims, preferred_element_type=f32).astype(kind)]
    dynamic_update_slice x18 -> x9, local copies, waits for them, and re-layouts: 16 us -> 3.2 us  [gather_rows(): lax.dynamic_update_slice_in_dim(whole, swap(rows, hop), (me ^ hop) * size...]
    all_gather x5 -> x2, waiting for transfers between devices: 41.5 us -> 53.4 us  [leaf_gather(): return lax.all_gather(block, 'leaf', axis=0, tiled=True)]
    convert_element_type x4 -> x11, other arithmetic: 1.61 us -> 10.3 us  [the longest x4 3.39 us: split_columns(): return jnp.swapaxes(weight.astype(bf16).reshape(own, count, -1), 0, 1)]
    unnamed x130 -> x134, local copies, waits for them, and re-layouts: 28.9 us -> 21.8 us
  transfers between devices with their start and end apart: 72 -> 36, of which waited for: 37 -> 16; matrix products, arithmetic and copies ran while one was open for 31% -> 24% of each run, Pallas kernels for 5% -> 2%
where the time goes in v3:
time: 844 us; the launch traced here: 840 us
  Pallas kernels  354 us (42%)
  waiting for transfers between devices  178 us (21%)
  matrix products  152 us (18%)
  local copies, waits for them, and re-layouts  56.8 us (7%)
  other arithmetic  49.2 us (6%)
  starting transfers between devices  34.9 us (4%)
  between operations  15.7 us (2%)
    pallas_call x1, Pallas kernels, front(): pl.pallas_call(front_kernel, in_specs=[pl.BlockSpec(memory_space=pl.ANY)]...  239 us
    dot_general x22, matrix products, dot(): lax.dot_general(left, right, dims, preferred_element_type=f32).astype(kind)  152 us
    ppermute x30, waiting for transfers between devices, swap(): return lax.ppermute(piece, 'row', [(i, i ^ hop) for i in range(count)])  124 us
    pallas_call x1, Pallas kernels, finish(): pl.pallas_call(final_kernel, in_specs=[pl.BlockSpec(memory_space=pl.ANY)]...  97.8 us
    all_gather x2, waiting for transfers between devices, leaf_gather(): return lax.all_gather(block, 'leaf', axis=0, tiled=True)  53.4 us
    ppermute x30, starting transfers between devices, swap(): return lax.ppermute(piece, 'row', [(i, i ^ hop) for i in range(count)])  34.6 us
    unnamed x134, local copies, waits for them, and re-layouts  21.8 us
  transfers between devices with their start and end apart: 36, of which 16 were waited for; matrix products, arithmetic and copies ran while one was open for 24% of the time, Pallas kernels for 2%

profile of v3, /device:TPU:0, one launch (start us, length us, event | category | flops | bytes accessed | tf_op | source)
XLA Modules:
  0.0 840.4 jit_solution(6545846677991092345)
XLA Ops:
  20.9 2.8 select_convert_fusion.bias_hbm.bias_ref
  26.4 239.4 %shard_map.246 = (bf16[2048,2048]{1,0:T(8,128)(2,1)}, bf16[2048,2048]{1,0:T(8,128)(2,1)}, bf16[2048,2048]{1,0:T(8,128)(2,1)}, bf16[256,2048]{1,0:T(8,128)(2,1)},...) custom-call(bf16[256,2048]{1,0:T(8,128)(2,1)} %bitcast.177, ...), custom_call_target="tpu_custom_call" | custom-call | flops 10737418240 | bytes 104857600 | tf_op jit(solution)/shard_map/pallas_call | solution.py:1134
  268.9 3.3 reshape.191
  276.3 11.4 %fusion.47 = f32[1024,2048]{1,0:T(8,128)S(1)} fusion(bf16[1024,2048]{1,0:T(8,128)(2,1)S(1)} %copy-done.53, bf16[2048,2048]{1,0:T(8,128)(2,1)} %get-tuple-element.69), kind=kOutput, calls=%fused_computation.162 | convolution fusion | flops 8589934592 | bytes 20971520 | tf_op jit(solution)/shard_map/dot_general | solution.py:25
  287.7 3.3 copy-done.52
  291.0 14.4 %multiply_convert_fusion.2 = (bf16[1024,2048]{1,0:T(8,128)(2,1)}, f32[1024,2048]{1,0:T(8,128)}) fusion(f32[1024,2048]{1,0:T(8,128)S(1)} %fusion.47, bf16[1024,2048]{1,0:T(8,128)(2,1)} %get-tuple-element.68, bf16[2048,2048]{1,0:T(8,128)(2,1)S(1)} %bitcast.182), kind=kOutput, calls=%fused_computation.2 | convolution fusion | flops 8602517504 | bytes 33554432 | tf_op jit(solution)/shard_map/dot_general | solution.py:25
  305.4 19.6 %all-gather.5.cloned.1.call-done = bf16[1024,2048]{1,0:T(8,128)(2,1)} async-done(((bf16[128,2048]{1,0:T(8,128)(2,1)}), bf16[1024,2048]{1,0:T(8,128)(2,1)}) %all-gather.5.cloned.1.call-update) | async-done | bytes 4194320 | tf_op jit(solution)/shard_map/all_gather | solution.py:1219
  325.0 3.9 convolution_convert_fusion.8
  328.9 2.4 collective-permute-start.3
  331.4 3.4 convolution_convert_fusion.7
  335.2 3.3 convolution_convert_fusion.6
  339.2 33.9 %all-gather.3.cloned.1.call-done = bf16[1024,2048]{1,0:T(8,128)(2,1)} async-done(((bf16[128,2048]{1,0:T(8,128)(2,1)}), bf16[1024,2048]{1,0:T(8,128)(2,1)}) %all-gather.3.cloned.1.call-update) | async-done | bytes 4194320 | tf_op jit(solution)/shard_map/all_gather | solution.py:1219
  373.1 4.8 convolution_convert_fusion.11
  380.2 3.3 convolution_convert_fusion.10
  384.1 3.3 convolution_convert_fusion.9
  388.2 6.6 slice_reduce_fusion
  396.4 4.7 multiply_reduce_fusion.4
  401.1 3.2 collective-permute-done.1
  404.4 3.0 multiply_reduce_fusion.5
  412.1 11.3 %collective-permute-done.9 = bf16[256,1024]{1,0:T(8,128)(2,1)S(1)} collective-permute-done((bf16[256,1024]{1,0:T(8,128)(2,1)S(1)}, bf16[256,1024]{1,0:T(8,128)(2,1)S(1)}, u32[]{:S(2)}, u32[]{:S(2)}) %collective-permute-start.9) | collective-permute-done | bytes 524320 | tf_op jit(solution)/shard_map/ppermute | solution.py:30
  423.8 11.1 %collective-permute-done.10 = bf16[256,1024]{1,0:T(8,128)(2,1)S(1)} collective-permute-done((bf16[256,1024]{1,0:T(8,128)(2,1)S(1)}, bf16[256,1024]{1,0:T(8,128)(2,1)S(1)}, u32[]{:S(2)}, u32[]{:S(2)}) %collective-permute-start.10) | collective-permute-done | bytes 524320 | tf_op jit(solution)/shard_map/ppermute | solution.py:30
  435.0 6.2 convolution_convert_fusion.2
  444.9 11.6 %collective-permute-done.6 = bf16[256,1024]{1,0:T(8,128)(2,1)S(1)} collective-permute-done((bf16[256,1024]{1,0:T(8,128)(2,1)}, bf16[256,1024]{1,0:T(8,128)(2,1)S(1)}, u32[]{:S(2)}, u32[]{:S(2)}) %collective-permute-start.6) | collective-permute-done | bytes 524320 | tf_op jit(solution)/shard_map/ppermute | solution.py:30
  456.8 9.9 %collective-permute-done.7 = bf16[256,1024]{1,0:T(8,128)(2,1)S(1)} collective-permute-done((bf16[256,1024]{1,0:T(8,128)(2,1)}, bf16[256,1024]{1,0:T(8,128)(2,1)S(1)}, u32[]{:S(2)}, u32[]{:S(2)}) %collective-permute-start.7) | collective-permute-done | bytes 524320 | tf_op jit(solution)/shard_map/ppermute | solution.py:30
  468.2 6.3 convolution_convert_fusion.3
  474.6 10.9 %fusion.48 = f32[1024,2048]{1,0:T(8,128)} fusion(bf16[1024,1024]{1,0:T(8,128)(2,1)} %copy-done.12, bf16[1024,2048]{1,0:T(8,128)(2,1)} %all-gather.3.cloned.1.call-done), kind=kOutput, calls=%fused_computation.163 | convolution fusion | flops 4294967296 | bytes 14680064 | tf_op jit(solution)/shard_map/dot_general | solution.py:25
  485.5 14.3 %multiply_convert_fusion.1 = (bf16[1024,2048]{1,0:T(8,128)(2,1)}, bf16[1024,2048]{1,0:T(8,128)(2,1)}) fusion(f32[1024,2048]{1,0:T(8,128)} %copy-done.52, f32[1024,2048]{1,0:T(8,128)} %get-tuple-element.174, f32[1024,2048]{1,0:T(8,128)} %fusion.48, bf16[1024,1024]{1,0:T(8,128)(2,1)S(1)} %constant_dynamic-update-slice_fusion.4, ...), kind=kOutput, calls=%fused_computation.1 | convolution fusion | flops 4324327424 | bytes 39845888 | tf_op jit(solution)/shard_map/dot_general | solution.py:25
  499.8 7.8 fusion.4
  507.6 7.4 add_convert_fusion.1
  515.1 7.1 fusion
  522.3 5.7 add_convert_fusion
  528.0 11.8 %convolution_convert_fusion.1 = bf16[2048,2048]{1,0:T(8,128)(2,1)} fusion(bf16[1024,2048]{1,0:T(8,128)(2,1)S(1)} %copy-done.54, bf16[1024,2048]{1,0:T(8,128)(2,1)S(1)} %copy-done.50), kind=kOutput, calls=%fused_computation.5 | convolution fusion | flops 8594128896 | bytes 16777216 | tf_op jit(solution)/shard_map/dot_general | solution.py:25
  547.4 8.5 %collective-permute-done.12 = bf16[256,1024]{1,0:T(8,128)(2,1)S(1)} collective-permute-done((bf16[256,1024]{1,0:T(8,128)(2,1)S(1)}, bf16[256,1024]{1,0:T(8,128)(2,1)S(1)}, u32[]{:S(2)}, u32[]{:S(2)}) %collective-permute-start.12) | collective-permute-done | bytes 524320 | tf_op jit(solution)/shard_map/ppermute | solution.py:30
  556.5 10.7 %collective-permute-done.13 = bf16[256,1024]{1,0:T(8,128)(2,1)S(1)} collective-permute-done((bf16[256,1024]{1,0:T(8,128)(2,1)S(1)}, bf16[256,1024]{1,0:T(8,128)(2,1)S(1)}, u32[]{:S(2)}, u32[]{:S(2)}) %collective-permute-start.13) | collective-permute-done | bytes 524320 | tf_op jit(solution)/shard_map/ppermute | solution.py:30
  568.6 9.8 %collective-permute-done.15 = bf16[256,1024]{1,0:T(8,128)(2,1)S(1)} collective-permute-done((bf16[256,1024]{1,0:T(8,128)(2,1)S(1)}, bf16[256,1024]{1,0:T(8,128)(2,1)S(1)}, u32[]{:S(2)}, u32[]{:S(2)}) %collective-permute-start.15) | collective-permute-done | bytes 524320 | tf_op jit(solution)/shard_map/ppermute | solution.py:30
  578.4 6.9 collective-permute-done.16
  591.5 11.6 %convolution_convert_fusion = bf16[2048,2048]{1,0:T(8,128)(2,1)} fusion(bf16[1024,2048]{1,0:T(8,128)(2,1)S(1)} %copy-done.55, bf16[1024,2048]{1,0:T(8,128)(2,1)S(1)} %copy-done.51), kind=kOutput, calls=%fused_computation.4 | convolution fusion | flops 8594128896 | bytes 16777216 | tf_op jit(solution)/shard_map/dot_general | solution.py:25
  612.7 16.7 %collective-permute-done.18 = bf16[256,2048]{1,0:T(8,128)(2,1)} collective-permute-done((bf16[256,2048]{1,0:T(8,128)(2,1)S(1)}, bf16[256,2048]{1,0:T(8,128)(2,1)}, u32[]{:S(2)}, u32[]{:S(2)}) %collective-permute-start.18) | collective-permute-done | bytes 1048608 | tf_op jit(solution)/shard_map/ppermute | solution.py:30
  631.4 20.6 %collective-permute-done.19 = bf16[256,2048]{1,0:T(8,128)(2,1)} collective-permute-done((bf16[256,2048]{1,0:T(8,128)(2,1)S(1)}, bf16[256,2048]{1,0:T(8,128)(2,1)}, u32[]{:S(2)}, u32[]{:S(2)}) %collective-permute-start.19) | collective-permute-done | bytes 1048608 | tf_op jit(solution)/shard_map/ppermute | solution.py:30
  655.7 3.3 convolution_convert_fusion.5.grad_ref
  659.0 16.6 %shard_map.247 = (f32[1024,512]{1,0:T(8,128)}, f32[1024,512]{1,0:T(8,128)}, bf16[1024,512]{1,0:T(8,128)(2,1)}, f32[1024,128]{1,0:T(8,128)}, f32[1024,128]{1,0:T(8,128)}, /*index=5*/f32[2,512]{1,0:T(2,128)}) custom-call(bf16[1024,512]{1,0:T(8,128)(2,1)} %get-tuple-element.72.query_ref, bf16[1024,512]{1,0:T(8,128)(2,1)} %get-tuple-element.73.key_ref, ...), custom_call_target="tpu_custom_call" | custom-call | flops 5368709120 | bytes 15728640 | tf_op jit(solution)/shard_map/pallas_call | solution.py:314
  682.7 3.2 pad_maximum_fusion.1
  685.9 2.9 reshape.185
  688.8 3.2 fusion.9
  708.0 2.8 multiply_convert_fusion.4
  711.9 3.8 convolution_convert_fusion.4
  721.3 3.7 collective-permute-done.26
  725.2 97.8 %shard_map.248 = (f32[64,2048]{1,0:T(8,128)}, f32[64,2048]{1,0:T(8,128)}, f32[64,2048]{1,0:T(8,128)}, f32[64,2048]{1,0:T(8,128)}, bf16[256,2048]{1,0:T(8,128)(2,...) custom-call(bf16[1024,2048]{1,0:T(8,128)(2,1)} %get-tuple-element.100.tokens_hbm, ...), custom_call_target="tpu_custom_call" | custom-call | flops 12884901888 | bytes 104857600 | tf_op jit(solution)/shard_map/pallas_call | solution.py:655
  (296 shorter events, 111.4 us)
Async XLA Ops:
  7.2 317.8 %all-gather.5.cloned.1.call-start = ((), (), s32[]{:S(2)}) async-start(), calls=%async_computation.5 | async-start | bytes 4718592 | tf_op jit(solution)/shard_map/all_gather | solution.py:1219
  26.4 242.5 %copy-start = (bf16[1,256,2048]{2,1,0:T(8,128)(2,1)S(1)}, bf16[1,256,2048]{2,1,0:T(8,128)(2,1)}, u32[]{:S(2)}) copy-start(bf16[1,256,2048]{2,1,0:T(8,128)(2,1)} %param.16) | copy-start | bytes 3145732
  268.1 105.0 %all-gather.3.cloned.1.call-start = ((), (), s32[]{:S(2)}) async-start(), calls=%async_computation.4 | async-start | bytes 4718592 | tf_op jit(solution)/shard_map/all_gather | solution.py:1219
  268.8 334.3 %reduce-scatter.7.cloned.1.call-start = ((), (), s32[]{:S(2)}) async-start(), calls=%async_computation.7 | async-start | bytes 4718592 | tf_op jit(solution)/shard_map/reduce_scatter | solution.py:1222
  274.4 16.6 %slice-start.2 = ((s8[8388608]{0:T(1024)(128)(4,1)}), s8[4194304]{0:T(1024)(128)(4,1)S(1)}, s32[]{:S(2)}) async-start(s8[8388608]{0:T(1024)(128)(4,1)} %bitcast.181), calls=%async_computation.12 | async-start | bytes 8388608
  328.9 58.4 %collective-permute-start.3 = (bf16[256,1024]{1,0:T(8,128)(2,1)S(1)}, bf16[256,1024]{1,0:T(8,128)(2,1)S(1)}, u32[]{:S(2)}, u32[]{:S(2)}) collective-permute-start(bf16[256,1024]{1,0:T(8,128)(2,1)S(1)} %convolution_convert_fusion.8), channel_id=1, source_target_pairs={{0,3},{1,2},{2,1},{3,0},{4,7},{5,6},{6,5},{7,4},{8,11},{9,10},{10,... | collective-permute-start | bytes 1572872 | tf_op jit(solution)/shard_map/ppermute | solution.py:30
  334.8 61.7 %collective-permute-start.4 = (bf16[256,1024]{1,0:T(8,128)(2,1)}, bf16[256,1024]{1,0:T(8,128)(2,1)}, u32[]{:S(2)}, u32[]{:S(2)}) collective-permute-start(bf16[256,1024]{1,0:T(8,128)(2,1)} %convolution_convert_fusion.7), channel_id=1, source_target_pairs={{0,2},{1,3},{2,0},{3,1},{4,6},{5,7},{6,4},{7,5},{8,10},{9,11},{10,... | collective-permute-start | bytes 1572872 | tf_op jit(solution)/shard_map/ppermute | solution.py:30
  338.5 57.9 %collective-permute-start.5 = (bf16[256,1024]{1,0:T(8,128)(2,1)}, bf16[256,1024]{1,0:T(8,128)(2,1)}, u32[]{:S(2)}, u32[]{:S(2)}) collective-permute-start(bf16[256,1024]{1,0:T(8,128)(2,1)} %convolution_convert_fusion.6), channel_id=1, source_target_pairs={{0,1},{1,0},{2,3},{3,2},{4,5},{5,4},{6,7},{7,6},{8,9},{9,8},{10,11... | collective-permute-start | bytes 1572872 | tf_op jit(solution)/shard_map/ppermute | solution.py:30
  377.8 23.3 %collective-permute-start = (bf16[256,1024]{1,0:T(8,128)(2,1)}, bf16[256,1024]{1,0:T(8,128)(2,1)}, u32[]{:S(2)}, u32[]{:S(2)}) collective-permute-start(bf16[256,1024]{1,0:T(8,128)(2,1)} %convolution_convert_fusion.11), channel_id=1, source_target_pairs={{0,3},{1,2},{2,1},{3,0},{4,7},{5,6},{6,5},{7,4},{8,11},{9,10},{10,... | collective-permute-start | bytes 1572872 | tf_op jit(solution)/shard_map/ppermute | solution.py:30
  383.5 20.8 %collective-permute-start.1 = (bf16[256,1024]{1,0:T(8,128)(2,1)}, bf16[256,1024]{1,0:T(8,128)(2,1)}, u32[]{:S(2)}, u32[]{:S(2)}) collective-permute-start(bf16[256,1024]{1,0:T(8,128)(2,1)} %convolution_convert_fusion.10), channel_id=1, source_target_pairs={{0,2},{1,3},{2,0},{3,1},{4,6},{5,7},{6,4},{7,5},{8,10},{9,11},{10,... | collective-permute-start | bytes 1572872 | tf_op jit(solution)/shard_map/ppermute | solution.py:30
  387.4 17.0 %collective-permute-start.2 = (bf16[256,1024]{1,0:T(8,128)(2,1)}, bf16[256,1024]{1,0:T(8,128)(2,1)}, u32[]{:S(2)}, u32[]{:S(2)}) collective-permute-start(bf16[256,1024]{1,0:T(8,128)(2,1)} %convolution_convert_fusion.9), channel_id=1, source_target_pairs={{0,1},{1,0},{2,3},{3,2},{4,5},{5,4},{6,7},{7,6},{8,9},{9,8},{10,11... | collective-permute-start | bytes 1572872 | tf_op jit(solution)/shard_map/ppermute | solution.py:30
  408.6 14.8 %collective-permute-start.9 = (bf16[256,1024]{1,0:T(8,128)(2,1)S(1)}, bf16[256,1024]{1,0:T(8,128)(2,1)S(1)}, u32[]{:S(2)}, u32[]{:S(2)}) collective-permute-start(bf16[256,1024]{1,0:T(8,128)(2,1)S(1)} %get-tuple-element.168), channel_id=1, source_target_pairs={{0,1},{1,0},{2,3},{3,2},{4,5},{5,4},{6,7},{7,6},{8,9},{9,8},{10,11... | collective-permute-start | bytes 1572872 | tf_op jit(solution)/shard_map/ppermute | solution.py:30
  410.1 24.8 %collective-permute-start.10 = (bf16[256,1024]{1,0:T(8,128)(2,1)S(1)}, bf16[256,1024]{1,0:T(8,128)(2,1)S(1)}, u32[]{:S(2)}, u32[]{:S(2)}) collective-permute-start(bf16[256,1024]{1,0:T(8,128)(2,1)S(1)} %get-tuple-element.168), channel_id=1, source_target_pairs={{0,2},{1,3},{2,0},{3,1},{4,6},{5,7},{6,4},{7,5},{8,10},{9,11},{10,... | collective-permute-start | bytes 1572872 | tf_op jit(solution)/shard_map/ppermute | solution.py:30
  411.5 23.4 %collective-permute-start.11 = (bf16[256,1024]{1,0:T(8,128)(2,1)S(1)}, bf16[256,1024]{1,0:T(8,128)(2,1)S(1)}, u32[]{:S(2)}, u32[]{:S(2)}) collective-permute-start(bf16[256,1024]{1,0:T(8,128)(2,1)S(1)} %get-tuple-element.168), channel_id=1, source_target_pairs={{0,3},{1,2},{2,1},{3,0},{4,7},{5,6},{6,5},{7,4},{8,11},{9,10},{10,... | collective-permute-start | bytes 1572872 | tf_op jit(solution)/shard_map/ppermute | solution.py:30
  441.3 161.9 %reduce-scatter.5.cloned.1.call-start = ((), (), s32[]{:S(2)}) async-start(), calls=%async_computation.6 | async-start | bytes 4718592 | tf_op jit(solution)/shard_map/reduce_scatter | solution.py:1222
  441.3 25.5 %copy-start.16 = (bf16[256,1024]{1,0:T(8,128)(2,1)S(1)}, bf16[256,1024]{1,0:T(8,128)(2,1)}, u32[]{:S(2)}) copy-start(bf16[256,1024]{1,0:T(8,128)(2,1)} %get-tuple-element.169) | copy-start | bytes 1572868
  441.3 26.9 %copy-start.47 = (bf16[1024,2048]{1,0:T(8,128)(2,1)S(1)}, bf16[1024,2048]{1,0:T(8,128)(2,1)}, u32[]{:S(2)}) copy-start(bf16[1024,2048]{1,0:T(8,128)(2,1)} %get-tuple-element.173) | copy-start | bytes 12582916
  441.3 15.1 %collective-permute-start.6 = (bf16[256,1024]{1,0:T(8,128)(2,1)}, bf16[256,1024]{1,0:T(8,128)(2,1)S(1)}, u32[]{:S(2)}, u32[]{:S(2)}) collective-permute-start(bf16[256,1024]{1,0:T(8,128)(2,1)} %get-tuple-element.169), channel_id=1, source_target_pairs={{0,1},{1,0},{2,3},{3,2},{4,5},{5,4},{6,7},{7,6},{8,9},{9,8},{10,11... | collective-permute-start | bytes 1572872 | tf_op jit(solution)/shard_map/ppermute | solution.py:30
  442.5 24.2 %collective-permute-start.7 = (bf16[256,1024]{1,0:T(8,128)(2,1)}, bf16[256,1024]{1,0:T(8,128)(2,1)S(1)}, u32[]{:S(2)}, u32[]{:S(2)}) collective-permute-start(bf16[256,1024]{1,0:T(8,128)(2,1)} %get-tuple-element.169), channel_id=1, source_target_pairs={{0,2},{1,3},{2,0},{3,1},{4,6},{5,7},{6,4},{7,5},{8,10},{9,11},{10,... | collective-permute-start | bytes 1572872 | tf_op jit(solution)/shard_map/ppermute | solution.py:30
  443.4 23.3 %collective-permute-start.8 = (bf16[256,1024]{1,0:T(8,128)(2,1)}, bf16[256,1024]{1,0:T(8,128)(2,1)S(1)}, u32[]{:S(2)}, u32[]{:S(2)}) collective-permute-start(bf16[256,1024]{1,0:T(8,128)(2,1)} %get-tuple-element.169), channel_id=1, source_target_pairs={{0,3},{1,2},{2,1},{3,0},{4,7},{5,6},{6,5},{7,4},{8,11},{9,10},{10,... | collective-permute-start | bytes 1572872 | tf_op jit(solution)/shard_map/ppermute | solution.py:30
  474.6 184.5 %reduce-scatter.9.cloned.1.call-start = ((), (), s32[]{:S(2)}) async-start(), calls=%async_computation.8 | async-start | bytes 9437184 | tf_op jit(solution)/shard_map/reduce_scatter | solution.py:1222
  499.8 22.5 %slice-start = ((s8[8388608]{0:T(1024)(128)(4,1)}), s8[4194304]{0:T(1024)(128)(4,1)S(1)}, s32[]{:S(2)}) async-start(s8[8388608]{0:T(1024)(128)(4,1)} %bitcast.179), calls=%async_computation.10 | async-start | bytes 8388608
  515.1 24.9 %copy-start.19 = (bf16[1024,1024]{1,0:T(8,128)(2,1)}, bf16[1024,1024]{1,0:T(8,128)(2,1)S(1)}, u32[]{:S(2)}) copy-start(bf16[1024,1024]{1,0:T(8,128)(2,1)S(1)} %add_convert_fusion.1) | copy-start | bytes 6291460
  539.9 185.3 %reduce-scatter.11.cloned.1.call-start = ((), (), s32[]{:S(2)}) async-start(), calls=%async_computation.9 | async-start | bytes 9437184 | tf_op jit(solution)/shard_map/reduce_scatter | solution.py:1222
  540.1 15.8 %collective-permute-start.12 = (bf16[256,1024]{1,0:T(8,128)(2,1)S(1)}, bf16[256,1024]{1,0:T(8,128)(2,1)S(1)}, u32[]{:S(2)}, u32[]{:S(2)}) collective-permute-start(bf16[256,1024]{1,0:T(8,128)(2,1)S(1)} %get-tuple-element.139), channel_id=1, source_target_pairs={{0,3},{1,2},{2,1},{3,0},{4,7},{5,6},{6,5},{7,4},{8,11},{9,10},{10,... | collective-permute-start | bytes 1572872 | tf_op jit(solution)/shard_map/ppermute | solution.py:30
  541.2 26.0 %collective-permute-start.13 = (bf16[256,1024]{1,0:T(8,128)(2,1)S(1)}, bf16[256,1024]{1,0:T(8,128)(2,1)S(1)}, u32[]{:S(2)}, u32[]{:S(2)}) collective-permute-start(bf16[256,1024]{1,0:T(8,128)(2,1)S(1)} %get-tuple-element.141), channel_id=1, source_target_pairs={{0,2},{1,3},{2,0},{3,1},{4,6},{5,7},{6,4},{7,5},{8,10},{9,11},{10,... | collective-permute-start | bytes 1572872 | tf_op jit(solution)/shard_map/ppermute | solution.py:30
  542.1 44.7 %copy-start.1 = (bf16[1,256,2048]{2,1,0:T(8,128)(2,1)S(1)}, bf16[1,256,2048]{2,1,0:T(8,128)(2,1)}, u32[]{:S(2)}) copy-start(bf16[1,256,2048]{2,1,0:T(8,128)(2,1)} %param.16) | copy-start | bytes 3145732
  542.1 44.7 %copy-start.3 = (f32[256,2048]{1,0:T(8,128)S(1)}, f32[256,2048]{1,0:T(8,128)}, u32[]{:S(2)}) copy-start(f32[256,2048]{1,0:T(8,128)} %get-tuple-element.87) | copy-start | bytes 6291460
  542.1 44.7 %copy-start.31 = (f32[1,2048]{1,0:T(1,128)S(1)}, f32[1,2048]{1,0:T(1,128)}, u32[]{:S(2)}) copy-start(f32[1,2048]{1,0:T(1,128)} %get-tuple-element.154) | copy-start | bytes 24580
  542.1 25.1 %collective-permute-start.14 = (bf16[256,1024]{1,0:T(8,128)(2,1)S(1)}, bf16[256,1024]{1,0:T(8,128)(2,1)S(1)}, u32[]{:S(2)}, u32[]{:S(2)}) collective-permute-start(bf16[256,1024]{1,0:T(8,128)(2,1)S(1)} %get-tuple-element.140), channel_id=1, source_target_pairs={{0,1},{1,0},{2,3},{3,2},{4,5},{5,4},{6,7},{7,6},{8,9},{9,8},{10,11... | collective-permute-start | bytes 1572872 | tf_op jit(solution)/shard_map/ppermute | solution.py:30
  545.1 33.3 %collective-permute-start.15 = (bf16[256,1024]{1,0:T(8,128)(2,1)S(1)}, bf16[256,1024]{1,0:T(8,128)(2,1)S(1)}, u32[]{:S(2)}, u32[]{:S(2)}) collective-permute-start(bf16[256,1024]{1,0:T(8,128)(2,1)S(1)} %get-tuple-element.142), channel_id=1, source_target_pairs={{0,3},{1,2},{2,1},{3,0},{4,7},{5,6},{6,5},{7,4},{8,11},{9,10},{10,... | collective-permute-start | bytes 1572872 | tf_op jit(solution)/shard_map/ppermute | solution.py:30
  546.3 39.1 %collective-permute-start.16 = (bf16[256,1024]{1,0:T(8,128)(2,1)S(1)}, bf16[256,1024]{1,0:T(8,128)(2,1)S(1)}, u32[]{:S(2)}, u32[]{:S(2)}) collective-permute-start(bf16[256,1024]{1,0:T(8,128)(2,1)S(1)} %get-tuple-element.144), channel_id=1, source_target_pairs={{0,2},{1,3},{2,0},{3,1},{4,6},{5,7},{6,4},{7,5},{8,10},{9,11},{10,... | collective-permute-start | bytes 1572872 | tf_op jit(solution)/shard_map/ppermute | solution.py:30
  555.9 29.5 %collective-permute-start.17 = (bf16[256,1024]{1,0:T(8,128)(2,1)S(1)}, bf16[256,1024]{1,0:T(8,128)(2,1)S(1)}, u32[]{:S(2)}, u32[]{:S(2)}) collective-permute-start(bf16[256,1024]{1,0:T(8,128)(2,1)S(1)} %get-tuple-element.143), channel_id=1, source_target_pairs={{0,1},{1,0},{2,3},{3,2},{4,5},{5,4},{6,7},{7,6},{8,9},{9,8},{10,11... | collective-permute-start | bytes 1572872 | tf_op jit(solution)/shard_map/ppermute | solution.py:30
  603.2 26.2 %collective-permute-start.18 = (bf16[256,2048]{1,0:T(8,128)(2,1)S(1)}, bf16[256,2048]{1,0:T(8,128)(2,1)}, u32[]{:S(2)}, u32[]{:S(2)}) collective-permute-start(bf16[256,2048]{1,0:T(8,128)(2,1)S(1)} %multiply_convert_fusion.5), channel_id=1, source_target_pairs={{0,1},{1,0},{2,3},{3,2},{4,5},{5,4},{6,7},{7,6},{8,9},{9,8},{10,11... | collective-permute-start | bytes 3145736 | tf_op jit(solution)/shard_map/ppermute | solution.py:30
  605.0 47.0 %collective-permute-start.19 = (bf16[256,2048]{1,0:T(8,128)(2,1)S(1)}, bf16[256,2048]{1,0:T(8,128)(2,1)}, u32[]{:S(2)}, u32[]{:S(2)}) collective-permute-start(bf16[256,2048]{1,0:T(8,128)(2,1)S(1)} %multiply_convert_fusion.5), channel_id=1, source_target_pairs={{0,2},{1,3},{2,0},{3,1},{4,6},{5,7},{6,4},{7,5},{8,10},{9,11},{10,... | collective-permute-start | bytes 3145736 | tf_op jit(solution)/shard_map/ppermute | solution.py:30
  608.0 45.3 %collective-permute-start.20 = (bf16[256,2048]{1,0:T(8,128)(2,1)S(1)}, bf16[256,2048]{1,0:T(8,128)(2,1)S(1)}, u32[]{:S(2)}, u32[]{:S(2)}) collective-permute-start(bf16[256,2048]{1,0:T(8,128)(2,1)S(1)} %multiply_convert_fusion.5), channel_id=1, source_target_pairs={{0,3},{1,2},{2,1},{3,0},{4,7},{5,6},{6,5},{7,4},{8,11},{9,10},{10,... | collective-permute-start | bytes 3145736 | tf_op jit(solution)/shard_map/ppermute | solution.py:30
  629.9 25.8 %copy-start.49 = (bf16[512,2048]{1,0:T(8,128)(2,1)S(1)}, bf16[512,2048]{1,0:T(8,128)(2,1)}, u32[]{:S(2)}) copy-start(bf16[512,2048]{1,0:T(8,128)(2,1)} %get-tuple-element.91) | copy-start | bytes 6291460
  659.0 23.2 %copy-start.5 = (f32[256,1024]{1,0:T(8,128)S(1)}, f32[256,1024]{1,0:T(8,128)}, u32[]{:S(2)}) copy-start(f32[256,1024]{1,0:T(8,128)} %copy-done.4) | copy-start | bytes 3145732
  678.8 20.9 %collective-permute-start.21 = (f32[2,1024]{1,0:T(2,128)}, f32[2,1024]{1,0:T(2,128)}, u32[]{:S(2)}, u32[]{:S(2)}) collective-permute-start(f32[2,1024]{1,0:T(2,128)} %pad_maximum_fusion.6), channel_id=1, source_target_pairs={{0,1},{1,0},{2,3},{3,2},{4,5},{5,4},{6,7},{7,6},{8,9},{9,8},{10,11... | collective-permute-start | bytes 24584 | tf_op jit(solution)/shard_map/ppermute | solution.py:30
  679.3 21.7 %collective-permute-start.22 = (f32[2,1024]{1,0:T(2,128)}, f32[2,1024]{1,0:T(2,128)}, u32[]{:S(2)}, u32[]{:S(2)}) collective-permute-start(f32[2,1024]{1,0:T(2,128)} %pad_maximum_fusion.6), channel_id=1, source_target_pairs={{0,2},{1,3},{2,0},{3,1},{4,6},{5,7},{6,4},{7,5},{8,10},{9,11},{10,... | collective-permute-start | bytes 24584 | tf_op jit(solution)/shard_map/ppermute | solution.py:30
  680.8 21.0 %collective-permute-start.23 = (f32[2,1024]{1,0:T(2,128)}, f32[2,1024]{1,0:T(2,128)}, u32[]{:S(2)}, u32[]{:S(2)}) collective-permute-start(f32[2,1024]{1,0:T(2,128)} %pad_maximum_fusion.6), channel_id=1, source_target_pairs={{0,3},{1,2},{2,1},{3,0},{4,7},{5,6},{6,5},{7,4},{8,11},{9,10},{10,... | collective-permute-start | bytes 24584 | tf_op jit(solution)/shard_map/ppermute | solution.py:30
  694.2 23.5 %collective-permute-start.27 = (bf16[64,2048]{1,0:T(8,128)(2,1)}, bf16[64,2048]{1,0:T(8,128)(2,1)}, u32[]{:S(2)}, u32[]{:S(2)}) collective-permute-start(bf16[64,2048]{1,0:T(8,128)(2,1)} %get-tuple-element.147), channel_id=1, source_target_pairs={{0,1},{1,0},{2,3},{3,2},{4,5},{5,4},{6,7},{7,6},{8,9},{9,8},{10,11... | collective-permute-start | bytes 786440 | tf_op jit(solution)/shard_map/ppermute | solution.py:30
  694.9 25.3 %collective-permute-start.28 = (bf16[64,2048]{1,0:T(8,128)(2,1)}, bf16[64,2048]{1,0:T(8,128)(2,1)}, u32[]{:S(2)}, u32[]{:S(2)}) collective-permute-start(bf16[64,2048]{1,0:T(8,128)(2,1)} %get-tuple-element.146), channel_id=1, source_target_pairs={{0,2},{1,3},{2,0},{3,1},{4,6},{5,7},{6,4},{7,5},{8,10},{9,11},{10,... | collective-permute-start | bytes 786440 | tf_op jit(solution)/shard_map/ppermute | solution.py:30
  699.7 21.6 %collective-permute-start.29 = (bf16[64,2048]{1,0:T(8,128)(2,1)S(1)}, bf16[64,2048]{1,0:T(8,128)(2,1)S(1)}, u32[]{:S(2)}, u32[]{:S(2)}) collective-permute-start(bf16[64,2048]{1,0:T(8,128)(2,1)S(1)} %get-tuple-element.145), channel_id=1, source_target_pairs={{0,3},{1,2},{2,1},{3,0},{4,7},{5,6},{6,5},{7,4},{8,11},{9,10},{10,... | collective-permute-start | bytes 786440 | tf_op jit(solution)/shard_map/ppermute | solution.py:30
  701.1 19.1 %collective-permute-start.24 = (bf16[64,2048]{1,0:T(8,128)(2,1)}, bf16[64,2048]{1,0:T(8,128)(2,1)S(1)}, u32[]{:S(2)}, u32[]{:S(2)}) collective-permute-start(bf16[64,2048]{1,0:T(8,128)(2,1)} %get-tuple-element.150), channel_id=1, source_target_pairs={{0,1},{1,0},{2,3},{3,2},{4,5},{5,4},{6,7},{7,6},{8,9},{9,8},{10,11... | collective-permute-start | bytes 786440 | tf_op jit(solution)/shard_map/ppermute | solution.py:30
  701.8 19.4 %collective-permute-start.25 = (bf16[64,2048]{1,0:T(8,128)(2,1)}, bf16[64,2048]{1,0:T(8,128)(2,1)S(1)}, u32[]{:S(2)}, u32[]{:S(2)}) collective-permute-start(bf16[64,2048]{1,0:T(8,128)(2,1)} %get-tuple-element.149), channel_id=1, source_target_pairs={{0,2},{1,3},{2,0},{3,1},{4,6},{5,7},{6,4},{7,5},{8,10},{9,11},{10,... | collective-permute-start | bytes 786440 | tf_op jit(solution)/shard_map/ppermute | solution.py:30
  717.7 7.3 collective-permute-start.26
  725.1 97.8 %copy-start.11 = (f32[64,8192]{1,0:T(8,128)}, f32[64,8192]{1,0:T(8,128)S(1)}, u32[]{:S(2)}) copy-start(f32[64,8192]{1,0:T(8,128)S(1)} %convert_dynamic-update-slice_fusion.4) | copy-start | bytes 6291460
  (50 other events, 291.1 us)
Sparse Core Ops, SparseCore 0:
  268.2 56.7 all-gather.4
  327.2 45.8 all-gather.2
  441.4 47.8 reduce-scatter.6
  491.4 48.1 reduce-scatter.4
  541.7 87.7 reduce-scatter.8
  631.7 87.9 reduce-scatter.10

commit v4 on v3

--- a/solution.py
+++ b/solution.py
@@ -574,17 +574,6 @@
     for i in range(4):
         landed(side_in.at[i], core_recv_sem.at[1, i])
         side_mine[i] = (side[2 * blocks[i] + core].astype(f32) + side_in[i].astype(f32)).astype(bf16)
-        if i < 2:
-            copy = line_copy(side_mine.at[i], side_line_in, 1, i)
-            copy.start()
-            sent.append(copy)
-        if i == 2:
-            side_last = line_copy(side_mine.at[2], side_line_in, 1, 2)
-            sent.append(side_last)
-
-            @pl.when(inner == 0)
-            def _():
-                side_last.start()
 
     loads[3].wait()
 
@@ -592,16 +581,39 @@
         hidden[:, columns] += values
 
     tokens_part(0, own_store)
-
-    def total(kind, came, kept):
-        landed(came.at[2], line_recv_sem.at[kind, 2])
-        kept[3] = (kept[3].astype(f32) + came[2].astype(f32)).astype(bf16)
+    gains_out[...] = gains[leaf]
+    for step in range(1, 8):
+        landed(gains_line.at[step - 1], leaf_recv_sem.at[step - 1])
+        gains_out[...] += gains_line[step - 1]
+
+    def near(kind, came, kept):
         for slot in range(2):
 
             @pl.when(inner + (1 - far) * slot + far * (1 - slot) > 0)
             def _():
                 landed(came.at[slot], line_recv_sem.at[kind, slot])
                 kept[3] = (kept[3].astype(f32) + came[slot].astype(f32)).astype(bf16)
+
+    def beyond(kind, came, kept):
+        landed(came.at[2], line_recv_sem.at[kind, 2])
+        kept[3] = (kept[3].astype(f32) + came[2].astype(f32)).astype(bf16)
+
+    near(0, line_in, mine)
+    for i in range(2):
+        copy = line_copy(side_mine.at[i], side_line_in, 1, i)
+        copy.start()
+        sent.append(copy)
+    side_last = line_copy(side_mine.at[2], side_line_in, 1, 2)
+    sent.append(side_last)
+
+    @pl.when(inner == 0)
+    def _():
+        side_last.start()
+
+    beyond(0, line_in, mine)
+    rows_send[...] = mine[3]
+    for hop in hops:
+        row_copy(rows_send.at[pl.ds(other(row, hop) * own, own)], rows_in.at[hop - 1], 3, hop)
 
     @pl.when(inner == 1)
     def _():
@@ -620,23 +632,14 @@
     for source in range(4):
         up_out[:, source * up_in.shape[2] : (source + 1) * up_in.shape[2]] = up_in[source].astype(f32)
 
-    gains_out[...] = gains[leaf]
-    for step in range(1, 8):
-        landed(gains_line.at[step - 1], leaf_recv_sem.at[step - 1])
-        gains_out[...] += gains_line[step - 1]
-
-    total(0, line_in, mine)
-    rows_send[...] = mine[3]
-    for hop in hops:
-        row_copy(rows_send.at[pl.ds((other(row, hop)) * own, own)], rows_in.at[hop - 1], 3, hop)
-
     def give(source, values):
         columns = pl.ds(pl.multiple_of(source * part, part), part)
         for i, out in enumerate((query_out, key_out, value_out)):
             out[:, columns] = values[:, i * part : (i + 1) * part].astype(f32)
 
     give(row, rows_send[pl.ds(pl.multiple_of(row * own, own), own), :])
-    total(1, side_line_in, side_mine)
+    near(1, side_line_in, side_mine)
+    beyond(1, side_line_in, side_mine)
     output_out[...] = side_mine[3].astype(f32)
     for hop in hops:
         landed(rows_in.at[hop - 1], row_recv_sem.at[3, hop - 1])
@@ -719,7 +722,11 @@
     attn_out,
     gate_out,
     up_out,
-    down_out,
+    first_out,
+    second_out,
+    gate_pre_out,
+    up_pre_out,
+    activated_out,
     tokens_out,
     query_pre_out,
     key_pre_out,
@@ -855,8 +862,10 @@
     for hop in hops:
         row_copy(down_hbm.at[:, lines(other(row, hop), units)], down_block.at[mine], 5, hop)
 
+    sizes = (size, size, size, size // 2, size // 2)
+
     def spread(kind, source, whole):
-        place = whole.at[lines(leaf, size)]
+        place = whole.at[lines(leaf, sizes[kind])]
         across = leaf_copy(
             source, place, line_send_sem.at[kind, 2], line_recv_sem.at[kind, 2], 2 * other(z, 2) + core
         )
@@ -896,7 +905,7 @@
 
     def pass_on(kind, whole, step):
         slot, chip = arrival(step)
-        place = whole.at[lines(2 * chip + core, size)]
+        place = whole.at[lines(2 * chip + core, sizes[kind])]
         landed(place, line_recv_sem.at[kind, slot])
         beside = leaf_copy(place, place, core_send_sem.at[kind, step], core_recv_sem.at[kind, step], 2 * z + 1 - core)
         beside.start()
@@ -916,10 +925,10 @@
             return done
 
     def gathered(kind, whole):
-        landed(whole.at[lines(2 * z + 1 - core, size)], core_recv_sem.at[kind, 3])
+        landed(whole.at[lines(2 * z + 1 - core, sizes[kind])], core_recv_sem.at[kind, 3])
         for step in range(3):
             chip = arrival(step)[1]
-            landed(whole.at[lines(2 * chip + 1 - core, size)], core_recv_sem.at[kind, step])
+            landed(whole.at[lines(2 * chip + 1 - core, sizes[kind])], core_recv_sem.at[kind, step])
 
     load_pack.wait()
     load_output.wait()
@@ -967,6 +976,7 @@
         row_copy(
             attn_mat.at[lines(other(row, hop), 2 * size), pl.ds(wide, part)], output_in.at[row], 6, hop
         )
+    swapped = len(sent)
     keep = load(attn_mat.at[lines(row, 2 * size), pl.ds(wide, part)], output_in.at[row], 10)
     load_up.wait()
     row_landed(lambda source, hop: up_block.at[lines(source, own)], 4)
@@ -1078,10 +1088,6 @@
     save(attn, unit_out)
     save(unit_scale, unit_scale_out)
     save(hidden, hidden_out)
-    load_down.wait()
-    row_landed(lambda source, hop: down_block.at[lines(source, own)], 5)
-    save(down_block, down_out)
-
     for hop in (1, 2):
         landed(hidden_all.at[lines(other(row, hop), rows)], row_recv_sem.at[9, hop - 1])
         place = hidden_all.at[lines(2 * other(row, hop) + hop - 1, half)]
@@ -1091,15 +1097,73 @@
     save(hidden_all, hidden_all_out)
     pass_on(1, gate_out, 2)
     pass_on(2, up_out, 1)
+    load_down.wait()
+    row_landed(lambda source, hop: down_block.at[lines(source, own)], 5)
+    downs = (first_out, second_out)
+    for h in range(2):
+        done.append(spread(3 + h, down_block.at[pl.ds(h * size // 2, size // 2)], downs[h]))
     pass_on(2, up_out, 2)
     gathered(1, gate_out)
     gathered(2, up_out)
 
-    for finish_sends in done:
+    for copy in sent[:swapped]:
+        copy.wait_send()
+    for finish_sends in done[:2]:
         finish_sends()
-    for copy in sent:
+    for copy in saved[1:]:
+        copy.wait()
+    saved.clear()
+
+    def quarter(j):
+        columns = pl.ds(j * part, part)
+        return [
+            load(source.at[:, columns], attn_mat.at[:, pl.ds((2 * i + j % 2) * part, part)], 11 + 2 * i + j % 2)
+            for i, source in enumerate((gate_out, up_out))
+        ]
+
+    coming = quarter(0)
+    for j in range(4):
+        for copy in coming:
+            copy.wait()
+        if j < 3:
+            coming = quarter(j + 1)
+        for copy in saved:
+            copy.wait()
+        saved.clear()
+
+        slot = j % 2
+
+        def units_step(i, carry):
+            at = lines(i, rows)
+            some = hidden_all[at, :]
+            gate = dot(some, attn_mat[:, slot * part : (slot + 1) * part], NN)
+            up = dot(some, attn_mat[:, (2 + slot) * part : (3 + slot) * part], NN)
+            query_pre[at, :] = gate
+            key_pre[at, :] = up
+            value[at, :] = (gate * jax.nn.sigmoid(gate) * up).astype(bf16)
+            return carry
+
+        lax.fori_loop(0, 4, units_step, 0)
+        columns = pl.ds(j * part, part)
+        save(query_pre, gate_pre_out.at[:, columns])
+        save(key_pre, up_pre_out.at[:, columns])
+        save(value, activated_out.at[:, columns])
+        if j == 1:
+            done.append(pass_on(3, first_out, 0))
+        if j == 2:
+            done.append(pass_on(4, second_out, 0))
+            pass_on(3, first_out, 1)
+    pass_on(3, first_out, 2)
+    pass_on(4, second_out, 1)
+    pass_on(4, second_out, 2)
+    gathered(3, first_out)
+    gathered(4, second_out)
+
+    for finish_sends in done[2:]:
+        finish_sends()
+    for copy in sent[swapped:]:
         copy.wait_send()
-    for copy in saved[1:]:
+    for copy in saved:
         copy.wait()
 
 
@@ -1113,7 +1177,11 @@
         shape((width, width), bf16),
         shape((width, units), bf16),
         shape((width, units), bf16),
-        shape((size, units), bf16),
+        shape((width // 2, units), bf16),
+        shape((width // 2, units), bf16),
+        shape((total, units), f32),
+        shape((total, units), f32),
+        shape((total, units), bf16),
         shape((total, width), bf16),
         shape((total, part), f32),
         shape((total, part), f32),
@@ -1169,16 +1237,16 @@
             vmem((4, 8, HEAD_DIM), f32),
             vmem((8, 4, 8, HEAD_DIM), f32),
             vmem((8, width), f32),
-            dma((11,)),
-            dma((24,)),
+            dma((15,)),
+            dma((32,)),
             dma((13, 3)),
             dma((13, 3)),
             dma((7,)),
             dma((7,)),
-            dma((3, 4)),
-            dma((3, 4)),
-            dma((3, 4)),
-            dma((3, 4)),
+            dma((5, 4)),
+            dma((5, 4)),
+            dma((5, 4)),
+            dma((5, 4)),
         ],
         compiler_params=pltpu.CompilerParams(
             collective_id=2, has_side_effects=True, vmem_limit_bytes=62 * 2**20
@@ -1233,7 +1301,11 @@
             attn_mat,
             gate_mat,
             up_mat,
-            down_block,
+            down_first,
+            down_second,
+            gate_pre,
+            up_pre,
+            activated,
             all_tokens,
             query_pre,
             key_pre,
@@ -1262,7 +1334,7 @@
             bias,
         )
         scales, attn_scale = scales[:2], attn_scale[:, :1]
-        down_halves = [leaf_gather(down_block[h * group : (h + 1) * group]) for h in range(2)]
+        down_halves = [down_first, down_second]
         query_scale, key_scale = scales[0][:, None], scales[1][:, None]
         attn_gain, mlp_gain = gains_all[2], gains_all[3]
         head_gains = lax.dynamic_slice_in_dim(gains_all[:2], me * part, part, 1)
@@ -1315,10 +1387,11 @@
         hidden = tokens.astype(f32) + attn_unit * attn_gain
         hidden_all = gather_rows(hidden.astype(bf16))
 
-    gate_pre = dot(hidden_all, gate_mat, NN)
-    up_pre = dot(hidden_all, up_mat, NN)
+    if not fast:
+        gate_pre = dot(hidden_all, gate_mat, NN)
+        up_pre = dot(hidden_all, up_mat, NN)
+        activated = (gate_pre * jax.nn.sigmoid(gate_pre) * up_pre).astype(bf16)
     sigmoid_gate = jax.nn.sigmoid(gate_pre)
-    activated = (gate_pre * sigmoid_gate * up_pre).astype(bf16)
     mlp_halves = [dot_scatter([activated], [down_halves[h]], NT) for h in range(2)]
     grad_final = cotangent.reshape(rows_dev, width).astype(f32)
     halves = range(2)
@@ -1342,17 +1415,17 @@
     grad_gate = (grad_act * up_pre * sigmoid_gate * (1.0 + gate_pre * (1.0 - sigmoid_gate))).astype(bf16)
     grad_up = (grad_act * gate_pre * sigmoid_gate).astype(bf16)
     wide = width // 2
+    gate_sum = dot(hidden_all, grad_gate, TN, bf16)
     parts, coming = [], []
     for h in range(2):
-        one = tie(grad_gate, *parts), tie(grad_up, *parts)
+        one = tie(grad_gate, gate_sum, *parts), tie(grad_up, gate_sum, *parts)
         part_h = sum(
             dot(left, right[h * wide : (h + 1) * wide], NT) for left, right in zip(one, (gate_mat, up_mat))
         ).astype(bf16)
         parts.append(part_h)
         coming.append(send_rows(part_h))
-    gate_sum = dot(hidden_all, tie(grad_gate, *parts), TN, bf16)
     grad_hidden = grad_final + jnp.concatenate(
-        [add_rows(part_h, pieces, gate_sum) for part_h, pieces in zip(parts, coming)], axis=1
+        [add_rows(part_h, pieces) for part_h, pieces in zip(parts, coming)], axis=1
     )
     gate_sum = tie(gate_sum, *down_sums)
     gate_shard = leaf_scatter(gate_sum)

time: 844 us -> 833 us (0.987)
  Pallas kernels: 354 us -> 419 us
  waiting for transfers between devices: 178 us -> 129 us
  matrix products: 152 us -> 132 us
    pallas_call x1, Pallas kernels: 239 us -> 306 us  [front(): pl.pallas_call(front_kernel, in_specs=[pl.BlockSpec(memory_space=pl.ANY)]...]
    all_gather x2 -> x0, waiting for transfers between devices: 53.4 us -> none  [leaf_gather(): return lax.all_gather(block, 'leaf', axis=0, tiled=True)]
    dot_general x22 -> x20, matrix products: 152 us -> 132 us  [dot(): lax.dot_general(left, right, dims, preferred_element_type=f32).astype(kind)]
    reduce_scatter x4, waiting for transfers between devices: 0.06 us -> 16.9 us  [leaf_scatter(): return lax.psum_scatter(block, 'leaf', scatter_dimension=0, tiled=True)]
    ppermute x30, waiting for transfers between devices: 124 us -> 112 us  [swap(): return lax.ppermute(piece, 'row', [(i, i ^ hop) for i in range(count)])]
    unnamed x134 -> x128, local copies, waits for them, and re-layouts: 21.8 us -> 20.9 us
  transfers between devices with their start and end apart: 36 -> 34, of which waited for: 16 -> 12; matrix products, arithmetic and copies ran while one was open for 24% -> 21% of each run, Pallas kernels for 2% -> 2%
where the time goes in v4:
time: 833 us; the launch traced here: 830 us
  Pallas kernels  419 us (50%)
  matrix products  132 us (16%)
  waiting for transfers between devices  129 us (15%)
  local copies, waits for them, and re-layouts  49.5 us (6%)
  other arithmetic  49.4 us (6%)
  starting transfers between devices  35.5 us (4%)
  between operations  15.1 us (2%)
    pallas_call x1, Pallas kernels, front(): pl.pallas_call(front_kernel, in_specs=[pl.BlockSpec(memory_space=pl.ANY)]...  306 us
    dot_general x20, matrix products, dot(): lax.dot_general(left, right, dims, preferred_element_type=f32).astype(kind)  132 us
    ppermute x30, waiting for transfers between devices, swap(): return lax.ppermute(piece, 'row', [(i, i ^ hop) for i in range(count)])  112 us
    pallas_call x1, Pallas kernels, finish(): pl.pallas_call(final_kernel, in_specs=[pl.BlockSpec(memory_space=pl.ANY)]...  95.3 us
    ppermute x30, starting transfers between devices, swap(): return lax.ppermute(piece, 'row', [(i, i ^ hop) for i in range(count)])  35.4 us
    unnamed x128, local copies, waits for them, and re-layouts  20.9 us
    reduce_scatter x4, waiting for transfers between devices, leaf_scatter(): return lax.psum_scatter(block, 'leaf', scatter_dimension=0, tiled=True)  16.9 us
    pallas_call x1, Pallas kernels, attend_back(): pl.pallas_call(functools.partial(attend_back_kernel, 256, 1.0 / math.sqrt...  16.8 us
  transfers between devices with their start and end apart: 34, of which 12 were waited for; matrix products, arithmetic and copies ran while one was open for 21% of the time, Pallas kernels for 2%

profile of v4, /device:TPU:0, one launch (start us, length us, event | category | flops | bytes accessed | tf_op | source)
XLA Modules:
  0.0 829.5 jit_solution(1089121571869637807)
XLA Ops:
  22.3 3.2 select_convert_fusion.bias_hbm.bias_ref
  28.2 306.3 %shard_map.246 = (bf16[2048,2048]{1,0:T(8,128)(2,1)}, bf16[2048,2048]{1,0:T(8,128)(2,1)}, bf16[2048,2048]{1,0:T(8,128)(2,1)}, bf16[1024,2048]{1,0:T(8,128)(2,1)}...) custom-call(bf16[256,2048]{1,0:T(8,128)(2,1)} %bitcast.173, ...), custom_call_target="tpu_custom_call" | custom-call | flops 10737418240 | bytes 104857600 | tf_op jit(solution)/shard_map/pallas_call | solution.py:1202
  334.6 4.6 convolution_convert_fusion.8
  339.2 4.6 convolution_convert_fusion.7
  344.5 4.7 convolution_convert_fusion.6
  349.2 2.8 collective-permute-start.5
  352.0 3.3 convolution_convert_fusion.11
  355.5 2.1 convolution_convert_fusion.10
  359.0 2.1 convolution_convert_fusion.9
  361.1 2.1 reshape.191
  365.4 6.8 slice_reduce_fusion
  374.8 4.7 multiply_reduce_fusion.4
  379.5 8.8 %collective-permute-done.1 = bf16[256,1024]{1,0:T(8,128)(2,1)} collective-permute-done((bf16[256,1024]{1,0:T(8,128)(2,1)}, bf16[256,1024]{1,0:T(8,128)(2,1)}, u32[]{:S(2)}, u32[]{:S(2)}) %collective-permute-start.1) | collective-permute-done | bytes 524320 | tf_op jit(solution)/shard_map/ppermute | solution.py:30
  388.3 3.3 multiply_reduce_fusion.5
  393.7 2.6 collective-permute-start.11
  396.4 11.3 %collective-permute-done.9 = bf16[256,1024]{1,0:T(8,128)(2,1)S(1)} collective-permute-done((bf16[256,1024]{1,0:T(8,128)(2,1)S(1)}, bf16[256,1024]{1,0:T(8,128)(2,1)S(1)}, u32[]{:S(2)}, u32[]{:S(2)}) %collective-permute-start.9) | collective-permute-done | bytes 524320 | tf_op jit(solution)/shard_map/ppermute | solution.py:30
  408.0 10.0 %collective-permute-done.10 = bf16[256,1024]{1,0:T(8,128)(2,1)S(1)} collective-permute-done((bf16[256,1024]{1,0:T(8,128)(2,1)S(1)}, bf16[256,1024]{1,0:T(8,128)(2,1)S(1)}, u32[]{:S(2)}, u32[]{:S(2)}) %collective-permute-start.10) | collective-permute-done | bytes 524320 | tf_op jit(solution)/shard_map/ppermute | solution.py:30
  419.5 6.3 convolution_convert_fusion.2
  430.4 11.4 %collective-permute-done.6 = bf16[256,1024]{1,0:T(8,128)(2,1)S(1)} collective-permute-done((bf16[256,1024]{1,0:T(8,128)(2,1)S(1)}, bf16[256,1024]{1,0:T(8,128)(2,1)S(1)}, u32[]{:S(2)}, u32[]{:S(2)}) %collective-permute-start.6) | collective-permute-done | bytes 524320 | tf_op jit(solution)/shard_map/ppermute | solution.py:30
  442.1 10.3 %collective-permute-done.7 = bf16[256,1024]{1,0:T(8,128)(2,1)S(1)} collective-permute-done((bf16[256,1024]{1,0:T(8,128)(2,1)S(1)}, bf16[256,1024]{1,0:T(8,128)(2,1)S(1)}, u32[]{:S(2)}, u32[]{:S(2)}) %collective-permute-start.7) | collective-permute-done | bytes 524320 | tf_op jit(solution)/shard_map/ppermute | solution.py:30
  453.8 6.7 convolution_convert_fusion.3
  460.6 10.8 %fusion.46 = f32[1024,2048]{1,0:T(8,128)} fusion(bf16[1024,1024]{1,0:T(8,128)(2,1)} %copy-done.14, bf16[1024,2048]{1,0:T(8,128)(2,1)} %get-tuple-element.72), kind=kOutput, calls=%fused_computation.160 | convolution fusion | flops 4294967296 | bytes 14680064 | tf_op jit(solution)/shard_map/dot_general | solution.py:25
  471.5 14.2 %multiply_convert_fusion.1 = (bf16[1024,2048]{1,0:T(8,128)(2,1)}, bf16[1024,2048]{1,0:T(8,128)(2,1)}) fusion(f32[1024,2048]{1,0:T(8,128)} %get-tuple-element.86, f32[1024,2048]{1,0:T(8,128)} %get-tuple-element.85, f32[1024,2048]{1,0:T(8,128)} %fusion.46, bf16[1024,1024]{1,0:T(8,128)(2,1)S(1)} %copy-done.13, bf16[1024,2048]{1,0:T(8,128)(2,1)S(1)} %copy-done.44), kind=kOutput, calls=%fused_computation.1 | convolution fusion | flops 4324327424 | bytes 39845888 | tf_op jit(solution)/shard_map/dot_general | solution.py:25
  485.6 14.0 %convolution_convert_fusion.1 = bf16[2048,2048]{1,0:T(8,128)(2,1)} fusion(bf16[1024,2048]{1,0:T(8,128)(2,1)} %get-tuple-element.80, bf16[1024,2048]{1,0:T(8,128)(2,1)} %get-tuple-element.91), kind=kOutput, calls=%fused_computation.4 | convolution fusion | flops 8594128896 | bytes 16777216 | tf_op jit(solution)/shard_map/dot_general | solution.py:25
  499.8 8.0 fusion.4
  507.8 7.4 add_convert_fusion.1
  518.9 9.1 %fusion = f32[1024,1024]{1,0:T(8,128)} fusion(bf16[1024,2048]{1,0:T(8,128)(2,1)} %get-tuple-element.95, bf16[2048,2048]{1,0:T(8,128)(2,1)S(1)} %bitcast.178), kind=kOutput, calls=%fused_computation.6 | convolution fusion | flops 4294967296 | bytes 12582912 | tf_op jit(solution)/shard_map/dot_general | solution.py:25
  528.1 7.7 add_convert_fusion
  537.5 2.0 collective-permute-start.17
  539.6 2.7 collective-permute-done.13
  542.6 10.9 %collective-permute-done.15 = bf16[256,1024]{1,0:T(8,128)(2,1)S(1)} collective-permute-done((bf16[256,1024]{1,0:T(8,128)(2,1)S(1)}, bf16[256,1024]{1,0:T(8,128)(2,1)S(1)}, u32[]{:S(2)}, u32[]{:S(2)}) %collective-permute-start.15) | collective-permute-done | bytes 524320 | tf_op jit(solution)/shard_map/ppermute | solution.py:30
  553.5 8.4 %collective-permute-done.16 = bf16[256,1024]{1,0:T(8,128)(2,1)S(1)} collective-permute-done((bf16[256,1024]{1,0:T(8,128)(2,1)S(1)}, bf16[256,1024]{1,0:T(8,128)(2,1)S(1)}, u32[]{:S(2)}, u32[]{:S(2)}) %collective-permute-start.16) | collective-permute-done | bytes 524320 | tf_op jit(solution)/shard_map/ppermute | solution.py:30
  566.9 11.6 %convolution_convert_fusion = bf16[2048,2048]{1,0:T(8,128)(2,1)} fusion(bf16[1024,2048]{1,0:T(8,128)(2,1)S(1)} %copy-done.54, bf16[1024,2048]{1,0:T(8,128)(2,1)S(1)} %copy-done.53), kind=kOutput, calls=%fused_computation.3 | convolution fusion | flops 8594128896 | bytes 16777216 | tf_op jit(solution)/shard_map/dot_general | solution.py:25
  585.0 2.3 pad_maximum_fusion.2
  587.4 17.4 %collective-permute-done.18 = bf16[256,2048]{1,0:T(8,128)(2,1)} collective-permute-done((bf16[256,2048]{1,0:T(8,128)(2,1)S(1)}, bf16[256,2048]{1,0:T(8,128)(2,1)}, u32[]{:S(2)}, u32[]{:S(2)}) %collective-permute-start.18) | collective-permute-done | bytes 1048608 | tf_op jit(solution)/shard_map/ppermute | solution.py:30
  606.8 19.7 %collective-permute-done.19 = bf16[256,2048]{1,0:T(8,128)(2,1)} collective-permute-done((bf16[256,2048]{1,0:T(8,128)(2,1)S(1)}, bf16[256,2048]{1,0:T(8,128)(2,1)}, u32[]{:S(2)}, u32[]{:S(2)}) %collective-permute-start.19) | collective-permute-done | bytes 1048608 | tf_op jit(solution)/shard_map/ppermute | solution.py:30
  628.1 2.0 copy-done.6
  630.1 3.3 convolution_convert_fusion.5.grad_ref
  633.5 16.8 %shard_map.247 = (f32[1024,512]{1,0:T(8,128)}, f32[1024,512]{1,0:T(8,128)}, bf16[1024,512]{1,0:T(8,128)(2,1)}, f32[1024,128]{1,0:T(8,128)}, f32[1024,128]{1,0:T(8,128)}, /*index=5*/f32[2,512]{1,0:T(2,128)}) custom-call(bf16[1024,512]{1,0:T(8,128)(2,1)} %get-tuple-element.74.query_ref, bf16[1024,512]{1,0:T(8,128)(2,1)} %get-tuple-element.75.key_ref, ...), custom_call_target="tpu_custom_call" | custom-call | flops 5368709120 | bytes 15728640 | tf_op jit(solution)/shard_map/pallas_call | solution.py:314
  657.4 3.2 pad_maximum_fusion.1
  660.6 3.0 reshape.185
  663.6 3.2 fusion.9
  666.9 2.0 constant_dynamic-slice_fusion.1
  683.1 2.8 multiply_convert_fusion.3
  687.1 3.8 convolution_convert_fusion.4
  700.3 16.8 %reduce-scatter.11.cloned.1.call-done.up_hbm = bf16[256,2048]{1,0:T(8,128)(2,1)} async-done(((bf16[2048,2048]{1,0:T(8,128)(2,1)}), bf16[256,2048]{1,0:T(8,128)(2,1)}) %reduce-scatter.11.cloned.1.call-update) | async-done | bytes 1048592 | tf_op jit(solution)/shard_map/reduce_scatter | solution.py:1290
  717.1 95.3 %shard_map.248 = (f32[64,2048]{1,0:T(8,128)}, f32[64,2048]{1,0:T(8,128)}, f32[64,2048]{1,0:T(8,128)}, f32[64,2048]{1,0:T(8,128)}, bf16[256,2048]{1,0:T(8,128)(2,...) custom-call(bf16[1024,2048]{1,0:T(8,128)(2,1)} %get-tuple-element.106.tokens_hbm, ...), custom_call_target="tpu_custom_call" | custom-call | flops 12884901888 | bytes 104857600 | tf_op jit(solution)/shard_map/pallas_call | solution.py:658
  813.9 2.3 copy.103
  (280 shorter events, 95.5 us)
Async XLA Ops:
  7.2 571.4 %reduce-scatter.7.cloned.1.call-start = ((), (), s32[]{:S(2)}) async-start(), calls=%async_computation.5 | async-start | bytes 4718592 | tf_op jit(solution)/shard_map/reduce_scatter | solution.py:1290
  339.2 24.3 %collective-permute-start.3 = (bf16[256,1024]{1,0:T(8,128)(2,1)}, bf16[256,1024]{1,0:T(8,128)(2,1)}, u32[]{:S(2)}, u32[]{:S(2)}) collective-permute-start(bf16[256,1024]{1,0:T(8,128)(2,1)} %convolution_convert_fusion.8), channel_id=1, source_target_pairs={{0,3},{1,2},{2,1},{3,0},{4,7},{5,6},{6,5},{7,4},{8,11},{9,10},{10,... | collective-permute-start | bytes 1572872 | tf_op jit(solution)/shard_map/ppermute | solution.py:30
  343.7 31.0 %collective-permute-start.4 = (bf16[256,1024]{1,0:T(8,128)(2,1)}, bf16[256,1024]{1,0:T(8,128)(2,1)}, u32[]{:S(2)}, u32[]{:S(2)}) collective-permute-start(bf16[256,1024]{1,0:T(8,128)(2,1)} %convolution_convert_fusion.7), channel_id=1, source_target_pairs={{0,2},{1,3},{2,0},{3,1},{4,6},{5,7},{6,4},{7,5},{8,10},{9,11},{10,... | collective-permute-start | bytes 1572872 | tf_op jit(solution)/shard_map/ppermute | solution.py:30
  349.2 25.5 %collective-permute-start.5 = (bf16[256,1024]{1,0:T(8,128)(2,1)}, bf16[256,1024]{1,0:T(8,128)(2,1)}, u32[]{:S(2)}, u32[]{:S(2)}) collective-permute-start(bf16[256,1024]{1,0:T(8,128)(2,1)} %convolution_convert_fusion.6), channel_id=1, source_target_pairs={{0,1},{1,0},{2,3},{3,2},{4,5},{5,4},{6,7},{7,6},{8,9},{9,8},{10,11... | collective-permute-start | bytes 1572872 | tf_op jit(solution)/shard_map/ppermute | solution.py:30
  355.3 24.2 %collective-permute-start = (bf16[256,1024]{1,0:T(8,128)(2,1)}, bf16[256,1024]{1,0:T(8,128)(2,1)}, u32[]{:S(2)}, u32[]{:S(2)}) collective-permute-start(bf16[256,1024]{1,0:T(8,128)(2,1)} %convolution_convert_fusion.11), channel_id=1, source_target_pairs={{0,3},{1,2},{2,1},{3,0},{4,7},{5,6},{6,5},{7,4},{8,11},{9,10},{10,... | collective-permute-start | bytes 1572872 | tf_op jit(solution)/shard_map/ppermute | solution.py:30
  357.6 30.7 %collective-permute-start.1 = (bf16[256,1024]{1,0:T(8,128)(2,1)}, bf16[256,1024]{1,0:T(8,128)(2,1)}, u32[]{:S(2)}, u32[]{:S(2)}) collective-permute-start(bf16[256,1024]{1,0:T(8,128)(2,1)} %convolution_convert_fusion.10), channel_id=1, source_target_pairs={{0,2},{1,3},{2,0},{3,1},{4,6},{5,7},{6,4},{7,5},{8,10},{9,11},{10,... | collective-permute-start | bytes 1572872 | tf_op jit(solution)/shard_map/ppermute | solution.py:30
  363.4 24.9 %collective-permute-start.2 = (bf16[256,1024]{1,0:T(8,128)(2,1)}, bf16[256,1024]{1,0:T(8,128)(2,1)}, u32[]{:S(2)}, u32[]{:S(2)}) collective-permute-start(bf16[256,1024]{1,0:T(8,128)(2,1)} %convolution_convert_fusion.9), channel_id=1, source_target_pairs={{0,1},{1,0},{2,3},{3,2},{4,5},{5,4},{6,7},{7,6},{8,9},{9,8},{10,11... | collective-permute-start | bytes 1572872 | tf_op jit(solution)/shard_map/ppermute | solution.py:30
  374.8 13.6 %copy-start.5 = (f32[32,8,8,128]{3,1,2,0:T(8,128)S(1)}, f32[32,8,8,128]{3,1,2,0:T(8,128)}, u32[]{:S(2)}) copy-start(f32[32,8,8,128]{3,1,2,0:T(8,128)} %copy.68) | copy-start | bytes 3145732
  374.8 13.6 %copy-start.46 = (bf16[1024,2048]{1,0:T(8,128)(2,1)S(1)}, bf16[1024,2048]{1,0:T(8,128)(2,1)}, u32[]{:S(2)}) copy-start(bf16[1024,2048]{1,0:T(8,128)(2,1)} %get-tuple-element.72) | copy-start | bytes 12582916
  391.6 16.3 %copy-start.3 = (f32[256,1024]{1,0:T(8,128)}, f32[256,1024]{1,0:T(8,128)S(1)}, u32[]{:S(2)}) copy-start(f32[256,1024]{1,0:T(8,128)S(1)} %get-tuple-element.104) | copy-start | bytes 3145732
  392.9 26.6 %copy-start.48 = (bf16[1024,2048]{1,0:T(8,128)(2,1)S(1)}, bf16[1024,2048]{1,0:T(8,128)(2,1)}, u32[]{:S(2)}) copy-start(bf16[1024,2048]{1,0:T(8,128)(2,1)} %get-tuple-element.71) | copy-start | bytes 12582916
  392.9 14.8 %collective-permute-start.9 = (bf16[256,1024]{1,0:T(8,128)(2,1)S(1)}, bf16[256,1024]{1,0:T(8,128)(2,1)S(1)}, u32[]{:S(2)}, u32[]{:S(2)}) collective-permute-start(bf16[256,1024]{1,0:T(8,128)(2,1)S(1)} %get-tuple-element.172), channel_id=1, source_target_pairs={{0,1},{1,0},{2,3},{3,2},{4,5},{5,4},{6,7},{7,6},{8,9},{9,8},{10,11... | collective-permute-start | bytes 1572872 | tf_op jit(solution)/shard_map/ppermute | solution.py:30
  393.0 25.0 %collective-permute-start.10 = (bf16[256,1024]{1,0:T(8,128)(2,1)S(1)}, bf16[256,1024]{1,0:T(8,128)(2,1)S(1)}, u32[]{:S(2)}, u32[]{:S(2)}) collective-permute-start(bf16[256,1024]{1,0:T(8,128)(2,1)S(1)} %get-tuple-element.172), channel_id=1, source_target_pairs={{0,2},{1,3},{2,0},{3,1},{4,6},{5,7},{6,4},{7,5},{8,10},{9,11},{10,... | collective-permute-start | bytes 1572872 | tf_op jit(solution)/shard_map/ppermute | solution.py:30
  393.7 24.3 %collective-permute-start.11 = (bf16[256,1024]{1,0:T(8,128)(2,1)S(1)}, bf16[256,1024]{1,0:T(8,128)(2,1)S(1)}, u32[]{:S(2)}, u32[]{:S(2)}) collective-permute-start(bf16[256,1024]{1,0:T(8,128)(2,1)S(1)} %get-tuple-element.172), channel_id=1, source_target_pairs={{0,3},{1,2},{2,1},{3,0},{4,7},{5,6},{6,5},{7,4},{8,11},{9,10},{10,... | collective-permute-start | bytes 1572872 | tf_op jit(solution)/shard_map/ppermute | solution.py:30
  425.9 152.7 %reduce-scatter.5.cloned.1.call-start = ((), (), s32[]{:S(2)}) async-start(), calls=%async_computation.4 | async-start | bytes 4718592 | tf_op jit(solution)/shard_map/reduce_scatter | solution.py:1290
  425.9 27.9 %copy-start.49 = (bf16[1024,2048]{1,0:T(8,128)(2,1)S(1)}, bf16[1024,2048]{1,0:T(8,128)(2,1)}, u32[]{:S(2)}) copy-start(bf16[1024,2048]{1,0:T(8,128)(2,1)} %get-tuple-element.71) | copy-start | bytes 12582916
  426.9 14.9 %collective-permute-start.6 = (bf16[256,1024]{1,0:T(8,128)(2,1)S(1)}, bf16[256,1024]{1,0:T(8,128)(2,1)S(1)}, u32[]{:S(2)}, u32[]{:S(2)}) collective-permute-start(bf16[256,1024]{1,0:T(8,128)(2,1)S(1)} %copy-done.18), channel_id=1, source_target_pairs={{0,1},{1,0},{2,3},{3,2},{4,5},{5,4},{6,7},{7,6},{8,9},{9,8},{10,11... | collective-permute-start | bytes 1572872 | tf_op jit(solution)/shard_map/ppermute | solution.py:30
  428.6 23.7 %collective-permute-start.7 = (bf16[256,1024]{1,0:T(8,128)(2,1)S(1)}, bf16[256,1024]{1,0:T(8,128)(2,1)S(1)}, u32[]{:S(2)}, u32[]{:S(2)}) collective-permute-start(bf16[256,1024]{1,0:T(8,128)(2,1)S(1)} %copy-done.18), channel_id=1, source_target_pairs={{0,2},{1,3},{2,0},{3,1},{4,6},{5,7},{6,4},{7,5},{8,10},{9,11},{10,... | collective-permute-start | bytes 1572872 | tf_op jit(solution)/shard_map/ppermute | solution.py:30
  428.9 23.5 %collective-permute-start.8 = (bf16[256,1024]{1,0:T(8,128)(2,1)S(1)}, bf16[256,1024]{1,0:T(8,128)(2,1)S(1)}, u32[]{:S(2)}, u32[]{:S(2)}) collective-permute-start(bf16[256,1024]{1,0:T(8,128)(2,1)S(1)} %copy-done.18), channel_id=1, source_target_pairs={{0,3},{1,2},{2,1},{3,0},{4,7},{5,6},{6,5},{7,4},{8,11},{9,10},{10,... | collective-permute-start | bytes 1572872 | tf_op jit(solution)/shard_map/ppermute | solution.py:30
  460.5 172.9 %reduce-scatter.9.cloned.1.call-start = ((), (), s32[]{:S(2)}) async-start(), calls=%async_computation.6 | async-start | bytes 9437184 | tf_op jit(solution)/shard_map/reduce_scatter | solution.py:1290
  499.7 217.4 %reduce-scatter.11.cloned.1.call-start = ((), (), s32[]{:S(2)}) async-start(), calls=%async_computation.7 | async-start | bytes 9437184 | tf_op jit(solution)/shard_map/reduce_scatter | solution.py:1290
  499.8 19.2 %slice-start.2 = ((s8[8388608]{0:T(1024)(128)(4,1)}), s8[4194304]{0:T(1024)(128)(4,1)S(1)}, s32[]{:S(2)}) async-start(s8[8388608]{0:T(1024)(128)(4,1)} %bitcast.177), calls=%async_computation.10 | async-start | bytes 8388608
  507.8 11.2 %slice-start.3 = ((s8[8388608]{0:T(1024)(128)(4,1)}), s8[4194304]{0:T(1024)(128)(4,1)S(1)}, s32[]{:S(2)}) async-start(s8[8388608]{0:T(1024)(128)(4,1)} %bitcast.177), calls=%async_computation.11 | async-start | bytes 8388608
  515.4 22.1 %collective-permute-start.12 = (bf16[256,1024]{1,0:T(8,128)(2,1)S(1)}, bf16[256,1024]{1,0:T(8,128)(2,1)S(1)}, u32[]{:S(2)}, u32[]{:S(2)}) collective-permute-start(bf16[256,1024]{1,0:T(8,128)(2,1)S(1)} %get-tuple-element.145), channel_id=1, source_target_pairs={{0,3},{1,2},{2,1},{3,0},{4,7},{5,6},{6,5},{7,4},{8,11},{9,10},{10,... | collective-permute-start | bytes 1572872 | tf_op jit(solution)/shard_map/ppermute | solution.py:30
  516.8 25.4 %collective-permute-start.13 = (bf16[256,1024]{1,0:T(8,128)(2,1)S(1)}, bf16[256,1024]{1,0:T(8,128)(2,1)S(1)}, u32[]{:S(2)}, u32[]{:S(2)}) collective-permute-start(bf16[256,1024]{1,0:T(8,128)(2,1)S(1)} %get-tuple-element.147), channel_id=1, source_target_pairs={{0,2},{1,3},{2,0},{3,1},{4,6},{5,7},{6,4},{7,5},{8,10},{9,11},{10,... | collective-permute-start | bytes 1572872 | tf_op jit(solution)/shard_map/ppermute | solution.py:30
  517.1 10.9 %slice-start = ((s8[8388608]{0:T(1024)(128)(4,1)}), s8[4194304]{0:T(1024)(128)(4,1)S(1)}, s32[]{:S(2)}) async-start(s8[8388608]{0:T(1024)(128)(4,1)} %bitcast.175), calls=%async_computation.8 | async-start | bytes 8388608
  517.1 10.9 %slice-start.1 = ((s8[8388608]{0:T(1024)(128)(4,1)}), s8[4194304]{0:T(1024)(128)(4,1)S(1)}, s32[]{:S(2)}) async-start(s8[8388608]{0:T(1024)(128)(4,1)} %bitcast.175), calls=%async_computation.9 | async-start | bytes 8388608
  517.1 25.1 %collective-permute-start.14 = (bf16[256,1024]{1,0:T(8,128)(2,1)S(1)}, bf16[256,1024]{1,0:T(8,128)(2,1)S(1)}, u32[]{:S(2)}, u32[]{:S(2)}) collective-permute-start(bf16[256,1024]{1,0:T(8,128)(2,1)S(1)} %get-tuple-element.146), channel_id=1, source_target_pairs={{0,1},{1,0},{2,3},{3,2},{4,5},{5,4},{6,7},{7,6},{8,9},{9,8},{10,11... | collective-permute-start | bytes 1572872 | tf_op jit(solution)/shard_map/ppermute | solution.py:30
  528.1 11.4 %copy-start.30 = (f32[256,128]{1,0:T(8,128)S(1)}, f32[256,128]{1,0:T(8,128)}, u32[]{:S(2)}) copy-start(f32[256,128]{1,0:T(8,128)} %get-tuple-element.78) | copy-start | bytes 393220
  535.8 26.5 %copy-start.2 = (f32[256,2048]{1,0:T(8,128)S(1)}, f32[256,2048]{1,0:T(8,128)}, u32[]{:S(2)}) copy-start(f32[256,2048]{1,0:T(8,128)} %get-tuple-element.93) | copy-start | bytes 6291460
  535.9 17.6 %collective-permute-start.15 = (bf16[256,1024]{1,0:T(8,128)(2,1)S(1)}, bf16[256,1024]{1,0:T(8,128)(2,1)S(1)}, u32[]{:S(2)}, u32[]{:S(2)}) collective-permute-start(bf16[256,1024]{1,0:T(8,128)(2,1)S(1)} %get-tuple-element.148), channel_id=1, source_target_pairs={{0,3},{1,2},{2,1},{3,0},{4,7},{5,6},{6,5},{7,4},{8,11},{9,10},{10,... | collective-permute-start | bytes 1572872 | tf_op jit(solution)/shard_map/ppermute | solution.py:30
  537.5 24.4 %collective-permute-start.16 = (bf16[256,1024]{1,0:T(8,128)(2,1)S(1)}, bf16[256,1024]{1,0:T(8,128)(2,1)S(1)}, u32[]{:S(2)}, u32[]{:S(2)}) collective-permute-start(bf16[256,1024]{1,0:T(8,128)(2,1)S(1)} %get-tuple-element.150), channel_id=1, source_target_pairs={{0,2},{1,3},{2,0},{3,1},{4,6},{5,7},{6,4},{7,5},{8,10},{9,11},{10,... | collective-permute-start | bytes 1572872 | tf_op jit(solution)/shard_map/ppermute | solution.py:30
  537.5 24.4 %collective-permute-start.17 = (bf16[256,1024]{1,0:T(8,128)(2,1)S(1)}, bf16[256,1024]{1,0:T(8,128)(2,1)S(1)}, u32[]{:S(2)}, u32[]{:S(2)}) collective-permute-start(bf16[256,1024]{1,0:T(8,128)(2,1)S(1)} %get-tuple-element.149), channel_id=1, source_target_pairs={{0,1},{1,0},{2,3},{3,2},{4,5},{5,4},{6,7},{7,6},{8,9},{9,8},{10,11... | collective-permute-start | bytes 1572872 | tf_op jit(solution)/shard_map/ppermute | solution.py:30
  578.6 26.2 %collective-permute-start.18 = (bf16[256,2048]{1,0:T(8,128)(2,1)S(1)}, bf16[256,2048]{1,0:T(8,128)(2,1)}, u32[]{:S(2)}, u32[]{:S(2)}) collective-permute-start(bf16[256,2048]{1,0:T(8,128)(2,1)S(1)} %multiply_convert_fusion.4), channel_id=1, source_target_pairs={{0,1},{1,0},{2,3},{3,2},{4,5},{5,4},{6,7},{7,6},{8,9},{9,8},{10,11... | collective-permute-start | bytes 3145736 | tf_op jit(solution)/shard_map/ppermute | solution.py:30
  579.1 47.4 %collective-permute-start.19 = (bf16[256,2048]{1,0:T(8,128)(2,1)S(1)}, bf16[256,2048]{1,0:T(8,128)(2,1)}, u32[]{:S(2)}, u32[]{:S(2)}) collective-permute-start(bf16[256,2048]{1,0:T(8,128)(2,1)S(1)} %multiply_convert_fusion.4), channel_id=1, source_target_pairs={{0,2},{1,3},{2,0},{3,1},{4,6},{5,7},{6,4},{7,5},{8,10},{9,11},{10,... | collective-permute-start | bytes 3145736 | tf_op jit(solution)/shard_map/ppermute | solution.py:30
  582.1 45.8 %collective-permute-start.20 = (bf16[256,2048]{1,0:T(8,128)(2,1)S(1)}, bf16[256,2048]{1,0:T(8,128)(2,1)S(1)}, u32[]{:S(2)}, u32[]{:S(2)}) collective-permute-start(bf16[256,2048]{1,0:T(8,128)(2,1)S(1)} %multiply_convert_fusion.4), channel_id=1, source_target_pairs={{0,3},{1,2},{2,1},{3,0},{4,7},{5,6},{6,5},{7,4},{8,11},{9,10},{10,... | collective-permute-start | bytes 3145736 | tf_op jit(solution)/shard_map/ppermute | solution.py:30
  605.3 24.8 %copy-start.51 = (bf16[512,2048]{1,0:T(8,128)(2,1)S(1)}, bf16[512,2048]{1,0:T(8,128)(2,1)}, u32[]{:S(2)}) copy-start(bf16[512,2048]{1,0:T(8,128)(2,1)} %get-tuple-element.97) | copy-start | bytes 6291460
  633.5 23.5 %copy-start.4 = (f32[256,1024]{1,0:T(8,128)S(1)}, f32[256,1024]{1,0:T(8,128)}, u32[]{:S(2)}) copy-start(f32[256,1024]{1,0:T(8,128)} %copy-done.3) | copy-start | bytes 3145732
  653.5 21.4 %collective-permute-start.21 = (f32[2,1024]{1,0:T(2,128)}, f32[2,1024]{1,0:T(2,128)}, u32[]{:S(2)}, u32[]{:S(2)}) collective-permute-start(f32[2,1024]{1,0:T(2,128)} %pad_maximum_fusion.6), channel_id=1, source_target_pairs={{0,1},{1,0},{2,3},{3,2},{4,5},{5,4},{6,7},{7,6},{8,9},{9,8},{10,11... | collective-permute-start | bytes 24584 | tf_op jit(solution)/shard_map/ppermute | solution.py:30
  655.2 20.7 %collective-permute-start.22 = (f32[2,1024]{1,0:T(2,128)}, f32[2,1024]{1,0:T(2,128)}, u32[]{:S(2)}, u32[]{:S(2)}) collective-permute-start(f32[2,1024]{1,0:T(2,128)} %pad_maximum_fusion.6), channel_id=1, source_target_pairs={{0,2},{1,3},{2,0},{3,1},{4,6},{5,7},{6,4},{7,5},{8,10},{9,11},{10,... | collective-permute-start | bytes 24584 | tf_op jit(solution)/shard_map/ppermute | solution.py:30
  655.9 21.6 %collective-permute-start.23 = (f32[2,1024]{1,0:T(2,128)}, f32[2,1024]{1,0:T(2,128)}, u32[]{:S(2)}, u32[]{:S(2)}) collective-permute-start(f32[2,1024]{1,0:T(2,128)} %pad_maximum_fusion.6), channel_id=1, source_target_pairs={{0,3},{1,2},{2,1},{3,0},{4,7},{5,6},{6,5},{7,4},{8,11},{9,10},{10,... | collective-permute-start | bytes 24584 | tf_op jit(solution)/shard_map/ppermute | solution.py:30
  668.9 23.8 %collective-permute-start.27 = (bf16[64,2048]{1,0:T(8,128)(2,1)}, bf16[64,2048]{1,0:T(8,128)(2,1)}, u32[]{:S(2)}, u32[]{:S(2)}) collective-permute-start(bf16[64,2048]{1,0:T(8,128)(2,1)} %get-tuple-element.153), channel_id=1, source_target_pairs={{0,1},{1,0},{2,3},{3,2},{4,5},{5,4},{6,7},{7,6},{8,9},{9,8},{10,11... | collective-permute-start | bytes 786440 | tf_op jit(solution)/shard_map/ppermute | solution.py:30
  670.6 25.3 %collective-permute-start.28 = (bf16[64,2048]{1,0:T(8,128)(2,1)}, bf16[64,2048]{1,0:T(8,128)(2,1)}, u32[]{:S(2)}, u32[]{:S(2)}) collective-permute-start(bf16[64,2048]{1,0:T(8,128)(2,1)} %get-tuple-element.152), channel_id=1, source_target_pairs={{0,2},{1,3},{2,0},{3,1},{4,6},{5,7},{6,4},{7,5},{8,10},{9,11},{10,... | collective-permute-start | bytes 786440 | tf_op jit(solution)/shard_map/ppermute | solution.py:30
  674.8 23.1 %collective-permute-start.29 = (bf16[64,2048]{1,0:T(8,128)(2,1)S(1)}, bf16[64,2048]{1,0:T(8,128)(2,1)}, u32[]{:S(2)}, u32[]{:S(2)}) collective-permute-start(bf16[64,2048]{1,0:T(8,128)(2,1)S(1)} %get-tuple-element.151), channel_id=1, source_target_pairs={{0,3},{1,2},{2,1},{3,0},{4,7},{5,6},{6,5},{7,4},{8,11},{9,10},{10,... | collective-permute-start | bytes 786440 | tf_op jit(solution)/shard_map/ppermute | solution.py:30
  675.8 19.1 %collective-permute-start.24 = (bf16[64,2048]{1,0:T(8,128)(2,1)}, bf16[64,2048]{1,0:T(8,128)(2,1)}, u32[]{:S(2)}, u32[]{:S(2)}) collective-permute-start(bf16[64,2048]{1,0:T(8,128)(2,1)} %get-tuple-element.156), channel_id=1, source_target_pairs={{0,1},{1,0},{2,3},{3,2},{4,5},{5,4},{6,7},{7,6},{8,9},{9,8},{10,11... | collective-permute-start | bytes 786440 | tf_op jit(solution)/shard_map/ppermute | solution.py:30
  677.5 19.4 %collective-permute-start.25 = (bf16[64,2048]{1,0:T(8,128)(2,1)}, bf16[64,2048]{1,0:T(8,128)(2,1)}, u32[]{:S(2)}, u32[]{:S(2)}) collective-permute-start(bf16[64,2048]{1,0:T(8,128)(2,1)} %get-tuple-element.155), channel_id=1, source_target_pairs={{0,2},{1,3},{2,0},{3,1},{4,6},{5,7},{6,4},{7,5},{8,10},{9,11},{10,... | collective-permute-start | bytes 786440 | tf_op jit(solution)/shard_map/ppermute | solution.py:30
  692.8 7.3 collective-permute-start.26
  700.3 112.2 %copy-start.11 = (f32[64,8192]{1,0:T(8,128)}, f32[64,8192]{1,0:T(8,128)S(1)}, u32[]{:S(2)}) copy-start(f32[64,8192]{1,0:T(8,128)S(1)} %convert_dynamic-update-slice_fusion.4) | copy-start | bytes 6291460
  (45 other events, 216.2 us)
Sparse Core Ops, SparseCore 0:
  426.0 60.3 reduce-scatter.6
  488.7 48.1 reduce-scatter.4
  539.2 87.7 reduce-scatter.8
  629.1 87.9 reduce-scatter.10

commit v5 on v4

--- a/solution.py
+++ b/solution.py
@@ -496,9 +496,12 @@
     def product(block):
         return dot(tokens[:, pl.ds(pl.multiple_of(block * size, size), size)], grads[...], TN)
 
-    for i in range(4):
+    def across(i):
         core_out[i] = product(2 * blocks[i] + 1 - core).astype(bf16)
         core_copy(core_out.at[i], core_in.at[i], 0, i)
+
+    across(0)
+    across(1)
 
     def pair(i):
         mine[i] = (product(2 * blocks[i] + core) + core_in[i].astype(f32)).astype(bf16)
@@ -510,6 +513,7 @@
             copy = line_copy(mine.at[i], line_in, 0, i)
             copy.start()
             sent.append(copy)
+            across(i + 2)
         if i == 2:
             last = line_copy(mine.at[2], line_in, 0, 2)
             sent.append(last)
@@ -710,7 +714,9 @@
 
 def front_kernel(
     tokens_hbm,
-    pack_hbm,
+    query_hbm,
+    key_hbm,
+    value_hbm,
     output_hbm,
     gate_hbm,
     up_hbm,
@@ -788,10 +794,9 @@
     leaf, row = lax.axis_index("leaf"), lax.axis_index("row")
     z, core = leaf // 2, leaf % 2
     far, inner = z // 2, ((z + 1) // 2) % 2
-    own = pack_hbm.shape[1]
-    wide = pack_hbm.shape[2]
-    part, size = wide // 3, 4 * own
-    rows, width = tokens_hbm.shape
+    own, width = query_hbm.shape
+    part, size = width // 4, 4 * own
+    rows, wide = tokens_hbm.shape[0], 3 * part
     units = gate_block.shape[1]
     heads = part // HEAD_DIM
     scale = 1.0 / math.sqrt(HEAD_DIM)
@@ -812,8 +817,10 @@
         saved.append(copy)
 
     mine = lines(row, own)
-    load_pack = load(pack_hbm.at[row], block.at[mine, pl.ds(0, wide)], 0)
-    load_output = load(output_hbm, block.at[:, pl.ds(wide, part)], 1)
+    load_weights = [
+        load(source, attn.at[pl.ds(i * own, own)], (0, 1, 15, 16)[i])
+        for i, source in enumerate((query_hbm, key_hbm, value_hbm, output_hbm))
+    ]
     load_gains = load(gains_hbm, gains_leaf.at[row], 2)
     load_gate = load(gate_hbm.at[:, lines(row, units)], gate_block.at[mine], 3)
     load_tokens = load(tokens_hbm, tokens.at[lines(row, rows)], 4)
@@ -849,8 +856,19 @@
             source, target, send_sem, recv_sem, device_id={"leaf": to}, device_id_type=MESH
         )
 
-    for hop in hops:
-        row_copy(pack_hbm.at[other(row, hop)], block.at[mine, pl.ds(0, wide)], 0, hop)
+    for copy in load_weights:
+        copy.wait()
+    for hop in hops:
+        for i in range(3):
+            some = attn[i * own : (i + 1) * own, lines(other(row, hop), part)]
+            rows_send[hop - 1, :own, i * part : (i + 1) * part] = some.astype(bf16)
+        row_copy(rows_send.at[hop - 1, pl.ds(0, own), pl.ds(0, wide)], block.at[mine, pl.ds(0, wide)], 0, hop)
+    packs = sent[:]
+    sent.clear()
+    for i in range(3):
+        block[mine, i * part : (i + 1) * part] = attn[i * own : (i + 1) * own, lines(row, part)].astype(bf16)
+    for i in range(4):
+        block[i * own : (i + 1) * own, wide:] = attn[3 * own :, i * part : (i + 1) * part].astype(bf16)
     for hop in hops:
         row_copy(gains_hbm, gains_leaf.at[row], 1, hop)
     for hop in hops:
@@ -930,8 +948,6 @@
             chip = arrival(step)[1]
             landed(whole.at[lines(2 * chip + 1 - core, sizes[kind])], core_recv_sem.at[kind, step])
 
-    load_pack.wait()
-    load_output.wait()
     row_landed(lambda source, hop: block.at[lines(source, own), pl.ds(0, wide)], 0)
     done = [spread(0, block, attn_mat)]
 
@@ -1044,6 +1060,8 @@
             columns = slice(j * part, (j + 1) * part)
             store(columns, dot(some, output_mat[:, columns], NN))
 
+    for copy in packs:
+        copy.wait_send()
     half = rows // 2
     top, bottom = pl.ds(0, half), pl.ds(half, half)
     for hop in hops:
@@ -1167,9 +1185,9 @@
         copy.wait()
 
 
-def front(tokens, pack, output_block, gate, up, down, gain_tile, cos_wide, sin_wide, bias):
+def front(tokens, weights, gate, up, down, gain_tile, cos_wide, sin_wide, bias):
     rows, width = tokens.shape
-    total, part, own = 4 * rows, width // 4, pack.shape[1]
+    total, part, own = 4 * rows, width // 4, gate.shape[0]
     wide, units, size = 3 * part, gate.shape[1] // 4, 4 * own
     heads = part // HEAD_DIM
     shape = jax.ShapeDtypeStruct
@@ -1201,7 +1219,7 @@
     vmem, dma = pltpu.VMEM, pltpu.SemaphoreType.DMA
     return pl.pallas_call(
         front_kernel,
-        in_specs=[pl.BlockSpec(memory_space=pl.ANY)] * 10,
+        in_specs=[pl.BlockSpec(memory_space=pl.ANY)] * 12,
         out_specs=[pl.BlockSpec(memory_space=pl.ANY)] * len(outs),
         out_shape=outs,
         scratch_shapes=[
@@ -1237,7 +1255,7 @@
             vmem((4, 8, HEAD_DIM), f32),
             vmem((8, 4, 8, HEAD_DIM), f32),
             vmem((8, width), f32),
-            dma((15,)),
+            dma((17,)),
             dma((32,)),
             dma((13, 3)),
             dma((13, 3)),
@@ -1254,7 +1272,7 @@
         cost_estimate=pl.CostEstimate(
             flops=10 * total * width * part, bytes_accessed=100 * 2**20, transcendentals=0
         ),
-    )(tokens, pack, output_block, gate, up, down, gain_tile, cos_wide, sin_wide, bias)
+    )(tokens, *weights, gate, up, down, gain_tile, cos_wide, sin_wide, bias)
 
 
 def body(
@@ -1292,9 +1310,6 @@
     bias, cos_wide, sin_wide = tree_tables(seg_lengths[0], seg_parents[0], tree_len)
     fast = leaves == 8 and count == 4
     if fast:
-        def split_columns(weight):
-            return jnp.swapaxes(weight.astype(bf16).reshape(own, count, -1), 0, 1)
-
         gain_own = jnp.stack([gain_query, gain_key, gain_attn, gain_mlp]).astype(bf16).astype(f32)
         gain_tile = lax.dynamic_update_slice(jnp.zeros((8, HEAD_DIM), f32), gain_own, (0, (me % 2) * own))
         (
@@ -1323,8 +1338,7 @@
             gains_all,
         ) = front(
             tokens,
-            jnp.concatenate([split_columns(w) for w in (w_query, w_key, w_value)], axis=2),
-            split_columns(w_output).reshape(count * own, part),
+            (w_query, w_key, w_value, w_output),
             w_gate.astype(bf16),
             w_up.astype(bf16),
             w_down.astype(bf16),

time: 833 us -> 828 us (level)
    unnamed x128 -> x120, local copies, waits for them, and re-layouts: 20.9 us -> 21.9 us
  transfers between devices with their start and end apart: 34 -> 34, of which waited for: 12 -> 13; matrix products, arithmetic and copies ran while one was open for 21% -> 21% of each run, Pallas kernels for 2% -> 2%
where the time goes in v5:
time: 828 us; the launch traced here: 824 us
  Pallas kernels  419 us (51%)
  matrix products  132 us (16%)
  waiting for transfers between devices  128 us (15%)
  local copies, waits for them, and re-layouts  49 us (6%)
  other arithmetic  46.1 us (6%)
  starting transfers between devices  35.4 us (4%)
  between operations  15.1 us (2%)
    pallas_call x1, Pallas kernels, front(): pl.pallas_call(front_kernel, in_specs=[pl.BlockSpec(memory_space=pl.ANY)]...  306 us
    dot_general x20, matrix products, dot(): lax.dot_general(left, right, dims, preferred_element_type=f32).astype(kind)  132 us
    ppermute x30, waiting for transfers between devices, swap(): return lax.ppermute(piece, 'row', [(i, i ^ hop) for i in range(count)])  111 us
    pallas_call x1, Pallas kernels, finish(): pl.pallas_call(final_kernel, in_specs=[pl.BlockSpec(memory_space=pl.ANY)]...  95.3 us
    ppermute x30, starting transfers between devices, swap(): return lax.ppermute(piece, 'row', [(i, i ^ hop) for i in range(count)])  35.3 us
    unnamed x120, local copies, waits for them, and re-layouts  21.9 us
    pallas_call x1, Pallas kernels, attend_back(): pl.pallas_call(functools.partial(attend_back_kernel, 256, 1.0 / math.sqrt...  17.3 us
    reduce_scatter x4, waiting for transfers between devices, leaf_scatter(): return lax.psum_scatter(block, 'leaf', scatter_dimension=0, tiled=True)  17.2 us
  transfers between devices with their start and end apart: 34, of which 13 were waited for; matrix products, arithmetic and copies ran while one was open for 21% of the time, Pallas kernels for 2%

profile of v5, /device:TPU:0, one launch (start us, length us, event | category | flops | bytes accessed | tf_op | source)
XLA Modules:
  0.0 824.5 jit_solution(1255857374967382906)
XLA Ops:
  11.6 2.7 convert_element_type.191.gate_hbm
  18.4 3.1 select_convert_fusion.bias_hbm.bias_ref
  23.2 306.0 %shard_map.246 = (bf16[2048,2048]{1,0:T(8,128)(2,1)}, bf16[2048,2048]{1,0:T(8,128)(2,1)}, bf16[2048,2048]{1,0:T(8,128)(2,1)}, bf16[1024,2048]{1,0:T(8,128)(2,1)}...) custom-call(bf16[256,2048]{1,0:T(8,128)(2,1)} %bitcast.143, ...), custom_call_target="tpu_custom_call" | custom-call | flops 10737418240 | bytes 104857600 | tf_op jit(solution)/shard_map/pallas_call | solution.py:1220
  329.2 4.6 convolution_convert_fusion.8
  334.9 4.6 convolution_convert_fusion.7
  339.5 4.7 convolution_convert_fusion.6
  344.2 2.4 collective-permute-start.5
  346.7 3.3 convolution_convert_fusion.11
  351.0 2.1 convolution_convert_fusion.10
  353.7 2.1 convolution_convert_fusion.9
  355.8 2.1 reshape.171
  360.0 6.8 slice_reduce_fusion
  369.4 4.7 multiply_reduce_fusion.4
  374.1 8.7 %collective-permute-done.1 = bf16[256,1024]{1,0:T(8,128)(2,1)} collective-permute-done((bf16[256,1024]{1,0:T(8,128)(2,1)}, bf16[256,1024]{1,0:T(8,128)(2,1)}, u32[]{:S(2)}, u32[]{:S(2)}) %collective-permute-start.1) | collective-permute-done | bytes 524320 | tf_op jit(solution)/shard_map/ppermute | solution.py:30
  382.9 3.3 multiply_reduce_fusion.5
  390.9 11.3 %collective-permute-done.9 = bf16[256,1024]{1,0:T(8,128)(2,1)S(1)} collective-permute-done((bf16[256,1024]{1,0:T(8,128)(2,1)S(1)}, bf16[256,1024]{1,0:T(8,128)(2,1)S(1)}, u32[]{:S(2)}, u32[]{:S(2)}) %collective-permute-start.9) | collective-permute-done | bytes 524320 | tf_op jit(solution)/shard_map/ppermute | solution.py:30
  402.5 10.0 %collective-permute-done.10 = bf16[256,1024]{1,0:T(8,128)(2,1)S(1)} collective-permute-done((bf16[256,1024]{1,0:T(8,128)(2,1)S(1)}, bf16[256,1024]{1,0:T(8,128)(2,1)S(1)}, u32[]{:S(2)}, u32[]{:S(2)}) %collective-permute-start.10) | collective-permute-done | bytes 524320 | tf_op jit(solution)/shard_map/ppermute | solution.py:30
  414.0 6.3 convolution_convert_fusion.2
  424.9 11.4 %collective-permute-done.6 = bf16[256,1024]{1,0:T(8,128)(2,1)S(1)} collective-permute-done((bf16[256,1024]{1,0:T(8,128)(2,1)S(1)}, bf16[256,1024]{1,0:T(8,128)(2,1)S(1)}, u32[]{:S(2)}, u32[]{:S(2)}) %collective-permute-start.6) | collective-permute-done | bytes 524320 | tf_op jit(solution)/shard_map/ppermute | solution.py:30
  436.6 8.0 collective-permute-done.7
  448.0 6.7 convolution_convert_fusion.3
  454.7 10.8 %fusion.46 = f32[1024,2048]{1,0:T(8,128)} fusion(bf16[1024,1024]{1,0:T(8,128)(2,1)} %copy-done.13, bf16[1024,2048]{1,0:T(8,128)(2,1)} %get-tuple-element.72), kind=kOutput, calls=%fused_computation.155 | convolution fusion | flops 4294967296 | bytes 14680064 | tf_op jit(solution)/shard_map/dot_general | solution.py:25
  465.5 14.2 %multiply_convert_fusion.1 = (bf16[1024,2048]{1,0:T(8,128)(2,1)}, bf16[1024,2048]{1,0:T(8,128)(2,1)}) fusion(f32[1024,2048]{1,0:T(8,128)} %get-tuple-element.86, f32[1024,2048]{1,0:T(8,128)} %get-tuple-element.85, f32[1024,2048]{1,0:T(8,128)} %fusion.46, bf16[1024,1024]{1,0:T(8,128)(2,1)S(1)} %copy-done.12, bf16[1024,2048]{1,0:T(8,128)(2,1)S(1)} %copy-done.40), kind=kOutput, calls=%fused_computation.1 | convolution fusion | flops 4324327424 | bytes 39845888 | tf_op jit(solution)/shard_map/dot_general | solution.py:25
  479.8 14.1 %convolution_convert_fusion.1 = bf16[2048,2048]{1,0:T(8,128)(2,1)} fusion(bf16[1024,2048]{1,0:T(8,128)(2,1)} %get-tuple-element.80, bf16[1024,2048]{1,0:T(8,128)(2,1)} %get-tuple-element.91), kind=kOutput, calls=%fused_computation.4 | convolution fusion | flops 8594128896 | bytes 16777216 | tf_op jit(solution)/shard_map/dot_general | solution.py:25
  493.9 8.0 fusion.4
  501.9 7.4 add_convert_fusion.1
  513.0 9.1 %fusion = f32[1024,1024]{1,0:T(8,128)} fusion(bf16[1024,2048]{1,0:T(8,128)(2,1)} %get-tuple-element.95, bf16[2048,2048]{1,0:T(8,128)(2,1)S(1)} %bitcast.148), kind=kOutput, calls=%fused_computation.6 | convolution fusion | flops 4294967296 | bytes 12582912 | tf_op jit(solution)/shard_map/dot_general | solution.py:25
  522.2 7.7 add_convert_fusion
  533.7 8.9 %collective-permute-done.13 = bf16[256,1024]{1,0:T(8,128)(2,1)S(1)} collective-permute-done((bf16[256,1024]{1,0:T(8,128)(2,1)S(1)}, bf16[256,1024]{1,0:T(8,128)(2,1)S(1)}, u32[]{:S(2)}, u32[]{:S(2)}) %collective-permute-start.13) | collective-permute-done | bytes 524320 | tf_op jit(solution)/shard_map/ppermute | solution.py:30
  542.9 4.9 collective-permute-done.15
  547.8 8.1 collective-permute-done.16
  560.9 11.6 %convolution_convert_fusion = bf16[2048,2048]{1,0:T(8,128)(2,1)} fusion(bf16[1024,2048]{1,0:T(8,128)(2,1)S(1)} %copy-done.50, bf16[1024,2048]{1,0:T(8,128)(2,1)S(1)} %copy-done.49), kind=kOutput, calls=%fused_computation.3 | convolution fusion | flops 8594128896 | bytes 16777216 | tf_op jit(solution)/shard_map/dot_general | solution.py:25
  579.0 2.4 pad_maximum_fusion.2
  581.5 17.4 %collective-permute-done.18 = bf16[256,2048]{1,0:T(8,128)(2,1)} collective-permute-done((bf16[256,2048]{1,0:T(8,128)(2,1)S(1)}, bf16[256,2048]{1,0:T(8,128)(2,1)}, u32[]{:S(2)}, u32[]{:S(2)}) %collective-permute-start.18) | collective-permute-done | bytes 1048608 | tf_op jit(solution)/shard_map/ppermute | solution.py:30
  600.8 19.8 %collective-permute-done.19 = bf16[256,2048]{1,0:T(8,128)(2,1)} collective-permute-done((bf16[256,2048]{1,0:T(8,128)(2,1)S(1)}, bf16[256,2048]{1,0:T(8,128)(2,1)}, u32[]{:S(2)}, u32[]{:S(2)}) %collective-permute-start.19) | collective-permute-done | bytes 1048608 | tf_op jit(solution)/shard_map/ppermute | solution.py:30
  624.3 3.3 convolution_convert_fusion.5.grad_ref
  627.6 17.3 %shard_map.247 = (f32[1024,512]{1,0:T(8,128)}, f32[1024,512]{1,0:T(8,128)}, bf16[1024,512]{1,0:T(8,128)(2,1)}, f32[1024,128]{1,0:T(8,128)}, f32[1024,128]{1,0:T(8,128)}, /*index=5*/f32[2,512]{1,0:T(2,128)}) custom-call(bf16[1024,512]{1,0:T(8,128)(2,1)} %get-tuple-element.74.query_ref, bf16[1024,512]{1,0:T(8,128)(2,1)} %get-tuple-element.75.key_ref, ...), custom_call_target="tpu_custom_call" | custom-call | flops 5368709120 | bytes 15728640 | tf_op jit(solution)/shard_map/pallas_call | solution.py:314
  649.5 2.1 collective-permute-start.23
  652.0 3.2 pad_maximum_fusion.1
  655.2 3.0 reshape.165
  658.2 3.2 fusion.9
  668.3 2.1 collective-permute-start.29
  676.8 2.8 multiply_convert_fusion.3
  680.8 3.8 convolution_convert_fusion.4
  686.5 2.1 collective-permute-start.26
  694.9 17.2 %reduce-scatter.11.cloned.1.call-done.up_hbm = bf16[256,2048]{1,0:T(8,128)(2,1)} async-done(((bf16[2048,2048]{1,0:T(8,128)(2,1)}), bf16[256,2048]{1,0:T(8,128)(2,1)}) %reduce-scatter.11.cloned.1.call-update) | async-done | bytes 1048592 | tf_op jit(solution)/shard_map/reduce_scatter | solution.py:1308
  712.1 95.3 %shard_map.248 = (f32[64,2048]{1,0:T(8,128)}, f32[64,2048]{1,0:T(8,128)}, f32[64,2048]{1,0:T(8,128)}, f32[64,2048]{1,0:T(8,128)}, bf16[256,2048]{1,0:T(8,128)(2,...) custom-call(bf16[1024,2048]{1,0:T(8,128)(2,1)} %get-tuple-element.106.tokens_hbm, ...), custom_call_target="tpu_custom_call" | custom-call | flops 12884901888 | bytes 104857600 | tf_op jit(solution)/shard_map/pallas_call | solution.py:662
  808.8 2.3 copy.84
  (264 shorter events, 92.4 us)
Async XLA Ops:
  7.2 565.4 %reduce-scatter.7.cloned.1.call-start = ((), (), s32[]{:S(2)}) async-start(), calls=%async_computation.5 | async-start | bytes 4718592 | tf_op jit(solution)/shard_map/reduce_scatter | solution.py:1308
  333.8 24.2 %collective-permute-start.3 = (bf16[256,1024]{1,0:T(8,128)(2,1)}, bf16[256,1024]{1,0:T(8,128)(2,1)}, u32[]{:S(2)}, u32[]{:S(2)}) collective-permute-start(bf16[256,1024]{1,0:T(8,128)(2,1)} %convolution_convert_fusion.8), channel_id=1, source_target_pairs={{0,3},{1,2},{2,1},{3,0},{4,7},{5,6},{6,5},{7,4},{8,11},{9,10},{10,... | collective-permute-start | bytes 1572872 | tf_op jit(solution)/shard_map/ppermute | solution.py:30
  339.5 29.9 %collective-permute-start.4 = (bf16[256,1024]{1,0:T(8,128)(2,1)}, bf16[256,1024]{1,0:T(8,128)(2,1)}, u32[]{:S(2)}, u32[]{:S(2)}) collective-permute-start(bf16[256,1024]{1,0:T(8,128)(2,1)} %convolution_convert_fusion.7), channel_id=1, source_target_pairs={{0,2},{1,3},{2,0},{3,1},{4,6},{5,7},{6,4},{7,5},{8,10},{9,11},{10,... | collective-permute-start | bytes 1572872 | tf_op jit(solution)/shard_map/ppermute | solution.py:30
  344.2 25.2 %collective-permute-start.5 = (bf16[256,1024]{1,0:T(8,128)(2,1)}, bf16[256,1024]{1,0:T(8,128)(2,1)}, u32[]{:S(2)}, u32[]{:S(2)}) collective-permute-start(bf16[256,1024]{1,0:T(8,128)(2,1)} %convolution_convert_fusion.6), channel_id=1, source_target_pairs={{0,1},{1,0},{2,3},{3,2},{4,5},{5,4},{6,7},{7,6},{8,9},{9,8},{10,11... | collective-permute-start | bytes 1572872 | tf_op jit(solution)/shard_map/ppermute | solution.py:30
  350.0 24.2 %collective-permute-start = (bf16[256,1024]{1,0:T(8,128)(2,1)}, bf16[256,1024]{1,0:T(8,128)(2,1)}, u32[]{:S(2)}, u32[]{:S(2)}) collective-permute-start(bf16[256,1024]{1,0:T(8,128)(2,1)} %convolution_convert_fusion.11), channel_id=1, source_target_pairs={{0,3},{1,2},{2,1},{3,0},{4,7},{5,6},{6,5},{7,4},{8,11},{9,10},{10,... | collective-permute-start | bytes 1572872 | tf_op jit(solution)/shard_map/ppermute | solution.py:30
  353.1 29.7 %collective-permute-start.1 = (bf16[256,1024]{1,0:T(8,128)(2,1)}, bf16[256,1024]{1,0:T(8,128)(2,1)}, u32[]{:S(2)}, u32[]{:S(2)}) collective-permute-start(bf16[256,1024]{1,0:T(8,128)(2,1)} %convolution_convert_fusion.10), channel_id=1, source_target_pairs={{0,2},{1,3},{2,0},{3,1},{4,6},{5,7},{6,4},{7,5},{8,10},{9,11},{10,... | collective-permute-start | bytes 1572872 | tf_op jit(solution)/shard_map/ppermute | solution.py:30
  358.1 24.8 %collective-permute-start.2 = (bf16[256,1024]{1,0:T(8,128)(2,1)}, bf16[256,1024]{1,0:T(8,128)(2,1)}, u32[]{:S(2)}, u32[]{:S(2)}) collective-permute-start(bf16[256,1024]{1,0:T(8,128)(2,1)} %convolution_convert_fusion.9), channel_id=1, source_target_pairs={{0,1},{1,0},{2,3},{3,2},{4,5},{5,4},{6,7},{7,6},{8,9},{9,8},{10,11... | collective-permute-start | bytes 1572872 | tf_op jit(solution)/shard_map/ppermute | solution.py:30
  369.4 13.4 %copy-start.5 = (f32[32,8,8,128]{3,1,2,0:T(8,128)S(1)}, f32[32,8,8,128]{3,1,2,0:T(8,128)}, u32[]{:S(2)}) copy-start(f32[32,8,8,128]{3,1,2,0:T(8,128)} %copy.51) | copy-start | bytes 3145732
  369.4 13.4 %copy-start.42 = (bf16[1024,2048]{1,0:T(8,128)(2,1)S(1)}, bf16[1024,2048]{1,0:T(8,128)(2,1)}, u32[]{:S(2)}) copy-start(bf16[1024,2048]{1,0:T(8,128)(2,1)} %get-tuple-element.72) | copy-start | bytes 12582916
  386.2 16.3 %copy-start.3 = (f32[256,1024]{1,0:T(8,128)}, f32[256,1024]{1,0:T(8,128)S(1)}, u32[]{:S(2)}) copy-start(f32[256,1024]{1,0:T(8,128)S(1)} %get-tuple-element.104) | copy-start | bytes 3145732
  387.4 26.6 %copy-start.44 = (bf16[1024,2048]{1,0:T(8,128)(2,1)S(1)}, bf16[1024,2048]{1,0:T(8,128)(2,1)}, u32[]{:S(2)}) copy-start(bf16[1024,2048]{1,0:T(8,128)(2,1)} %get-tuple-element.71) | copy-start | bytes 12582916
  387.4 14.8 %collective-permute-start.9 = (bf16[256,1024]{1,0:T(8,128)(2,1)S(1)}, bf16[256,1024]{1,0:T(8,128)(2,1)S(1)}, u32[]{:S(2)}, u32[]{:S(2)}) collective-permute-start(bf16[256,1024]{1,0:T(8,128)(2,1)S(1)} %get-tuple-element.172), channel_id=1, source_target_pairs={{0,1},{1,0},{2,3},{3,2},{4,5},{5,4},{6,7},{7,6},{8,9},{9,8},{10,11... | collective-permute-start | bytes 1572872 | tf_op jit(solution)/shard_map/ppermute | solution.py:30
  387.9 24.7 %collective-permute-start.10 = (bf16[256,1024]{1,0:T(8,128)(2,1)S(1)}, bf16[256,1024]{1,0:T(8,128)(2,1)S(1)}, u32[]{:S(2)}, u32[]{:S(2)}) collective-permute-start(bf16[256,1024]{1,0:T(8,128)(2,1)S(1)} %get-tuple-element.172), channel_id=1, source_target_pairs={{0,2},{1,3},{2,0},{3,1},{4,6},{5,7},{6,4},{7,5},{8,10},{9,11},{10,... | collective-permute-start | bytes 1572872 | tf_op jit(solution)/shard_map/ppermute | solution.py:30
  389.3 23.3 %collective-permute-start.11 = (bf16[256,1024]{1,0:T(8,128)(2,1)S(1)}, bf16[256,1024]{1,0:T(8,128)(2,1)S(1)}, u32[]{:S(2)}, u32[]{:S(2)}) collective-permute-start(bf16[256,1024]{1,0:T(8,128)(2,1)S(1)} %get-tuple-element.172), channel_id=1, source_target_pairs={{0,3},{1,2},{2,1},{3,0},{4,7},{5,6},{6,5},{7,4},{8,11},{9,10},{10,... | collective-permute-start | bytes 1572872 | tf_op jit(solution)/shard_map/ppermute | solution.py:30
  420.4 152.2 %reduce-scatter.5.cloned.1.call-start = ((), (), s32[]{:S(2)}) async-start(), calls=%async_computation.4 | async-start | bytes 4718592 | tf_op jit(solution)/shard_map/reduce_scatter | solution.py:1308
  420.4 27.5 %copy-start.45 = (bf16[1024,2048]{1,0:T(8,128)(2,1)S(1)}, bf16[1024,2048]{1,0:T(8,128)(2,1)}, u32[]{:S(2)}) copy-start(bf16[1024,2048]{1,0:T(8,128)(2,1)} %get-tuple-element.71) | copy-start | bytes 12582916
  421.4 14.9 %collective-permute-start.6 = (bf16[256,1024]{1,0:T(8,128)(2,1)S(1)}, bf16[256,1024]{1,0:T(8,128)(2,1)S(1)}, u32[]{:S(2)}, u32[]{:S(2)}) collective-permute-start(bf16[256,1024]{1,0:T(8,128)(2,1)S(1)} %copy-done.17), channel_id=1, source_target_pairs={{0,1},{1,0},{2,3},{3,2},{4,5},{5,4},{6,7},{7,6},{8,9},{9,8},{10,11... | collective-permute-start | bytes 1572872 | tf_op jit(solution)/shard_map/ppermute | solution.py:30
  423.1 21.5 %collective-permute-start.7 = (bf16[256,1024]{1,0:T(8,128)(2,1)S(1)}, bf16[256,1024]{1,0:T(8,128)(2,1)S(1)}, u32[]{:S(2)}, u32[]{:S(2)}) collective-permute-start(bf16[256,1024]{1,0:T(8,128)(2,1)S(1)} %copy-done.17), channel_id=1, source_target_pairs={{0,2},{1,3},{2,0},{3,1},{4,6},{5,7},{6,4},{7,5},{8,10},{9,11},{10,... | collective-permute-start | bytes 1572872 | tf_op jit(solution)/shard_map/ppermute | solution.py:30
  423.4 23.1 %collective-permute-start.8 = (bf16[256,1024]{1,0:T(8,128)(2,1)S(1)}, bf16[256,1024]{1,0:T(8,128)(2,1)S(1)}, u32[]{:S(2)}, u32[]{:S(2)}) collective-permute-start(bf16[256,1024]{1,0:T(8,128)(2,1)S(1)} %copy-done.17), channel_id=1, source_target_pairs={{0,3},{1,2},{2,1},{3,0},{4,7},{5,6},{6,5},{7,4},{8,11},{9,10},{10,... | collective-permute-start | bytes 1572872 | tf_op jit(solution)/shard_map/ppermute | solution.py:30
  454.7 172.9 %reduce-scatter.9.cloned.1.call-start = ((), (), s32[]{:S(2)}) async-start(), calls=%async_computation.6 | async-start | bytes 9437184 | tf_op jit(solution)/shard_map/reduce_scatter | solution.py:1308
  454.7 10.8 %copy-start.12 = (bf16[1024,1024]{1,0:T(8,128)(2,1)S(1)}, bf16[1024,1024]{1,0:T(8,128)(2,1)}, u32[]{:S(2)}) copy-start(bf16[1024,1024]{1,0:T(8,128)(2,1)} %copy-done.11) | copy-start | bytes 6291460
  454.7 10.8 %copy-start.40 = (bf16[1024,2048]{1,0:T(8,128)(2,1)S(1)}, bf16[1024,2048]{1,0:T(8,128)(2,1)}, u32[]{:S(2)}) copy-start(bf16[1024,2048]{1,0:T(8,128)(2,1)} %get-tuple-element.73) | copy-start | bytes 12582916
  493.8 218.3 %reduce-scatter.11.cloned.1.call-start = ((), (), s32[]{:S(2)}) async-start(), calls=%async_computation.7 | async-start | bytes 9437184 | tf_op jit(solution)/shard_map/reduce_scatter | solution.py:1308
  493.9 19.2 %slice-start.2 = ((s8[8388608]{0:T(1024)(128)(4,1)}), s8[4194304]{0:T(1024)(128)(4,1)S(1)}, s32[]{:S(2)}) async-start(s8[8388608]{0:T(1024)(128)(4,1)} %bitcast.147), calls=%async_computation.10 | async-start | bytes 8388608
  501.9 11.1 %slice-start.3 = ((s8[8388608]{0:T(1024)(128)(4,1)}), s8[4194304]{0:T(1024)(128)(4,1)S(1)}, s32[]{:S(2)}) async-start(s8[8388608]{0:T(1024)(128)(4,1)} %bitcast.147), calls=%async_computation.11 | async-start | bytes 8388608
  509.5 22.5 %collective-permute-start.12 = (bf16[256,1024]{1,0:T(8,128)(2,1)S(1)}, bf16[256,1024]{1,0:T(8,128)(2,1)S(1)}, u32[]{:S(2)}, u32[]{:S(2)}) collective-permute-start(bf16[256,1024]{1,0:T(8,128)(2,1)S(1)} %get-tuple-element.145), channel_id=1, source_target_pairs={{0,3},{1,2},{2,1},{3,0},{4,7},{5,6},{6,5},{7,4},{8,11},{9,10},{10,... | collective-permute-start | bytes 1572872 | tf_op jit(solution)/shard_map/ppermute | solution.py:30
  511.4 31.2 %collective-permute-start.13 = (bf16[256,1024]{1,0:T(8,128)(2,1)S(1)}, bf16[256,1024]{1,0:T(8,128)(2,1)S(1)}, u32[]{:S(2)}, u32[]{:S(2)}) collective-permute-start(bf16[256,1024]{1,0:T(8,128)(2,1)S(1)} %get-tuple-element.147), channel_id=1, source_target_pairs={{0,2},{1,3},{2,0},{3,1},{4,6},{5,7},{6,4},{7,5},{8,10},{9,11},{10,... | collective-permute-start | bytes 1572872 | tf_op jit(solution)/shard_map/ppermute | solution.py:30
  511.6 30.9 %collective-permute-start.14 = (bf16[256,1024]{1,0:T(8,128)(2,1)S(1)}, bf16[256,1024]{1,0:T(8,128)(2,1)S(1)}, u32[]{:S(2)}, u32[]{:S(2)}) collective-permute-start(bf16[256,1024]{1,0:T(8,128)(2,1)S(1)} %get-tuple-element.146), channel_id=1, source_target_pairs={{0,1},{1,0},{2,3},{3,2},{4,5},{5,4},{6,7},{7,6},{8,9},{9,8},{10,11... | collective-permute-start | bytes 1572872 | tf_op jit(solution)/shard_map/ppermute | solution.py:30
  522.2 11.4 %copy-start.26 = (f32[256,128]{1,0:T(8,128)S(1)}, f32[256,128]{1,0:T(8,128)}, u32[]{:S(2)}) copy-start(f32[256,128]{1,0:T(8,128)} %get-tuple-element.78) | copy-start | bytes 393220
  529.9 26.4 %copy-start.2 = (f32[256,2048]{1,0:T(8,128)S(1)}, f32[256,2048]{1,0:T(8,128)}, u32[]{:S(2)}) copy-start(f32[256,2048]{1,0:T(8,128)} %get-tuple-element.93) | copy-start | bytes 6291460
  530.0 17.8 %collective-permute-start.15 = (bf16[256,1024]{1,0:T(8,128)(2,1)S(1)}, bf16[256,1024]{1,0:T(8,128)(2,1)S(1)}, u32[]{:S(2)}, u32[]{:S(2)}) collective-permute-start(bf16[256,1024]{1,0:T(8,128)(2,1)S(1)} %get-tuple-element.148), channel_id=1, source_target_pairs={{0,3},{1,2},{2,1},{3,0},{4,7},{5,6},{6,5},{7,4},{8,11},{9,10},{10,... | collective-permute-start | bytes 1572872 | tf_op jit(solution)/shard_map/ppermute | solution.py:30
  531.9 23.9 %collective-permute-start.16 = (bf16[256,1024]{1,0:T(8,128)(2,1)S(1)}, bf16[256,1024]{1,0:T(8,128)(2,1)S(1)}, u32[]{:S(2)}, u32[]{:S(2)}) collective-permute-start(bf16[256,1024]{1,0:T(8,128)(2,1)S(1)} %get-tuple-element.150), channel_id=1, source_target_pairs={{0,2},{1,3},{2,0},{3,1},{4,6},{5,7},{6,4},{7,5},{8,10},{9,11},{10,... | collective-permute-start | bytes 1572872 | tf_op jit(solution)/shard_map/ppermute | solution.py:30
  532.0 23.9 %collective-permute-start.17 = (bf16[256,1024]{1,0:T(8,128)(2,1)S(1)}, bf16[256,1024]{1,0:T(8,128)(2,1)S(1)}, u32[]{:S(2)}, u32[]{:S(2)}) collective-permute-start(bf16[256,1024]{1,0:T(8,128)(2,1)S(1)} %get-tuple-element.149), channel_id=1, source_target_pairs={{0,1},{1,0},{2,3},{3,2},{4,5},{5,4},{6,7},{7,6},{8,9},{9,8},{10,11... | collective-permute-start | bytes 1572872 | tf_op jit(solution)/shard_map/ppermute | solution.py:30
  572.6 26.2 %collective-permute-start.18 = (bf16[256,2048]{1,0:T(8,128)(2,1)S(1)}, bf16[256,2048]{1,0:T(8,128)(2,1)}, u32[]{:S(2)}, u32[]{:S(2)}) collective-permute-start(bf16[256,2048]{1,0:T(8,128)(2,1)S(1)} %multiply_convert_fusion.4), channel_id=1, source_target_pairs={{0,1},{1,0},{2,3},{3,2},{4,5},{5,4},{6,7},{7,6},{8,9},{9,8},{10,11... | collective-permute-start | bytes 3145736 | tf_op jit(solution)/shard_map/ppermute | solution.py:30
  573.1 47.6 %collective-permute-start.19 = (bf16[256,2048]{1,0:T(8,128)(2,1)S(1)}, bf16[256,2048]{1,0:T(8,128)(2,1)}, u32[]{:S(2)}, u32[]{:S(2)}) collective-permute-start(bf16[256,2048]{1,0:T(8,128)(2,1)S(1)} %multiply_convert_fusion.4), channel_id=1, source_target_pairs={{0,2},{1,3},{2,0},{3,1},{4,6},{5,7},{6,4},{7,5},{8,10},{9,11},{10,... | collective-permute-start | bytes 3145736 | tf_op jit(solution)/shard_map/ppermute | solution.py:30
  576.0 46.0 %collective-permute-start.20 = (bf16[256,2048]{1,0:T(8,128)(2,1)S(1)}, bf16[256,2048]{1,0:T(8,128)(2,1)S(1)}, u32[]{:S(2)}, u32[]{:S(2)}) collective-permute-start(bf16[256,2048]{1,0:T(8,128)(2,1)S(1)} %multiply_convert_fusion.4), channel_id=1, source_target_pairs={{0,3},{1,2},{2,1},{3,0},{4,7},{5,6},{6,5},{7,4},{8,11},{9,10},{10,... | collective-permute-start | bytes 3145736 | tf_op jit(solution)/shard_map/ppermute | solution.py:30
  599.4 24.9 %copy-start.47 = (bf16[512,2048]{1,0:T(8,128)(2,1)S(1)}, bf16[512,2048]{1,0:T(8,128)(2,1)}, u32[]{:S(2)}) copy-start(bf16[512,2048]{1,0:T(8,128)(2,1)} %get-tuple-element.97) | copy-start | bytes 6291460
  627.6 23.9 %copy-start.4 = (f32[256,1024]{1,0:T(8,128)S(1)}, f32[256,1024]{1,0:T(8,128)}, u32[]{:S(2)}) copy-start(f32[256,1024]{1,0:T(8,128)} %copy-done.3) | copy-start | bytes 3145732
  648.1 20.3 %collective-permute-start.21 = (f32[2,1024]{1,0:T(2,128)}, f32[2,1024]{1,0:T(2,128)}, u32[]{:S(2)}, u32[]{:S(2)}) collective-permute-start(f32[2,1024]{1,0:T(2,128)} %pad_maximum_fusion.5), channel_id=1, source_target_pairs={{0,1},{1,0},{2,3},{3,2},{4,5},{5,4},{6,7},{7,6},{8,9},{9,8},{10,11... | collective-permute-start | bytes 24584 | tf_op jit(solution)/shard_map/ppermute | solution.py:30
  648.1 22.4 %collective-permute-start.22 = (f32[2,1024]{1,0:T(2,128)}, f32[2,1024]{1,0:T(2,128)}, u32[]{:S(2)}, u32[]{:S(2)}) collective-permute-start(f32[2,1024]{1,0:T(2,128)} %pad_maximum_fusion.5), channel_id=1, source_target_pairs={{0,2},{1,3},{2,0},{3,1},{4,6},{5,7},{6,4},{7,5},{8,10},{9,11},{10,... | collective-permute-start | bytes 24584 | tf_op jit(solution)/shard_map/ppermute | solution.py:30
  649.5 21.1 %collective-permute-start.23 = (f32[2,1024]{1,0:T(2,128)}, f32[2,1024]{1,0:T(2,128)}, u32[]{:S(2)}, u32[]{:S(2)}) collective-permute-start(f32[2,1024]{1,0:T(2,128)} %pad_maximum_fusion.5), channel_id=1, source_target_pairs={{0,3},{1,2},{2,1},{3,0},{4,7},{5,6},{6,5},{7,4},{8,11},{9,10},{10,... | collective-permute-start | bytes 24584 | tf_op jit(solution)/shard_map/ppermute | solution.py:30
  663.6 22.9 %collective-permute-start.27 = (bf16[64,2048]{1,0:T(8,128)(2,1)}, bf16[64,2048]{1,0:T(8,128)(2,1)}, u32[]{:S(2)}, u32[]{:S(2)}) collective-permute-start(bf16[64,2048]{1,0:T(8,128)(2,1)} %get-tuple-element.153), channel_id=1, source_target_pairs={{0,1},{1,0},{2,3},{3,2},{4,5},{5,4},{6,7},{7,6},{8,9},{9,8},{10,11... | collective-permute-start | bytes 786440 | tf_op jit(solution)/shard_map/ppermute | solution.py:30
  663.6 27.0 %collective-permute-start.28 = (bf16[64,2048]{1,0:T(8,128)(2,1)}, bf16[64,2048]{1,0:T(8,128)(2,1)}, u32[]{:S(2)}, u32[]{:S(2)}) collective-permute-start(bf16[64,2048]{1,0:T(8,128)(2,1)} %get-tuple-element.152), channel_id=1, source_target_pairs={{0,2},{1,3},{2,0},{3,1},{4,6},{5,7},{6,4},{7,5},{8,10},{9,11},{10,... | collective-permute-start | bytes 786440 | tf_op jit(solution)/shard_map/ppermute | solution.py:30
  668.3 24.2 %collective-permute-start.29 = (bf16[64,2048]{1,0:T(8,128)(2,1)S(1)}, bf16[64,2048]{1,0:T(8,128)(2,1)}, u32[]{:S(2)}, u32[]{:S(2)}) collective-permute-start(bf16[64,2048]{1,0:T(8,128)(2,1)S(1)} %get-tuple-element.151), channel_id=1, source_target_pairs={{0,3},{1,2},{2,1},{3,0},{4,7},{5,6},{6,5},{7,4},{8,11},{9,10},{10,... | collective-permute-start | bytes 786440 | tf_op jit(solution)/shard_map/ppermute | solution.py:30
  670.5 19.0 %collective-permute-start.24 = (bf16[64,2048]{1,0:T(8,128)(2,1)}, bf16[64,2048]{1,0:T(8,128)(2,1)}, u32[]{:S(2)}, u32[]{:S(2)}) collective-permute-start(bf16[64,2048]{1,0:T(8,128)(2,1)} %get-tuple-element.156), channel_id=1, source_target_pairs={{0,1},{1,0},{2,3},{3,2},{4,5},{5,4},{6,7},{7,6},{8,9},{9,8},{10,11... | collective-permute-start | bytes 786440 | tf_op jit(solution)/shard_map/ppermute | solution.py:30
  670.5 21.0 %collective-permute-start.25 = (bf16[64,2048]{1,0:T(8,128)(2,1)}, bf16[64,2048]{1,0:T(8,128)(2,1)}, u32[]{:S(2)}, u32[]{:S(2)}) collective-permute-start(bf16[64,2048]{1,0:T(8,128)(2,1)} %get-tuple-element.155), channel_id=1, source_target_pairs={{0,2},{1,3},{2,0},{3,1},{4,6},{5,7},{6,4},{7,5},{8,10},{9,11},{10,... | collective-permute-start | bytes 786440 | tf_op jit(solution)/shard_map/ppermute | solution.py:30
  686.5 7.3 collective-permute-start.26
  694.9 112.5 %copy-start.10 = (f32[64,8192]{1,0:T(8,128)}, f32[64,8192]{1,0:T(8,128)S(1)}, u32[]{:S(2)}) copy-start(f32[64,8192]{1,0:T(8,128)S(1)} %convert_dynamic-update-slice_fusion.4) | copy-start | bytes 6291460
  (41 other events, 192.6 us)
Sparse Core Ops, SparseCore 0:
  420.5 60.7 reduce-scatter.6
  483.6 48.1 reduce-scatter.4
  534.1 87.7 reduce-scatter.8
  624.1 87.9 reduce-scatter.10

commit v6 on v5

--- a/solution.py
+++ b/solution.py
@@ -882,13 +882,16 @@
 
     sizes = (size, size, size, size // 2, size // 2)
 
-    def spread(kind, source, whole):
+    def spread(kind, source, whole, stage=0):
         place = whole.at[lines(leaf, sizes[kind])]
         across = leaf_copy(
             source, place, line_send_sem.at[kind, 2], line_recv_sem.at[kind, 2], 2 * other(z, 2) + core
         )
-        across.start()
-        sent.append(across)
+        if stage < 2:
+            across.start()
+            sent.append(across)
+        if stage == 1:
+            return None
         forth = leaf_copy(source, place, line_send_sem.at[kind, 0], line_recv_sem.at[kind, 0], 2 * z + 2 + core)
         back = leaf_copy(source, place, line_send_sem.at[kind, 1], line_recv_sem.at[kind, 1], 2 * z - 2 + core)
 
@@ -1118,8 +1121,11 @@
     load_down.wait()
     row_landed(lambda source, hop: down_block.at[lines(source, own)], 5)
     downs = (first_out, second_out)
+    down_parts = [down_block.at[pl.ds(h * size // 2, size // 2)] for h in range(2)]
     for h in range(2):
-        done.append(spread(3 + h, down_block.at[pl.ds(h * size // 2, size // 2)], downs[h]))
+        spread(3 + h, down_parts[h], downs[h], 1)
+    for h in range(2):
+        done.append(spread(3 + h, down_parts[h], downs[h], 2))
     pass_on(2, up_out, 2)
     gathered(1, gate_out)
     gathered(2, up_out)

time: 828 us -> 828 us (level)
  no operation moved by 1% of the time
where the time goes in v6:
time: 828 us; the launch traced here: 825 us
  Pallas kernels  419 us (51%)
  matrix products  132 us (16%)
  waiting for transfers between devices  128 us (15%)
  local copies, waits for them, and re-layouts  49.1 us (6%)
  other arithmetic  46.1 us (6%)
  starting transfers between devices  35.4 us (4%)
  between operations  15.1 us (2%)
    pallas_call x1, Pallas kernels, front(): pl.pallas_call(front_kernel, in_specs=[pl.BlockSpec(memory_space=pl.ANY)]...  306 us
    dot_general x20, matrix products, dot(): lax.dot_general(left, right, dims, preferred_element_type=f32).astype(kind)  132 us
    ppermute x30, waiting for transfers between devices, swap(): return lax.ppermute(piece, 'row', [(i, i ^ hop) for i in range(count)])  110 us
    pallas_call x1, Pallas kernels, finish(): pl.pallas_call(final_kernel, in_specs=[pl.BlockSpec(memory_space=pl.ANY)]...  95.3 us
    ppermute x30, starting transfers between devices, swap(): return lax.ppermute(piece, 'row', [(i, i ^ hop) for i in range(count)])  35.3 us
    unnamed x120, local copies, waits for them, and re-layouts  22 us
    pallas_call x1, Pallas kernels, attend_back(): pl.pallas_call(functools.partial(attend_back_kernel, 256, 1.0 / math.sqrt...  17.4 us
    reduce_scatter x4, waiting for transfers between devices, leaf_scatter(): return lax.psum_scatter(block, 'leaf', scatter_dimension=0, tiled=True)  17.3 us
  transfers between devices with their start and end apart: 34, of which 13 were waited for; matrix products, arithmetic and copies ran while one was open for 21% of the time, Pallas kernels for 2%

profile of v6, /device:TPU:0, one launch (start us, length us, event | category | flops | bytes accessed | tf_op | source)
XLA Modules:
  0.0 824.5 jit_solution(11158808206212874588)
XLA Ops:
  11.6 2.7 convert_element_type.191.gate_hbm
  18.4 3.1 select_convert_fusion.bias_hbm.bias_ref
  23.2 306.0 %shard_map.246 = (bf16[2048,2048]{1,0:T(8,128)(2,1)}, bf16[2048,2048]{1,0:T(8,128)(2,1)}, bf16[2048,2048]{1,0:T(8,128)(2,1)}, bf16[1024,2048]{1,0:T(8,128)(2,1)}...) custom-call(bf16[256,2048]{1,0:T(8,128)(2,1)} %bitcast.143, ...), custom_call_target="tpu_custom_call" | custom-call | flops 10737418240 | bytes 104857600 | tf_op jit(solution)/shard_map/pallas_call | solution.py:1226
  329.2 4.6 convolution_convert_fusion.8
  334.9 4.6 convolution_convert_fusion.7
  339.5 4.7 convolution_convert_fusion.6
  344.2 2.4 collective-permute-start.5
  346.7 3.3 convolution_convert_fusion.11
  351.0 2.1 convolution_convert_fusion.10
  353.7 2.1 convolution_convert_fusion.9
  355.8 2.1 reshape.171
  360.0 6.8 slice_reduce_fusion
  369.4 4.7 multiply_reduce_fusion.4
  374.1 8.7 %collective-permute-done.1 = bf16[256,1024]{1,0:T(8,128)(2,1)} collective-permute-done((bf16[256,1024]{1,0:T(8,128)(2,1)}, bf16[256,1024]{1,0:T(8,128)(2,1)}, u32[]{:S(2)}, u32[]{:S(2)}) %collective-permute-start.1) | collective-permute-done | bytes 524320 | tf_op jit(solution)/shard_map/ppermute | solution.py:30
  382.9 3.3 multiply_reduce_fusion.5
  390.9 11.3 %collective-permute-done.9 = bf16[256,1024]{1,0:T(8,128)(2,1)S(1)} collective-permute-done((bf16[256,1024]{1,0:T(8,128)(2,1)S(1)}, bf16[256,1024]{1,0:T(8,128)(2,1)S(1)}, u32[]{:S(2)}, u32[]{:S(2)}) %collective-permute-start.9) | collective-permute-done | bytes 524320 | tf_op jit(solution)/shard_map/ppermute | solution.py:30
  402.5 10.0 %collective-permute-done.10 = bf16[256,1024]{1,0:T(8,128)(2,1)S(1)} collective-permute-done((bf16[256,1024]{1,0:T(8,128)(2,1)S(1)}, bf16[256,1024]{1,0:T(8,128)(2,1)S(1)}, u32[]{:S(2)}, u32[]{:S(2)}) %collective-permute-start.10) | collective-permute-done | bytes 524320 | tf_op jit(solution)/shard_map/ppermute | solution.py:30
  414.0 6.3 convolution_convert_fusion.2
  424.9 11.4 %collective-permute-done.6 = bf16[256,1024]{1,0:T(8,128)(2,1)S(1)} collective-permute-done((bf16[256,1024]{1,0:T(8,128)(2,1)S(1)}, bf16[256,1024]{1,0:T(8,128)(2,1)S(1)}, u32[]{:S(2)}, u32[]{:S(2)}) %collective-permute-start.6) | collective-permute-done | bytes 524320 | tf_op jit(solution)/shard_map/ppermute | solution.py:30
  436.6 8.0 collective-permute-done.7
  448.0 6.7 convolution_convert_fusion.3
  454.7 10.8 %fusion.46 = f32[1024,2048]{1,0:T(8,128)} fusion(bf16[1024,1024]{1,0:T(8,128)(2,1)} %copy-done.13, bf16[1024,2048]{1,0:T(8,128)(2,1)} %get-tuple-element.72), kind=kOutput, calls=%fused_computation.155 | convolution fusion | flops 4294967296 | bytes 14680064 | tf_op jit(solution)/shard_map/dot_general | solution.py:25
  465.5 14.2 %multiply_convert_fusion.1 = (bf16[1024,2048]{1,0:T(8,128)(2,1)}, bf16[1024,2048]{1,0:T(8,128)(2,1)}) fusion(f32[1024,2048]{1,0:T(8,128)} %get-tuple-element.86, f32[1024,2048]{1,0:T(8,128)} %get-tuple-element.85, f32[1024,2048]{1,0:T(8,128)} %fusion.46, bf16[1024,1024]{1,0:T(8,128)(2,1)S(1)} %copy-done.12, bf16[1024,2048]{1,0:T(8,128)(2,1)S(1)} %copy-done.40), kind=kOutput, calls=%fused_computation.1 | convolution fusion | flops 4324327424 | bytes 39845888 | tf_op jit(solution)/shard_map/dot_general | solution.py:25
  479.8 14.1 %convolution_convert_fusion.1 = bf16[2048,2048]{1,0:T(8,128)(2,1)} fusion(bf16[1024,2048]{1,0:T(8,128)(2,1)} %get-tuple-element.80, bf16[1024,2048]{1,0:T(8,128)(2,1)} %get-tuple-element.91), kind=kOutput, calls=%fused_computation.4 | convolution fusion | flops 8594128896 | bytes 16777216 | tf_op jit(solution)/shard_map/dot_general | solution.py:25
  493.9 8.0 fusion.4
  501.9 7.4 add_convert_fusion.1
  513.1 9.1 %fusion = f32[1024,1024]{1,0:T(8,128)} fusion(bf16[1024,2048]{1,0:T(8,128)(2,1)} %get-tuple-element.95, bf16[2048,2048]{1,0:T(8,128)(2,1)S(1)} %bitcast.148), kind=kOutput, calls=%fused_computation.6 | convolution fusion | flops 4294967296 | bytes 12582912 | tf_op jit(solution)/shard_map/dot_general | solution.py:25
  522.2 7.7 add_convert_fusion
  533.7 8.9 %collective-permute-done.13 = bf16[256,1024]{1,0:T(8,128)(2,1)S(1)} collective-permute-done((bf16[256,1024]{1,0:T(8,128)(2,1)S(1)}, bf16[256,1024]{1,0:T(8,128)(2,1)S(1)}, u32[]{:S(2)}, u32[]{:S(2)}) %collective-permute-start.13) | collective-permute-done | bytes 524320 | tf_op jit(solution)/shard_map/ppermute | solution.py:30
  542.9 4.9 collective-permute-done.15
  547.8 8.0 collective-permute-done.16
  560.8 11.6 %convolution_convert_fusion = bf16[2048,2048]{1,0:T(8,128)(2,1)} fusion(bf16[1024,2048]{1,0:T(8,128)(2,1)S(1)} %copy-done.50, bf16[1024,2048]{1,0:T(8,128)(2,1)S(1)} %copy-done.49), kind=kOutput, calls=%fused_computation.3 | convolution fusion | flops 8594128896 | bytes 16777216 | tf_op jit(solution)/shard_map/dot_general | solution.py:25
  579.0 2.4 pad_maximum_fusion.2
  581.4 17.4 %collective-permute-done.18 = bf16[256,2048]{1,0:T(8,128)(2,1)} collective-permute-done((bf16[256,2048]{1,0:T(8,128)(2,1)S(1)}, bf16[256,2048]{1,0:T(8,128)(2,1)}, u32[]{:S(2)}, u32[]{:S(2)}) %collective-permute-start.18) | collective-permute-done | bytes 1048608 | tf_op jit(solution)/shard_map/ppermute | solution.py:30
  600.8 19.8 %collective-permute-done.19 = bf16[256,2048]{1,0:T(8,128)(2,1)} collective-permute-done((bf16[256,2048]{1,0:T(8,128)(2,1)S(1)}, bf16[256,2048]{1,0:T(8,128)(2,1)}, u32[]{:S(2)}, u32[]{:S(2)}) %collective-permute-start.19) | collective-permute-done | bytes 1048608 | tf_op jit(solution)/shard_map/ppermute | solution.py:30
  624.2 3.3 convolution_convert_fusion.5.grad_ref
  627.6 17.4 %shard_map.247 = (f32[1024,512]{1,0:T(8,128)}, f32[1024,512]{1,0:T(8,128)}, bf16[1024,512]{1,0:T(8,128)(2,1)}, f32[1024,128]{1,0:T(8,128)}, f32[1024,128]{1,0:T(8,128)}, /*index=5*/f32[2,512]{1,0:T(2,128)}) custom-call(bf16[1024,512]{1,0:T(8,128)(2,1)} %get-tuple-element.74.query_ref, bf16[1024,512]{1,0:T(8,128)(2,1)} %get-tuple-element.75.key_ref, ...), custom_call_target="tpu_custom_call" | custom-call | flops 5368709120 | bytes 15728640 | tf_op jit(solution)/shard_map/pallas_call | solution.py:314
  649.4 2.2 collective-permute-start.23
  652.0 3.2 pad_maximum_fusion.1
  655.2 3.0 reshape.165
  658.2 3.2 fusion.9
  668.3 2.2 collective-permute-start.29
  676.7 2.8 multiply_convert_fusion.3
  680.7 3.8 convolution_convert_fusion.4
  686.4 2.1 collective-permute-start.26
  695.0 17.2 %reduce-scatter.11.cloned.1.call-done.up_hbm = bf16[256,2048]{1,0:T(8,128)(2,1)} async-done(((bf16[2048,2048]{1,0:T(8,128)(2,1)}), bf16[256,2048]{1,0:T(8,128)(2,1)}) %reduce-scatter.11.cloned.1.call-update) | async-done | bytes 1048592 | tf_op jit(solution)/shard_map/reduce_scatter | solution.py:1314
  712.2 95.3 %shard_map.248 = (f32[64,2048]{1,0:T(8,128)}, f32[64,2048]{1,0:T(8,128)}, f32[64,2048]{1,0:T(8,128)}, f32[64,2048]{1,0:T(8,128)}, bf16[256,2048]{1,0:T(8,128)(2,...) custom-call(bf16[1024,2048]{1,0:T(8,128)(2,1)} %get-tuple-element.106.tokens_hbm, ...), custom_call_target="tpu_custom_call" | custom-call | flops 12884901888 | bytes 104857600 | tf_op jit(solution)/shard_map/pallas_call | solution.py:662
  808.9 2.3 copy.84
  (264 shorter events, 92.2 us)
Async XLA Ops:
  7.2 565.3 %reduce-scatter.7.cloned.1.call-start = ((), (), s32[]{:S(2)}) async-start(), calls=%async_computation.5 | async-start | bytes 4718592 | tf_op jit(solution)/shard_map/reduce_scatter | solution.py:1314
  333.8 24.2 %collective-permute-start.3 = (bf16[256,1024]{1,0:T(8,128)(2,1)}, bf16[256,1024]{1,0:T(8,128)(2,1)}, u32[]{:S(2)}, u32[]{:S(2)}) collective-permute-start(bf16[256,1024]{1,0:T(8,128)(2,1)} %convolution_convert_fusion.8), channel_id=1, source_target_pairs={{0,3},{1,2},{2,1},{3,0},{4,7},{5,6},{6,5},{7,4},{8,11},{9,10},{10,... | collective-permute-start | bytes 1572872 | tf_op jit(solution)/shard_map/ppermute | solution.py:30
  339.5 29.9 %collective-permute-start.4 = (bf16[256,1024]{1,0:T(8,128)(2,1)}, bf16[256,1024]{1,0:T(8,128)(2,1)}, u32[]{:S(2)}, u32[]{:S(2)}) collective-permute-start(bf16[256,1024]{1,0:T(8,128)(2,1)} %convolution_convert_fusion.7), channel_id=1, source_target_pairs={{0,2},{1,3},{2,0},{3,1},{4,6},{5,7},{6,4},{7,5},{8,10},{9,11},{10,... | collective-permute-start | bytes 1572872 | tf_op jit(solution)/shard_map/ppermute | solution.py:30
  344.2 25.2 %collective-permute-start.5 = (bf16[256,1024]{1,0:T(8,128)(2,1)}, bf16[256,1024]{1,0:T(8,128)(2,1)}, u32[]{:S(2)}, u32[]{:S(2)}) collective-permute-start(bf16[256,1024]{1,0:T(8,128)(2,1)} %convolution_convert_fusion.6), channel_id=1, source_target_pairs={{0,1},{1,0},{2,3},{3,2},{4,5},{5,4},{6,7},{7,6},{8,9},{9,8},{10,11... | collective-permute-start | bytes 1572872 | tf_op jit(solution)/shard_map/ppermute | solution.py:30
  350.0 24.2 %collective-permute-start = (bf16[256,1024]{1,0:T(8,128)(2,1)}, bf16[256,1024]{1,0:T(8,128)(2,1)}, u32[]{:S(2)}, u32[]{:S(2)}) collective-permute-start(bf16[256,1024]{1,0:T(8,128)(2,1)} %convolution_convert_fusion.11), channel_id=1, source_target_pairs={{0,3},{1,2},{2,1},{3,0},{4,7},{5,6},{6,5},{7,4},{8,11},{9,10},{10,... | collective-permute-start | bytes 1572872 | tf_op jit(solution)/shard_map/ppermute | solution.py:30
  353.1 29.7 %collective-permute-start.1 = (bf16[256,1024]{1,0:T(8,128)(2,1)}, bf16[256,1024]{1,0:T(8,128)(2,1)}, u32[]{:S(2)}, u32[]{:S(2)}) collective-permute-start(bf16[256,1024]{1,0:T(8,128)(2,1)} %convolution_convert_fusion.10), channel_id=1, source_target_pairs={{0,2},{1,3},{2,0},{3,1},{4,6},{5,7},{6,4},{7,5},{8,10},{9,11},{10,... | collective-permute-start | bytes 1572872 | tf_op jit(solution)/shard_map/ppermute | solution.py:30
  358.1 24.8 %collective-permute-start.2 = (bf16[256,1024]{1,0:T(8,128)(2,1)}, bf16[256,1024]{1,0:T(8,128)(2,1)}, u32[]{:S(2)}, u32[]{:S(2)}) collective-permute-start(bf16[256,1024]{1,0:T(8,128)(2,1)} %convolution_convert_fusion.9), channel_id=1, source_target_pairs={{0,1},{1,0},{2,3},{3,2},{4,5},{5,4},{6,7},{7,6},{8,9},{9,8},{10,11... | collective-permute-start | bytes 1572872 | tf_op jit(solution)/shard_map/ppermute | solution.py:30
  369.4 13.4 %copy-start.5 = (f32[32,8,8,128]{3,1,2,0:T(8,128)S(1)}, f32[32,8,8,128]{3,1,2,0:T(8,128)}, u32[]{:S(2)}) copy-start(f32[32,8,8,128]{3,1,2,0:T(8,128)} %copy.51) | copy-start | bytes 3145732
  369.4 13.4 %copy-start.42 = (bf16[1024,2048]{1,0:T(8,128)(2,1)S(1)}, bf16[1024,2048]{1,0:T(8,128)(2,1)}, u32[]{:S(2)}) copy-start(bf16[1024,2048]{1,0:T(8,128)(2,1)} %get-tuple-element.72) | copy-start | bytes 12582916
  386.2 16.3 %copy-start.3 = (f32[256,1024]{1,0:T(8,128)}, f32[256,1024]{1,0:T(8,128)S(1)}, u32[]{:S(2)}) copy-start(f32[256,1024]{1,0:T(8,128)S(1)} %get-tuple-element.104) | copy-start | bytes 3145732
  387.4 26.6 %copy-start.44 = (bf16[1024,2048]{1,0:T(8,128)(2,1)S(1)}, bf16[1024,2048]{1,0:T(8,128)(2,1)}, u32[]{:S(2)}) copy-start(bf16[1024,2048]{1,0:T(8,128)(2,1)} %get-tuple-element.71) | copy-start | bytes 12582916
  387.4 14.8 %collective-permute-start.9 = (bf16[256,1024]{1,0:T(8,128)(2,1)S(1)}, bf16[256,1024]{1,0:T(8,128)(2,1)S(1)}, u32[]{:S(2)}, u32[]{:S(2)}) collective-permute-start(bf16[256,1024]{1,0:T(8,128)(2,1)S(1)} %get-tuple-element.172), channel_id=1, source_target_pairs={{0,1},{1,0},{2,3},{3,2},{4,5},{5,4},{6,7},{7,6},{8,9},{9,8},{10,11... | collective-permute-start | bytes 1572872 | tf_op jit(solution)/shard_map/ppermute | solution.py:30
  387.9 24.7 %collective-permute-start.10 = (bf16[256,1024]{1,0:T(8,128)(2,1)S(1)}, bf16[256,1024]{1,0:T(8,128)(2,1)S(1)}, u32[]{:S(2)}, u32[]{:S(2)}) collective-permute-start(bf16[256,1024]{1,0:T(8,128)(2,1)S(1)} %get-tuple-element.172), channel_id=1, source_target_pairs={{0,2},{1,3},{2,0},{3,1},{4,6},{5,7},{6,4},{7,5},{8,10},{9,11},{10,... | collective-permute-start | bytes 1572872 | tf_op jit(solution)/shard_map/ppermute | solution.py:30
  389.3 23.3 %collective-permute-start.11 = (bf16[256,1024]{1,0:T(8,128)(2,1)S(1)}, bf16[256,1024]{1,0:T(8,128)(2,1)S(1)}, u32[]{:S(2)}, u32[]{:S(2)}) collective-permute-start(bf16[256,1024]{1,0:T(8,128)(2,1)S(1)} %get-tuple-element.172), channel_id=1, source_target_pairs={{0,3},{1,2},{2,1},{3,0},{4,7},{5,6},{6,5},{7,4},{8,11},{9,10},{10,... | collective-permute-start | bytes 1572872 | tf_op jit(solution)/shard_map/ppermute | solution.py:30
  420.4 152.2 %reduce-scatter.5.cloned.1.call-start = ((), (), s32[]{:S(2)}) async-start(), calls=%async_computation.4 | async-start | bytes 4718592 | tf_op jit(solution)/shard_map/reduce_scatter | solution.py:1314
  420.4 27.5 %copy-start.45 = (bf16[1024,2048]{1,0:T(8,128)(2,1)S(1)}, bf16[1024,2048]{1,0:T(8,128)(2,1)}, u32[]{:S(2)}) copy-start(bf16[1024,2048]{1,0:T(8,128)(2,1)} %get-tuple-element.71) | copy-start | bytes 12582916
  421.4 14.9 %collective-permute-start.6 = (bf16[256,1024]{1,0:T(8,128)(2,1)S(1)}, bf16[256,1024]{1,0:T(8,128)(2,1)S(1)}, u32[]{:S(2)}, u32[]{:S(2)}) collective-permute-start(bf16[256,1024]{1,0:T(8,128)(2,1)S(1)} %copy-done.17), channel_id=1, source_target_pairs={{0,1},{1,0},{2,3},{3,2},{4,5},{5,4},{6,7},{7,6},{8,9},{9,8},{10,11... | collective-permute-start | bytes 1572872 | tf_op jit(solution)/shard_map/ppermute | solution.py:30
  423.1 21.5 %collective-permute-start.7 = (bf16[256,1024]{1,0:T(8,128)(2,1)S(1)}, bf16[256,1024]{1,0:T(8,128)(2,1)S(1)}, u32[]{:S(2)}, u32[]{:S(2)}) collective-permute-start(bf16[256,1024]{1,0:T(8,128)(2,1)S(1)} %copy-done.17), channel_id=1, source_target_pairs={{0,2},{1,3},{2,0},{3,1},{4,6},{5,7},{6,4},{7,5},{8,10},{9,11},{10,... | collective-permute-start | bytes 1572872 | tf_op jit(solution)/shard_map/ppermute | solution.py:30
  423.4 23.1 %collective-permute-start.8 = (bf16[256,1024]{1,0:T(8,128)(2,1)S(1)}, bf16[256,1024]{1,0:T(8,128)(2,1)S(1)}, u32[]{:S(2)}, u32[]{:S(2)}) collective-permute-start(bf16[256,1024]{1,0:T(8,128)(2,1)S(1)} %copy-done.17), channel_id=1, source_target_pairs={{0,3},{1,2},{2,1},{3,0},{4,7},{5,6},{6,5},{7,4},{8,11},{9,10},{10,... | collective-permute-start | bytes 1572872 | tf_op jit(solution)/shard_map/ppermute | solution.py:30
  454.7 172.9 %reduce-scatter.9.cloned.1.call-start = ((), (), s32[]{:S(2)}) async-start(), calls=%async_computation.6 | async-start | bytes 9437184 | tf_op jit(solution)/shard_map/reduce_scatter | solution.py:1314
  454.7 10.8 %copy-start.12 = (bf16[1024,1024]{1,0:T(8,128)(2,1)S(1)}, bf16[1024,1024]{1,0:T(8,128)(2,1)}, u32[]{:S(2)}) copy-start(bf16[1024,1024]{1,0:T(8,128)(2,1)} %copy-done.11) | copy-start | bytes 6291460
  454.7 10.8 %copy-start.40 = (bf16[1024,2048]{1,0:T(8,128)(2,1)S(1)}, bf16[1024,2048]{1,0:T(8,128)(2,1)}, u32[]{:S(2)}) copy-start(bf16[1024,2048]{1,0:T(8,128)(2,1)} %get-tuple-element.73) | copy-start | bytes 12582916
  493.8 218.3 %reduce-scatter.11.cloned.1.call-start = ((), (), s32[]{:S(2)}) async-start(), calls=%async_computation.7 | async-start | bytes 9437184 | tf_op jit(solution)/shard_map/reduce_scatter | solution.py:1314
  493.9 19.2 %slice-start.2 = ((s8[8388608]{0:T(1024)(128)(4,1)}), s8[4194304]{0:T(1024)(128)(4,1)S(1)}, s32[]{:S(2)}) async-start(s8[8388608]{0:T(1024)(128)(4,1)} %bitcast.147), calls=%async_computation.10 | async-start | bytes 8388608
  501.9 11.2 %slice-start.3 = ((s8[8388608]{0:T(1024)(128)(4,1)}), s8[4194304]{0:T(1024)(128)(4,1)S(1)}, s32[]{:S(2)}) async-start(s8[8388608]{0:T(1024)(128)(4,1)} %bitcast.147), calls=%async_computation.11 | async-start | bytes 8388608
  509.5 22.5 %collective-permute-start.12 = (bf16[256,1024]{1,0:T(8,128)(2,1)S(1)}, bf16[256,1024]{1,0:T(8,128)(2,1)S(1)}, u32[]{:S(2)}, u32[]{:S(2)}) collective-permute-start(bf16[256,1024]{1,0:T(8,128)(2,1)S(1)} %get-tuple-element.145), channel_id=1, source_target_pairs={{0,3},{1,2},{2,1},{3,0},{4,7},{5,6},{6,5},{7,4},{8,11},{9,10},{10,... | collective-permute-start | bytes 1572872 | tf_op jit(solution)/shard_map/ppermute | solution.py:30
  511.4 31.2 %collective-permute-start.13 = (bf16[256,1024]{1,0:T(8,128)(2,1)S(1)}, bf16[256,1024]{1,0:T(8,128)(2,1)S(1)}, u32[]{:S(2)}, u32[]{:S(2)}) collective-permute-start(bf16[256,1024]{1,0:T(8,128)(2,1)S(1)} %get-tuple-element.147), channel_id=1, source_target_pairs={{0,2},{1,3},{2,0},{3,1},{4,6},{5,7},{6,4},{7,5},{8,10},{9,11},{10,... | collective-permute-start | bytes 1572872 | tf_op jit(solution)/shard_map/ppermute | solution.py:30
  511.6 30.9 %collective-permute-start.14 = (bf16[256,1024]{1,0:T(8,128)(2,1)S(1)}, bf16[256,1024]{1,0:T(8,128)(2,1)S(1)}, u32[]{:S(2)}, u32[]{:S(2)}) collective-permute-start(bf16[256,1024]{1,0:T(8,128)(2,1)S(1)} %get-tuple-element.146), channel_id=1, source_target_pairs={{0,1},{1,0},{2,3},{3,2},{4,5},{5,4},{6,7},{7,6},{8,9},{9,8},{10,11... | collective-permute-start | bytes 1572872 | tf_op jit(solution)/shard_map/ppermute | solution.py:30
  522.2 11.4 %copy-start.26 = (f32[256,128]{1,0:T(8,128)S(1)}, f32[256,128]{1,0:T(8,128)}, u32[]{:S(2)}) copy-start(f32[256,128]{1,0:T(8,128)} %get-tuple-element.78) | copy-start | bytes 393220
  529.9 26.3 %copy-start.2 = (f32[256,2048]{1,0:T(8,128)S(1)}, f32[256,2048]{1,0:T(8,128)}, u32[]{:S(2)}) copy-start(f32[256,2048]{1,0:T(8,128)} %get-tuple-element.93) | copy-start | bytes 6291460
  530.0 17.8 %collective-permute-start.15 = (bf16[256,1024]{1,0:T(8,128)(2,1)S(1)}, bf16[256,1024]{1,0:T(8,128)(2,1)S(1)}, u32[]{:S(2)}, u32[]{:S(2)}) collective-permute-start(bf16[256,1024]{1,0:T(8,128)(2,1)S(1)} %get-tuple-element.148), channel_id=1, source_target_pairs={{0,3},{1,2},{2,1},{3,0},{4,7},{5,6},{6,5},{7,4},{8,11},{9,10},{10,... | collective-permute-start | bytes 1572872 | tf_op jit(solution)/shard_map/ppermute | solution.py:30
  531.9 23.9 %collective-permute-start.16 = (bf16[256,1024]{1,0:T(8,128)(2,1)S(1)}, bf16[256,1024]{1,0:T(8,128)(2,1)S(1)}, u32[]{:S(2)}, u32[]{:S(2)}) collective-permute-start(bf16[256,1024]{1,0:T(8,128)(2,1)S(1)} %get-tuple-element.150), channel_id=1, source_target_pairs={{0,2},{1,3},{2,0},{3,1},{4,6},{5,7},{6,4},{7,5},{8,10},{9,11},{10,... | collective-permute-start | bytes 1572872 | tf_op jit(solution)/shard_map/ppermute | solution.py:30
  531.9 23.9 %collective-permute-start.17 = (bf16[256,1024]{1,0:T(8,128)(2,1)S(1)}, bf16[256,1024]{1,0:T(8,128)(2,1)S(1)}, u32[]{:S(2)}, u32[]{:S(2)}) collective-permute-start(bf16[256,1024]{1,0:T(8,128)(2,1)S(1)} %get-tuple-element.149), channel_id=1, source_target_pairs={{0,1},{1,0},{2,3},{3,2},{4,5},{5,4},{6,7},{7,6},{8,9},{9,8},{10,11... | collective-permute-start | bytes 1572872 | tf_op jit(solution)/shard_map/ppermute | solution.py:30
  572.6 26.2 %collective-permute-start.18 = (bf16[256,2048]{1,0:T(8,128)(2,1)S(1)}, bf16[256,2048]{1,0:T(8,128)(2,1)}, u32[]{:S(2)}, u32[]{:S(2)}) collective-permute-start(bf16[256,2048]{1,0:T(8,128)(2,1)S(1)} %multiply_convert_fusion.4), channel_id=1, source_target_pairs={{0,1},{1,0},{2,3},{3,2},{4,5},{5,4},{6,7},{7,6},{8,9},{9,8},{10,11... | collective-permute-start | bytes 3145736 | tf_op jit(solution)/shard_map/ppermute | solution.py:30
  573.1 47.6 %collective-permute-start.19 = (bf16[256,2048]{1,0:T(8,128)(2,1)S(1)}, bf16[256,2048]{1,0:T(8,128)(2,1)}, u32[]{:S(2)}, u32[]{:S(2)}) collective-permute-start(bf16[256,2048]{1,0:T(8,128)(2,1)S(1)} %multiply_convert_fusion.4), channel_id=1, source_target_pairs={{0,2},{1,3},{2,0},{3,1},{4,6},{5,7},{6,4},{7,5},{8,10},{9,11},{10,... | collective-permute-start | bytes 3145736 | tf_op jit(solution)/shard_map/ppermute | solution.py:30
  576.0 46.0 %collective-permute-start.20 = (bf16[256,2048]{1,0:T(8,128)(2,1)S(1)}, bf16[256,2048]{1,0:T(8,128)(2,1)S(1)}, u32[]{:S(2)}, u32[]{:S(2)}) collective-permute-start(bf16[256,2048]{1,0:T(8,128)(2,1)S(1)} %multiply_convert_fusion.4), channel_id=1, source_target_pairs={{0,3},{1,2},{2,1},{3,0},{4,7},{5,6},{6,5},{7,4},{8,11},{9,10},{10,... | collective-permute-start | bytes 3145736 | tf_op jit(solution)/shard_map/ppermute | solution.py:30
  599.3 24.9 %copy-start.47 = (bf16[512,2048]{1,0:T(8,128)(2,1)S(1)}, bf16[512,2048]{1,0:T(8,128)(2,1)}, u32[]{:S(2)}) copy-start(bf16[512,2048]{1,0:T(8,128)(2,1)} %get-tuple-element.97) | copy-start | bytes 6291460
  627.6 24.0 %copy-start.4 = (f32[256,1024]{1,0:T(8,128)S(1)}, f32[256,1024]{1,0:T(8,128)}, u32[]{:S(2)}) copy-start(f32[256,1024]{1,0:T(8,128)} %copy-done.3) | copy-start | bytes 3145732
  648.1 20.2 %collective-permute-start.21 = (f32[2,1024]{1,0:T(2,128)}, f32[2,1024]{1,0:T(2,128)}, u32[]{:S(2)}, u32[]{:S(2)}) collective-permute-start(f32[2,1024]{1,0:T(2,128)} %pad_maximum_fusion.5), channel_id=1, source_target_pairs={{0,1},{1,0},{2,3},{3,2},{4,5},{5,4},{6,7},{7,6},{8,9},{9,8},{10,11... | collective-permute-start | bytes 24584 | tf_op jit(solution)/shard_map/ppermute | solution.py:30
  648.1 22.4 %collective-permute-start.22 = (f32[2,1024]{1,0:T(2,128)}, f32[2,1024]{1,0:T(2,128)}, u32[]{:S(2)}, u32[]{:S(2)}) collective-permute-start(f32[2,1024]{1,0:T(2,128)} %pad_maximum_fusion.5), channel_id=1, source_target_pairs={{0,2},{1,3},{2,0},{3,1},{4,6},{5,7},{6,4},{7,5},{8,10},{9,11},{10,... | collective-permute-start | bytes 24584 | tf_op jit(solution)/shard_map/ppermute | solution.py:30
  649.4 21.1 %collective-permute-start.23 = (f32[2,1024]{1,0:T(2,128)}, f32[2,1024]{1,0:T(2,128)}, u32[]{:S(2)}, u32[]{:S(2)}) collective-permute-start(f32[2,1024]{1,0:T(2,128)} %pad_maximum_fusion.5), channel_id=1, source_target_pairs={{0,3},{1,2},{2,1},{3,0},{4,7},{5,6},{6,5},{7,4},{8,11},{9,10},{10,... | collective-permute-start | bytes 24584 | tf_op jit(solution)/shard_map/ppermute | solution.py:30
  663.6 22.8 %collective-permute-start.27 = (bf16[64,2048]{1,0:T(8,128)(2,1)}, bf16[64,2048]{1,0:T(8,128)(2,1)}, u32[]{:S(2)}, u32[]{:S(2)}) collective-permute-start(bf16[64,2048]{1,0:T(8,128)(2,1)} %get-tuple-element.153), channel_id=1, source_target_pairs={{0,1},{1,0},{2,3},{3,2},{4,5},{5,4},{6,7},{7,6},{8,9},{9,8},{10,11... | collective-permute-start | bytes 786440 | tf_op jit(solution)/shard_map/ppermute | solution.py:30
  663.6 27.0 %collective-permute-start.28 = (bf16[64,2048]{1,0:T(8,128)(2,1)}, bf16[64,2048]{1,0:T(8,128)(2,1)}, u32[]{:S(2)}, u32[]{:S(2)}) collective-permute-start(bf16[64,2048]{1,0:T(8,128)(2,1)} %get-tuple-element.152), channel_id=1, source_target_pairs={{0,2},{1,3},{2,0},{3,1},{4,6},{5,7},{6,4},{7,5},{8,10},{9,11},{10,... | collective-permute-start | bytes 786440 | tf_op jit(solution)/shard_map/ppermute | solution.py:30
  668.3 24.3 %collective-permute-start.29 = (bf16[64,2048]{1,0:T(8,128)(2,1)S(1)}, bf16[64,2048]{1,0:T(8,128)(2,1)}, u32[]{:S(2)}, u32[]{:S(2)}) collective-permute-start(bf16[64,2048]{1,0:T(8,128)(2,1)S(1)} %get-tuple-element.151), channel_id=1, source_target_pairs={{0,3},{1,2},{2,1},{3,0},{4,7},{5,6},{6,5},{7,4},{8,11},{9,10},{10,... | collective-permute-start | bytes 786440 | tf_op jit(solution)/shard_map/ppermute | solution.py:30
  670.5 19.0 %collective-permute-start.24 = (bf16[64,2048]{1,0:T(8,128)(2,1)}, bf16[64,2048]{1,0:T(8,128)(2,1)}, u32[]{:S(2)}, u32[]{:S(2)}) collective-permute-start(bf16[64,2048]{1,0:T(8,128)(2,1)} %get-tuple-element.156), channel_id=1, source_target_pairs={{0,1},{1,0},{2,3},{3,2},{4,5},{5,4},{6,7},{7,6},{8,9},{9,8},{10,11... | collective-permute-start | bytes 786440 | tf_op jit(solution)/shard_map/ppermute | solution.py:30
  670.5 21.1 %collective-permute-start.25 = (bf16[64,2048]{1,0:T(8,128)(2,1)}, bf16[64,2048]{1,0:T(8,128)(2,1)}, u32[]{:S(2)}, u32[]{:S(2)}) collective-permute-start(bf16[64,2048]{1,0:T(8,128)(2,1)} %get-tuple-element.155), channel_id=1, source_target_pairs={{0,2},{1,3},{2,0},{3,1},{4,6},{5,7},{6,4},{7,5},{8,10},{9,11},{10,... | collective-permute-start | bytes 786440 | tf_op jit(solution)/shard_map/ppermute | solution.py:30
  686.4 7.3 collective-permute-start.26
  695.0 112.5 %copy-start.10 = (f32[64,8192]{1,0:T(8,128)}, f32[64,8192]{1,0:T(8,128)S(1)}, u32[]{:S(2)}) copy-start(f32[64,8192]{1,0:T(8,128)S(1)} %convert_dynamic-update-slice_fusion.4) | copy-start | bytes 6291460
  (41 other events, 192.6 us)
Sparse Core Ops, SparseCore 0:
  420.5 60.8 reduce-scatter.6
  483.7 48.1 reduce-scatter.4
  534.2 87.7 reduce-scatter.8
  624.2 87.9 reduce-scatter.10
